TPU v7x, 32 devices: a whole 2x2x4 slice. The times are simulated.
32 devices in a mesh: row: 4 (over y, core), col: 8 (over z, x).
Axes of the slice: x: 2, y: 2, z: 4, core: 2. Of those that a mesh axis runs over, the one named last changes fastest.
Arguments:
- amplitudes: bfloat16 [2048, 1024], P('row', 'col'), may hold values from -6 to 6
- packed_tiles: bfloat16 [4, 128, 128, 128], P('row', 'col'), may hold values from -0.1875 to 0.1875
- tile_ids: int32 [4, 128], P('row', 'col'), may hold values from 0 to 127, as said below
- residual_in: float32 [2048, 8192], P('row', 'col'), may hold values from -6 to 6
Outputs:
- ladder: float32 [2048, 8192], P('row', 'col')
Inputs may be any that keep to these rules, and one draw needn't show every extreme that they name: `tile_ids`: in each grid row the ids are a permutation of 0 to 127; no device holds more than 2 ids of one value of id // 16, and some device holds exactly 2.
All inputs are finite; a program needn't handle non-finite values.
Results may differ from a plain program's by a relative error of at most 0.0003.
Values may be sent and summed in bfloat16 or wider, within the bound.
No kernel may reach another device: no remote copies, remote signals or barrier semaphores. Data moves between devices by JAX's collectives and lax.ppermute only.
A program may use at most 64 MiB of HBM per device.

v0:
```python
import jax
import jax.numpy as jnp
from jax import lax
from jax.sharding import PartitionSpec as P

KT_DEV = 2
QT_DEV = 8


def body(amplitudes, packed_tiles, tile_ids, residual_in):
    col_count = lax.axis_size("col")
    col_index = lax.axis_index("col")
    per_device = packed_tiles.shape[1]
    tile_width = packed_tiles.shape[2]
    capacity = (per_device + col_count - 1) // col_count
    slot_total = col_count * capacity
    own_ids = tile_ids[0]
    target_col = own_ids // per_device
    earlier = jnp.arange(per_device)[:, None] > jnp.arange(per_device)[None, :]
    same_target = target_col[:, None] == target_col[None, :]
    order_rank = jnp.sum(earlier & same_target, axis=1)
    slot_of = target_col * capacity + order_rank
    chooser = (jnp.arange(slot_total)[:, None] == slot_of[None, :]).astype(jnp.float32)
    outgoing = jnp.einsum(
        "sl,lij->sij",
        chooser.astype(jnp.bfloat16),
        packed_tiles[0],
        preferred_element_type=jnp.float32,
    )
    outgoing = outgoing.astype(jnp.bfloat16).reshape(col_count, capacity, tile_width, tile_width)
    all_ids = lax.all_gather(tile_ids, "col", axis=1, tiled=True)[0]
    incoming = lax.all_to_all(outgoing, "col", split_axis=0, concat_axis=0, tiled=True)
    source_ids = all_ids.reshape(col_count, per_device)
    source_target = source_ids // per_device
    source_same = source_target[:, :, None] == source_target[:, None, :]
    source_rank = jnp.sum(source_same & earlier[None], axis=2)
    source_slot = (jnp.arange(col_count)[:, None] * capacity + source_rank).reshape(-1)
    for_me = (source_target == col_index).reshape(-1)
    source_pos = (source_ids % per_device).reshape(-1)
    pos_table = ((jnp.arange(per_device)[:, None] == source_pos[None, :]) & for_me[None, :]).astype(
        jnp.float32
    )
    slot_table = (jnp.arange(slot_total)[:, None] == source_slot[None, :]).astype(jnp.float32)
    unpack = jnp.dot(pos_table, slot_table.T)
    unpacked = jnp.einsum(
        "ps,sij->pij",
        unpack.astype(jnp.bfloat16),
        incoming.reshape(slot_total, tile_width, tile_width),
        preferred_element_type=jnp.float32,
    )
    unpacked = unpacked.astype(jnp.bfloat16).reshape(KT_DEV, QT_DEV, tile_width, tile_width)
    integral_block = unpacked.transpose(0, 2, 1, 3).reshape(
        KT_DEV * tile_width, QT_DEV * tile_width
    )
    amp_full = lax.all_gather(amplitudes, "col", axis=1, tiled=True)
    product = jnp.dot(
        amp_full,
        lax.all_gather(integral_block, "row", axis=0, tiled=True),
        preferred_element_type=jnp.float32,
    )
    return residual_in + product


def solution(mesh):
    in_specs = (P("row", "col"), P("row", "col", None, None), P("row", "col"), P("row", "col"))
    out_specs = P("row", "col")
    return jax.shard_map(body, mesh=mesh, in_specs=in_specs, out_specs=out_specs, check_vma=False)
```

profile of v0, /device:TPU:0, one launch (start us, length us, event | category | flops | bytes accessed | tf_op | source)
XLA Modules:
  0.0 93.8 jit_solution(13653820851252631797)
XLA Ops:
  6.5 0.7 all-gather.5.cloned.1.call-update
  7.3 0.7 fusion.22
  7.9 1.2 %dynamic-slice = u32[1]{0:T(128)} dynamic-slice(u32[32]{0:T(128)} %constant.49, u32[]{:T(128)S(6)} %add.52), dynamic_slice_sizes={1} | dynamic-slice | bytes 12
  9.8 0.8 bitcast_dynamic-update-slice_fusion
  10.6 0.2 convert_reduce_fusion.1
  10.8 0.7 fusion.18
  11.4 0.4 convolution_convert_fusion.1
  11.8 1.2 %copy.19 = bf16[8,2,128,128]{3,1,2,0:T(2,128)(2,1)} copy(bf16[8,2,128,128]{3,1,0,2:T(2,128)(2,1)S(1)} %bitcast.65) | data formatting | bytes 1048576 | tf_op jit(solution)/shard_map/reshape | solution.py:30
  13.0 7.3 %all-to-all-start = ((bf16[8,2,128,128]{3,1,2,0:T(2,128)(2,1)}), bf16[8,2,128,128]{3,1,2,0:T(2,128)(2,1)S(1)}, u32[]{:S(2)}, u32[]{:S(2)}) async-start(bf16[8,2,128,128]{3,1,2,0:T(2,128)(2,1)} %copy.19), calls=%async_computation | async-start | bytes 1048576 | tf_op jit(solution)/shard_map/all_to_all | solution.py:32
  20.3 0.0 all-gather.3.cloned.1.call-start
  20.3 19.0 %all-reduce = s32[128]{0:T(128)S(1)} all-reduce(s32[128]{0:T(128)S(1)} %get-tuple-element.5), channel_id=1, replica_groups=mesh['row'=4,'col'=8] {'col'}, use_global_device_ids=true, to_apply=%add | all-reduce | flops 128 | bytes 1024
  39.4 0.1 reshape_squeeze.3
  39.5 0.3 convert_reduce_fusion
  39.8 0.1 broadcast_add_fusion
  39.9 0.1 add.49
  40.0 0.4 copy.20
  40.4 1.2 %fusion = bf16[2,8,128,128]{3,1,0,2:T(8,128)(2,1)} fusion(bf16[16,128,128]{2,0,1:T(8,128)(2,1)S(1)} %bitcast.64, s32[128]{0:T(128)S(1)} %add.49, s32[128]{0:T(128)S(1)} %fusion.17, pred[128]{0:T(512)(128)(4,1)S(1)} %compare_bitcast_fusion), kind=kOutput, calls=%fused_computation.3 | convolution fusion | flops 8722688 | bytes 1049728 | tf_op jit(solution)/shard_map/ps,sij->pij/dot_general | solution.py:45
  41.6 1.1 %copy.21 = bf16[2,8,128,128]{3,1,2,0:T(8,128)(2,1)S(1)} copy(bf16[2,8,128,128]{3,1,0,2:T(8,128)(2,1)} %fusion) | data formatting | bytes 1048576 | tf_op jit(solution)/shard_map/reshape | solution.py:51
  42.7 0.9 copy.28
  43.6 1.8 %copy.22 = f32[512,1024]{0,1:T(8,128)} copy(f32[512,1024]{1,0:T(8,128)S(1)} %copy-done.1) | data formatting | bytes 4194304 | tf_op args[3]
  45.4 12.7 %all-gather.5.cloned.1.call-done = bf16[512,1024]{1,0:T(8,128)(2,1)} async-done(((bf16[512,128]{1,0:T(8,128)(2,1)}), bf16[512,1024]{1,0:T(8,128)(2,1)}) %all-gather.5.cloned.1.call-update) | async-done | bytes 1048592 | tf_op jit(solution)/shard_map/all_gather | solution.py:55
  58.2 23.1 %all-gather.3.cloned.1.call-done = bf16[1024,1024]{1,0:T(8,128)(2,1)} async-done(((bf16[256,1024]{1,0:T(8,128)(2,1)}), bf16[1024,1024]{1,0:T(8,128)(2,1)}) %all-gather.3.cloned.1.call-update) | async-done | bytes 2097168 | tf_op jit(solution)/shard_map/all_gather | solution.py:58
  81.2 3.8 %bitcast_add_fusion = f32[512,1024]{0,1:T(8,128)S(1)} fusion(f32[512,1024]{0,1:T(8,128)} %copy.22, bf16[1024,1024]{1,0:T(8,128)(2,1)} %all-gather.3.cloned.1.call-done, bf16[512,1024]{1,0:T(8,128)(2,1)} %all-gather.5.cloned.1.call-done), kind=kOutput, calls=%fused_computation | convolution fusion | flops 1074266112 | bytes 7340032 | tf_op jit(solution)/shard_map/dot_general | solution.py:56
  85.1 1.8 %copy.23 = f32[512,1024]{1,0:T(8,128)} copy(f32[512,1024]{0,1:T(8,128)S(1)} %bitcast_add_fusion) | data formatting | bytes 4194304 | tf_op jit(solution)/shard_map/add | solution.py:61
  (13 shorter events, 0.1 us)
Async XLA Ops:
  6.5 4.9 %copy-start = (bf16[1,16,128,128]{3,2,1,0:T(8,128)(2,1)S(1)}, bf16[1,16,128,128]{3,2,1,0:T(8,128)(2,1)}, u32[]{:S(2)}) copy-start(bf16[1,16,128,128]{3,2,1,0:T(8,128)(2,1)} %param.5) | copy-start | bytes 1572868
  6.5 51.6 %all-gather.5.cloned.1.call-start = ((), (), s32[]{:S(2)}) async-start(), calls=%async_computation.2 | async-start | bytes 1179648 | tf_op jit(solution)/shard_map/all_gather | solution.py:55
  13.0 26.9 %all-to-all-start = ((bf16[8,2,128,128]{3,1,2,0:T(2,128)(2,1)}), bf16[8,2,128,128]{3,1,2,0:T(2,128)(2,1)S(1)}, u32[]{:S(2)}, u32[]{:S(2)}) async-start(bf16[8,2,128,128]{3,1,2,0:T(2,128)(2,1)} %copy.19), calls=%async_computation | async-start | bytes 1048576 | tf_op jit(solution)/shard_map/all_to_all | solution.py:32
  20.3 60.9 %all-gather.3.cloned.1.call-start = ((), (), s32[]{:S(2)}) async-start(), calls=%async_computation.1 | async-start | bytes 2621440 | tf_op jit(solution)/shard_map/all_gather | solution.py:58
  40.4 3.3 %copy-start.1 = (f32[512,1024]{1,0:T(8,128)S(1)}, f32[512,1024]{1,0:T(8,128)}, u32[]{:S(2)}) copy-start(f32[512,1024]{1,0:T(8,128)} %param.7) | copy-start | bytes 6291460
Sparse Core Ops, SparseCore 0:
  9.4 48.7 all-gather.4
  59.7 21.4 all-gather.2
where the time goes:
time: 94 us; the launch traced here: 93.8 us
  waiting for transfers between devices  36.5 us (39%)
  blocking collectives  19 us (20%)
  between operations  14.1 us (15%)
  local copies, waits for them, and re-layouts  8.63 us (9%)
  starting transfers between devices  7.29 us (8%)
  matrix products  5.45 us (6%)
  other arithmetic  2.68 us (3%)
    all_gather x1, waiting for transfers between devices, body(): lax.all_gather(integral_block, 'row', axis=0, tiled=True)  23.1 us
    unnamed x1, blocking collectives  19 us
    all_gather x1, waiting for transfers between devices, body(): amp_full = lax.all_gather(amplitudes, 'col', axis=1, tiled=True)  12.7 us
    all_to_all x1, starting transfers between devices, body(): lax.all_to_all(outgoing, 'col', split_axis=0, concat_axis=0, tiled=True)  7.25 us
    unnamed x8, local copies, waits for them, and re-layouts  3.96 us
    dot_general x1, matrix products, body(): jnp.dot(amp_full, lax.all_gather(integral_block, 'row', axis=0, tiled=Tru...  3.85 us
  transfers between devices with their start and end apart: 3, of which 2 were waited for; matrix products, arithmetic and copies ran while one was open for 12% of the time, Pallas kernels for 0%

commit v1 on v0

v1 whole, which is shorter than its diff:
```python
import functools
import math

import jax
import jax.numpy as jnp
from jax import lax
from jax.experimental import pallas as pl
from jax.experimental.pallas import tpu as pltpu
from jax.sharding import PartitionSpec as P

KT_DEV = 2
QT_DEV = 8
CORES = 2
META = 16
MIB = 1024 * 1024


def pack_kernel(columns, capacity, me_ref, ids_ref, tiles_ref, *refs):
    outs, slot_tile, slot_place, count = refs[:columns], *refs[columns:]
    per_device, width = tiles_ref.shape[1], tiles_ref.shape[2]
    shift = per_device.bit_length() - 1
    for d in range(columns):
        count[d] = 0
        for s in range(capacity):
            slot_place[d * capacity + s] = per_device
    for t in range(per_device):
        tile_id = ids_ref[0, t]
        target = lax.shift_right_logical(tile_id, shift)
        rank = count[target]
        count[target] = rank + 1
        slot_tile[target * capacity + rank] = t
        slot_place[target * capacity + rank] = tile_id & (per_device - 1)
    lane = lax.broadcasted_iota(jnp.int32, (META, width), 1)
    for d, out in enumerate(outs):
        target = me_ref[0] ^ d
        row = jnp.full((META, width), per_device, jnp.int32)
        for s in range(capacity):
            place = slot_place[target * capacity + s]
            row = jnp.where(lane == s, place, row)

            @pl.when(place < per_device)
            def _():
                out[s * width : (s + 1) * width, :] = tiles_ref[
                    0, slot_tile[target * capacity + s]
                ]

        out[capacity * width :, :] = row.astype(jnp.float32).astype(jnp.bfloat16)


def pack(col, packed_tiles, tile_ids, columns, capacity):
    _, per_device, width, _ = packed_tiles.shape
    chunk = jax.ShapeDtypeStruct((capacity * width + META, width), packed_tiles.dtype)
    smem = pl.BlockSpec(memory_space=pltpu.SMEM)
    vmem = pl.BlockSpec(memory_space=pltpu.VMEM)
    return pl.pallas_call(
        functools.partial(pack_kernel, columns, capacity),
        out_shape=[chunk] * columns,
        in_specs=[smem, smem, vmem],
        out_specs=[vmem] * columns,
        scratch_shapes=[
            pltpu.SMEM((columns * capacity,), jnp.int32),
            pltpu.SMEM((columns * capacity,), jnp.int32),
            pltpu.SMEM((columns,), jnp.int32),
        ],
        compiler_params=pltpu.CompilerParams(vmem_limit_bytes=8 * MIB),
        name="pack",
    )(col[None], tile_ids, packed_tiles)


def join_kernel(*refs):
    for c, chunk in enumerate(refs[:-1]):
        refs[-1][c] = chunk[...]


def join(chunks):
    vmem = pl.BlockSpec(memory_space=pltpu.VMEM)
    return pl.pallas_call(
        join_kernel,
        out_shape=jax.ShapeDtypeStruct((len(chunks), *chunks[0].shape), chunks[0].dtype),
        in_specs=[vmem] * len(chunks),
        out_specs=vmem,
        compiler_params=pltpu.CompilerParams(vmem_limit_bytes=8 * MIB),
        name="join",
    )(*chunks)


def ladder_kernel(n_pieces, n_amps, capacity, where_ref, *refs):
    pieces = refs[:n_pieces]
    amps = refs[n_pieces : n_pieces + n_amps]
    residual, out = refs[n_pieces + n_amps : n_pieces + n_amps + 2]
    places, table, amp, block, total, table_sem, res_sem, out_sem = refs[
        n_pieces + n_amps + 2 :
    ]
    columns = pieces[0].shape[0]
    width = pieces[0].shape[2]
    per_device = KT_DEV * QT_DEV
    res_copy = pltpu.make_async_copy(residual, total, res_sem)
    res_copy.start()
    for p, piece in enumerate(pieces):
        rows = piece[:, capacity * width :, :]
        places[p * columns : (p + 1) * columns] = jnp.max(
            rows.astype(jnp.float32), axis=1
        ).astype(jnp.int32)
    table_copy = pltpu.make_async_copy(places, table, table_sem)
    table_copy.start()
    for a, source in enumerate(amps):
        column = where_ref[n_pieces + a]
        amp[:, pl.ds(pl.multiple_of(column * width, width), width)] = source[...]
    table_copy.wait()
    for p, piece in enumerate(pieces):
        row = where_ref[p]

        def place(c, _, p=p, piece=piece, row=row):
            for s in range(capacity):
                position = table[p * columns + c, s]
                k = row * KT_DEV + lax.shift_right_logical(position, QT_DEV.bit_length() - 1)
                q = position & (QT_DEV - 1)

                @pl.when(position < per_device)
                def _():
                    block[
                        pl.ds(pl.multiple_of(k * width, width), width),
                        pl.ds(pl.multiple_of(q * width, width), width),
                    ] = piece[c, s * width : (s + 1) * width, :]

            return 0

        lax.fori_loop(0, columns, place, 0)
    res_copy.wait()
    step = 2 * width
    outs = []
    for n in range(block.shape[1] // step):
        cols = slice(n * step, (n + 1) * step)
        total[:, cols] += jnp.dot(
            amp[...], block[:, cols], preferred_element_type=jnp.float32
        )
        copy = pltpu.make_async_copy(
            total.at[:, pl.ds(n * step, step)],
            out.at[:, pl.ds(n * step, step)],
            out_sem.at[n],
        )
        copy.start()
        outs.append(copy)
    for copy in outs:
        copy.wait()


def ladder(where, pieces, amps, residual, capacity):
    columns, _, width = pieces[0].shape
    n_pieces, n_amps = len(pieces), len(amps)
    rows, n_cols = residual.shape
    depth = n_amps * width
    any_spec = pl.BlockSpec(memory_space=pl.ANY)
    vmem = pl.BlockSpec(memory_space=pltpu.VMEM)
    held = sum(x.size * x.dtype.itemsize for x in (*pieces, *amps))
    held += 2 * rows * depth + 2 * depth * n_cols + 4 * rows * n_cols
    return pl.pallas_call(
        functools.partial(ladder_kernel, n_pieces, n_amps, capacity),
        out_shape=jax.ShapeDtypeStruct(residual.shape, residual.dtype),
        in_specs=[pl.BlockSpec(memory_space=pltpu.SMEM)]
        + [vmem] * (n_pieces + n_amps)
        + [any_spec],
        out_specs=any_spec,
        scratch_shapes=[
            pltpu.VMEM((n_pieces * columns, width), jnp.int32),
            pltpu.SMEM((n_pieces * columns, width), jnp.int32),
            pltpu.VMEM((rows, depth), jnp.bfloat16),
            pltpu.VMEM((depth, n_cols), jnp.bfloat16),
            pltpu.VMEM((rows, n_cols), jnp.float32),
            pltpu.SemaphoreType.DMA,
            pltpu.SemaphoreType.DMA,
            pltpu.SemaphoreType.DMA((n_cols // (2 * width),)),
        ],
        compiler_params=pltpu.CompilerParams(vmem_limit_bytes=held + 6 * MIB),
        name="ladder",
    )(where, *pieces, *amps, residual)


def exchange(x, axis, flip):
    size = lax.axis_size(axis)
    return lax.ppermute(x, axis, [(i, i ^ flip) for i in range(size)])


def body(amplitudes, packed_tiles, tile_ids, residual_in):
    n_col, n_row = lax.axis_size("col"), lax.axis_size("row")
    col, row = lax.axis_index("col"), lax.axis_index("row")
    inner = 2 ** (int(math.log2(n_col)) // 2)
    capacity = -(-packed_tiles.shape[1] // n_col)
    near = n_col // 2
    outgoing = pack(col, packed_tiles, tile_ids, n_col, capacity)
    chunks = [outgoing[0]] + [exchange(outgoing[s], "col", s) for s in range(1, n_col)]
    groups = [join(chunks[:near]), join(chunks[near:])]
    pieces, rows = [], []
    for group in groups:
        for flip in range(0, n_row, CORES):
            mine = exchange(group, "row", flip) if flip else group
            pieces += [mine, exchange(mine, "row", 1)]
            rows += [row ^ flip, row ^ flip ^ 1]
    shards, columns = [], []
    for flip in range(0, n_col, inner):
        shard = exchange(amplitudes, "col", flip) if flip else amplitudes
        for lane in range(inner):
            shards.append(exchange(shard, "col", lane) if lane else shard)
            columns.append(col ^ flip ^ lane)
    where = jnp.stack(rows + columns).astype(jnp.int32)
    return ladder(where, pieces, shards, residual_in, capacity)


def solution(mesh):
    in_specs = (P("row", "col"), P("row", "col", None, None), P("row", "col"), P("row", "col"))
    out_specs = P("row", "col")
    return jax.shard_map(body, mesh=mesh, in_specs=in_specs, out_specs=out_specs, check_vma=False)
```

time: 94 us -> 58.8 us (0.63)
  starting transfers between devices: 7.29 us -> 27.8 us
  blocking collectives: 19 us -> 0 us
  waiting for transfers between devices: 36.5 us -> 20.3 us
  between operations: 14.1 us -> 0.06 us
  Pallas kernels: 0 us -> 6.14 us
  matrix products: 5.45 us -> 0 us
  local copies, waits for them, and re-layouts: 8.63 us -> 4.28 us
  other arithmetic: 2.68 us -> 0 us
    all_gather x2 -> x0, waiting for transfers between devices: 35.8 us -> none  [the longest x1 23.1 us: body(): lax.all_gather(integral_block, 'row', axis=0, tiled=True)]
    ppermute x0 -> x20, starting transfers between devices: none -> 27.8 us  [exchange(): return lax.ppermute(x, axis, [(i, i ^ flip) for i in range(size)])]
    ppermute x0 -> x20, waiting for transfers between devices: none -> 20.3 us  [exchange(): return lax.ppermute(x, axis, [(i, i ^ flip) for i in range(size)])]
    unnamed x1 -> x0, blocking collectives: 19 us -> none
    all_to_all x1 -> x0, starting transfers between devices: 7.25 us -> none  [body(): lax.all_to_all(outgoing, 'col', split_axis=0, concat_axis=0, tiled=True)]
    pallas_call x0 -> x4, Pallas kernels: none -> 6.14 us  [the longest x1 5.25 us: ladder(): pl.pallas_call(functools.partial(ladder_kernel, n_pieces, n_amps, capacit...]
    dot_general x3 -> x0, matrix products: 5.45 us -> none  [the longest x1 3.85 us: body(): jnp.dot(amp_full, lax.all_gather(integral_block, 'row', axis=0, tiled=Tru...]
    reshape x2 -> x0, local copies, waits for them, and re-layouts: 2.33 us -> none  [the longest x1 1.2 us: body(): outgoing.astype(jnp.bfloat16)]
  transfers between devices with their start and end apart: 3 -> 20, of which waited for: 2 -> 8; matrix products, arithmetic and copies ran while one was open for 12% -> 0% of each run, Pallas kernels for 0% -> 0%
where the time goes in v1:
time: 58.8 us; the launch traced here: 58.5 us
  starting transfers between devices  27.8 us (47%)
  waiting for transfers between devices  20.3 us (35%)
  Pallas kernels  6.14 us (10%)
  local copies, waits for them, and re-layouts  4.28 us (7%)
    ppermute x20, starting transfers between devices, exchange(): return lax.ppermute(x, axis, [(i, i ^ flip) for i in range(size)])  27.8 us
    ppermute x20, waiting for transfers between devices, exchange(): return lax.ppermute(x, axis, [(i, i ^ flip) for i in range(size)])  20.3 us
    pallas_call x1, Pallas kernels, ladder(): pl.pallas_call(functools.partial(ladder_kernel, n_pieces, n_amps, capacit...  5.25 us
    unnamed x8, local copies, waits for them, and re-layouts  4.19 us
  transfers between devices with their start and end apart: 20, of which 8 were waited for; matrix products, arithmetic and copies ran while one was open for 0% of the time, Pallas kernels for 0%

profile of v1, /device:TPU:0, one launch (start us, length us, event | category | flops | bytes accessed | tf_op | source)
XLA Modules:
  0.0 58.5 jit_solution(14407733396380948611)
XLA Ops:
  0.0 1.0 %copy-done.1 = bf16[1,16,128,128]{3,2,1,0:T(8,128)(2,1)S(1)} copy-done((bf16[1,16,128,128]{3,2,1,0:T(8,128)(2,1)S(1)}, bf16[1,16,128,128]{3,2,1,0:T(8,128)(2,1)}, u32[]{:S(2)}) %copy-start.1) | copy-done | bytes 524312
  2.6 4.1 %collective-permute-start.6 = (bf16[272,128]{1,0:T(8,128)(2,1)S(1)}, bf16[272,128]{1,0:T(8,128)(2,1)S(1)}, u32[]{:S(2)}, u32[]{:S(2)}) collective-permute-start(bf16[272,128]{1,0:T(8,128)(2,1)S(1)} %get-tuple-element.17), channel_id=1, source_target_pairs={{0,4},{1,5},{2,6},{3,7},{4,0},{5,1},{6,2},{7,3},{8,12},{9,13},{10,... | collective-permute-start | bytes 208904 | tf_op jit(solution)/shard_map/ppermute | solution.py:181
  6.7 1.3 %collective-permute-start.7 = (bf16[272,128]{1,0:T(8,128)(2,1)S(1)}, bf16[272,128]{1,0:T(8,128)(2,1)S(1)}, u32[]{:S(2)}, u32[]{:S(2)}) collective-permute-start(bf16[272,128]{1,0:T(8,128)(2,1)S(1)} %get-tuple-element.18), channel_id=1, source_target_pairs={{0,5},{1,4},{2,7},{3,6},{4,1},{5,0},{6,3},{7,2},{8,13},{9,12},{10,... | collective-permute-start | bytes 208904 | tf_op jit(solution)/shard_map/ppermute | solution.py:181
  8.2 3.9 %collective-permute-start.8 = (bf16[272,128]{1,0:T(8,128)(2,1)S(1)}, bf16[272,128]{1,0:T(8,128)(2,1)S(1)}, u32[]{:S(2)}, u32[]{:S(2)}) collective-permute-start(bf16[272,128]{1,0:T(8,128)(2,1)S(1)} %get-tuple-element.19), channel_id=1, source_target_pairs={{0,6},{1,7},{2,4},{3,5},{4,2},{5,3},{6,0},{7,1},{8,14},{9,15},{10,... | collective-permute-start | bytes 208904 | tf_op jit(solution)/shard_map/ppermute | solution.py:181
  12.1 1.1 %collective-permute-start.9 = (bf16[272,128]{1,0:T(8,128)(2,1)S(1)}, bf16[272,128]{1,0:T(8,128)(2,1)S(1)}, u32[]{:S(2)}, u32[]{:S(2)}) collective-permute-start(bf16[272,128]{1,0:T(8,128)(2,1)S(1)} %get-tuple-element.20), channel_id=1, source_target_pairs={{0,7},{1,6},{2,5},{3,4},{4,3},{5,2},{6,1},{7,0},{8,15},{9,14},{10,... | collective-permute-start | bytes 208904 | tf_op jit(solution)/shard_map/ppermute | solution.py:181
  13.2 4.0 %collective-permute-done.7.refs_1_ = bf16[272,128]{1,0:T(8,128)(2,1)S(1)} collective-permute-done((bf16[272,128]{1,0:T(8,128)(2,1)S(1)}, bf16[272,128]{1,0:T(8,128)(2,1)S(1)}, u32[]{:S(2)}, u32[]{:S(2)}) %collective-permute-start.7) | collective-permute-done | bytes 69664 | tf_op jit(solution)/shard_map/ppermute | solution.py:181
  18.0 1.2 %collective-permute-done.9.refs_3_ = bf16[272,128]{1,0:T(8,128)(2,1)S(1)} collective-permute-done((bf16[272,128]{1,0:T(8,128)(2,1)S(1)}, bf16[272,128]{1,0:T(8,128)(2,1)S(1)}, u32[]{:S(2)}, u32[]{:S(2)}) %collective-permute-start.9) | collective-permute-done | bytes 69664 | tf_op jit(solution)/shard_map/ppermute | solution.py:181
  19.2 1.6 %collective-permute-start.11 = (bf16[4,272,128]{2,1,0:T(8,128)(2,1)S(1)}, bf16[4,272,128]{2,1,0:T(8,128)(2,1)S(1)}, u32[]{:S(2)}, u32[]{:S(2)}) collective-permute-start(bf16[4,272,128]{2,1,0:T(8,128)(2,1)S(1)} %join.3.refs_4_), channel_id=1, source_target_pairs={{0,16},{8,24},{16,0},{24,8},{1,17},{9,25},{17,1},{25,9},{2,18},{10... | collective-permute-start | bytes 835592 | tf_op jit(solution)/shard_map/ppermute | solution.py:181
  20.8 1.6 %collective-permute-done.2.refs_3_ = bf16[272,128]{1,0:T(8,128)(2,1)S(1)} collective-permute-done((bf16[272,128]{1,0:T(8,128)(2,1)S(1)}, bf16[272,128]{1,0:T(8,128)(2,1)S(1)}, u32[]{:S(2)}, u32[]{:S(2)}) %collective-permute-start.2) | collective-permute-done | bytes 69664 | tf_op jit(solution)/shard_map/ppermute | solution.py:181
  22.4 1.6 %collective-permute-start.4 = (bf16[4,272,128]{2,1,0:T(8,128)(2,1)S(1)}, bf16[4,272,128]{2,1,0:T(8,128)(2,1)S(1)}, u32[]{:S(2)}, u32[]{:S(2)}) collective-permute-start(bf16[4,272,128]{2,1,0:T(8,128)(2,1)S(1)} %join.2.refs_0_), channel_id=1, source_target_pairs={{0,16},{8,24},{16,0},{24,8},{1,17},{9,25},{17,1},{25,9},{2,18},{10... | collective-permute-start | bytes 835592 | tf_op jit(solution)/shard_map/ppermute | solution.py:181
  24.0 2.0 %collective-permute-start.16 = (bf16[512,128]{1,0:T(8,128)(2,1)}, bf16[512,128]{1,0:T(8,128)(2,1)S(1)}, u32[]{:S(2)}, u32[]{:S(2)}) collective-permute-start(bf16[512,128]{1,0:T(8,128)(2,1)} %refs_8_.1), channel_id=1, source_target_pairs={{0,4},{1,5},{2,6},{3,7},{4,0},{5,1},{6,2},{7,3},{8,12},{9,13},{10,... | collective-permute-start | bytes 393224 | tf_op jit(solution)/shard_map/ppermute | solution.py:181
  26.0 2.3 %collective-permute-start.14 = (bf16[512,128]{1,0:T(8,128)(2,1)}, bf16[512,128]{1,0:T(8,128)(2,1)S(1)}, u32[]{:S(2)}, u32[]{:S(2)}) collective-permute-start(bf16[512,128]{1,0:T(8,128)(2,1)} %refs_8_.1), channel_id=1, source_target_pairs={{0,2},{1,3},{2,0},{3,1},{4,6},{5,7},{6,4},{7,5},{8,10},{9,11},{10,... | collective-permute-start | bytes 393224 | tf_op jit(solution)/shard_map/ppermute | solution.py:181
  29.0 2.8 %collective-permute-done.16.refs_12_ = bf16[512,128]{1,0:T(8,128)(2,1)S(1)} collective-permute-done((bf16[512,128]{1,0:T(8,128)(2,1)}, bf16[512,128]{1,0:T(8,128)(2,1)S(1)}, u32[]{:S(2)}, u32[]{:S(2)}) %collective-permute-start.16) | collective-permute-done | bytes 131104 | tf_op jit(solution)/shard_map/ppermute | solution.py:181
  31.8 4.1 %collective-permute-start.18 = (bf16[512,128]{1,0:T(8,128)(2,1)}, bf16[512,128]{1,0:T(8,128)(2,1)S(1)}, u32[]{:S(2)}, u32[]{:S(2)}) collective-permute-start(bf16[512,128]{1,0:T(8,128)(2,1)} %refs_8_.1), channel_id=1, source_target_pairs={{0,6},{1,7},{2,4},{3,5},{4,2},{5,3},{6,0},{7,1},{8,14},{9,15},{10,... | collective-permute-start | bytes 393224 | tf_op jit(solution)/shard_map/ppermute | solution.py:181
  35.9 1.2 %collective-permute-start.17 = (bf16[512,128]{1,0:T(8,128)(2,1)S(1)}, bf16[512,128]{1,0:T(8,128)(2,1)S(1)}, u32[]{:S(2)}, u32[]{:S(2)}) collective-permute-start(bf16[512,128]{1,0:T(8,128)(2,1)S(1)} %collective-permute-done.16.refs_12_), channel_id=1, source_target_pairs={{0,1},{1,0},{2,3},{3,2},{4,5},{5,4},{6,7},{7,6},{8,9},{9,8},{10,11... | collective-permute-start | bytes 393224 | tf_op jit(solution)/shard_map/ppermute | solution.py:181
  37.0 2.1 %collective-permute-done.18.refs_14_ = bf16[512,128]{1,0:T(8,128)(2,1)S(1)} collective-permute-done((bf16[512,128]{1,0:T(8,128)(2,1)}, bf16[512,128]{1,0:T(8,128)(2,1)S(1)}, u32[]{:S(2)}, u32[]{:S(2)}) %collective-permute-start.18) | collective-permute-done | bytes 131104 | tf_op jit(solution)/shard_map/ppermute | solution.py:181
  39.7 1.1 %collective-permute-done.17.refs_13_ = bf16[512,128]{1,0:T(8,128)(2,1)S(1)} collective-permute-done((bf16[512,128]{1,0:T(8,128)(2,1)S(1)}, bf16[512,128]{1,0:T(8,128)(2,1)S(1)}, u32[]{:S(2)}, u32[]{:S(2)}) %collective-permute-start.17) | collective-permute-done | bytes 131104 | tf_op jit(solution)/shard_map/ppermute | solution.py:181
  40.8 1.2 %collective-permute-start.15 = (bf16[512,128]{1,0:T(8,128)(2,1)S(1)}, bf16[512,128]{1,0:T(8,128)(2,1)S(1)}, u32[]{:S(2)}, u32[]{:S(2)}) collective-permute-start(bf16[512,128]{1,0:T(8,128)(2,1)S(1)} %collective-permute-done.14.refs_10_), channel_id=1, source_target_pairs={{0,1},{1,0},{2,3},{3,2},{4,5},{5,4},{6,7},{7,6},{8,9},{9,8},{10,11... | collective-permute-start | bytes 393224 | tf_op jit(solution)/shard_map/ppermute | solution.py:181
  42.0 3.8 %collective-permute-done.15.refs_11_ = bf16[512,128]{1,0:T(8,128)(2,1)S(1)} collective-permute-done((bf16[512,128]{1,0:T(8,128)(2,1)S(1)}, bf16[512,128]{1,0:T(8,128)(2,1)S(1)}, u32[]{:S(2)}, u32[]{:S(2)}) %collective-permute-start.15) | collective-permute-done | bytes 131104 | tf_op jit(solution)/shard_map/ppermute | solution.py:181
  45.8 1.2 %collective-permute-start.19 = (bf16[512,128]{1,0:T(8,128)(2,1)S(1)}, bf16[512,128]{1,0:T(8,128)(2,1)S(1)}, u32[]{:S(2)}, u32[]{:S(2)}) collective-permute-start(bf16[512,128]{1,0:T(8,128)(2,1)S(1)} %collective-permute-done.18.refs_14_), channel_id=1, source_target_pairs={{0,1},{1,0},{2,3},{3,2},{4,5},{5,4},{6,7},{7,6},{8,9},{9,8},{10,11... | collective-permute-start | bytes 393224 | tf_op jit(solution)/shard_map/ppermute | solution.py:181
  47.1 3.7 %collective-permute-done.19.refs_15_ = bf16[512,128]{1,0:T(8,128)(2,1)S(1)} collective-permute-done((bf16[512,128]{1,0:T(8,128)(2,1)S(1)}, bf16[512,128]{1,0:T(8,128)(2,1)S(1)}, u32[]{:S(2)}, u32[]{:S(2)}) %collective-permute-start.19) | collective-permute-done | bytes 131104 | tf_op jit(solution)/shard_map/ppermute | solution.py:181
  50.8 1.6 %copy-done = f32[512,1024]{1,0:T(8,128)S(1)} copy-done((f32[512,1024]{1,0:T(8,128)S(1)}, f32[512,1024]{1,0:T(8,128)}, u32[]{:S(2)}) %copy-start) | copy-done | bytes 2097176
  52.4 0.9 %copy-done.2 = bf16[512,128]{1,0:T(8,128)(2,1)S(1)} copy-done((bf16[512,128]{1,0:T(8,128)(2,1)S(1)}, bf16[512,128]{1,0:T(8,128)(2,1)}, u32[]{:S(2)}) %copy-start.2) | copy-done | bytes 131096
  53.3 5.3 %ladder.1 = f32[512,1024]{1,0:T(8,128)} custom-call(s32[16]{0:T(128)S(1)} %stack.55.where_ref, bf16[4,272,128]{2,1,0:T(8,128)(2,1)S(1)} %join.2.refs_0_, bf16[4,272,128]{2,1,0:T(8,128)(2,1)S(1)} %collective-permute-done.3.refs_1_, bf16[4,272,128]{2,1,0:T(8,128)(2,1)S(1)} %collective-permute-done.4.refs_2_, ...), custom_call_target="tpu_custom_call" | custom-call | tf_op jit(solution)/shard_map/ladder/pallas_call | solution.py:157
  (29 shorter events, 4.0 us)
Async XLA Ops:
  0.0 1.0 %copy-start.1 = (bf16[1,16,128,128]{3,2,1,0:T(8,128)(2,1)S(1)}, bf16[1,16,128,128]{3,2,1,0:T(8,128)(2,1)}, u32[]{:S(2)}) copy-start(bf16[1,16,128,128]{3,2,1,0:T(8,128)(2,1)} %tiles_ref.1) | copy-start | bytes 1572868
  1.0 0.7 %copy-start.3 = (s32[1,16]{1,0:T(1,128)S(1)}, s32[1,16]{1,0:T(1,128)}, u32[]{:S(2)}) copy-start(s32[1,16]{1,0:T(1,128)} %ids_ref.1) | copy-start | bytes 196
  2.6 10.7 %collective-permute-start.6 = (bf16[272,128]{1,0:T(8,128)(2,1)S(1)}, bf16[272,128]{1,0:T(8,128)(2,1)S(1)}, u32[]{:S(2)}, u32[]{:S(2)}) collective-permute-start(bf16[272,128]{1,0:T(8,128)(2,1)S(1)} %get-tuple-element.17), channel_id=1, source_target_pairs={{0,4},{1,5},{2,6},{3,7},{4,0},{5,1},{6,2},{7,3},{8,12},{9,13},{10,... | collective-permute-start | bytes 208904 | tf_op jit(solution)/shard_map/ppermute | solution.py:181
  6.7 10.5 %collective-permute-start.7 = (bf16[272,128]{1,0:T(8,128)(2,1)S(1)}, bf16[272,128]{1,0:T(8,128)(2,1)S(1)}, u32[]{:S(2)}, u32[]{:S(2)}) collective-permute-start(bf16[272,128]{1,0:T(8,128)(2,1)S(1)} %get-tuple-element.18), channel_id=1, source_target_pairs={{0,5},{1,4},{2,7},{3,6},{4,1},{5,0},{6,3},{7,2},{8,13},{9,12},{10,... | collective-permute-start | bytes 208904 | tf_op jit(solution)/shard_map/ppermute | solution.py:181
  7.9 12.9 %collective-permute-start = (bf16[272,128]{1,0:T(8,128)(2,1)S(1)}, bf16[272,128]{1,0:T(8,128)(2,1)S(1)}, u32[]{:S(2)}, u32[]{:S(2)}) collective-permute-start(bf16[272,128]{1,0:T(8,128)(2,1)S(1)} %get-tuple-element.14), channel_id=1, source_target_pairs={{0,1},{1,0},{2,3},{3,2},{4,5},{5,4},{6,7},{7,6},{8,9},{9,8},{10,11... | collective-permute-start | bytes 208904 | tf_op jit(solution)/shard_map/ppermute | solution.py:181
  8.2 9.8 %collective-permute-start.8 = (bf16[272,128]{1,0:T(8,128)(2,1)S(1)}, bf16[272,128]{1,0:T(8,128)(2,1)S(1)}, u32[]{:S(2)}, u32[]{:S(2)}) collective-permute-start(bf16[272,128]{1,0:T(8,128)(2,1)S(1)} %get-tuple-element.19), channel_id=1, source_target_pairs={{0,6},{1,7},{2,4},{3,5},{4,2},{5,3},{6,0},{7,1},{8,14},{9,15},{10,... | collective-permute-start | bytes 208904 | tf_op jit(solution)/shard_map/ppermute | solution.py:181
  12.1 7.1 %collective-permute-start.9 = (bf16[272,128]{1,0:T(8,128)(2,1)S(1)}, bf16[272,128]{1,0:T(8,128)(2,1)S(1)}, u32[]{:S(2)}, u32[]{:S(2)}) collective-permute-start(bf16[272,128]{1,0:T(8,128)(2,1)S(1)} %get-tuple-element.20), channel_id=1, source_target_pairs={{0,7},{1,6},{2,5},{3,4},{4,3},{5,2},{6,1},{7,0},{8,15},{9,14},{10,... | collective-permute-start | bytes 208904 | tf_op jit(solution)/shard_map/ppermute | solution.py:181
  13.2 7.6 %collective-permute-start.1 = (bf16[272,128]{1,0:T(8,128)(2,1)S(1)}, bf16[272,128]{1,0:T(8,128)(2,1)S(1)}, u32[]{:S(2)}, u32[]{:S(2)}) collective-permute-start(bf16[272,128]{1,0:T(8,128)(2,1)S(1)} %get-tuple-element.15), channel_id=1, source_target_pairs={{0,2},{1,3},{2,0},{3,1},{4,6},{5,7},{6,4},{7,5},{8,10},{9,11},{10,... | collective-permute-start | bytes 208904 | tf_op jit(solution)/shard_map/ppermute | solution.py:181
  17.2 5.2 %collective-permute-start.2 = (bf16[272,128]{1,0:T(8,128)(2,1)S(1)}, bf16[272,128]{1,0:T(8,128)(2,1)S(1)}, u32[]{:S(2)}, u32[]{:S(2)}) collective-permute-start(bf16[272,128]{1,0:T(8,128)(2,1)S(1)} %get-tuple-element.16), channel_id=1, source_target_pairs={{0,3},{1,2},{2,1},{3,0},{4,7},{5,6},{6,5},{7,4},{8,11},{9,10},{10,... | collective-permute-start | bytes 208904 | tf_op jit(solution)/shard_map/ppermute | solution.py:181
  19.2 19.9 %collective-permute-start.11 = (bf16[4,272,128]{2,1,0:T(8,128)(2,1)S(1)}, bf16[4,272,128]{2,1,0:T(8,128)(2,1)S(1)}, u32[]{:S(2)}, u32[]{:S(2)}) collective-permute-start(bf16[4,272,128]{2,1,0:T(8,128)(2,1)S(1)} %join.3.refs_4_), channel_id=1, source_target_pairs={{0,16},{8,24},{16,0},{24,8},{1,17},{9,25},{17,1},{25,9},{2,18},{10... | collective-permute-start | bytes 835592 | tf_op jit(solution)/shard_map/ppermute | solution.py:181
  22.4 17.2 %collective-permute-start.4 = (bf16[4,272,128]{2,1,0:T(8,128)(2,1)S(1)}, bf16[4,272,128]{2,1,0:T(8,128)(2,1)S(1)}, u32[]{:S(2)}, u32[]{:S(2)}) collective-permute-start(bf16[4,272,128]{2,1,0:T(8,128)(2,1)S(1)} %join.2.refs_0_), channel_id=1, source_target_pairs={{0,16},{8,24},{16,0},{24,8},{1,17},{9,25},{17,1},{25,9},{2,18},{10... | collective-permute-start | bytes 835592 | tf_op jit(solution)/shard_map/ppermute | solution.py:181
  24.0 7.8 %collective-permute-start.16 = (bf16[512,128]{1,0:T(8,128)(2,1)}, bf16[512,128]{1,0:T(8,128)(2,1)S(1)}, u32[]{:S(2)}, u32[]{:S(2)}) collective-permute-start(bf16[512,128]{1,0:T(8,128)(2,1)} %refs_8_.1), channel_id=1, source_target_pairs={{0,4},{1,5},{2,6},{3,7},{4,0},{5,1},{6,2},{7,3},{8,12},{9,13},{10,... | collective-permute-start | bytes 393224 | tf_op jit(solution)/shard_map/ppermute | solution.py:181
  26.0 9.9 %collective-permute-start.14 = (bf16[512,128]{1,0:T(8,128)(2,1)}, bf16[512,128]{1,0:T(8,128)(2,1)S(1)}, u32[]{:S(2)}, u32[]{:S(2)}) collective-permute-start(bf16[512,128]{1,0:T(8,128)(2,1)} %refs_8_.1), channel_id=1, source_target_pairs={{0,2},{1,3},{2,0},{3,1},{4,6},{5,7},{6,4},{7,5},{8,10},{9,11},{10,... | collective-permute-start | bytes 393224 | tf_op jit(solution)/shard_map/ppermute | solution.py:181
  28.3 8.8 %collective-permute-start.13 = (bf16[512,128]{1,0:T(8,128)(2,1)}, bf16[512,128]{1,0:T(8,128)(2,1)S(1)}, u32[]{:S(2)}, u32[]{:S(2)}) collective-permute-start(bf16[512,128]{1,0:T(8,128)(2,1)} %refs_8_.1), channel_id=1, source_target_pairs={{0,1},{1,0},{2,3},{3,2},{4,5},{5,4},{6,7},{7,6},{8,9},{9,8},{10,11... | collective-permute-start | bytes 393224 | tf_op jit(solution)/shard_map/ppermute | solution.py:181
  31.8 7.3 %collective-permute-start.18 = (bf16[512,128]{1,0:T(8,128)(2,1)}, bf16[512,128]{1,0:T(8,128)(2,1)S(1)}, u32[]{:S(2)}, u32[]{:S(2)}) collective-permute-start(bf16[512,128]{1,0:T(8,128)(2,1)} %refs_8_.1), channel_id=1, source_target_pairs={{0,6},{1,7},{2,4},{3,5},{4,2},{5,3},{6,0},{7,1},{8,14},{9,15},{10,... | collective-permute-start | bytes 393224 | tf_op jit(solution)/shard_map/ppermute | solution.py:181
  35.9 5.0 %collective-permute-start.17 = (bf16[512,128]{1,0:T(8,128)(2,1)S(1)}, bf16[512,128]{1,0:T(8,128)(2,1)S(1)}, u32[]{:S(2)}, u32[]{:S(2)}) collective-permute-start(bf16[512,128]{1,0:T(8,128)(2,1)S(1)} %collective-permute-done.16.refs_12_), channel_id=1, source_target_pairs={{0,1},{1,0},{2,3},{3,2},{4,5},{5,4},{6,7},{7,6},{8,9},{9,8},{10,11... | collective-permute-start | bytes 393224 | tf_op jit(solution)/shard_map/ppermute | solution.py:181
  37.0 13.7 %collective-permute-start.10 = (bf16[4,272,128]{2,1,0:T(8,128)(2,1)S(1)}, bf16[4,272,128]{2,1,0:T(8,128)(2,1)S(1)}, u32[]{:S(2)}, u32[]{:S(2)}) collective-permute-start(bf16[4,272,128]{2,1,0:T(8,128)(2,1)S(1)} %join.3.refs_4_), channel_id=1, source_target_pairs={{0,8},{8,0},{16,24},{24,16},{1,9},{9,1},{17,25},{25,17},{2,10},{10... | collective-permute-start | bytes 835592 | tf_op jit(solution)/shard_map/ppermute | solution.py:181
  39.1 11.7 %collective-permute-start.3 = (bf16[4,272,128]{2,1,0:T(8,128)(2,1)S(1)}, bf16[4,272,128]{2,1,0:T(8,128)(2,1)S(1)}, u32[]{:S(2)}, u32[]{:S(2)}) collective-permute-start(bf16[4,272,128]{2,1,0:T(8,128)(2,1)S(1)} %join.2.refs_0_), channel_id=1, source_target_pairs={{0,8},{8,0},{16,24},{24,16},{1,9},{9,1},{17,25},{25,17},{2,10},{10... | collective-permute-start | bytes 835592 | tf_op jit(solution)/shard_map/ppermute | solution.py:181
  39.1 11.7 %collective-permute-start.12 = (bf16[4,272,128]{2,1,0:T(8,128)(2,1)S(1)}, bf16[4,272,128]{2,1,0:T(8,128)(2,1)S(1)}, u32[]{:S(2)}, u32[]{:S(2)}) collective-permute-start(bf16[4,272,128]{2,1,0:T(8,128)(2,1)S(1)} %collective-permute-done.11.refs_6_), channel_id=1, source_target_pairs={{0,8},{8,0},{16,24},{24,16},{1,9},{9,1},{17,25},{25,17},{2,10},{10... | collective-permute-start | bytes 835592 | tf_op jit(solution)/shard_map/ppermute | solution.py:181
  39.6 11.1 %collective-permute-start.5 = (bf16[4,272,128]{2,1,0:T(8,128)(2,1)S(1)}, bf16[4,272,128]{2,1,0:T(8,128)(2,1)S(1)}, u32[]{:S(2)}, u32[]{:S(2)}) collective-permute-start(bf16[4,272,128]{2,1,0:T(8,128)(2,1)S(1)} %collective-permute-done.4.refs_2_), channel_id=1, source_target_pairs={{0,8},{8,0},{16,24},{24,16},{1,9},{9,1},{17,25},{25,17},{2,10},{10... | collective-permute-start | bytes 835592 | tf_op jit(solution)/shard_map/ppermute | solution.py:181
  40.8 5.0 %collective-permute-start.15 = (bf16[512,128]{1,0:T(8,128)(2,1)S(1)}, bf16[512,128]{1,0:T(8,128)(2,1)S(1)}, u32[]{:S(2)}, u32[]{:S(2)}) collective-permute-start(bf16[512,128]{1,0:T(8,128)(2,1)S(1)} %collective-permute-done.14.refs_10_), channel_id=1, source_target_pairs={{0,1},{1,0},{2,3},{3,2},{4,5},{5,4},{6,7},{7,6},{8,9},{9,8},{10,11... | collective-permute-start | bytes 393224 | tf_op jit(solution)/shard_map/ppermute | solution.py:181
  45.8 5.0 %collective-permute-start.19 = (bf16[512,128]{1,0:T(8,128)(2,1)S(1)}, bf16[512,128]{1,0:T(8,128)(2,1)S(1)}, u32[]{:S(2)}, u32[]{:S(2)}) collective-permute-start(bf16[512,128]{1,0:T(8,128)(2,1)S(1)} %collective-permute-done.18.refs_14_), channel_id=1, source_target_pairs={{0,1},{1,0},{2,3},{3,2},{4,5},{5,4},{6,7},{7,6},{8,9},{9,8},{10,11... | collective-permute-start | bytes 393224 | tf_op jit(solution)/shard_map/ppermute | solution.py:181
  50.8 1.6 %copy-start = (f32[512,1024]{1,0:T(8,128)S(1)}, f32[512,1024]{1,0:T(8,128)}, u32[]{:S(2)}) copy-start(f32[512,1024]{1,0:T(8,128)} %refs_16_.1) | copy-start | bytes 6291460
  52.4 0.9 %copy-start.2 = (bf16[512,128]{1,0:T(8,128)(2,1)S(1)}, bf16[512,128]{1,0:T(8,128)(2,1)}, u32[]{:S(2)}) copy-start(bf16[512,128]{1,0:T(8,128)(2,1)} %refs_8_.1) | copy-start | bytes 393220

commit v2 on v1

--- a/solution.py
+++ b/solution.py
@@ -68,15 +68,18 @@
 
 
 def join_kernel(*refs):
-    for c, chunk in enumerate(refs[:-1]):
-        refs[-1][c] = chunk[...]
+    at = 0
+    for part in refs[:-1]:
+        refs[-1][at : at + part.shape[0]] = part[...]
+        at += part.shape[0]
 
 
 def join(chunks):
     vmem = pl.BlockSpec(memory_space=pltpu.VMEM)
+    total = sum(c.shape[0] for c in chunks)
     return pl.pallas_call(
         join_kernel,
-        out_shape=jax.ShapeDtypeStruct((len(chunks), *chunks[0].shape), chunks[0].dtype),
+        out_shape=jax.ShapeDtypeStruct((total, *chunks[0].shape[1:]), chunks[0].dtype),
         in_specs=[vmem] * len(chunks),
         out_specs=vmem,
         compiler_params=pltpu.CompilerParams(vmem_limit_bytes=8 * MIB),
@@ -84,7 +87,8 @@
     )(*chunks)
 
 
-def ladder_kernel(n_pieces, n_amps, capacity, where_ref, *refs):
+def ladder_kernel(n_pieces, offsets, capacity, where_ref, *refs):
+    n_amps = len(offsets)
     pieces = refs[:n_pieces]
     amps = refs[n_pieces : n_pieces + n_amps]
     residual, out = refs[n_pieces + n_amps : n_pieces + n_amps + 2]
@@ -103,10 +107,11 @@
         ).astype(jnp.int32)
     table_copy = pltpu.make_async_copy(places, table, table_sem)
     table_copy.start()
-    for a, source in enumerate(amps):
-        column = where_ref[n_pieces + a]
-        amp[:, pl.ds(pl.multiple_of(column * width, width), width)] = source[...]
+    for source, slots in zip(amps, offsets):
+        for i, slot in enumerate(slots):
+            amp[:, slot * width : (slot + 1) * width] = source[i]
     table_copy.wait()
+    col = where_ref[n_pieces]
     for p, piece in enumerate(pieces):
         row = where_ref[p]
 
@@ -119,7 +124,7 @@
                 @pl.when(position < per_device)
                 def _():
                     block[
-                        pl.ds(pl.multiple_of(k * width, width), width),
+                        pl.ds(pl.multiple_of((k ^ col) * width, width), width),
                         pl.ds(pl.multiple_of(q * width, width), width),
                     ] = piece[c, s * width : (s + 1) * width, :]
 
@@ -145,22 +150,22 @@
         copy.wait()
 
 
-def ladder(where, pieces, amps, residual, capacity):
+def ladder(where, pieces, amps, offsets, residual, capacity):
     columns, _, width = pieces[0].shape
     n_pieces, n_amps = len(pieces), len(amps)
     rows, n_cols = residual.shape
-    depth = n_amps * width
-    any_spec = pl.BlockSpec(memory_space=pl.ANY)
+    depth = sum(map(len, offsets)) * width
+    hbm = pl.BlockSpec(memory_space=pltpu.HBM)
     vmem = pl.BlockSpec(memory_space=pltpu.VMEM)
     held = sum(x.size * x.dtype.itemsize for x in (*pieces, *amps))
     held += 2 * rows * depth + 2 * depth * n_cols + 4 * rows * n_cols
     return pl.pallas_call(
-        functools.partial(ladder_kernel, n_pieces, n_amps, capacity),
+        functools.partial(ladder_kernel, n_pieces, offsets, capacity),
         out_shape=jax.ShapeDtypeStruct(residual.shape, residual.dtype),
         in_specs=[pl.BlockSpec(memory_space=pltpu.SMEM)]
         + [vmem] * (n_pieces + n_amps)
-        + [any_spec],
-        out_specs=any_spec,
+        + [hbm],
+        out_specs=hbm,
         scratch_shapes=[
             pltpu.VMEM((n_pieces * columns, width), jnp.int32),
             pltpu.SMEM((n_pieces * columns, width), jnp.int32),
@@ -181,6 +186,25 @@
     return lax.ppermute(x, axis, [(i, i ^ flip) for i in range(size)])
 
 
+def gather_amps(amplitudes, n_col, inner):
+    held, slots = [amplitudes[None]], [[0]]
+    flip = inner
+    while flip < n_col:
+        if len(held) > 1:
+            held = [join(held)]
+            slots = [sum(slots, [])]
+        held.append(exchange(held[0], "col", flip))
+        slots.append([s ^ flip for s in slots[0]])
+        if flip == inner:
+            held, slots = [join(held)], [sum(slots, [])]
+        flip *= 2
+    for lane in range(1, inner):
+        for group in range(len(held)):
+            held.append(exchange(held[group], "col", lane))
+            slots.append([s ^ lane for s in slots[group]])
+    return held, slots
+
+
 def body(amplitudes, packed_tiles, tile_ids, residual_in):
     n_col, n_row = lax.axis_size("col"), lax.axis_size("row")
     col, row = lax.axis_index("col"), lax.axis_index("row")
@@ -188,22 +212,18 @@
     capacity = -(-packed_tiles.shape[1] // n_col)
     near = n_col // 2
     outgoing = pack(col, packed_tiles, tile_ids, n_col, capacity)
-    chunks = [outgoing[0]] + [exchange(outgoing[s], "col", s) for s in range(1, n_col)]
-    groups = [join(chunks[:near]), join(chunks[near:])]
+    chunks = [outgoing[0][None]]
+    chunks += [exchange(outgoing[s][None], "col", s) for s in range(1, n_col)]
+    shards, slots = gather_amps(amplitudes, n_col, inner)
+    groups = [join(chunks[near:]), join(chunks[:near])]
     pieces, rows = [], []
     for group in groups:
         for flip in range(0, n_row, CORES):
             mine = exchange(group, "row", flip) if flip else group
             pieces += [mine, exchange(mine, "row", 1)]
             rows += [row ^ flip, row ^ flip ^ 1]
-    shards, columns = [], []
-    for flip in range(0, n_col, inner):
-        shard = exchange(amplitudes, "col", flip) if flip else amplitudes
-        for lane in range(inner):
-            shards.append(exchange(shard, "col", lane) if lane else shard)
-            columns.append(col ^ flip ^ lane)
-    where = jnp.stack(rows + columns).astype(jnp.int32)
-    return ladder(where, pieces, shards, residual_in, capacity)
+    where = jnp.stack(rows + [col]).astype(jnp.int32)
+    return ladder(where, pieces, shards, slots, residual_in, capacity)
 
 
 def solution(mesh):

time: 58.8 us -> 57 us (0.969)
  starting transfers between devices: 27.8 us -> 23.3 us
  waiting for transfers between devices: 20.3 us -> 22.1 us
  Pallas kernels: 6.14 us -> 6.76 us
    ppermute x20 -> x17, starting transfers between devices: 27.8 us -> 23.3 us  [exchange(): return lax.ppermute(x, axis, [(i, i ^ flip) for i in range(size)])]
    ppermute x20 -> x17, waiting for transfers between devices: 20.3 us -> 22.1 us  [exchange(): return lax.ppermute(x, axis, [(i, i ^ flip) for i in range(size)])]
    pallas_call x3 -> x4, Pallas kernels: 5.29 us -> 5.91 us  [the longest x1 5.85 us: ladder(): pl.pallas_call(functools.partial(ladder_kernel, n_pieces, offsets, capaci...]
    unnamed x8 -> x12, local copies, waits for them, and re-layouts: 4.19 us -> 4.41 us
  transfers between devices with their start and end apart: 20 -> 17, of which waited for: 8 -> 4; matrix products, arithmetic and copies ran while one was open for 0% -> 0% of each run, Pallas kernels for 0% -> 0%
where the time goes in v2:
time: 57 us; the launch traced here: 56.8 us
  starting transfers between devices  23.3 us (41%)
  waiting for transfers between devices  22.1 us (39%)
  Pallas kernels  6.76 us (12%)
  local copies, waits for them, and re-layouts  4.5 us (8%)
    ppermute x17, starting transfers between devices, exchange(): return lax.ppermute(x, axis, [(i, i ^ flip) for i in range(size)])  23.3 us
    ppermute x17, waiting for transfers between devices, exchange(): return lax.ppermute(x, axis, [(i, i ^ flip) for i in range(size)])  22.1 us
    pallas_call x1, Pallas kernels, ladder(): pl.pallas_call(functools.partial(ladder_kernel, n_pieces, offsets, capaci...  5.85 us
    unnamed x12, local copies, waits for them, and re-layouts  4.41 us
  transfers between devices with their start and end apart: 17, of which 4 were waited for; matrix products, arithmetic and copies ran while one was open for 0% of the time, Pallas kernels for 0%

profile of v2, /device:TPU:0, one launch (start us, length us, event | category | flops | bytes accessed | tf_op | source)
XLA Modules:
  0.0 56.8 jit_solution(15793768182147681685)
XLA Ops:
  0.0 1.2 %copy-done.1 = bf16[1,16,128,128]{3,2,1,0:T(8,128)(2,1)S(1)} copy-done((bf16[1,16,128,128]{3,2,1,0:T(8,128)(2,1)S(1)}, bf16[1,16,128,128]{3,2,1,0:T(8,128)(2,1)}, u32[]{:S(2)}) %copy-start.1) | copy-done | bytes 524312
  1.2 0.7 %copy-done.5 = s32[1,16]{1,0:T(1,128)S(1)} copy-done((s32[1,16]{1,0:T(1,128)S(1)}, s32[1,16]{1,0:T(1,128)}, u32[]{:S(2)}) %copy-start.5) | copy-done | bytes 88
  1.9 0.8 %pack.1 = (bf16[272,128]{1,0:T(8,128)(2,1)S(1)}, bf16[272,128]{1,0:T(8,128)(2,1)S(1)}, bf16[272,128]{1,0:T(8,128)(2,1)S(1)}, bf16[272,128]{1,0:T(8,128)(2,1)S(1)...) custom-call(s32[1]{0:T(128)} %bitcast.4.me_ref, ...), custom_call_target="tpu_custom_call" | custom-call | tf_op jit(solution)/shard_map/pack/pallas_call | solution.py:55
  2.7 3.0 %collective-permute-start.7 = (bf16[1,272,128]{2,1,0:T(8,128)(2,1)S(1)}, bf16[1,272,128]{2,1,0:T(8,128)(2,1)S(1)}, u32[]{:S(2)}, u32[]{:S(2)}) collective-permute-start(bf16[1,272,128]{2,1,0:T(8,128)(2,1)S(1)} %bitcast.23), channel_id=1, source_target_pairs={{0,1},{1,0},{2,3},{3,2},{4,5},{5,4},{6,7},{7,6},{8,9},{9,8},{10,11... | collective-permute-start | bytes 208904 | tf_op jit(solution)/shard_map/ppermute | solution.py:186
  5.7 1.6 %collective-permute-start.8 = (bf16[1,272,128]{2,1,0:T(8,128)(2,1)S(1)}, bf16[1,272,128]{2,1,0:T(8,128)(2,1)S(1)}, u32[]{:S(2)}, u32[]{:S(2)}) collective-permute-start(bf16[1,272,128]{2,1,0:T(8,128)(2,1)S(1)} %bitcast.22), channel_id=1, source_target_pairs={{0,2},{1,3},{2,0},{3,1},{4,6},{5,7},{6,4},{7,5},{8,10},{9,11},{10,... | collective-permute-start | bytes 208904 | tf_op jit(solution)/shard_map/ppermute | solution.py:186
  7.3 2.0 %collective-permute-start.13 = (bf16[1,512,128]{2,1,0:T(8,128)(2,1)}, bf16[1,512,128]{2,1,0:T(8,128)(2,1)S(1)}, u32[]{:S(2)}, u32[]{:S(2)}) collective-permute-start(bf16[1,512,128]{2,1,0:T(8,128)(2,1)} %bitcast.14), channel_id=1, source_target_pairs={{0,2},{1,3},{2,0},{3,1},{4,6},{5,7},{6,4},{7,5},{8,10},{9,11},{10,... | collective-permute-start | bytes 393224 | tf_op jit(solution)/shard_map/ppermute | solution.py:186
  9.3 3.5 %collective-permute-start.1 = (bf16[1,272,128]{2,1,0:T(8,128)(2,1)S(1)}, bf16[1,272,128]{2,1,0:T(8,128)(2,1)S(1)}, u32[]{:S(2)}, u32[]{:S(2)}) collective-permute-start(bf16[1,272,128]{2,1,0:T(8,128)(2,1)S(1)} %bitcast.20), channel_id=1, source_target_pairs={{0,5},{1,4},{2,7},{3,6},{4,1},{5,0},{6,3},{7,2},{8,13},{9,12},{10,... | collective-permute-start | bytes 208904 | tf_op jit(solution)/shard_map/ppermute | solution.py:186
  12.8 0.3 collective-permute-start
  13.1 2.5 %collective-permute-start.2 = (bf16[1,272,128]{2,1,0:T(8,128)(2,1)S(1)}, bf16[1,272,128]{2,1,0:T(8,128)(2,1)S(1)}, u32[]{:S(2)}, u32[]{:S(2)}) collective-permute-start(bf16[1,272,128]{2,1,0:T(8,128)(2,1)S(1)} %bitcast.18), channel_id=1, source_target_pairs={{0,6},{1,7},{2,4},{3,5},{4,2},{5,3},{6,0},{7,1},{8,14},{9,15},{10,... | collective-permute-start | bytes 208904 | tf_op jit(solution)/shard_map/ppermute | solution.py:186
  15.6 2.7 %collective-permute-start.3 = (bf16[1,272,128]{2,1,0:T(8,128)(2,1)S(1)}, bf16[1,272,128]{2,1,0:T(8,128)(2,1)S(1)}, u32[]{:S(2)}, u32[]{:S(2)}) collective-permute-start(bf16[1,272,128]{2,1,0:T(8,128)(2,1)S(1)} %bitcast.17), channel_id=1, source_target_pairs={{0,7},{1,6},{2,5},{3,4},{4,3},{5,2},{6,1},{7,0},{8,15},{9,14},{10,... | collective-permute-start | bytes 208904 | tf_op jit(solution)/shard_map/ppermute | solution.py:186
  18.3 1.6 %collective-permute-start.11 = (bf16[4,272,128]{2,1,0:T(8,128)(2,1)S(1)}, bf16[4,272,128]{2,1,0:T(8,128)(2,1)S(1)}, u32[]{:S(2)}, u32[]{:S(2)}) collective-permute-start(bf16[4,272,128]{2,1,0:T(8,128)(2,1)S(1)} %join.4.refs_4_), channel_id=1, source_target_pairs={{0,16},{8,24},{16,0},{24,8},{1,17},{9,25},{17,1},{25,9},{2,18},{10... | collective-permute-start | bytes 835592 | tf_op jit(solution)/shard_map/ppermute | solution.py:186
  19.9 3.9 %collective-permute-done.refs_0_ = bf16[1,272,128]{2,1,0:T(8,128)(2,1)S(1)} collective-permute-done((bf16[1,272,128]{2,1,0:T(8,128)(2,1)S(1)}, bf16[1,272,128]{2,1,0:T(8,128)(2,1)S(1)}, u32[]{:S(2)}, u32[]{:S(2)}) %collective-permute-start) | collective-permute-done | bytes 69664 | tf_op jit(solution)/shard_map/ppermute | solution.py:186
  23.8 1.6 %collective-permute-start.5 = (bf16[4,272,128]{2,1,0:T(8,128)(2,1)S(1)}, bf16[4,272,128]{2,1,0:T(8,128)(2,1)S(1)}, u32[]{:S(2)}, u32[]{:S(2)}) collective-permute-start(bf16[4,272,128]{2,1,0:T(8,128)(2,1)S(1)} %join.3.refs_0_), channel_id=1, source_target_pairs={{0,16},{8,24},{16,0},{24,8},{1,17},{9,25},{17,1},{25,9},{2,18},{10... | collective-permute-start | bytes 835592 | tf_op jit(solution)/shard_map/ppermute | solution.py:186
  25.4 0.9 %copy-done.4 = bf16[512,128]{1,0:T(8,128)(2,1)S(1)} copy-done((bf16[512,128]{1,0:T(8,128)(2,1)S(1)}, bf16[512,128]{1,0:T(8,128)(2,1)}, u32[]{:S(2)}) %copy-start.4) | copy-done | bytes 131096
  26.3 2.4 %collective-permute-start.14 = (bf16[2,512,128]{2,1,0:T(8,128)(2,1)S(1)}, bf16[2,512,128]{2,1,0:T(8,128)(2,1)}, u32[]{:S(2)}, u32[]{:S(2)}) collective-permute-start(bf16[2,512,128]{2,1,0:T(8,128)(2,1)S(1)} %join.5.refs_8_), channel_id=1, source_target_pairs={{0,4},{1,5},{2,6},{3,7},{4,0},{5,1},{6,2},{7,3},{8,12},{9,13},{10,... | collective-permute-start | bytes 786440 | tf_op jit(solution)/shard_map/ppermute | solution.py:186
  29.0 0.3 collective-permute-start.12
  29.3 1.6 %collective-permute-done.5.refs_2_ = bf16[4,272,128]{2,1,0:T(8,128)(2,1)S(1)} collective-permute-done((bf16[4,272,128]{2,1,0:T(8,128)(2,1)S(1)}, bf16[4,272,128]{2,1,0:T(8,128)(2,1)S(1)}, u32[]{:S(2)}, u32[]{:S(2)}) %collective-permute-start.5) | collective-permute-done | bytes 278560 | tf_op jit(solution)/shard_map/ppermute | solution.py:186
  30.9 0.7 %copy-done.2 = bf16[4,272,128]{2,1,0:T(8,128)(2,1)} copy-done((bf16[4,272,128]{2,1,0:T(8,128)(2,1)}, bf16[4,272,128]{2,1,0:T(8,128)(2,1)S(1)}, u32[]{:S(2)}) %copy-start.2) | copy-done | bytes 278552
  31.6 0.5 collective-permute-start.15
  32.1 9.6 %collective-permute-done.14.refs_9_ = bf16[2,512,128]{2,1,0:T(8,128)(2,1)} collective-permute-done((bf16[2,512,128]{2,1,0:T(8,128)(2,1)S(1)}, bf16[2,512,128]{2,1,0:T(8,128)(2,1)}, u32[]{:S(2)}, u32[]{:S(2)}) %collective-permute-start.14) | collective-permute-done | bytes 262176 | tf_op jit(solution)/shard_map/ppermute | solution.py:186
  41.7 1.2 %collective-permute-start.16 = (bf16[2,512,128]{2,1,0:T(8,128)(2,1)}, bf16[2,512,128]{2,1,0:T(8,128)(2,1)}, u32[]{:S(2)}, u32[]{:S(2)}) collective-permute-start(bf16[2,512,128]{2,1,0:T(8,128)(2,1)} %collective-permute-done.14.refs_9_), channel_id=1, source_target_pairs={{0,1},{1,0},{2,3},{3,2},{4,5},{5,4},{6,7},{7,6},{8,9},{9,8},{10,11... | collective-permute-start | bytes 786440 | tf_op jit(solution)/shard_map/ppermute | solution.py:186
  43.0 7.0 %collective-permute-done.16.refs_11_ = bf16[2,512,128]{2,1,0:T(8,128)(2,1)} collective-permute-done((bf16[2,512,128]{2,1,0:T(8,128)(2,1)}, bf16[2,512,128]{2,1,0:T(8,128)(2,1)}, u32[]{:S(2)}, u32[]{:S(2)}) %collective-permute-start.16) | collective-permute-done | bytes 262176 | tf_op jit(solution)/shard_map/ppermute | solution.py:186
  50.0 1.0 %copy-done.3 = bf16[4,272,128]{2,1,0:T(8,128)(2,1)S(1)} copy-done((bf16[4,272,128]{2,1,0:T(8,128)(2,1)S(1)}, bf16[4,272,128]{2,1,0:T(8,128)(2,1)}, u32[]{:S(2)}) %copy-start.3) | copy-done | bytes 278552
  50.9 5.9 %ladder.1 = f32[512,1024]{1,0:T(8,128)} custom-call(s32[9]{0:T(128)S(1)} %stack.27.where_ref, bf16[4,272,128]{2,1,0:T(8,128)(2,1)S(1)} %join.3.refs_0_, bf16[4,272,128]{2,1,0:T(8,128)(2,1)} %collective-permute-done.4.refs_1_, bf16[4,272,128]{2,1,0:T(8,128)(2,1)S(1)} %collective-permute-done.5.refs_2_, bf16[4,272,128]{2,1,0:T(8,128)(2,1)} %collective-permute-done.6.refs_3_, ...), custom_call_target="tpu_custom_call" | custom-call | tf_op jit(solution)/shard_map/ladder/pallas_call | solution.py:162
  (28 shorter events, 0.4 us)
Async XLA Ops:
  0.0 50.0 %copy-start = (f32[512,1024]{1,0:T(8,128)S(1)}, f32[512,1024]{1,0:T(8,128)}, u32[]{:S(2)}) copy-start(f32[512,1024]{1,0:T(8,128)} %refs_12_.1) | copy-start | bytes 6291460
  0.0 1.2 %copy-start.1 = (bf16[1,16,128,128]{3,2,1,0:T(8,128)(2,1)S(1)}, bf16[1,16,128,128]{3,2,1,0:T(8,128)(2,1)}, u32[]{:S(2)}) copy-start(bf16[1,16,128,128]{3,2,1,0:T(8,128)(2,1)} %tiles_ref.1) | copy-start | bytes 1572868
  1.2 0.7 %copy-start.5 = (s32[1,16]{1,0:T(1,128)S(1)}, s32[1,16]{1,0:T(1,128)}, u32[]{:S(2)}) copy-start(s32[1,16]{1,0:T(1,128)} %ids_ref.1) | copy-start | bytes 196
  2.7 10.1 %collective-permute-start.7 = (bf16[1,272,128]{2,1,0:T(8,128)(2,1)S(1)}, bf16[1,272,128]{2,1,0:T(8,128)(2,1)S(1)}, u32[]{:S(2)}, u32[]{:S(2)}) collective-permute-start(bf16[1,272,128]{2,1,0:T(8,128)(2,1)S(1)} %bitcast.23), channel_id=1, source_target_pairs={{0,1},{1,0},{2,3},{3,2},{4,5},{5,4},{6,7},{7,6},{8,9},{9,8},{10,11... | collective-permute-start | bytes 208904 | tf_op jit(solution)/shard_map/ppermute | solution.py:186
  5.7 7.4 %collective-permute-start.8 = (bf16[1,272,128]{2,1,0:T(8,128)(2,1)S(1)}, bf16[1,272,128]{2,1,0:T(8,128)(2,1)S(1)}, u32[]{:S(2)}, u32[]{:S(2)}) collective-permute-start(bf16[1,272,128]{2,1,0:T(8,128)(2,1)S(1)} %bitcast.22), channel_id=1, source_target_pairs={{0,2},{1,3},{2,0},{3,1},{4,6},{5,7},{6,4},{7,5},{8,10},{9,11},{10,... | collective-permute-start | bytes 208904 | tf_op jit(solution)/shard_map/ppermute | solution.py:186
  7.3 8.3 %collective-permute-start.9 = (bf16[1,272,128]{2,1,0:T(8,128)(2,1)S(1)}, bf16[1,272,128]{2,1,0:T(8,128)(2,1)S(1)}, u32[]{:S(2)}, u32[]{:S(2)}) collective-permute-start(bf16[1,272,128]{2,1,0:T(8,128)(2,1)S(1)} %bitcast.21), channel_id=1, source_target_pairs={{0,3},{1,2},{2,1},{3,0},{4,7},{5,6},{6,5},{7,4},{8,11},{9,10},{10,... | collective-permute-start | bytes 208904 | tf_op jit(solution)/shard_map/ppermute | solution.py:186
  7.3 18.1 %collective-permute-start.13 = (bf16[1,512,128]{2,1,0:T(8,128)(2,1)}, bf16[1,512,128]{2,1,0:T(8,128)(2,1)S(1)}, u32[]{:S(2)}, u32[]{:S(2)}) collective-permute-start(bf16[1,512,128]{2,1,0:T(8,128)(2,1)} %bitcast.14), channel_id=1, source_target_pairs={{0,2},{1,3},{2,0},{3,1},{4,6},{5,7},{6,4},{7,5},{8,10},{9,11},{10,... | collective-permute-start | bytes 393224 | tf_op jit(solution)/shard_map/ppermute | solution.py:186
  9.3 9.0 %collective-permute-start.1 = (bf16[1,272,128]{2,1,0:T(8,128)(2,1)S(1)}, bf16[1,272,128]{2,1,0:T(8,128)(2,1)S(1)}, u32[]{:S(2)}, u32[]{:S(2)}) collective-permute-start(bf16[1,272,128]{2,1,0:T(8,128)(2,1)S(1)} %bitcast.20), channel_id=1, source_target_pairs={{0,5},{1,4},{2,7},{3,6},{4,1},{5,0},{6,3},{7,2},{8,13},{9,12},{10,... | collective-permute-start | bytes 208904 | tf_op jit(solution)/shard_map/ppermute | solution.py:186
  12.8 11.0 %collective-permute-start = (bf16[1,272,128]{2,1,0:T(8,128)(2,1)S(1)}, bf16[1,272,128]{2,1,0:T(8,128)(2,1)S(1)}, u32[]{:S(2)}, u32[]{:S(2)}) collective-permute-start(bf16[1,272,128]{2,1,0:T(8,128)(2,1)S(1)} %bitcast.19), channel_id=1, source_target_pairs={{0,4},{1,5},{2,6},{3,7},{4,0},{5,1},{6,2},{7,3},{8,12},{9,13},{10,... | collective-permute-start | bytes 208904 | tf_op jit(solution)/shard_map/ppermute | solution.py:186
  13.1 10.6 %collective-permute-start.2 = (bf16[1,272,128]{2,1,0:T(8,128)(2,1)S(1)}, bf16[1,272,128]{2,1,0:T(8,128)(2,1)S(1)}, u32[]{:S(2)}, u32[]{:S(2)}) collective-permute-start(bf16[1,272,128]{2,1,0:T(8,128)(2,1)S(1)} %bitcast.18), channel_id=1, source_target_pairs={{0,6},{1,7},{2,4},{3,5},{4,2},{5,3},{6,0},{7,1},{8,14},{9,15},{10,... | collective-permute-start | bytes 208904 | tf_op jit(solution)/shard_map/ppermute | solution.py:186
  15.6 8.1 %collective-permute-start.3 = (bf16[1,272,128]{2,1,0:T(8,128)(2,1)S(1)}, bf16[1,272,128]{2,1,0:T(8,128)(2,1)S(1)}, u32[]{:S(2)}, u32[]{:S(2)}) collective-permute-start(bf16[1,272,128]{2,1,0:T(8,128)(2,1)S(1)} %bitcast.17), channel_id=1, source_target_pairs={{0,7},{1,6},{2,5},{3,4},{4,3},{5,2},{6,1},{7,0},{8,15},{9,14},{10,... | collective-permute-start | bytes 208904 | tf_op jit(solution)/shard_map/ppermute | solution.py:186
  18.3 10.7 %collective-permute-start.11 = (bf16[4,272,128]{2,1,0:T(8,128)(2,1)S(1)}, bf16[4,272,128]{2,1,0:T(8,128)(2,1)S(1)}, u32[]{:S(2)}, u32[]{:S(2)}) collective-permute-start(bf16[4,272,128]{2,1,0:T(8,128)(2,1)S(1)} %join.4.refs_4_), channel_id=1, source_target_pairs={{0,16},{8,24},{16,0},{24,8},{1,17},{9,25},{17,1},{25,9},{2,18},{10... | collective-permute-start | bytes 835592 | tf_op jit(solution)/shard_map/ppermute | solution.py:186
  23.8 7.1 %collective-permute-start.5 = (bf16[4,272,128]{2,1,0:T(8,128)(2,1)S(1)}, bf16[4,272,128]{2,1,0:T(8,128)(2,1)S(1)}, u32[]{:S(2)}, u32[]{:S(2)}) collective-permute-start(bf16[4,272,128]{2,1,0:T(8,128)(2,1)S(1)} %join.3.refs_0_), channel_id=1, source_target_pairs={{0,16},{8,24},{16,0},{24,8},{1,17},{9,25},{17,1},{25,9},{2,18},{10... | collective-permute-start | bytes 835592 | tf_op jit(solution)/shard_map/ppermute | solution.py:186
  25.4 5.5 %collective-permute-start.10 = (bf16[4,272,128]{2,1,0:T(8,128)(2,1)S(1)}, bf16[4,272,128]{2,1,0:T(8,128)(2,1)S(1)}, u32[]{:S(2)}, u32[]{:S(2)}) collective-permute-start(bf16[4,272,128]{2,1,0:T(8,128)(2,1)S(1)} %join.4.refs_4_), channel_id=1, source_target_pairs={{0,8},{8,0},{16,24},{24,16},{1,9},{9,1},{17,25},{25,17},{2,10},{10... | collective-permute-start | bytes 835592 | tf_op jit(solution)/shard_map/ppermute | solution.py:186
  25.4 0.9 %copy-start.4 = (bf16[512,128]{1,0:T(8,128)(2,1)S(1)}, bf16[512,128]{1,0:T(8,128)(2,1)}, u32[]{:S(2)}) copy-start(bf16[512,128]{1,0:T(8,128)(2,1)} %param.4) | copy-start | bytes 393220
  26.3 15.4 %collective-permute-start.14 = (bf16[2,512,128]{2,1,0:T(8,128)(2,1)S(1)}, bf16[2,512,128]{2,1,0:T(8,128)(2,1)}, u32[]{:S(2)}, u32[]{:S(2)}) collective-permute-start(bf16[2,512,128]{2,1,0:T(8,128)(2,1)S(1)} %join.5.refs_8_), channel_id=1, source_target_pairs={{0,4},{1,5},{2,6},{3,7},{4,0},{5,1},{6,2},{7,3},{8,12},{9,13},{10,... | collective-permute-start | bytes 786440 | tf_op jit(solution)/shard_map/ppermute | solution.py:186
  28.7 14.2 %collective-permute-start.4 = (bf16[4,272,128]{2,1,0:T(8,128)(2,1)S(1)}, bf16[4,272,128]{2,1,0:T(8,128)(2,1)}, u32[]{:S(2)}, u32[]{:S(2)}) collective-permute-start(bf16[4,272,128]{2,1,0:T(8,128)(2,1)S(1)} %join.3.refs_0_), channel_id=1, source_target_pairs={{0,8},{8,0},{16,24},{24,16},{1,9},{9,1},{17,25},{25,17},{2,10},{10... | collective-permute-start | bytes 835592 | tf_op jit(solution)/shard_map/ppermute | solution.py:186
  29.0 14.0 %collective-permute-start.12 = (bf16[4,272,128]{2,1,0:T(8,128)(2,1)S(1)}, bf16[4,272,128]{2,1,0:T(8,128)(2,1)}, u32[]{:S(2)}, u32[]{:S(2)}) collective-permute-start(bf16[4,272,128]{2,1,0:T(8,128)(2,1)S(1)} %collective-permute-done.11.refs_6_), channel_id=1, source_target_pairs={{0,8},{8,0},{16,24},{24,16},{1,9},{9,1},{17,25},{25,17},{2,10},{10... | collective-permute-start | bytes 835592 | tf_op jit(solution)/shard_map/ppermute | solution.py:186
  30.9 12.1 %collective-permute-start.6 = (bf16[4,272,128]{2,1,0:T(8,128)(2,1)S(1)}, bf16[4,272,128]{2,1,0:T(8,128)(2,1)}, u32[]{:S(2)}, u32[]{:S(2)}) collective-permute-start(bf16[4,272,128]{2,1,0:T(8,128)(2,1)S(1)} %collective-permute-done.5.refs_2_), channel_id=1, source_target_pairs={{0,8},{8,0},{16,24},{24,16},{1,9},{9,1},{17,25},{25,17},{2,10},{10... | collective-permute-start | bytes 835592 | tf_op jit(solution)/shard_map/ppermute | solution.py:186
  30.9 0.7 %copy-start.2 = (bf16[4,272,128]{2,1,0:T(8,128)(2,1)}, bf16[4,272,128]{2,1,0:T(8,128)(2,1)S(1)}, u32[]{:S(2)}) copy-start(bf16[4,272,128]{2,1,0:T(8,128)(2,1)S(1)} %collective-permute-done.10.refs_5_) | copy-start | bytes 835588
  31.6 11.4 %collective-permute-start.15 = (bf16[2,512,128]{2,1,0:T(8,128)(2,1)S(1)}, bf16[2,512,128]{2,1,0:T(8,128)(2,1)}, u32[]{:S(2)}, u32[]{:S(2)}) collective-permute-start(bf16[2,512,128]{2,1,0:T(8,128)(2,1)S(1)} %join.5.refs_8_), channel_id=1, source_target_pairs={{0,1},{1,0},{2,3},{3,2},{4,5},{5,4},{6,7},{7,6},{8,9},{9,8},{10,11... | collective-permute-start | bytes 786440 | tf_op jit(solution)/shard_map/ppermute | solution.py:186
  41.7 8.3 %collective-permute-start.16 = (bf16[2,512,128]{2,1,0:T(8,128)(2,1)}, bf16[2,512,128]{2,1,0:T(8,128)(2,1)}, u32[]{:S(2)}, u32[]{:S(2)}) collective-permute-start(bf16[2,512,128]{2,1,0:T(8,128)(2,1)} %collective-permute-done.14.refs_9_), channel_id=1, source_target_pairs={{0,1},{1,0},{2,3},{3,2},{4,5},{5,4},{6,7},{7,6},{8,9},{9,8},{10,11... | collective-permute-start | bytes 786440 | tf_op jit(solution)/shard_map/ppermute | solution.py:186
  50.0 1.0 %copy-start.3 = (bf16[4,272,128]{2,1,0:T(8,128)(2,1)S(1)}, bf16[4,272,128]{2,1,0:T(8,128)(2,1)}, u32[]{:S(2)}) copy-start(bf16[4,272,128]{2,1,0:T(8,128)(2,1)} %copy-done.2) | copy-start | bytes 835588

commit v3 on v2

v3 whole, which is shorter than its diff:
```python
import functools
import math

import jax
import jax.numpy as jnp
from jax import lax
from jax.experimental import pallas as pl
from jax.experimental.pallas import tpu as pltpu
from jax.sharding import PartitionSpec as P

KT_DEV = 2
QT_DEV = 8
CORES = 2
META = 16
MIB = 1024 * 1024


def pack_kernel(columns, capacity, me_ref, ids_hbm, tiles_hbm, *refs):
    outs = refs[:columns]
    ids_ref, tiles_ref, slot_tile, slot_place, count, ids_sem, tiles_sem = refs[columns:]
    ids_copy = pltpu.make_async_copy(ids_hbm, ids_ref, ids_sem)
    tiles_copy = pltpu.make_async_copy(tiles_hbm, tiles_ref, tiles_sem)
    ids_copy.start()
    tiles_copy.start()
    per_device, width = tiles_ref.shape[1], tiles_ref.shape[2]
    shift = per_device.bit_length() - 1
    for d in range(columns):
        count[d] = 0
        for s in range(capacity):
            slot_place[d * capacity + s] = per_device
    ids_copy.wait()
    for t in range(per_device):
        tile_id = ids_ref[0, t]
        target = lax.shift_right_logical(tile_id, shift)
        rank = count[target]
        count[target] = rank + 1
        slot_tile[target * capacity + rank] = t
        slot_place[target * capacity + rank] = tile_id & (per_device - 1)
    tiles_copy.wait()
    lane = lax.broadcasted_iota(jnp.int32, (META, width), 1)
    for d, out in enumerate(outs):
        target = me_ref[0] ^ d
        row = jnp.full((META, width), per_device, jnp.int32)
        for s in range(capacity):
            place = slot_place[target * capacity + s]
            row = jnp.where(lane == s, place, row)

            @pl.when(place < per_device)
            def _():
                out[s * width : (s + 1) * width, :] = tiles_ref[
                    0, slot_tile[target * capacity + s]
                ]

        out[capacity * width :, :] = row.astype(jnp.float32).astype(jnp.bfloat16)


def pack(col, packed_tiles, tile_ids, columns, capacity):
    _, per_device, width, _ = packed_tiles.shape
    chunk = jax.ShapeDtypeStruct((capacity * width + META, width), packed_tiles.dtype)
    smem = pl.BlockSpec(memory_space=pltpu.SMEM)
    vmem = pl.BlockSpec(memory_space=pltpu.VMEM)
    hbm = pl.BlockSpec(memory_space=pltpu.HBM)
    return pl.pallas_call(
        functools.partial(pack_kernel, columns, capacity),
        out_shape=[chunk] * columns,
        in_specs=[smem, hbm, hbm],
        out_specs=[vmem] * columns,
        scratch_shapes=[
            pltpu.SMEM(tile_ids.shape, jnp.int32),
            pltpu.VMEM(packed_tiles.shape, packed_tiles.dtype),
            pltpu.SMEM((columns * capacity,), jnp.int32),
            pltpu.SMEM((columns * capacity,), jnp.int32),
            pltpu.SMEM((columns,), jnp.int32),
            pltpu.SemaphoreType.DMA,
            pltpu.SemaphoreType.DMA,
        ],
        compiler_params=pltpu.CompilerParams(vmem_limit_bytes=8 * MIB),
        name="pack",
    )(col[None], tile_ids, packed_tiles)


def join_kernel(*refs):
    at = 0
    for part in refs[:-1]:
        refs[-1][at : at + part.shape[0]] = part[...]
        at += part.shape[0]


def join(chunks):
    vmem = pl.BlockSpec(memory_space=pltpu.VMEM)
    total = sum(c.shape[0] for c in chunks)
    return pl.pallas_call(
        join_kernel,
        out_shape=jax.ShapeDtypeStruct((total, *chunks[0].shape[1:]), chunks[0].dtype),
        in_specs=[vmem] * len(chunks),
        out_specs=vmem,
        compiler_params=pltpu.CompilerParams(vmem_limit_bytes=8 * MIB),
        name="join",
    )(*chunks)


def multiply(amp, block, start, out, sems, step):
    copies = []
    for n in range(block.shape[1] // step):
        cols = slice(n * step, (n + 1) * step)
        held = out[0] if sems is not None else out
        held[:, cols] = start[:, cols] + jnp.dot(
            amp[...], block[:, cols], preferred_element_type=jnp.float32
        )
        if sems is not None:
            part = pl.ds(n * step, step)
            copies.append(
                pltpu.make_async_copy(held.at[:, part], out[1].at[:, part], sems.at[n])
            )
            copies[-1].start()
    for copy in copies:
        copy.wait()


def near_kernel(n_pieces, offsets, capacity, where_ref, *refs):
    n_amps = len(offsets)
    pieces = refs[:n_pieces]
    amps = refs[n_pieces : n_pieces + n_amps]
    residual, total, far = refs[n_pieces + n_amps : n_pieces + n_amps + 3]
    places, table, amp, near, res, table_sem, res_sem = refs[n_pieces + n_amps + 3 :]
    columns = pieces[0].shape[0]
    width = pieces[0].shape[2]
    per_device = KT_DEV * QT_DEV
    half = amp.shape[1] // width
    res_copy = pltpu.make_async_copy(residual, res, res_sem)
    res_copy.start()
    for p, piece in enumerate(pieces):
        rows = piece[:, capacity * width :, :]
        places[p * columns : (p + 1) * columns] = jnp.max(
            rows.astype(jnp.float32), axis=1
        ).astype(jnp.int32)
    table_copy = pltpu.make_async_copy(places, table, table_sem)
    table_copy.start()
    for source, slots in zip(amps, offsets):
        for i, slot in enumerate(slots):
            amp[:, slot * width : (slot + 1) * width] = source[i]
    table_copy.wait()
    col = where_ref[n_pieces]
    for p, piece in enumerate(pieces):
        row = where_ref[p]

        def place(c, _, p=p, piece=piece, row=row):
            for s in range(capacity):
                position = table[p * columns + c, s]
                k = row * KT_DEV + lax.shift_right_logical(position, QT_DEV.bit_length() - 1)
                slot = k ^ col
                q = pl.multiple_of((position & (QT_DEV - 1)) * width, width)
                at = pl.multiple_of((slot & (half - 1)) * width, width)
                tile = piece.at[c, pl.ds(s * width, width), :]

                @pl.when((position < per_device) & (slot < half))
                def _():
                    near[pl.ds(at, width), pl.ds(q, width)] = tile[...]

                @pl.when((position < per_device) & (slot >= half))
                def _():
                    far[pl.ds(at, width), pl.ds(q, width)] = tile[...]

            return 0

        lax.fori_loop(0, columns, place, 0)
    res_copy.wait()
    multiply(amp, near, res, total, None, 2 * width)


def near_half(where, pieces, amps, offsets, residual, capacity):
    columns, _, width = pieces[0].shape
    n_pieces, n_amps = len(pieces), len(amps)
    rows, n_cols = residual.shape
    depth = sum(map(len, offsets)) * width
    hbm = pl.BlockSpec(memory_space=pltpu.HBM)
    vmem = pl.BlockSpec(memory_space=pltpu.VMEM)
    held = 2 * rows * depth + 4 * depth * n_cols + 8 * rows * n_cols
    held += sum(x.size * x.dtype.itemsize for x in pieces) // 2
    return pl.pallas_call(
        functools.partial(near_kernel, n_pieces, offsets, capacity),
        out_shape=[
            jax.ShapeDtypeStruct(residual.shape, residual.dtype),
            jax.ShapeDtypeStruct((depth, n_cols), pieces[0].dtype),
        ],
        in_specs=[pl.BlockSpec(memory_space=pltpu.SMEM)]
        + [vmem] * (n_pieces + n_amps)
        + [hbm],
        out_specs=[vmem, vmem],
        scratch_shapes=[
            pltpu.VMEM((n_pieces * columns, width), jnp.int32),
            pltpu.SMEM((n_pieces * columns, width), jnp.int32),
            pltpu.VMEM((rows, depth), pieces[0].dtype),
            pltpu.VMEM((depth, n_cols), pieces[0].dtype),
            pltpu.VMEM((rows, n_cols), residual.dtype),
            pltpu.SemaphoreType.DMA,
            pltpu.SemaphoreType.DMA,
        ],
        compiler_params=pltpu.CompilerParams(vmem_limit_bytes=held + 2 * MIB),
        cost_estimate=pl.CostEstimate(
            flops=2 * rows * depth * n_cols,
            bytes_accessed=16 * rows * n_cols,
            transcendentals=0,
        ),
        name="near_half",
    )(where, *pieces, *amps, residual)


def far_kernel(offsets, half, *refs):
    amps = refs[: len(offsets)]
    start, far, out, amp, total, sems = refs[len(offsets) :]
    width = amps[0].shape[2]
    for source, slots in zip(amps, offsets):
        for i, slot in enumerate(slots):
            at = (slot - half) * width
            amp[:, at : at + width] = source[i]
    multiply(amp, far, start, (total, out), sems, 2 * width)


def far_half(amps, offsets, total, far):
    rows, n_cols = total.shape
    depth, width = far.shape[0], amps[0].shape[2]
    vmem = pl.BlockSpec(memory_space=pltpu.VMEM)
    held = 4 * rows * depth + 2 * depth * n_cols + 8 * rows * n_cols
    return pl.pallas_call(
        functools.partial(far_kernel, offsets, depth // width),
        out_shape=jax.ShapeDtypeStruct(total.shape, total.dtype),
        in_specs=[vmem] * (len(amps) + 2),
        out_specs=pl.BlockSpec(memory_space=pltpu.HBM),
        scratch_shapes=[
            pltpu.VMEM((rows, depth), far.dtype),
            pltpu.VMEM((rows, n_cols), total.dtype),
            pltpu.SemaphoreType.DMA((n_cols // (2 * width),)),
        ],
        compiler_params=pltpu.CompilerParams(vmem_limit_bytes=held + 2 * MIB),
        cost_estimate=pl.CostEstimate(
            flops=2 * rows * depth * n_cols,
            bytes_accessed=16 * rows * n_cols,
            transcendentals=0,
        ),
        name="far_half",
    )(*amps, total, far)


def exchange(x, axis, flip):
    size = lax.axis_size(axis)
    return lax.ppermute(x, axis, [(i, i ^ flip) for i in range(size)])


def over_lanes(shard, slots, inner):
    held = [(shard, slots)]
    for lane in range(1, inner):
        held.append((exchange(shard, "col", lane), [s ^ lane for s in slots]))
    return held


def body(amplitudes, packed_tiles, tile_ids, residual_in):
    n_col, n_row = lax.axis_size("col"), lax.axis_size("row")
    col, row = lax.axis_index("col"), lax.axis_index("row")
    inner = 2 ** (int(math.log2(n_col)) // 2)
    capacity = -(-packed_tiles.shape[1] // n_col)
    half = n_col // 2
    outgoing = list(pack(col, packed_tiles, tile_ids, n_col, capacity))
    flips = range(inner, half, inner)
    held = [amplitudes[None]] + [exchange(amplitudes[None], "col", f) for f in flips]
    outgoing[half:], held = lax.optimization_barrier((outgoing[half:], held))
    chunks = [outgoing[0][None]]
    chunks += [exchange(outgoing[s][None], "col", s) for s in range(1, n_col)]
    slots = [0, *flips]
    passed = [exchange(shard, "col", half) for shard in held]
    near = over_lanes(join(held), slots, inner)
    pieces, rows = [], []
    for group in (join(chunks[half:]), join(chunks[:half])):
        for flip in range(0, n_row, CORES):
            mine = exchange(group, "row", flip) if flip else group
            if flip == CORES and len(pieces) > CORES:
                mine, passed[0] = lax.optimization_barrier((mine, passed[0]))
            pieces += [mine, exchange(mine, "row", 1)]
            rows += [row ^ flip, row ^ flip ^ 1]
    far = []
    for shard, slot in zip(passed, slots):
        far += over_lanes(shard, [slot ^ half], inner)
    where = jnp.stack(rows + [col]).astype(jnp.int32)
    total, far_block = near_half(where, pieces, *zip(*near), residual_in, capacity)
    return far_half(*zip(*far), total, far_block)


def solution(mesh):
    in_specs = (P("row", "col"), P("row", "col", None, None), P("row", "col"), P("row", "col"))
    out_specs = P("row", "col")
    return jax.shard_map(body, mesh=mesh, in_specs=in_specs, out_specs=out_specs, check_vma=False)
```

time: 57 us -> 55.1 us (0.967)
  waiting for transfers between devices: 22.1 us -> 18 us
  Pallas kernels: 6.76 us -> 9.19 us
  starting transfers between devices: 23.3 us -> 21.5 us
  local copies, waits for them, and re-layouts: 4.5 us -> 6.01 us
    ppermute x17 -> x19, waiting for transfers between devices: 22.1 us -> 18 us  [exchange(): return lax.ppermute(x, axis, [(i, i ^ flip) for i in range(size)])]
    ppermute x17 -> x19, starting transfers between devices: 23.3 us -> 21.5 us  [exchange(): return lax.ppermute(x, axis, [(i, i ^ flip) for i in range(size)])]
    pallas_call x1 -> x2, Pallas kernels: 5.85 us -> 7.37 us  [the longest x1 4.41 us: near_half(): pl.pallas_call(functools.partial(near_kernel, n_pieces, offsets, capacity...]
    unnamed x12 -> x16, local copies, waits for them, and re-layouts: 4.41 us -> 5.93 us
    pallas_call x3, Pallas kernels: 0.06 us -> 0.96 us  [join(): pl.pallas_call(join_kernel, out_shape=jax.ShapeDtypeStruct((total, *chunk...]
  transfers between devices with their start and end apart: 17 -> 19, of which waited for: 4 -> 5; matrix products, arithmetic and copies ran while one was open for 0% -> 0% of each run, Pallas kernels for 0% -> 11%
where the time goes in v3:
time: 55.1 us; the launch traced here: 54.8 us
  starting transfers between devices  21.5 us (39%)
  waiting for transfers between devices  18 us (33%)
  Pallas kernels  9.19 us (17%)
  local copies, waits for them, and re-layouts  6.01 us (11%)
    ppermute x19, starting transfers between devices, exchange(): return lax.ppermute(x, axis, [(i, i ^ flip) for i in range(size)])  21.5 us
    ppermute x19, waiting for transfers between devices, exchange(): return lax.ppermute(x, axis, [(i, i ^ flip) for i in range(size)])  18 us
    unnamed x16, local copies, waits for them, and re-layouts  5.93 us
    pallas_call x1, Pallas kernels, near_half(): pl.pallas_call(functools.partial(near_kernel, n_pieces, offsets, capacity...  4.41 us
    pallas_call x1, Pallas kernels, far_half(): pl.pallas_call(functools.partial(far_kernel, offsets, depth // width), ou...  2.96 us
  transfers between devices with their start and end apart: 19, of which 5 were waited for; matrix products, arithmetic and copies ran while one was open for 0% of the time, Pallas kernels for 11%

profile of v3, /device:TPU:0, one launch (start us, length us, event | category | flops | bytes accessed | tf_op | source)
XLA Modules:
  0.0 54.8 jit_solution(2666607915179783528)
XLA Ops:
  0.0 3.0 %collective-permute-start.4 = (bf16[1,512,128]{2,1,0:T(8,128)(2,1)}, bf16[1,512,128]{2,1,0:T(8,128)(2,1)}, u32[]{:S(2)}, u32[]{:S(2)}) collective-permute-start(bf16[1,512,128]{2,1,0:T(8,128)(2,1)} %bitcast.14), channel_id=1, source_target_pairs={{0,2},{1,3},{2,0},{3,1},{4,6},{5,7},{6,4},{7,5},{8,10},{9,11},{10,... | collective-permute-start | bytes 393224 | tf_op jit(solution)/shard_map/ppermute | solution.py:247
  3.0 1.0 %copy-done.1 = bf16[1,16,128,128]{3,2,1,0:T(8,128)(2,1)S(1)} copy-done((bf16[1,16,128,128]{3,2,1,0:T(8,128)(2,1)S(1)}, bf16[1,16,128,128]{3,2,1,0:T(8,128)(2,1)}, u32[]{:S(2)}) %copy-start.1) | copy-done | bytes 524312
  4.7 0.9 %pack.1 = (bf16[272,128]{1,0:T(8,128)(2,1)S(1)}, bf16[272,128]{1,0:T(8,128)(2,1)S(1)}, bf16[272,128]{1,0:T(8,128)(2,1)S(1)}, bf16[272,128]{1,0:T(8,128)(2,1)S(1)...) custom-call(s32[1]{0:T(128)} %bitcast.me_ref, ...), custom_call_target="tpu_custom_call" | custom-call | tf_op jit(solution)/shard_map/pack/pallas_call | solution.py:63
  5.6 1.6 %collective-permute-start = (bf16[1,272,128]{2,1,0:T(8,128)(2,1)S(1)}, bf16[1,272,128]{2,1,0:T(8,128)(2,1)S(1)}, u32[]{:S(2)}, u32[]{:S(2)}) collective-permute-start(bf16[1,272,128]{2,1,0:T(8,128)(2,1)S(1)} %bitcast.24), channel_id=1, source_target_pairs={{0,1},{1,0},{2,3},{3,2},{4,5},{5,4},{6,7},{7,6},{8,9},{9,8},{10,11... | collective-permute-start | bytes 208904 | tf_op jit(solution)/shard_map/ppermute | solution.py:247
  7.8 1.4 %collective-permute-start.2 = (bf16[1,272,128]{2,1,0:T(8,128)(2,1)S(1)}, bf16[1,272,128]{2,1,0:T(8,128)(2,1)S(1)}, u32[]{:S(2)}, u32[]{:S(2)}) collective-permute-start(bf16[1,272,128]{2,1,0:T(8,128)(2,1)S(1)} %bitcast.22), channel_id=1, source_target_pairs={{0,3},{1,2},{2,1},{3,0},{4,7},{5,6},{6,5},{7,4},{8,11},{9,10},{10,... | collective-permute-start | bytes 208904 | tf_op jit(solution)/shard_map/ppermute | solution.py:247
  9.2 3.5 %collective-permute-start.10 = (bf16[1,272,128]{2,1,0:T(8,128)(2,1)S(1)}, bf16[1,272,128]{2,1,0:T(8,128)(2,1)S(1)}, u32[]{:S(2)}, u32[]{:S(2)}) collective-permute-start(bf16[1,272,128]{2,1,0:T(8,128)(2,1)S(1)} %bitcast.21), channel_id=1, source_target_pairs={{0,5},{1,4},{2,7},{3,6},{4,1},{5,0},{6,3},{7,2},{8,13},{9,12},{10,... | collective-permute-start | bytes 208904 | tf_op jit(solution)/shard_map/ppermute | solution.py:247
  13.1 3.4 %collective-permute-start.12 = (bf16[1,272,128]{2,1,0:T(8,128)(2,1)S(1)}, bf16[1,272,128]{2,1,0:T(8,128)(2,1)S(1)}, u32[]{:S(2)}, u32[]{:S(2)}) collective-permute-start(bf16[1,272,128]{2,1,0:T(8,128)(2,1)S(1)} %bitcast.19), channel_id=1, source_target_pairs={{0,7},{1,6},{2,5},{3,4},{4,3},{5,2},{6,1},{7,0},{8,15},{9,14},{10,... | collective-permute-start | bytes 208904 | tf_op jit(solution)/shard_map/ppermute | solution.py:247
  16.5 1.6 %collective-permute-start.3 = (bf16[4,272,128]{2,1,0:T(8,128)(2,1)S(1)}, bf16[4,272,128]{2,1,0:T(8,128)(2,1)S(1)}, u32[]{:S(2)}, u32[]{:S(2)}) collective-permute-start(bf16[4,272,128]{2,1,0:T(8,128)(2,1)S(1)} %join.3.refs_4_), channel_id=1, source_target_pairs={{0,16},{8,24},{16,0},{24,8},{1,17},{9,25},{17,1},{25,9},{2,18},{10... | collective-permute-start | bytes 835592 | tf_op jit(solution)/shard_map/ppermute | solution.py:247
  18.1 3.2 %collective-permute-done.10.refs_1_ = bf16[1,272,128]{2,1,0:T(8,128)(2,1)S(1)} collective-permute-done((bf16[1,272,128]{2,1,0:T(8,128)(2,1)S(1)}, bf16[1,272,128]{2,1,0:T(8,128)(2,1)S(1)}, u32[]{:S(2)}, u32[]{:S(2)}) %collective-permute-start.10) | collective-permute-done | bytes 69664 | tf_op jit(solution)/shard_map/ppermute | solution.py:247
  21.3 2.9 %collective-permute-done.9.refs_0_ = bf16[1,272,128]{2,1,0:T(8,128)(2,1)S(1)} collective-permute-done((bf16[1,272,128]{2,1,0:T(8,128)(2,1)S(1)}, bf16[1,272,128]{2,1,0:T(8,128)(2,1)S(1)}, u32[]{:S(2)}, u32[]{:S(2)}) %collective-permute-start.9) | collective-permute-done | bytes 69664 | tf_op jit(solution)/shard_map/ppermute | solution.py:247
  24.2 1.6 %collective-permute-start.14 = (bf16[4,272,128]{2,1,0:T(8,128)(2,1)S(1)}, bf16[4,272,128]{2,1,0:T(8,128)(2,1)S(1)}, u32[]{:S(2)}, u32[]{:S(2)}) collective-permute-start(bf16[4,272,128]{2,1,0:T(8,128)(2,1)S(1)} %join.4.refs_0_), channel_id=1, source_target_pairs={{0,16},{8,24},{16,0},{24,8},{1,17},{9,25},{17,1},{25,9},{2,18},{10... | collective-permute-start | bytes 835592 | tf_op jit(solution)/shard_map/ppermute | solution.py:247
  25.8 0.9 %collective-permute-start.5 = (bf16[1,512,128]{2,1,0:T(8,128)(2,1)}, bf16[1,512,128]{2,1,0:T(8,128)(2,1)}, u32[]{:S(2)}, u32[]{:S(2)}) collective-permute-start(bf16[1,512,128]{2,1,0:T(8,128)(2,1)} %bitcast.15), channel_id=1, source_target_pairs={{0,4},{1,5},{2,6},{3,7},{4,0},{5,1},{6,2},{7,3},{8,12},{9,13},{10,... | collective-permute-start | bytes 393224 | tf_op jit(solution)/shard_map/ppermute | solution.py:247
  26.8 2.0 %collective-permute-start.7 = (bf16[1,512,128]{2,1,0:T(8,128)(2,1)}, bf16[1,512,128]{2,1,0:T(8,128)(2,1)}, u32[]{:S(2)}, u32[]{:S(2)}) collective-permute-start(bf16[1,512,128]{2,1,0:T(8,128)(2,1)} %collective-permute-done.4.refs_1_), channel_id=1, source_target_pairs={{0,4},{1,5},{2,6},{3,7},{4,0},{5,1},{6,2},{7,3},{8,12},{9,13},{10,... | collective-permute-start | bytes 393224 | tf_op jit(solution)/shard_map/ppermute | solution.py:247
  28.8 0.9 %copy-done.6 = bf16[512,128]{1,0:T(8,128)(2,1)S(1)} copy-done((bf16[512,128]{1,0:T(8,128)(2,1)S(1)}, bf16[512,128]{1,0:T(8,128)(2,1)}, u32[]{:S(2)}) %copy-start.6) | copy-done | bytes 131096
  29.7 0.9 %join.5.refs_8_ = bf16[2,512,128]{2,1,0:T(8,128)(2,1)S(1)} custom-call(bf16[1,512,128]{2,1,0:T(8,128)(2,1)S(1)} %bitcast.16, bf16[1,512,128]{2,1,0:T(8,128)(2,1)} %collective-permute-done.4.refs_1_), custom_call_target="tpu_custom_call" | custom-call | tf_op jit(solution)/shard_map/join/pallas_call | solution.py:92
  30.6 6.8 %collective-permute-done.5.refs_0_ = bf16[1,512,128]{2,1,0:T(8,128)(2,1)} collective-permute-done((bf16[1,512,128]{2,1,0:T(8,128)(2,1)}, bf16[1,512,128]{2,1,0:T(8,128)(2,1)}, u32[]{:S(2)}, u32[]{:S(2)}) %collective-permute-start.5) | collective-permute-done | bytes 131104 | tf_op jit(solution)/shard_map/ppermute | solution.py:247
  37.7 1.1 %collective-permute-done.7.refs_2_ = bf16[1,512,128]{2,1,0:T(8,128)(2,1)} collective-permute-done((bf16[1,512,128]{2,1,0:T(8,128)(2,1)}, bf16[1,512,128]{2,1,0:T(8,128)(2,1)}, u32[]{:S(2)}, u32[]{:S(2)}) %collective-permute-start.7) | collective-permute-done | bytes 131104 | tf_op jit(solution)/shard_map/ppermute | solution.py:247
  39.4 0.7 %copy-done.2 = bf16[4,272,128]{2,1,0:T(8,128)(2,1)} copy-done((bf16[4,272,128]{2,1,0:T(8,128)(2,1)}, bf16[4,272,128]{2,1,0:T(8,128)(2,1)S(1)}, u32[]{:S(2)}) %copy-start.2) | copy-done | bytes 278552
  40.8 3.9 %collective-permute-done.18.refs_9_ = bf16[2,512,128]{2,1,0:T(8,128)(2,1)S(1)} collective-permute-done((bf16[2,512,128]{2,1,0:T(8,128)(2,1)S(1)}, bf16[2,512,128]{2,1,0:T(8,128)(2,1)S(1)}, u32[]{:S(2)}, u32[]{:S(2)}) %collective-permute-start.18) | collective-permute-done | bytes 262176 | tf_op jit(solution)/shard_map/ppermute | solution.py:247
  44.7 0.7 %copy-done.4 = bf16[2,512,128]{2,1,0:T(8,128)(2,1)} copy-done((bf16[2,512,128]{2,1,0:T(8,128)(2,1)}, bf16[2,512,128]{2,1,0:T(8,128)(2,1)S(1)}, u32[]{:S(2)}) %copy-start.4) | copy-done | bytes 262168
  45.5 0.9 %copy-done.3 = bf16[4,272,128]{2,1,0:T(8,128)(2,1)S(1)} copy-done((bf16[4,272,128]{2,1,0:T(8,128)(2,1)S(1)}, bf16[4,272,128]{2,1,0:T(8,128)(2,1)}, u32[]{:S(2)}) %copy-start.3) | copy-done | bytes 278552
  46.5 0.9 %copy-done.5 = bf16[2,512,128]{2,1,0:T(8,128)(2,1)S(1)} copy-done((bf16[2,512,128]{2,1,0:T(8,128)(2,1)S(1)}, bf16[2,512,128]{2,1,0:T(8,128)(2,1)}, u32[]{:S(2)}) %copy-start.5) | copy-done | bytes 262168
  47.4 4.4 %near_half.1 = (f32[512,1024]{1,0:T(8,128)S(1)}, bf16[512,1024]{1,0:T(8,128)(2,1)S(1)}) custom-call(s32[9]{0:T(128)S(1)} %stack.24.where_ref, bf16[4,272,128]{2,1,0:T(8,128)(2,1)S(1)} %join.4.refs_0_, bf16[4,272,128]{2,1,0:T(8,128)(2,1)} %collective-permute-done.13.refs_1_, bf16[4,272,128]{2,1,0:T(8,128)(2,1)S(1)} %collective-permute-done.14.refs_2_, ...), custom_call_target="tpu_custom_call" | custom-call | flops 536870912 | bytes 8388608 | tf_op jit(solution)/shard_map/near_half/pallas_call | solution.py:180
  51.9 3.0 %far_half.1 = f32[512,1024]{1,0:T(8,128)} custom-call(bf16[1,512,128]{2,1,0:T(8,128)(2,1)} %collective-permute-done.5.refs_0_, bf16[1,512,128]{2,1,0:T(8,128)(2,1)} %collective-permute-done.6.refs_1_, bf16[1,512,128]{2,1,0:T(8,128)(2,1)} %collective-permute-done.7.refs_2_, bf16[1,512,128]{2,1,0:T(8,128)(2,1)} %collective-permute-done.8.refs_3_, ...), custom_call_target="tpu_custom_call" | custom-call | flops 536870912 | bytes 8388608 | tf_op jit(solution)/shard_map/far_half/pallas_call | solution.py:225
  (37 shorter events, 3.4 us)
Async XLA Ops:
  0.0 45.5 %copy-start = (f32[512,1024]{1,0:T(8,128)S(1)}, f32[512,1024]{1,0:T(8,128)}, u32[]{:S(2)}) copy-start(f32[512,1024]{1,0:T(8,128)} %refs_10_.1) | copy-start | bytes 6291460
  0.0 9.1 %collective-permute-start.4 = (bf16[1,512,128]{2,1,0:T(8,128)(2,1)}, bf16[1,512,128]{2,1,0:T(8,128)(2,1)}, u32[]{:S(2)}, u32[]{:S(2)}) collective-permute-start(bf16[1,512,128]{2,1,0:T(8,128)(2,1)} %bitcast.14), channel_id=1, source_target_pairs={{0,2},{1,3},{2,0},{3,1},{4,6},{5,7},{6,4},{7,5},{8,10},{9,11},{10,... | collective-permute-start | bytes 393224 | tf_op jit(solution)/shard_map/ppermute | solution.py:247
  3.0 1.0 %copy-start.1 = (bf16[1,16,128,128]{3,2,1,0:T(8,128)(2,1)S(1)}, bf16[1,16,128,128]{3,2,1,0:T(8,128)(2,1)}, u32[]{:S(2)}) copy-start(bf16[1,16,128,128]{3,2,1,0:T(8,128)(2,1)} %tiles_hbm.1) | copy-start | bytes 1572868
  5.6 7.5 %collective-permute-start = (bf16[1,272,128]{2,1,0:T(8,128)(2,1)S(1)}, bf16[1,272,128]{2,1,0:T(8,128)(2,1)S(1)}, u32[]{:S(2)}, u32[]{:S(2)}) collective-permute-start(bf16[1,272,128]{2,1,0:T(8,128)(2,1)S(1)} %bitcast.24), channel_id=1, source_target_pairs={{0,1},{1,0},{2,3},{3,2},{4,5},{5,4},{6,7},{7,6},{8,9},{9,8},{10,11... | collective-permute-start | bytes 208904 | tf_op jit(solution)/shard_map/ppermute | solution.py:247
  7.2 9.3 %collective-permute-start.1 = (bf16[1,272,128]{2,1,0:T(8,128)(2,1)S(1)}, bf16[1,272,128]{2,1,0:T(8,128)(2,1)S(1)}, u32[]{:S(2)}, u32[]{:S(2)}) collective-permute-start(bf16[1,272,128]{2,1,0:T(8,128)(2,1)S(1)} %bitcast.23), channel_id=1, source_target_pairs={{0,2},{1,3},{2,0},{3,1},{4,6},{5,7},{6,4},{7,5},{8,10},{9,11},{10,... | collective-permute-start | bytes 208904 | tf_op jit(solution)/shard_map/ppermute | solution.py:247
  7.8 8.7 %collective-permute-start.2 = (bf16[1,272,128]{2,1,0:T(8,128)(2,1)S(1)}, bf16[1,272,128]{2,1,0:T(8,128)(2,1)S(1)}, u32[]{:S(2)}, u32[]{:S(2)}) collective-permute-start(bf16[1,272,128]{2,1,0:T(8,128)(2,1)S(1)} %bitcast.22), channel_id=1, source_target_pairs={{0,3},{1,2},{2,1},{3,0},{4,7},{5,6},{6,5},{7,4},{8,11},{9,10},{10,... | collective-permute-start | bytes 208904 | tf_op jit(solution)/shard_map/ppermute | solution.py:247
  9.2 12.1 %collective-permute-start.10 = (bf16[1,272,128]{2,1,0:T(8,128)(2,1)S(1)}, bf16[1,272,128]{2,1,0:T(8,128)(2,1)S(1)}, u32[]{:S(2)}, u32[]{:S(2)}) collective-permute-start(bf16[1,272,128]{2,1,0:T(8,128)(2,1)S(1)} %bitcast.21), channel_id=1, source_target_pairs={{0,5},{1,4},{2,7},{3,6},{4,1},{5,0},{6,3},{7,2},{8,13},{9,12},{10,... | collective-permute-start | bytes 208904 | tf_op jit(solution)/shard_map/ppermute | solution.py:247
  12.7 8.6 %collective-permute-start.11 = (bf16[1,272,128]{2,1,0:T(8,128)(2,1)S(1)}, bf16[1,272,128]{2,1,0:T(8,128)(2,1)S(1)}, u32[]{:S(2)}, u32[]{:S(2)}) collective-permute-start(bf16[1,272,128]{2,1,0:T(8,128)(2,1)S(1)} %bitcast.20), channel_id=1, source_target_pairs={{0,6},{1,7},{2,4},{3,5},{4,2},{5,3},{6,0},{7,1},{8,14},{9,15},{10,... | collective-permute-start | bytes 208904 | tf_op jit(solution)/shard_map/ppermute | solution.py:247
  13.1 8.2 %collective-permute-start.12 = (bf16[1,272,128]{2,1,0:T(8,128)(2,1)S(1)}, bf16[1,272,128]{2,1,0:T(8,128)(2,1)S(1)}, u32[]{:S(2)}, u32[]{:S(2)}) collective-permute-start(bf16[1,272,128]{2,1,0:T(8,128)(2,1)S(1)} %bitcast.19), channel_id=1, source_target_pairs={{0,7},{1,6},{2,5},{3,4},{4,3},{5,2},{6,1},{7,0},{8,15},{9,14},{10,... | collective-permute-start | bytes 208904 | tf_op jit(solution)/shard_map/ppermute | solution.py:247
  16.5 7.8 %collective-permute-start.9 = (bf16[1,272,128]{2,1,0:T(8,128)(2,1)S(1)}, bf16[1,272,128]{2,1,0:T(8,128)(2,1)S(1)}, u32[]{:S(2)}, u32[]{:S(2)}) collective-permute-start(bf16[1,272,128]{2,1,0:T(8,128)(2,1)S(1)} %bitcast.18), channel_id=1, source_target_pairs={{0,4},{1,5},{2,6},{3,7},{4,0},{5,1},{6,2},{7,3},{8,12},{9,13},{10,... | collective-permute-start | bytes 208904 | tf_op jit(solution)/shard_map/ppermute | solution.py:247
  16.5 21.2 %collective-permute-start.3 = (bf16[4,272,128]{2,1,0:T(8,128)(2,1)S(1)}, bf16[4,272,128]{2,1,0:T(8,128)(2,1)S(1)}, u32[]{:S(2)}, u32[]{:S(2)}) collective-permute-start(bf16[4,272,128]{2,1,0:T(8,128)(2,1)S(1)} %join.3.refs_4_), channel_id=1, source_target_pairs={{0,16},{8,24},{16,0},{24,8},{1,17},{9,25},{17,1},{25,9},{2,18},{10... | collective-permute-start | bytes 835592 | tf_op jit(solution)/shard_map/ppermute | solution.py:247
  24.2 14.6 %collective-permute-start.14 = (bf16[4,272,128]{2,1,0:T(8,128)(2,1)S(1)}, bf16[4,272,128]{2,1,0:T(8,128)(2,1)S(1)}, u32[]{:S(2)}, u32[]{:S(2)}) collective-permute-start(bf16[4,272,128]{2,1,0:T(8,128)(2,1)S(1)} %join.4.refs_0_), channel_id=1, source_target_pairs={{0,16},{8,24},{16,0},{24,8},{1,17},{9,25},{17,1},{25,9},{2,18},{10... | collective-permute-start | bytes 835592 | tf_op jit(solution)/shard_map/ppermute | solution.py:247
  25.8 11.6 %collective-permute-start.5 = (bf16[1,512,128]{2,1,0:T(8,128)(2,1)}, bf16[1,512,128]{2,1,0:T(8,128)(2,1)}, u32[]{:S(2)}, u32[]{:S(2)}) collective-permute-start(bf16[1,512,128]{2,1,0:T(8,128)(2,1)} %bitcast.15), channel_id=1, source_target_pairs={{0,4},{1,5},{2,6},{3,7},{4,0},{5,1},{6,2},{7,3},{8,12},{9,13},{10,... | collective-permute-start | bytes 393224 | tf_op jit(solution)/shard_map/ppermute | solution.py:247
  26.8 12.1 %collective-permute-start.7 = (bf16[1,512,128]{2,1,0:T(8,128)(2,1)}, bf16[1,512,128]{2,1,0:T(8,128)(2,1)}, u32[]{:S(2)}, u32[]{:S(2)}) collective-permute-start(bf16[1,512,128]{2,1,0:T(8,128)(2,1)} %collective-permute-done.4.refs_1_), channel_id=1, source_target_pairs={{0,4},{1,5},{2,6},{3,7},{4,0},{5,1},{6,2},{7,3},{8,12},{9,13},{10,... | collective-permute-start | bytes 393224 | tf_op jit(solution)/shard_map/ppermute | solution.py:247
  28.8 10.6 %collective-permute-start.16 = (bf16[4,272,128]{2,1,0:T(8,128)(2,1)S(1)}, bf16[4,272,128]{2,1,0:T(8,128)(2,1)S(1)}, u32[]{:S(2)}, u32[]{:S(2)}) collective-permute-start(bf16[4,272,128]{2,1,0:T(8,128)(2,1)S(1)} %join.3.refs_4_), channel_id=1, source_target_pairs={{0,8},{8,0},{16,24},{24,16},{1,9},{9,1},{17,25},{25,17},{2,10},{10... | collective-permute-start | bytes 835592 | tf_op jit(solution)/shard_map/ppermute | solution.py:247
  28.8 0.9 %copy-start.6 = (bf16[512,128]{1,0:T(8,128)(2,1)S(1)}, bf16[512,128]{1,0:T(8,128)(2,1)}, u32[]{:S(2)}) copy-start(bf16[512,128]{1,0:T(8,128)(2,1)} %param.4) | copy-start | bytes 393220
  37.4 7.2 %collective-permute-start.18 = (bf16[2,512,128]{2,1,0:T(8,128)(2,1)S(1)}, bf16[2,512,128]{2,1,0:T(8,128)(2,1)S(1)}, u32[]{:S(2)}, u32[]{:S(2)}) collective-permute-start(bf16[2,512,128]{2,1,0:T(8,128)(2,1)S(1)} %join.5.refs_8_), channel_id=1, source_target_pairs={{0,1},{1,0},{2,3},{3,2},{4,5},{5,4},{6,7},{7,6},{8,9},{9,8},{10,11... | collective-permute-start | bytes 786440 | tf_op jit(solution)/shard_map/ppermute | solution.py:247
  37.7 7.8 %collective-permute-start.13 = (bf16[4,272,128]{2,1,0:T(8,128)(2,1)S(1)}, bf16[4,272,128]{2,1,0:T(8,128)(2,1)}, u32[]{:S(2)}, u32[]{:S(2)}) collective-permute-start(bf16[4,272,128]{2,1,0:T(8,128)(2,1)S(1)} %join.4.refs_0_), channel_id=1, source_target_pairs={{0,8},{8,0},{16,24},{24,16},{1,9},{9,1},{17,25},{25,17},{2,10},{10... | collective-permute-start | bytes 835592 | tf_op jit(solution)/shard_map/ppermute | solution.py:247
  38.8 6.6 %collective-permute-start.17 = (bf16[4,272,128]{2,1,0:T(8,128)(2,1)S(1)}, bf16[4,272,128]{2,1,0:T(8,128)(2,1)}, u32[]{:S(2)}, u32[]{:S(2)}) collective-permute-start(bf16[4,272,128]{2,1,0:T(8,128)(2,1)S(1)} %collective-permute-done.3.refs_6_), channel_id=1, source_target_pairs={{0,8},{8,0},{16,24},{24,16},{1,9},{9,1},{17,25},{25,17},{2,10},{10... | collective-permute-start | bytes 835592 | tf_op jit(solution)/shard_map/ppermute | solution.py:247
  38.8 6.6 %collective-permute-start.15 = (bf16[4,272,128]{2,1,0:T(8,128)(2,1)S(1)}, bf16[4,272,128]{2,1,0:T(8,128)(2,1)}, u32[]{:S(2)}, u32[]{:S(2)}) collective-permute-start(bf16[4,272,128]{2,1,0:T(8,128)(2,1)S(1)} %collective-permute-done.14.refs_2_), channel_id=1, source_target_pairs={{0,8},{8,0},{16,24},{24,16},{1,9},{9,1},{17,25},{25,17},{2,10},{10... | collective-permute-start | bytes 835592 | tf_op jit(solution)/shard_map/ppermute | solution.py:247
  40.1 11.8 %collective-permute-start.8 = (bf16[1,512,128]{2,1,0:T(8,128)(2,1)}, bf16[1,512,128]{2,1,0:T(8,128)(2,1)}, u32[]{:S(2)}, u32[]{:S(2)}) collective-permute-start(bf16[1,512,128]{2,1,0:T(8,128)(2,1)} %collective-permute-done.7.refs_2_), channel_id=1, source_target_pairs={{0,1},{1,0},{2,3},{3,2},{4,5},{5,4},{6,7},{7,6},{8,9},{9,8},{10,11... | collective-permute-start | bytes 393224 | tf_op jit(solution)/shard_map/ppermute | solution.py:247
  45.4 6.5 %collective-permute-start.6 = (bf16[1,512,128]{2,1,0:T(8,128)(2,1)}, bf16[1,512,128]{2,1,0:T(8,128)(2,1)}, u32[]{:S(2)}, u32[]{:S(2)}) collective-permute-start(bf16[1,512,128]{2,1,0:T(8,128)(2,1)} %collective-permute-done.5.refs_0_), channel_id=1, source_target_pairs={{0,1},{1,0},{2,3},{3,2},{4,5},{5,4},{6,7},{7,6},{8,9},{9,8},{10,11... | collective-permute-start | bytes 393224 | tf_op jit(solution)/shard_map/ppermute | solution.py:247
  45.5 1.0 %copy-start.3 = (bf16[4,272,128]{2,1,0:T(8,128)(2,1)S(1)}, bf16[4,272,128]{2,1,0:T(8,128)(2,1)}, u32[]{:S(2)}) copy-start(bf16[4,272,128]{2,1,0:T(8,128)(2,1)} %copy-done.2) | copy-start | bytes 835588
  46.5 0.9 %copy-start.5 = (bf16[2,512,128]{2,1,0:T(8,128)(2,1)S(1)}, bf16[2,512,128]{2,1,0:T(8,128)(2,1)}, u32[]{:S(2)}) copy-start(bf16[2,512,128]{2,1,0:T(8,128)(2,1)} %copy-done.4) | copy-start | bytes 786436
  (3 other events, 2.1 us)

commit v4 on v3

--- a/solution.py
+++ b/solution.py
@@ -76,7 +76,11 @@
         ],
         compiler_params=pltpu.CompilerParams(vmem_limit_bytes=8 * MIB),
         name="pack",
-    )(col[None], tile_ids, packed_tiles)
+    )(
+        col[None],
+        pltpu.with_memory_space_constraint(tile_ids, pltpu.HBM),
+        pltpu.with_memory_space_constraint(packed_tiles, pltpu.HBM),
+    )
 
 
 def join_kernel(*refs):
@@ -121,12 +125,14 @@
     n_amps = len(offsets)
     pieces = refs[:n_pieces]
     amps = refs[n_pieces : n_pieces + n_amps]
-    residual, total, far = refs[n_pieces + n_amps : n_pieces + n_amps + 3]
-    places, table, amp, near, res, table_sem, res_sem = refs[n_pieces + n_amps + 3 :]
+    own, residual, total, far = refs[n_pieces + n_amps : n_pieces + n_amps + 4]
+    places, table, amp, near, res, table_sem, own_sem, res_sem = refs[n_pieces + n_amps + 4 :]
     columns = pieces[0].shape[0]
     width = pieces[0].shape[2]
     per_device = KT_DEV * QT_DEV
     half = amp.shape[1] // width
+    own_copy = pltpu.make_async_copy(own, amp.at[:, pl.ds(0, width)], own_sem)
+    own_copy.start()
     res_copy = pltpu.make_async_copy(residual, res, res_sem)
     res_copy.start()
     for p, piece in enumerate(pieces):
@@ -136,9 +142,8 @@
         ).astype(jnp.int32)
     table_copy = pltpu.make_async_copy(places, table, table_sem)
     table_copy.start()
-    for source, slots in zip(amps, offsets):
-        for i, slot in enumerate(slots):
-            amp[:, slot * width : (slot + 1) * width] = source[i]
+    for source, slot in zip(amps, offsets):
+        amp[:, slot * width : (slot + 1) * width] = source[...]
     table_copy.wait()
     col = where_ref[n_pieces]
     for p, piece in enumerate(pieces):
@@ -164,15 +169,16 @@
             return 0
 
         lax.fori_loop(0, columns, place, 0)
+    own_copy.wait()
     res_copy.wait()
     multiply(amp, near, res, total, None, 2 * width)
 
 
-def near_half(where, pieces, amps, offsets, residual, capacity):
+def near_half(where, pieces, amps, offsets, own, residual, capacity):
     columns, _, width = pieces[0].shape
     n_pieces, n_amps = len(pieces), len(amps)
     rows, n_cols = residual.shape
-    depth = sum(map(len, offsets)) * width
+    depth = (1 + n_amps) * width
     hbm = pl.BlockSpec(memory_space=pltpu.HBM)
     vmem = pl.BlockSpec(memory_space=pltpu.VMEM)
     held = 2 * rows * depth + 4 * depth * n_cols + 8 * rows * n_cols
@@ -185,7 +191,7 @@
         ],
         in_specs=[pl.BlockSpec(memory_space=pltpu.SMEM)]
         + [vmem] * (n_pieces + n_amps)
-        + [hbm],
+        + [hbm, hbm],
         out_specs=[vmem, vmem],
         scratch_shapes=[
             pltpu.VMEM((n_pieces * columns, width), jnp.int32),
@@ -193,6 +199,7 @@
             pltpu.VMEM((rows, depth), pieces[0].dtype),
             pltpu.VMEM((depth, n_cols), pieces[0].dtype),
             pltpu.VMEM((rows, n_cols), residual.dtype),
+            pltpu.SemaphoreType.DMA,
             pltpu.SemaphoreType.DMA,
             pltpu.SemaphoreType.DMA,
         ],
@@ -203,23 +210,28 @@
             transcendentals=0,
         ),
         name="near_half",
-    )(where, *pieces, *amps, residual)
+    )(
+        where,
+        *pieces,
+        *amps,
+        pltpu.with_memory_space_constraint(own, pltpu.HBM),
+        pltpu.with_memory_space_constraint(residual, pltpu.HBM),
+    )
 
 
 def far_kernel(offsets, half, *refs):
     amps = refs[: len(offsets)]
     start, far, out, amp, total, sems = refs[len(offsets) :]
-    width = amps[0].shape[2]
-    for source, slots in zip(amps, offsets):
-        for i, slot in enumerate(slots):
-            at = (slot - half) * width
-            amp[:, at : at + width] = source[i]
+    width = amps[0].shape[1]
+    for source, slot in zip(amps, offsets):
+        at = (slot - half) * width
+        amp[:, at : at + width] = source[...]
     multiply(amp, far, start, (total, out), sems, 2 * width)
 
 
 def far_half(amps, offsets, total, far):
     rows, n_cols = total.shape
-    depth, width = far.shape[0], amps[0].shape[2]
+    depth, width = far.shape[0], amps[0].shape[1]
     vmem = pl.BlockSpec(memory_space=pltpu.VMEM)
     held = 4 * rows * depth + 2 * depth * n_cols + 8 * rows * n_cols
     return pl.pallas_call(
@@ -247,11 +259,8 @@
     return lax.ppermute(x, axis, [(i, i ^ flip) for i in range(size)])
 
 
-def over_lanes(shard, slots, inner):
-    held = [(shard, slots)]
-    for lane in range(1, inner):
-        held.append((exchange(shard, "col", lane), [s ^ lane for s in slots]))
-    return held
+def tie(late, *early):
+    return lax.optimization_barrier((late, *early))
 
 
 def body(amplitudes, packed_tiles, tile_ids, residual_in):
@@ -261,28 +270,44 @@
     capacity = -(-packed_tiles.shape[1] // n_col)
     half = n_col // 2
     outgoing = list(pack(col, packed_tiles, tile_ids, n_col, capacity))
-    flips = range(inner, half, inner)
-    held = [amplitudes[None]] + [exchange(amplitudes[None], "col", f) for f in flips]
-    outgoing[half:], held = lax.optimization_barrier((outgoing[half:], held))
+
+    amps = {0: amplitudes}
+    for s in [*range(1, inner), *range(inner, half, inner), half]:
+        amps[s] = exchange(amplitudes, "col", s)
+    outgoing[half:], amps = tie(outgoing[half:], amps)
+
     chunks = [outgoing[0][None]]
     chunks += [exchange(outgoing[s][None], "col", s) for s in range(1, n_col)]
-    slots = [0, *flips]
-    passed = [exchange(shard, "col", half) for shard in held]
-    near = over_lanes(join(held), slots, inner)
+    for flip in range(inner, half, inner):
+        for lane in range(1, inner):
+            amps[flip ^ lane] = exchange(amps[flip], "col", lane)
+        amps[flip ^ half] = exchange(amps[flip], "col", half)
+    for lane in range(1, inner):
+        amps[half ^ lane] = exchange(amps[half], "col", lane)
+
+    early = [s for s in amps if s and (s < half or half < s < half + inner)]
+    late = [flip ^ half for flip in range(inner, half, inner)]
     pieces, rows = [], []
     for group in (join(chunks[half:]), join(chunks[:half])):
-        for flip in range(0, n_row, CORES):
-            mine = exchange(group, "row", flip) if flip else group
-            if flip == CORES and len(pieces) > CORES:
-                mine, passed[0] = lax.optimization_barrier((mine, passed[0]))
+        passed = [exchange(group, "row", flip) for flip in range(CORES, n_row, CORES)]
+        due = late if pieces else early
+        passed, got = tie(passed, [amps[s] for s in due])
+        amps.update(zip(due, got))
+        own, passed = tie(group, passed)
+        for flip, mine in zip(range(0, n_row, CORES), [own, *passed]):
             pieces += [mine, exchange(mine, "row", 1)]
             rows += [row ^ flip, row ^ flip ^ 1]
-    far = []
-    for shard, slot in zip(passed, slots):
-        far += over_lanes(shard, [slot ^ half], inner)
+    for flip in range(half + inner, n_col, inner):
+        for lane in range(1, inner):
+            amps[flip ^ lane] = exchange(amps[flip], "col", lane)
+
     where = jnp.stack(rows + [col]).astype(jnp.int32)
-    total, far_block = near_half(where, pieces, *zip(*near), residual_in, capacity)
-    return far_half(*zip(*far), total, far_block)
+    near = [s for s in sorted(amps) if 0 < s < half]
+    far = [s for s in sorted(amps) if s >= half]
+    total, far_block = near_half(
+        where, pieces, [amps[s] for s in near], near, amplitudes, residual_in, capacity
+    )
+    return far_half([amps[s] for s in far], far, total, far_block)
 
 
 def solution(mesh):

time: 55.1 us -> 44 us (0.80)
  waiting for transfers between devices: 18 us -> 9.71 us
  local copies, waits for them, and re-layouts: 6.01 us -> 0.08 us
  starting transfers between devices: 21.5 us -> 27.1 us
  Pallas kernels: 9.19 us -> 6.84 us
    ppermute x19 -> x20, waiting for transfers between devices: 18 us -> 9.71 us  [exchange(): return lax.ppermute(x, axis, [(i, i ^ flip) for i in range(size)])]
    unnamed x16 -> x0, local copies, waits for them, and re-layouts: 5.93 us -> none
    ppermute x19 -> x20, starting transfers between devices: 21.5 us -> 27.1 us  [exchange(): return lax.ppermute(x, axis, [(i, i ^ flip) for i in range(size)])]
    pallas_call x1, Pallas kernels: 2.96 us -> 1.86 us  [far_half(): pl.pallas_call(functools.partial(far_kernel, offsets, depth // width), ou...]
    pallas_call x3 -> x2, Pallas kernels: 0.96 us -> 0.04 us  [join(): pl.pallas_call(join_kernel, out_shape=jax.ShapeDtypeStruct((total, *chunk...]
    pallas_call x1, Pallas kernels: 4.41 us -> 3.69 us  [near_half(): pl.pallas_call(functools.partial(near_kernel, n_pieces, offsets, capacity...]
  transfers between devices with their start and end apart: 19 -> 20, of which waited for: 5 -> 7; matrix products, arithmetic and copies ran while one was open for 0% -> 0% of each run, Pallas kernels for 11% -> 11%
where the time goes in v4:
time: 44 us; the launch traced here: 43.8 us
  starting transfers between devices  27.1 us (62%)
  waiting for transfers between devices  9.71 us (22%)
  Pallas kernels  6.84 us (16%)
    ppermute x20, starting transfers between devices, exchange(): return lax.ppermute(x, axis, [(i, i ^ flip) for i in range(size)])  27.1 us
    ppermute x20, waiting for transfers between devices, exchange(): return lax.ppermute(x, axis, [(i, i ^ flip) for i in range(size)])  9.71 us
    pallas_call x1, Pallas kernels, near_half(): pl.pallas_call(functools.partial(near_kernel, n_pieces, offsets, capacity...  3.69 us
    pallas_call x1, Pallas kernels, far_half(): pl.pallas_call(functools.partial(far_kernel, offsets, depth // width), ou...  1.86 us
    pallas_call x1, Pallas kernels, pack(): pl.pallas_call(functools.partial(pack_kernel, columns, capacity), out_sha...  1.25 us
  transfers between devices with their start and end apart: 20, of which 7 were waited for; matrix products, arithmetic and copies ran while one was open for 0% of the time, Pallas kernels for 11%

profile of v4, /device:TPU:0, one launch (start us, length us, event | category | flops | bytes accessed | tf_op | source)
XLA Modules:
  0.0 43.8 jit_solution(13380724135518459096)
XLA Ops:
  0.0 2.9 %collective-permute-start = (bf16[512,128]{1,0:T(8,128)(2,1)}, bf16[512,128]{1,0:T(8,128)(2,1)S(1)}, u32[]{:S(2)}, u32[]{:S(2)}) collective-permute-start(bf16[512,128]{1,0:T(8,128)(2,1)} %refs_11_.1), channel_id=1, source_target_pairs={{0,1},{1,0},{2,3},{3,2},{4,5},{5,4},{6,7},{7,6},{8,9},{9,8},{10,11... | collective-permute-start | bytes 393224 | tf_op jit(solution)/shard_map/ppermute | solution.py:259
  2.9 1.6 %collective-permute-start.1 = (bf16[512,128]{1,0:T(8,128)(2,1)}, bf16[512,128]{1,0:T(8,128)(2,1)S(1)}, u32[]{:S(2)}, u32[]{:S(2)}) collective-permute-start(bf16[512,128]{1,0:T(8,128)(2,1)} %refs_11_.1), channel_id=1, source_target_pairs={{0,2},{1,3},{2,0},{3,1},{4,6},{5,7},{6,4},{7,5},{8,10},{9,11},{10,... | collective-permute-start | bytes 393224 | tf_op jit(solution)/shard_map/ppermute | solution.py:259
  4.5 2.6 %collective-permute-start.2 = (bf16[512,128]{1,0:T(8,128)(2,1)}, bf16[512,128]{1,0:T(8,128)(2,1)S(1)}, u32[]{:S(2)}, u32[]{:S(2)}) collective-permute-start(bf16[512,128]{1,0:T(8,128)(2,1)} %refs_11_.1), channel_id=1, source_target_pairs={{0,4},{1,5},{2,6},{3,7},{4,0},{5,1},{6,2},{7,3},{8,12},{9,13},{10,... | collective-permute-start | bytes 393224 | tf_op jit(solution)/shard_map/ppermute | solution.py:259
  7.1 1.3 %pack.1 = (bf16[272,128]{1,0:T(8,128)(2,1)S(1)}, bf16[272,128]{1,0:T(8,128)(2,1)S(1)}, bf16[272,128]{1,0:T(8,128)(2,1)S(1)}, bf16[272,128]{1,0:T(8,128)(2,1)S(1)...) custom-call(s32[1]{0:T(128)} %bitcast.me_ref, ...), custom_call_target="tpu_custom_call" | custom-call | tf_op jit(solution)/shard_map/pack/pallas_call | solution.py:63
  8.4 0.6 %collective-permute-start.10 = (bf16[1,272,128]{2,1,0:T(8,128)(2,1)S(1)}, bf16[1,272,128]{2,1,0:T(8,128)(2,1)S(1)}, u32[]{:S(2)}, u32[]{:S(2)}) collective-permute-start(bf16[1,272,128]{2,1,0:T(8,128)(2,1)S(1)} %bitcast.20), channel_id=1, source_target_pairs={{0,1},{1,0},{2,3},{3,2},{4,5},{5,4},{6,7},{7,6},{8,9},{9,8},{10,11... | collective-permute-start | bytes 208904 | tf_op jit(solution)/shard_map/ppermute | solution.py:259
  9.0 0.4 %collective-permute-start.11 = (bf16[1,272,128]{2,1,0:T(8,128)(2,1)S(1)}, bf16[1,272,128]{2,1,0:T(8,128)(2,1)S(1)}, u32[]{:S(2)}, u32[]{:S(2)}) collective-permute-start(bf16[1,272,128]{2,1,0:T(8,128)(2,1)S(1)} %bitcast.19), channel_id=1, source_target_pairs={{0,2},{1,3},{2,0},{3,1},{4,6},{5,7},{6,4},{7,5},{8,10},{9,11},{10,... | collective-permute-start | bytes 208904 | tf_op jit(solution)/shard_map/ppermute | solution.py:259
  9.4 2.5 %collective-permute-start.12 = (bf16[1,272,128]{2,1,0:T(8,128)(2,1)S(1)}, bf16[1,272,128]{2,1,0:T(8,128)(2,1)S(1)}, u32[]{:S(2)}, u32[]{:S(2)}) collective-permute-start(bf16[1,272,128]{2,1,0:T(8,128)(2,1)S(1)} %bitcast.18), channel_id=1, source_target_pairs={{0,3},{1,2},{2,1},{3,0},{4,7},{5,6},{6,5},{7,4},{8,11},{9,10},{10,... | collective-permute-start | bytes 208904 | tf_op jit(solution)/shard_map/ppermute | solution.py:259
  11.9 2.4 %collective-permute-start.3 = (bf16[1,272,128]{2,1,0:T(8,128)(2,1)S(1)}, bf16[1,272,128]{2,1,0:T(8,128)(2,1)S(1)}, u32[]{:S(2)}, u32[]{:S(2)}) collective-permute-start(bf16[1,272,128]{2,1,0:T(8,128)(2,1)S(1)} %bitcast.17), channel_id=1, source_target_pairs={{0,4},{1,5},{2,6},{3,7},{4,0},{5,1},{6,2},{7,3},{8,12},{9,13},{10,... | collective-permute-start | bytes 208904 | tf_op jit(solution)/shard_map/ppermute | solution.py:259
  14.4 0.5 %collective-permute-start.4 = (bf16[1,272,128]{2,1,0:T(8,128)(2,1)S(1)}, bf16[1,272,128]{2,1,0:T(8,128)(2,1)S(1)}, u32[]{:S(2)}, u32[]{:S(2)}) collective-permute-start(bf16[1,272,128]{2,1,0:T(8,128)(2,1)S(1)} %bitcast.16), channel_id=1, source_target_pairs={{0,5},{1,4},{2,7},{3,6},{4,1},{5,0},{6,3},{7,2},{8,13},{9,12},{10,... | collective-permute-start | bytes 208904 | tf_op jit(solution)/shard_map/ppermute | solution.py:259
  14.8 4.6 %collective-permute-start.5 = (bf16[1,272,128]{2,1,0:T(8,128)(2,1)S(1)}, bf16[1,272,128]{2,1,0:T(8,128)(2,1)S(1)}, u32[]{:S(2)}, u32[]{:S(2)}) collective-permute-start(bf16[1,272,128]{2,1,0:T(8,128)(2,1)S(1)} %bitcast.15), channel_id=1, source_target_pairs={{0,6},{1,7},{2,4},{3,5},{4,2},{5,3},{6,0},{7,1},{8,14},{9,15},{10,... | collective-permute-start | bytes 208904 | tf_op jit(solution)/shard_map/ppermute | solution.py:259
  19.4 1.0 %collective-permute-start.6 = (bf16[1,272,128]{2,1,0:T(8,128)(2,1)S(1)}, bf16[1,272,128]{2,1,0:T(8,128)(2,1)S(1)}, u32[]{:S(2)}, u32[]{:S(2)}) collective-permute-start(bf16[1,272,128]{2,1,0:T(8,128)(2,1)S(1)} %bitcast.14), channel_id=1, source_target_pairs={{0,7},{1,6},{2,5},{3,4},{4,3},{5,2},{6,1},{7,0},{8,15},{9,14},{10,... | collective-permute-start | bytes 208904 | tf_op jit(solution)/shard_map/ppermute | solution.py:259
  20.4 1.6 %collective-permute-start.13 = (bf16[4,272,128]{2,1,0:T(8,128)(2,1)S(1)}, bf16[4,272,128]{2,1,0:T(8,128)(2,1)S(1)}, u32[]{:S(2)}, u32[]{:S(2)}) collective-permute-start(bf16[4,272,128]{2,1,0:T(8,128)(2,1)S(1)} %join.3.refs_4_), channel_id=1, source_target_pairs={{0,16},{8,24},{16,0},{24,8},{1,17},{9,25},{17,1},{25,9},{2,18},{10... | collective-permute-start | bytes 835592 | tf_op jit(solution)/shard_map/ppermute | solution.py:259
  22.0 1.8 %collective-permute-done.4.refs_1_ = bf16[1,272,128]{2,1,0:T(8,128)(2,1)S(1)} collective-permute-done((bf16[1,272,128]{2,1,0:T(8,128)(2,1)S(1)}, bf16[1,272,128]{2,1,0:T(8,128)(2,1)S(1)}, u32[]{:S(2)}, u32[]{:S(2)}) %collective-permute-start.4) | collective-permute-done | bytes 69664 | tf_op jit(solution)/shard_map/ppermute | solution.py:259
  23.8 2.7 %collective-permute-done.6.refs_3_ = bf16[1,272,128]{2,1,0:T(8,128)(2,1)S(1)} collective-permute-done((bf16[1,272,128]{2,1,0:T(8,128)(2,1)S(1)}, bf16[1,272,128]{2,1,0:T(8,128)(2,1)S(1)}, u32[]{:S(2)}, u32[]{:S(2)}) %collective-permute-start.6) | collective-permute-done | bytes 69664 | tf_op jit(solution)/shard_map/ppermute | solution.py:259
  26.5 1.6 %collective-permute-start.7 = (bf16[4,272,128]{2,1,0:T(8,128)(2,1)S(1)}, bf16[4,272,128]{2,1,0:T(8,128)(2,1)S(1)}, u32[]{:S(2)}, u32[]{:S(2)}) collective-permute-start(bf16[4,272,128]{2,1,0:T(8,128)(2,1)S(1)} %join.2.refs_0_), channel_id=1, source_target_pairs={{0,16},{8,24},{16,0},{24,8},{1,17},{9,25},{17,1},{25,9},{2,18},{10... | collective-permute-start | bytes 835592 | tf_op jit(solution)/shard_map/ppermute | solution.py:259
  28.1 1.2 %collective-permute-start.14 = (bf16[512,128]{1,0:T(8,128)(2,1)S(1)}, bf16[512,128]{1,0:T(8,128)(2,1)S(1)}, u32[]{:S(2)}, u32[]{:S(2)}) collective-permute-start(bf16[512,128]{1,0:T(8,128)(2,1)S(1)} %collective-permute-done.1.refs_9_), channel_id=1, source_target_pairs={{0,4},{1,5},{2,6},{3,7},{4,0},{5,1},{6,2},{7,3},{8,12},{9,13},{10,... | collective-permute-start | bytes 393224 | tf_op jit(solution)/shard_map/ppermute | solution.py:259
  29.3 0.8 %collective-permute-start.8 = (bf16[512,128]{1,0:T(8,128)(2,1)S(1)}, bf16[512,128]{1,0:T(8,128)(2,1)S(1)}, u32[]{:S(2)}, u32[]{:S(2)}) collective-permute-start(bf16[512,128]{1,0:T(8,128)(2,1)S(1)} %collective-permute-done.1.refs_9_), channel_id=1, source_target_pairs={{0,1},{1,0},{2,3},{3,2},{4,5},{5,4},{6,7},{7,6},{8,9},{9,8},{10,11... | collective-permute-start | bytes 393224 | tf_op jit(solution)/shard_map/ppermute | solution.py:259
  30.1 1.2 %collective-permute-start.9 = (bf16[512,128]{1,0:T(8,128)(2,1)S(1)}, bf16[512,128]{1,0:T(8,128)(2,1)S(1)}, u32[]{:S(2)}, u32[]{:S(2)}) collective-permute-start(bf16[512,128]{1,0:T(8,128)(2,1)S(1)} %collective-permute-done.2.refs_0_), channel_id=1, source_target_pairs={{0,1},{1,0},{2,3},{3,2},{4,5},{5,4},{6,7},{7,6},{8,9},{9,8},{10,11... | collective-permute-start | bytes 393224 | tf_op jit(solution)/shard_map/ppermute | solution.py:259
  31.3 4.0 %collective-permute-done.14.refs_2_ = bf16[512,128]{1,0:T(8,128)(2,1)S(1)} collective-permute-done((bf16[512,128]{1,0:T(8,128)(2,1)S(1)}, bf16[512,128]{1,0:T(8,128)(2,1)S(1)}, u32[]{:S(2)}, u32[]{:S(2)}) %collective-permute-start.14) | collective-permute-done | bytes 131104 | tf_op jit(solution)/shard_map/ppermute | solution.py:259
  35.4 0.5 %collective-permute-start.19 = (bf16[4,272,128]{2,1,0:T(8,128)(2,1)S(1)}, bf16[4,272,128]{2,1,0:T(8,128)(2,1)S(1)}, u32[]{:S(2)}, u32[]{:S(2)}) collective-permute-start(bf16[4,272,128]{2,1,0:T(8,128)(2,1)S(1)} %collective-permute-done.13.refs_6_), channel_id=1, source_target_pairs={{0,8},{8,0},{16,24},{24,16},{1,9},{9,1},{17,25},{25,17},{2,10},{10... | collective-permute-start | bytes 835592 | tf_op jit(solution)/shard_map/ppermute | solution.py:259
  36.0 0.5 %collective-permute-start.17 = (bf16[4,272,128]{2,1,0:T(8,128)(2,1)S(1)}, bf16[4,272,128]{2,1,0:T(8,128)(2,1)S(1)}, u32[]{:S(2)}, u32[]{:S(2)}) collective-permute-start(bf16[4,272,128]{2,1,0:T(8,128)(2,1)S(1)} %collective-permute-done.7.refs_2_), channel_id=1, source_target_pairs={{0,8},{8,0},{16,24},{24,16},{1,9},{9,1},{17,25},{25,17},{2,10},{10... | collective-permute-start | bytes 835592 | tf_op jit(solution)/shard_map/ppermute | solution.py:259
  36.5 0.6 %collective-permute-start.15 = (bf16[512,128]{1,0:T(8,128)(2,1)S(1)}, bf16[512,128]{1,0:T(8,128)(2,1)S(1)}, u32[]{:S(2)}, u32[]{:S(2)}) collective-permute-start(bf16[512,128]{1,0:T(8,128)(2,1)S(1)} %collective-permute-done.14.refs_2_), channel_id=1, source_target_pairs={{0,1},{1,0},{2,3},{3,2},{4,5},{5,4},{6,7},{7,6},{8,9},{9,8},{10,11... | collective-permute-start | bytes 393224 | tf_op jit(solution)/shard_map/ppermute | solution.py:259
  38.1 3.7 %near_half.1 = (f32[512,1024]{1,0:T(8,128)S(1)}, bf16[512,1024]{1,0:T(8,128)(2,1)S(1)}) custom-call(s32[9]{0:T(128)S(1)} %stack.24.where_ref, bf16[4,272,128]{2,1,0:T(8,128)(2,1)S(1)} %join.2.refs_0_, bf16[4,272,128]{2,1,0:T(8,128)(2,1)S(1)} %collective-permute-done.16.refs_1_, bf16[4,272,128]{2,1,0:T(8,128)(2,1)S(1)} %collective-permute-done.7.refs_2_, ...), custom_call_target="tpu_custom_call" | custom-call | flops 536870912 | bytes 8388608 | tf_op jit(solution)/shard_map/near_half/pallas_call | solution.py:186
  42.0 1.9 %far_half.1 = f32[512,1024]{1,0:T(8,128)} custom-call(bf16[512,128]{1,0:T(8,128)(2,1)S(1)} %collective-permute-done.2.refs_0_, bf16[512,128]{1,0:T(8,128)(2,1)S(1)} %collective-permute-done.9.refs_1_, bf16[512,128]{1,0:T(8,128)(2,1)S(1)} %collective-permute-done.14.refs_2_, bf16[512,128]{1,0:T(8,128)(2,1)S(1)} %collective-permute-done.15.refs_3_, ...), custom_call_target="tpu_custom_call" | custom-call | flops 536870912 | bytes 8388608 | tf_op jit(solution)/shard_map/far_half/pallas_call | solution.py:237
  (22 shorter events, 1.4 us)
Async XLA Ops:
  0.0 9.4 %collective-permute-start = (bf16[512,128]{1,0:T(8,128)(2,1)}, bf16[512,128]{1,0:T(8,128)(2,1)S(1)}, u32[]{:S(2)}, u32[]{:S(2)}) collective-permute-start(bf16[512,128]{1,0:T(8,128)(2,1)} %refs_11_.1), channel_id=1, source_target_pairs={{0,1},{1,0},{2,3},{3,2},{4,5},{5,4},{6,7},{7,6},{8,9},{9,8},{10,11... | collective-permute-start | bytes 393224 | tf_op jit(solution)/shard_map/ppermute | solution.py:259
  2.9 9.0 %collective-permute-start.1 = (bf16[512,128]{1,0:T(8,128)(2,1)}, bf16[512,128]{1,0:T(8,128)(2,1)S(1)}, u32[]{:S(2)}, u32[]{:S(2)}) collective-permute-start(bf16[512,128]{1,0:T(8,128)(2,1)} %refs_11_.1), channel_id=1, source_target_pairs={{0,2},{1,3},{2,0},{3,1},{4,6},{5,7},{6,4},{7,5},{8,10},{9,11},{10,... | collective-permute-start | bytes 393224 | tf_op jit(solution)/shard_map/ppermute | solution.py:259
  4.5 7.4 %collective-permute-start.2 = (bf16[512,128]{1,0:T(8,128)(2,1)}, bf16[512,128]{1,0:T(8,128)(2,1)S(1)}, u32[]{:S(2)}, u32[]{:S(2)}) collective-permute-start(bf16[512,128]{1,0:T(8,128)(2,1)} %refs_11_.1), channel_id=1, source_target_pairs={{0,4},{1,5},{2,6},{3,7},{4,0},{5,1},{6,2},{7,3},{8,12},{9,13},{10,... | collective-permute-start | bytes 393224 | tf_op jit(solution)/shard_map/ppermute | solution.py:259
  8.4 6.5 %collective-permute-start.10 = (bf16[1,272,128]{2,1,0:T(8,128)(2,1)S(1)}, bf16[1,272,128]{2,1,0:T(8,128)(2,1)S(1)}, u32[]{:S(2)}, u32[]{:S(2)}) collective-permute-start(bf16[1,272,128]{2,1,0:T(8,128)(2,1)S(1)} %bitcast.20), channel_id=1, source_target_pairs={{0,1},{1,0},{2,3},{3,2},{4,5},{5,4},{6,7},{7,6},{8,9},{9,8},{10,11... | collective-permute-start | bytes 208904 | tf_op jit(solution)/shard_map/ppermute | solution.py:259
  9.0 10.4 %collective-permute-start.11 = (bf16[1,272,128]{2,1,0:T(8,128)(2,1)S(1)}, bf16[1,272,128]{2,1,0:T(8,128)(2,1)S(1)}, u32[]{:S(2)}, u32[]{:S(2)}) collective-permute-start(bf16[1,272,128]{2,1,0:T(8,128)(2,1)S(1)} %bitcast.19), channel_id=1, source_target_pairs={{0,2},{1,3},{2,0},{3,1},{4,6},{5,7},{6,4},{7,5},{8,10},{9,11},{10,... | collective-permute-start | bytes 208904 | tf_op jit(solution)/shard_map/ppermute | solution.py:259
  9.4 11.0 %collective-permute-start.12 = (bf16[1,272,128]{2,1,0:T(8,128)(2,1)S(1)}, bf16[1,272,128]{2,1,0:T(8,128)(2,1)S(1)}, u32[]{:S(2)}, u32[]{:S(2)}) collective-permute-start(bf16[1,272,128]{2,1,0:T(8,128)(2,1)S(1)} %bitcast.18), channel_id=1, source_target_pairs={{0,3},{1,2},{2,1},{3,0},{4,7},{5,6},{6,5},{7,4},{8,11},{9,10},{10,... | collective-permute-start | bytes 208904 | tf_op jit(solution)/shard_map/ppermute | solution.py:259
  11.9 10.1 %collective-permute-start.3 = (bf16[1,272,128]{2,1,0:T(8,128)(2,1)S(1)}, bf16[1,272,128]{2,1,0:T(8,128)(2,1)S(1)}, u32[]{:S(2)}, u32[]{:S(2)}) collective-permute-start(bf16[1,272,128]{2,1,0:T(8,128)(2,1)S(1)} %bitcast.17), channel_id=1, source_target_pairs={{0,4},{1,5},{2,6},{3,7},{4,0},{5,1},{6,2},{7,3},{8,12},{9,13},{10,... | collective-permute-start | bytes 208904 | tf_op jit(solution)/shard_map/ppermute | solution.py:259
  14.4 9.4 %collective-permute-start.4 = (bf16[1,272,128]{2,1,0:T(8,128)(2,1)S(1)}, bf16[1,272,128]{2,1,0:T(8,128)(2,1)S(1)}, u32[]{:S(2)}, u32[]{:S(2)}) collective-permute-start(bf16[1,272,128]{2,1,0:T(8,128)(2,1)S(1)} %bitcast.16), channel_id=1, source_target_pairs={{0,5},{1,4},{2,7},{3,6},{4,1},{5,0},{6,3},{7,2},{8,13},{9,12},{10,... | collective-permute-start | bytes 208904 | tf_op jit(solution)/shard_map/ppermute | solution.py:259
  14.8 9.0 %collective-permute-start.5 = (bf16[1,272,128]{2,1,0:T(8,128)(2,1)S(1)}, bf16[1,272,128]{2,1,0:T(8,128)(2,1)S(1)}, u32[]{:S(2)}, u32[]{:S(2)}) collective-permute-start(bf16[1,272,128]{2,1,0:T(8,128)(2,1)S(1)} %bitcast.15), channel_id=1, source_target_pairs={{0,6},{1,7},{2,4},{3,5},{4,2},{5,3},{6,0},{7,1},{8,14},{9,15},{10,... | collective-permute-start | bytes 208904 | tf_op jit(solution)/shard_map/ppermute | solution.py:259
  19.4 7.1 %collective-permute-start.6 = (bf16[1,272,128]{2,1,0:T(8,128)(2,1)S(1)}, bf16[1,272,128]{2,1,0:T(8,128)(2,1)S(1)}, u32[]{:S(2)}, u32[]{:S(2)}) collective-permute-start(bf16[1,272,128]{2,1,0:T(8,128)(2,1)S(1)} %bitcast.14), channel_id=1, source_target_pairs={{0,7},{1,6},{2,5},{3,4},{4,3},{5,2},{6,1},{7,0},{8,15},{9,14},{10,... | collective-permute-start | bytes 208904 | tf_op jit(solution)/shard_map/ppermute | solution.py:259
  20.4 15.0 %collective-permute-start.13 = (bf16[4,272,128]{2,1,0:T(8,128)(2,1)S(1)}, bf16[4,272,128]{2,1,0:T(8,128)(2,1)S(1)}, u32[]{:S(2)}, u32[]{:S(2)}) collective-permute-start(bf16[4,272,128]{2,1,0:T(8,128)(2,1)S(1)} %join.3.refs_4_), channel_id=1, source_target_pairs={{0,16},{8,24},{16,0},{24,8},{1,17},{9,25},{17,1},{25,9},{2,18},{10... | collective-permute-start | bytes 835592 | tf_op jit(solution)/shard_map/ppermute | solution.py:259
  26.5 9.4 %collective-permute-start.7 = (bf16[4,272,128]{2,1,0:T(8,128)(2,1)S(1)}, bf16[4,272,128]{2,1,0:T(8,128)(2,1)S(1)}, u32[]{:S(2)}, u32[]{:S(2)}) collective-permute-start(bf16[4,272,128]{2,1,0:T(8,128)(2,1)S(1)} %join.2.refs_0_), channel_id=1, source_target_pairs={{0,16},{8,24},{16,0},{24,8},{1,17},{9,25},{17,1},{25,9},{2,18},{10... | collective-permute-start | bytes 835592 | tf_op jit(solution)/shard_map/ppermute | solution.py:259
  28.1 7.3 %collective-permute-start.14 = (bf16[512,128]{1,0:T(8,128)(2,1)S(1)}, bf16[512,128]{1,0:T(8,128)(2,1)S(1)}, u32[]{:S(2)}, u32[]{:S(2)}) collective-permute-start(bf16[512,128]{1,0:T(8,128)(2,1)S(1)} %collective-permute-done.1.refs_9_), channel_id=1, source_target_pairs={{0,4},{1,5},{2,6},{3,7},{4,0},{5,1},{6,2},{7,3},{8,12},{9,13},{10,... | collective-permute-start | bytes 393224 | tf_op jit(solution)/shard_map/ppermute | solution.py:259
  29.3 6.6 %collective-permute-start.8 = (bf16[512,128]{1,0:T(8,128)(2,1)S(1)}, bf16[512,128]{1,0:T(8,128)(2,1)S(1)}, u32[]{:S(2)}, u32[]{:S(2)}) collective-permute-start(bf16[512,128]{1,0:T(8,128)(2,1)S(1)} %collective-permute-done.1.refs_9_), channel_id=1, source_target_pairs={{0,1},{1,0},{2,3},{3,2},{4,5},{5,4},{6,7},{7,6},{8,9},{9,8},{10,11... | collective-permute-start | bytes 393224 | tf_op jit(solution)/shard_map/ppermute | solution.py:259
  30.1 5.8 %collective-permute-start.9 = (bf16[512,128]{1,0:T(8,128)(2,1)S(1)}, bf16[512,128]{1,0:T(8,128)(2,1)S(1)}, u32[]{:S(2)}, u32[]{:S(2)}) collective-permute-start(bf16[512,128]{1,0:T(8,128)(2,1)S(1)} %collective-permute-done.2.refs_0_), channel_id=1, source_target_pairs={{0,1},{1,0},{2,3},{3,2},{4,5},{5,4},{6,7},{7,6},{8,9},{9,8},{10,11... | collective-permute-start | bytes 393224 | tf_op jit(solution)/shard_map/ppermute | solution.py:259
  35.4 1.8 %collective-permute-start.18 = (bf16[4,272,128]{2,1,0:T(8,128)(2,1)S(1)}, bf16[4,272,128]{2,1,0:T(8,128)(2,1)S(1)}, u32[]{:S(2)}, u32[]{:S(2)}) collective-permute-start(bf16[4,272,128]{2,1,0:T(8,128)(2,1)S(1)} %join.3.refs_4_), channel_id=1, source_target_pairs={{0,8},{8,0},{16,24},{24,16},{1,9},{9,1},{17,25},{25,17},{2,10},{10... | collective-permute-start | bytes 835592 | tf_op jit(solution)/shard_map/ppermute | solution.py:259
  35.4 2.0 %collective-permute-start.19 = (bf16[4,272,128]{2,1,0:T(8,128)(2,1)S(1)}, bf16[4,272,128]{2,1,0:T(8,128)(2,1)S(1)}, u32[]{:S(2)}, u32[]{:S(2)}) collective-permute-start(bf16[4,272,128]{2,1,0:T(8,128)(2,1)S(1)} %collective-permute-done.13.refs_6_), channel_id=1, source_target_pairs={{0,8},{8,0},{16,24},{24,16},{1,9},{9,1},{17,25},{25,17},{2,10},{10... | collective-permute-start | bytes 835592 | tf_op jit(solution)/shard_map/ppermute | solution.py:259
  35.9 1.8 %collective-permute-start.16 = (bf16[4,272,128]{2,1,0:T(8,128)(2,1)S(1)}, bf16[4,272,128]{2,1,0:T(8,128)(2,1)S(1)}, u32[]{:S(2)}, u32[]{:S(2)}) collective-permute-start(bf16[4,272,128]{2,1,0:T(8,128)(2,1)S(1)} %join.2.refs_0_), channel_id=1, source_target_pairs={{0,8},{8,0},{16,24},{24,16},{1,9},{9,1},{17,25},{25,17},{2,10},{10... | collective-permute-start | bytes 835592 | tf_op jit(solution)/shard_map/ppermute | solution.py:259
  36.0 2.2 %collective-permute-start.17 = (bf16[4,272,128]{2,1,0:T(8,128)(2,1)S(1)}, bf16[4,272,128]{2,1,0:T(8,128)(2,1)S(1)}, u32[]{:S(2)}, u32[]{:S(2)}) collective-permute-start(bf16[4,272,128]{2,1,0:T(8,128)(2,1)S(1)} %collective-permute-done.7.refs_2_), channel_id=1, source_target_pairs={{0,8},{8,0},{16,24},{24,16},{1,9},{9,1},{17,25},{25,17},{2,10},{10... | collective-permute-start | bytes 835592 | tf_op jit(solution)/shard_map/ppermute | solution.py:259
  36.5 5.5 %collective-permute-start.15 = (bf16[512,128]{1,0:T(8,128)(2,1)S(1)}, bf16[512,128]{1,0:T(8,128)(2,1)S(1)}, u32[]{:S(2)}, u32[]{:S(2)}) collective-permute-start(bf16[512,128]{1,0:T(8,128)(2,1)S(1)} %collective-permute-done.14.refs_2_), channel_id=1, source_target_pairs={{0,1},{1,0},{2,3},{3,2},{4,5},{5,4},{6,7},{7,6},{8,9},{9,8},{10,11... | collective-permute-start | bytes 393224 | tf_op jit(solution)/shard_map/ppermute | solution.py:259

commit v5 on v4

--- a/solution.py
+++ b/solution.py
@@ -121,8 +121,7 @@
         copy.wait()
 
 
-def near_kernel(n_pieces, offsets, capacity, where_ref, *refs):
-    n_amps = len(offsets)
+def near_kernel(n_pieces, n_amps, capacity, where_ref, *refs):
     pieces = refs[:n_pieces]
     amps = refs[n_pieces : n_pieces + n_amps]
     own, residual, total, far = refs[n_pieces + n_amps : n_pieces + n_amps + 4]
@@ -142,8 +141,9 @@
         ).astype(jnp.int32)
     table_copy = pltpu.make_async_copy(places, table, table_sem)
     table_copy.start()
-    for source, slot in zip(amps, offsets):
-        amp[:, slot * width : (slot + 1) * width] = source[...]
+    for i, source in enumerate(amps):
+        at = pl.multiple_of(where_ref[n_pieces + 1 + i] * width, width)
+        amp[:, pl.ds(at, width)] = source[...]
     table_copy.wait()
     col = where_ref[n_pieces]
     for p, piece in enumerate(pieces):
@@ -174,7 +174,7 @@
     multiply(amp, near, res, total, None, 2 * width)
 
 
-def near_half(where, pieces, amps, offsets, own, residual, capacity):
+def near_half(where, pieces, amps, own, residual, capacity):
     columns, _, width = pieces[0].shape
     n_pieces, n_amps = len(pieces), len(amps)
     rows, n_cols = residual.shape
@@ -184,7 +184,7 @@
     held = 2 * rows * depth + 4 * depth * n_cols + 8 * rows * n_cols
     held += sum(x.size * x.dtype.itemsize for x in pieces) // 2
     return pl.pallas_call(
-        functools.partial(near_kernel, n_pieces, offsets, capacity),
+        functools.partial(near_kernel, n_pieces, n_amps, capacity),
         out_shape=[
             jax.ShapeDtypeStruct(residual.shape, residual.dtype),
             jax.ShapeDtypeStruct((depth, n_cols), pieces[0].dtype),
@@ -219,25 +219,24 @@
     )
 
 
-def far_kernel(offsets, half, *refs):
-    amps = refs[: len(offsets)]
-    start, far, out, amp, total, sems = refs[len(offsets) :]
+def far_kernel(half, slots_ref, *refs):
+    amps, (start, far, out, amp, total, sems) = refs[:-6], refs[-6:]
     width = amps[0].shape[1]
-    for source, slot in zip(amps, offsets):
-        at = (slot - half) * width
-        amp[:, at : at + width] = source[...]
+    for i, source in enumerate(amps):
+        at = pl.multiple_of((slots_ref[i] - half) * width, width)
+        amp[:, pl.ds(at, width)] = source[...]
     multiply(amp, far, start, (total, out), sems, 2 * width)
 
 
-def far_half(amps, offsets, total, far):
+def far_half(slots, amps, total, far):
     rows, n_cols = total.shape
     depth, width = far.shape[0], amps[0].shape[1]
     vmem = pl.BlockSpec(memory_space=pltpu.VMEM)
     held = 4 * rows * depth + 2 * depth * n_cols + 8 * rows * n_cols
     return pl.pallas_call(
-        functools.partial(far_kernel, offsets, depth // width),
+        functools.partial(far_kernel, depth // width),
         out_shape=jax.ShapeDtypeStruct(total.shape, total.dtype),
-        in_specs=[vmem] * (len(amps) + 2),
+        in_specs=[pl.BlockSpec(memory_space=pltpu.SMEM)] + [vmem] * (len(amps) + 2),
         out_specs=pl.BlockSpec(memory_space=pltpu.HBM),
         scratch_shapes=[
             pltpu.VMEM((rows, depth), far.dtype),
@@ -251,12 +250,34 @@
             transcendentals=0,
         ),
         name="far_half",
-    )(*amps, total, far)
+    )(slots, *amps, total, far)
 
 
 def exchange(x, axis, flip):
     size = lax.axis_size(axis)
     return lax.ppermute(x, axis, [(i, i ^ flip) for i in range(size)])
+
+
+def choose_kernel(flag_ref, first, second, out):
+    @pl.when(flag_ref[0] == 1)
+    def _():
+        out[...] = first[...]
+
+    @pl.when(flag_ref[0] == 0)
+    def _():
+        out[...] = second[...]
+
+
+def choose(flag, first, second):
+    vmem = pl.BlockSpec(memory_space=pltpu.VMEM)
+    return pl.pallas_call(
+        choose_kernel,
+        out_shape=jax.ShapeDtypeStruct(first.shape, first.dtype),
+        in_specs=[pl.BlockSpec(memory_space=pltpu.SMEM), vmem, vmem],
+        out_specs=vmem,
+        compiler_params=pltpu.CompilerParams(vmem_limit_bytes=4 * MIB),
+        name="choose",
+    )(flag[None], first, second)
 
 
 def tie(late, *early):
@@ -269,45 +290,65 @@
     inner = 2 ** (int(math.log2(n_col)) // 2)
     capacity = -(-packed_tiles.shape[1] // n_col)
     half = n_col // 2
+    lanes = range(1, inner)
     outgoing = list(pack(col, packed_tiles, tile_ids, n_col, capacity))
 
     amps = {0: amplitudes}
-    for s in [*range(1, inner), *range(inner, half, inner), half]:
+    for s in [*lanes, inner]:
         amps[s] = exchange(amplitudes, "col", s)
-    outgoing[half:], amps = tie(outgoing[half:], amps)
+    mids = [(i // inner) % 4 in (1, 2) for i in range(n_col)]
+    swap = [(i, i ^ (3 * inner) if m else i) for i, m in enumerate(mids)]
+    across = lax.ppermute(amplitudes, "col", swap)
+    outgoing[half:], amps, across = tie(outgoing[half:], amps, across)
 
     chunks = [outgoing[0][None]]
     chunks += [exchange(outgoing[s][None], "col", s) for s in range(1, n_col)]
-    for flip in range(inner, half, inner):
-        for lane in range(1, inner):
-            amps[flip ^ lane] = exchange(amps[flip], "col", lane)
-        amps[flip ^ half] = exchange(amps[flip], "col", half)
-    for lane in range(1, inner):
-        amps[half ^ lane] = exchange(amps[half], "col", lane)
-
-    early = [s for s in amps if s and (s < half or half < s < half + inner)]
-    late = [flip ^ half for flip in range(inner, half, inner)]
+    outer = col // inner % 4
+    is_mid = ((outer == 1) | (outer == 2)).astype(jnp.int32)
+    onward = exchange(across, "col", inner)
+    leaving = choose(is_mid, amps[inner], amplitudes)
+    chunks[half], onward, leaving = tie(chunks[half], onward, leaving)
+    passed_on = choose(is_mid, across, onward)
+    straight = exchange(leaving, "col", 2 * inner)
+    for lane in lanes:
+        amps[inner ^ lane] = exchange(amps[inner], "col", lane)
+    passed_over = [exchange(passed_on, "col", lane) for lane in lanes]
+
+    early = [inner ^ lane for lane in lanes]
     pieces, rows = [], []
     for group in (join(chunks[half:]), join(chunks[:half])):
         passed = [exchange(group, "row", flip) for flip in range(CORES, n_row, CORES)]
-        due = late if pieces else early
-        passed, got = tie(passed, [amps[s] for s in due])
-        amps.update(zip(due, got))
+        if pieces:
+            passed, straight = tie(passed, straight)
+        else:
+            passed, got, passed_over = tie(passed, [amps[s] for s in early], passed_over)
+            amps.update(zip(early, got))
         own, passed = tie(group, passed)
         for flip, mine in zip(range(0, n_row, CORES), [own, *passed]):
             pieces += [mine, exchange(mine, "row", 1)]
             rows += [row ^ flip, row ^ flip ^ 1]
-    for flip in range(half + inner, n_col, inner):
-        for lane in range(1, inner):
-            amps[flip ^ lane] = exchange(amps[flip], "col", lane)
-
+    straight_over = [exchange(straight, "col", lane) for lane in lanes]
+
+    here, there = (2 + is_mid) * inner, (3 - is_mid) * inner
+    far = [(here, passed_on), *zip([here ^ x for x in lanes], passed_over)]
+    far += [(there, straight), *zip([there ^ x for x in lanes], straight_over)]
+    near = [(s, amps[s]) for s in sorted(amps) if s]
+    flip = 4 * inner
+    while flip < n_col:
+        near, far = near + far, [
+            (s ^ flip, exchange(x, "col", flip)) for s, x in [(0, amplitudes), *near, *far]
+        ]
+        flip *= 2
     where = jnp.stack(rows + [col]).astype(jnp.int32)
-    near = [s for s in sorted(amps) if 0 < s < half]
-    far = [s for s in sorted(amps) if s >= half]
+    near_slots, near_amps = zip(*near)
+    far_slots, far_amps = zip(*far)
+    near_slots = jnp.stack([jnp.asarray(s, jnp.int32) for s in near_slots])
+    far_slots = jnp.stack([jnp.asarray(s, jnp.int32) for s in far_slots])
+    where = jnp.concatenate([where, near_slots])
     total, far_block = near_half(
-        where, pieces, [amps[s] for s in near], near, amplitudes, residual_in, capacity
+        where, pieces, near_amps, amplitudes, residual_in, capacity
     )
-    return far_half([amps[s] for s in far], far, total, far_block)
+    return far_half(far_slots, far_amps, total, far_block)
 
 
 def solution(mesh):

time: 44 us -> 46 us (1.045)
  starting transfers between devices: 27.1 us -> 30.3 us
  waiting for transfers between devices: 9.71 us -> 6.93 us
  local copies, waits for them, and re-layouts: 0.08 us -> 0.99 us
  Pallas kernels: 6.84 us -> 7.48 us
    ppermute x20, waiting for transfers between devices: 9.71 us -> 6.93 us  [exchange(): return lax.ppermute(x, axis, [(i, i ^ flip) for i in range(size)])]
    ppermute x20, starting transfers between devices: 27.1 us -> 28.7 us  [exchange(): return lax.ppermute(x, axis, [(i, i ^ flip) for i in range(size)])]
    ppermute x0 -> x1, starting transfers between devices: none -> 1.55 us  [body(): across = lax.ppermute(amplitudes, 'col', swap)]
    unnamed x0 -> x2, local copies, waits for them, and re-layouts: none -> 0.9 us
    pallas_call x2 -> x4, Pallas kernels: 5.55 us -> 6.18 us  [the longest x1 3.7 us: near_half(): pl.pallas_call(functools.partial(near_kernel, n_pieces, n_amps, capacity)...]
  transfers between devices with their start and end apart: 20 -> 21, of which waited for: 7 -> 5; matrix products, arithmetic and copies ran while one was open for 0% -> 0% of each run, Pallas kernels for 11% -> 11%
where the time goes in v5:
time: 46 us; the launch traced here: 45.9 us
  starting transfers between devices  30.3 us (66%)
  Pallas kernels  7.48 us (16%)
  waiting for transfers between devices  6.93 us (15%)
  local copies, waits for them, and re-layouts  0.99 us (2%)
    ppermute x20, starting transfers between devices, exchange(): return lax.ppermute(x, axis, [(i, i ^ flip) for i in range(size)])  28.7 us
    ppermute x20, waiting for transfers between devices, exchange(): return lax.ppermute(x, axis, [(i, i ^ flip) for i in range(size)])  6.93 us
    pallas_call x1, Pallas kernels, near_half(): pl.pallas_call(functools.partial(near_kernel, n_pieces, n_amps, capacity)...  3.7 us
    pallas_call x1, Pallas kernels, far_half(): pl.pallas_call(functools.partial(far_kernel, depth // width), out_shape=j...  2.47 us
    ppermute x1, starting transfers between devices, body(): across = lax.ppermute(amplitudes, 'col', swap)  1.55 us
    pallas_call x1, Pallas kernels, pack(): pl.pallas_call(functools.partial(pack_kernel, columns, capacity), out_sha...  1.25 us
  transfers between devices with their start and end apart: 21, of which 5 were waited for; matrix products, arithmetic and copies ran while one was open for 0% of the time, Pallas kernels for 11%

profile of v5, /device:TPU:0, one launch (start us, length us, event | category | flops | bytes accessed | tf_op | source)
XLA Modules:
  0.0 45.9 jit_solution(7436151026335491143)
XLA Ops:
  0.0 2.9 %collective-permute-start = (bf16[512,128]{1,0:T(8,128)(2,1)}, bf16[512,128]{1,0:T(8,128)(2,1)S(1)}, u32[]{:S(2)}, u32[]{:S(2)}) collective-permute-start(bf16[512,128]{1,0:T(8,128)(2,1)} %refs_11_.1), channel_id=1, source_target_pairs={{0,1},{1,0},{2,3},{3,2},{4,5},{5,4},{6,7},{7,6},{8,9},{9,8},{10,11... | collective-permute-start | bytes 393224 | tf_op jit(solution)/shard_map/ppermute | solution.py:258
  2.9 1.6 %collective-permute-start.1 = (bf16[512,128]{1,0:T(8,128)(2,1)}, bf16[512,128]{1,0:T(8,128)(2,1)S(1)}, u32[]{:S(2)}, u32[]{:S(2)}) collective-permute-start(bf16[512,128]{1,0:T(8,128)(2,1)} %refs_11_.1), channel_id=1, source_target_pairs={{0,2},{1,3},{2,0},{3,1},{4,6},{5,7},{6,4},{7,5},{8,10},{9,11},{10,... | collective-permute-start | bytes 393224 | tf_op jit(solution)/shard_map/ppermute | solution.py:258
  4.5 1.6 %collective-permute-start.2 = (bf16[512,128]{1,0:T(8,128)(2,1)}, bf16[512,128]{1,0:T(8,128)(2,1)S(1)}, u32[]{:S(2)}, u32[]{:S(2)}) collective-permute-start(bf16[512,128]{1,0:T(8,128)(2,1)} %refs_11_.1), channel_id=1, source_target_pairs={{0,0},{1,1},{2,4},{3,5},{4,2},{5,3},{6,6},{7,7},{8,8},{9,9},{10,12... | collective-permute-start | bytes 393224 | tf_op jit(solution)/shard_map/ppermute | solution.py:301
  6.1 1.3 %pack.1 = (bf16[272,128]{1,0:T(8,128)(2,1)S(1)}, bf16[272,128]{1,0:T(8,128)(2,1)S(1)}, bf16[272,128]{1,0:T(8,128)(2,1)S(1)}, bf16[272,128]{1,0:T(8,128)(2,1)S(1)...) custom-call(s32[1]{0:T(128)} %bitcast.5.me_ref, ...), custom_call_target="tpu_custom_call" | custom-call | tf_op jit(solution)/shard_map/pack/pallas_call | solution.py:63
  7.3 0.6 %collective-permute-start.11 = (bf16[1,272,128]{2,1,0:T(8,128)(2,1)S(1)}, bf16[1,272,128]{2,1,0:T(8,128)(2,1)S(1)}, u32[]{:S(2)}, u32[]{:S(2)}) collective-permute-start(bf16[1,272,128]{2,1,0:T(8,128)(2,1)S(1)} %bitcast.25), channel_id=1, source_target_pairs={{0,1},{1,0},{2,3},{3,2},{4,5},{5,4},{6,7},{7,6},{8,9},{9,8},{10,11... | collective-permute-start | bytes 208904 | tf_op jit(solution)/shard_map/ppermute | solution.py:258
  7.9 3.5 %collective-permute-start.12 = (bf16[1,272,128]{2,1,0:T(8,128)(2,1)S(1)}, bf16[1,272,128]{2,1,0:T(8,128)(2,1)S(1)}, u32[]{:S(2)}, u32[]{:S(2)}) collective-permute-start(bf16[1,272,128]{2,1,0:T(8,128)(2,1)S(1)} %bitcast.24), channel_id=1, source_target_pairs={{0,2},{1,3},{2,0},{3,1},{4,6},{5,7},{6,4},{7,5},{8,10},{9,11},{10,... | collective-permute-start | bytes 208904 | tf_op jit(solution)/shard_map/ppermute | solution.py:258
  11.4 0.9 %collective-permute-start.13 = (bf16[1,272,128]{2,1,0:T(8,128)(2,1)S(1)}, bf16[1,272,128]{2,1,0:T(8,128)(2,1)S(1)}, u32[]{:S(2)}, u32[]{:S(2)}) collective-permute-start(bf16[1,272,128]{2,1,0:T(8,128)(2,1)S(1)} %bitcast.23), channel_id=1, source_target_pairs={{0,3},{1,2},{2,1},{3,0},{4,7},{5,6},{6,5},{7,4},{8,11},{9,10},{10,... | collective-permute-start | bytes 208904 | tf_op jit(solution)/shard_map/ppermute | solution.py:258
  12.4 2.0 %collective-permute-start.4 = (bf16[512,128]{1,0:T(8,128)(2,1)S(1)}, bf16[512,128]{1,0:T(8,128)(2,1)S(1)}, u32[]{:S(2)}, u32[]{:S(2)}) collective-permute-start(bf16[512,128]{1,0:T(8,128)(2,1)S(1)} %collective-permute-done.2.first), channel_id=1, source_target_pairs={{0,2},{1,3},{2,0},{3,1},{4,6},{5,7},{6,4},{7,5},{8,10},{9,11},{10,... | collective-permute-start | bytes 393224 | tf_op jit(solution)/shard_map/ppermute | solution.py:258
  14.4 2.9 %collective-permute-start.5 = (bf16[1,272,128]{2,1,0:T(8,128)(2,1)S(1)}, bf16[1,272,128]{2,1,0:T(8,128)(2,1)S(1)}, u32[]{:S(2)}, u32[]{:S(2)}) collective-permute-start(bf16[1,272,128]{2,1,0:T(8,128)(2,1)S(1)} %bitcast.21), channel_id=1, source_target_pairs={{0,5},{1,4},{2,7},{3,6},{4,1},{5,0},{6,3},{7,2},{8,13},{9,12},{10,... | collective-permute-start | bytes 208904 | tf_op jit(solution)/shard_map/ppermute | solution.py:258
  17.3 1.2 %collective-permute-start.6 = (bf16[1,272,128]{2,1,0:T(8,128)(2,1)S(1)}, bf16[1,272,128]{2,1,0:T(8,128)(2,1)S(1)}, u32[]{:S(2)}, u32[]{:S(2)}) collective-permute-start(bf16[1,272,128]{2,1,0:T(8,128)(2,1)S(1)} %bitcast.20), channel_id=1, source_target_pairs={{0,6},{1,7},{2,4},{3,5},{4,2},{5,3},{6,0},{7,1},{8,14},{9,15},{10,... | collective-permute-start | bytes 208904 | tf_op jit(solution)/shard_map/ppermute | solution.py:258
  18.5 3.5 %collective-permute-start.7 = (bf16[1,272,128]{2,1,0:T(8,128)(2,1)S(1)}, bf16[1,272,128]{2,1,0:T(8,128)(2,1)S(1)}, u32[]{:S(2)}, u32[]{:S(2)}) collective-permute-start(bf16[1,272,128]{2,1,0:T(8,128)(2,1)S(1)} %bitcast.19), channel_id=1, source_target_pairs={{0,7},{1,6},{2,5},{3,4},{4,3},{5,2},{6,1},{7,0},{8,15},{9,14},{10,... | collective-permute-start | bytes 208904 | tf_op jit(solution)/shard_map/ppermute | solution.py:258
  22.1 2.3 %collective-permute-done.3.refs_0_ = bf16[1,272,128]{2,1,0:T(8,128)(2,1)S(1)} collective-permute-done((bf16[1,272,128]{2,1,0:T(8,128)(2,1)S(1)}, bf16[1,272,128]{2,1,0:T(8,128)(2,1)S(1)}, u32[]{:S(2)}, u32[]{:S(2)}) %collective-permute-start.3) | collective-permute-done | bytes 69664 | tf_op jit(solution)/shard_map/ppermute | solution.py:258
  24.4 1.5 %collective-permute-start.14 = (bf16[4,272,128]{2,1,0:T(8,128)(2,1)S(1)}, bf16[4,272,128]{2,1,0:T(8,128)(2,1)S(1)}, u32[]{:S(2)}, u32[]{:S(2)}) collective-permute-start(bf16[4,272,128]{2,1,0:T(8,128)(2,1)S(1)} %join.3.refs_4_), channel_id=1, source_target_pairs={{0,16},{8,24},{16,0},{24,8},{1,17},{9,25},{17,1},{25,9},{2,18},{10... | collective-permute-start | bytes 835592 | tf_op jit(solution)/shard_map/ppermute | solution.py:258
  25.9 0.9 %copy-done = bf16[512,128]{1,0:T(8,128)(2,1)S(1)} copy-done((bf16[512,128]{1,0:T(8,128)(2,1)S(1)}, bf16[512,128]{1,0:T(8,128)(2,1)}, u32[]{:S(2)}) %copy-start) | copy-done | bytes 131096
  26.9 1.1 %collective-permute-start.8 = (bf16[4,272,128]{2,1,0:T(8,128)(2,1)S(1)}, bf16[4,272,128]{2,1,0:T(8,128)(2,1)S(1)}, u32[]{:S(2)}, u32[]{:S(2)}) collective-permute-start(bf16[4,272,128]{2,1,0:T(8,128)(2,1)S(1)} %join.2.refs_0_), channel_id=1, source_target_pairs={{0,16},{8,24},{16,0},{24,8},{1,17},{9,25},{17,1},{25,9},{2,18},{10... | collective-permute-start | bytes 835592 | tf_op jit(solution)/shard_map/ppermute | solution.py:258
  28.0 3.0 %collective-permute-start.15 = (bf16[512,128]{1,0:T(8,128)(2,1)S(1)}, bf16[512,128]{1,0:T(8,128)(2,1)S(1)}, u32[]{:S(2)}, u32[]{:S(2)}) collective-permute-start(bf16[512,128]{1,0:T(8,128)(2,1)S(1)} %choose.2), channel_id=1, source_target_pairs={{0,4},{1,5},{2,6},{3,7},{4,0},{5,1},{6,2},{7,3},{8,12},{9,13},{10,... | collective-permute-start | bytes 393224 | tf_op jit(solution)/shard_map/ppermute | solution.py:258
  30.9 0.8 %collective-permute-start.9 = (bf16[512,128]{1,0:T(8,128)(2,1)S(1)}, bf16[512,128]{1,0:T(8,128)(2,1)S(1)}, u32[]{:S(2)}, u32[]{:S(2)}) collective-permute-start(bf16[512,128]{1,0:T(8,128)(2,1)S(1)} %collective-permute-done.1.first.refs_9_), channel_id=1, source_target_pairs={{0,1},{1,0},{2,3},{3,2},{4,5},{5,4},{6,7},{7,6},{8,9},{9,8},{10,11... | collective-permute-start | bytes 393224 | tf_op jit(solution)/shard_map/ppermute | solution.py:258
  31.7 1.3 %collective-permute-start.10 = (bf16[512,128]{1,0:T(8,128)(2,1)S(1)}, bf16[512,128]{1,0:T(8,128)(2,1)S(1)}, u32[]{:S(2)}, u32[]{:S(2)}) collective-permute-start(bf16[512,128]{1,0:T(8,128)(2,1)S(1)} %choose.3.refs_0_), channel_id=1, source_target_pairs={{0,1},{1,0},{2,3},{3,2},{4,5},{5,4},{6,7},{7,6},{8,9},{9,8},{10,11... | collective-permute-start | bytes 393224 | tf_op jit(solution)/shard_map/ppermute | solution.py:258
  33.0 2.7 %collective-permute-done.15.refs_2_ = bf16[512,128]{1,0:T(8,128)(2,1)S(1)} collective-permute-done((bf16[512,128]{1,0:T(8,128)(2,1)S(1)}, bf16[512,128]{1,0:T(8,128)(2,1)S(1)}, u32[]{:S(2)}, u32[]{:S(2)}) %collective-permute-start.15) | collective-permute-done | bytes 131104 | tf_op jit(solution)/shard_map/ppermute | solution.py:258
  36.2 1.1 %collective-permute-done.10.refs_1_ = bf16[512,128]{1,0:T(8,128)(2,1)S(1)} collective-permute-done((bf16[512,128]{1,0:T(8,128)(2,1)S(1)}, bf16[512,128]{1,0:T(8,128)(2,1)S(1)}, u32[]{:S(2)}, u32[]{:S(2)}) %collective-permute-start.10) | collective-permute-done | bytes 131104 | tf_op jit(solution)/shard_map/ppermute | solution.py:258
  37.3 0.5 %collective-permute-start.18 = (bf16[4,272,128]{2,1,0:T(8,128)(2,1)S(1)}, bf16[4,272,128]{2,1,0:T(8,128)(2,1)S(1)}, u32[]{:S(2)}, u32[]{:S(2)}) collective-permute-start(bf16[4,272,128]{2,1,0:T(8,128)(2,1)S(1)} %collective-permute-done.8.refs_2_), channel_id=1, source_target_pairs={{0,8},{8,0},{16,24},{24,16},{1,9},{9,1},{17,25},{25,17},{2,10},{10... | collective-permute-start | bytes 835592 | tf_op jit(solution)/shard_map/ppermute | solution.py:258
  37.9 0.8 %collective-permute-start.16 = (bf16[512,128]{1,0:T(8,128)(2,1)S(1)}, bf16[512,128]{1,0:T(8,128)(2,1)S(1)}, u32[]{:S(2)}, u32[]{:S(2)}) collective-permute-start(bf16[512,128]{1,0:T(8,128)(2,1)S(1)} %collective-permute-done.15.refs_2_), channel_id=1, source_target_pairs={{0,1},{1,0},{2,3},{3,2},{4,5},{5,4},{6,7},{7,6},{8,9},{9,8},{10,11... | collective-permute-start | bytes 393224 | tf_op jit(solution)/shard_map/ppermute | solution.py:258
  39.3 3.7 %near_half.1 = (f32[512,1024]{1,0:T(8,128)S(1)}, bf16[512,1024]{1,0:T(8,128)(2,1)S(1)}) custom-call(s32[12]{0:T(128)S(1)} %concatenate.3.where_ref, bf16[4,272,128]{2,1,0:T(8,128)(2,1)S(1)} %join.2.refs_0_, bf16[4,272,128]{2,1,0:T(8,128)(2,1)S(1)} %collective-permute-done.17.refs_1_, bf16[4,272,128]{2,1,0:T(8,128)(2,1)S(1)} %collective-permute-done.8.refs_2_, ...), custom_call_target="tpu_custom_call" | custom-call | flops 536870912 | bytes 8388608 | tf_op jit(solution)/shard_map/near_half/pallas_call | solution.py:186
  43.4 2.5 %far_half.1 = f32[512,1024]{1,0:T(8,128)} custom-call(s32[4]{0:T(128)S(1)} %pad_add_fusion.slots_ref, bf16[512,128]{1,0:T(8,128)(2,1)S(1)} %choose.3.refs_0_, bf16[512,128]{1,0:T(8,128)(2,1)S(1)} %collective-permute-done.10.refs_1_, bf16[512,128]{1,0:T(8,128)(2,1)S(1)} %collective-permute-done.15.refs_2_, ...), custom_call_target="tpu_custom_call" | custom-call | flops 536870912 | bytes 8388608 | tf_op jit(solution)/shard_map/far_half/pallas_call | solution.py:236
  (29 shorter events, 1.6 us)
Async XLA Ops:
  0.0 11.4 %collective-permute-start = (bf16[512,128]{1,0:T(8,128)(2,1)}, bf16[512,128]{1,0:T(8,128)(2,1)S(1)}, u32[]{:S(2)}, u32[]{:S(2)}) collective-permute-start(bf16[512,128]{1,0:T(8,128)(2,1)} %refs_11_.1), channel_id=1, source_target_pairs={{0,1},{1,0},{2,3},{3,2},{4,5},{5,4},{6,7},{7,6},{8,9},{9,8},{10,11... | collective-permute-start | bytes 393224 | tf_op jit(solution)/shard_map/ppermute | solution.py:258
  2.9 9.4 %collective-permute-start.1 = (bf16[512,128]{1,0:T(8,128)(2,1)}, bf16[512,128]{1,0:T(8,128)(2,1)S(1)}, u32[]{:S(2)}, u32[]{:S(2)}) collective-permute-start(bf16[512,128]{1,0:T(8,128)(2,1)} %refs_11_.1), channel_id=1, source_target_pairs={{0,2},{1,3},{2,0},{3,1},{4,6},{5,7},{6,4},{7,5},{8,10},{9,11},{10,... | collective-permute-start | bytes 393224 | tf_op jit(solution)/shard_map/ppermute | solution.py:258
  4.5 7.9 %collective-permute-start.2 = (bf16[512,128]{1,0:T(8,128)(2,1)}, bf16[512,128]{1,0:T(8,128)(2,1)S(1)}, u32[]{:S(2)}, u32[]{:S(2)}) collective-permute-start(bf16[512,128]{1,0:T(8,128)(2,1)} %refs_11_.1), channel_id=1, source_target_pairs={{0,0},{1,1},{2,4},{3,5},{4,2},{5,3},{6,6},{7,7},{8,8},{9,9},{10,12... | collective-permute-start | bytes 393224 | tf_op jit(solution)/shard_map/ppermute | solution.py:301
  7.3 7.1 %collective-permute-start.11 = (bf16[1,272,128]{2,1,0:T(8,128)(2,1)S(1)}, bf16[1,272,128]{2,1,0:T(8,128)(2,1)S(1)}, u32[]{:S(2)}, u32[]{:S(2)}) collective-permute-start(bf16[1,272,128]{2,1,0:T(8,128)(2,1)S(1)} %bitcast.25), channel_id=1, source_target_pairs={{0,1},{1,0},{2,3},{3,2},{4,5},{5,4},{6,7},{7,6},{8,9},{9,8},{10,11... | collective-permute-start | bytes 208904 | tf_op jit(solution)/shard_map/ppermute | solution.py:258
  7.9 9.4 %collective-permute-start.12 = (bf16[1,272,128]{2,1,0:T(8,128)(2,1)S(1)}, bf16[1,272,128]{2,1,0:T(8,128)(2,1)S(1)}, u32[]{:S(2)}, u32[]{:S(2)}) collective-permute-start(bf16[1,272,128]{2,1,0:T(8,128)(2,1)S(1)} %bitcast.24), channel_id=1, source_target_pairs={{0,2},{1,3},{2,0},{3,1},{4,6},{5,7},{6,4},{7,5},{8,10},{9,11},{10,... | collective-permute-start | bytes 208904 | tf_op jit(solution)/shard_map/ppermute | solution.py:258
  11.4 7.1 %collective-permute-start.13 = (bf16[1,272,128]{2,1,0:T(8,128)(2,1)S(1)}, bf16[1,272,128]{2,1,0:T(8,128)(2,1)S(1)}, u32[]{:S(2)}, u32[]{:S(2)}) collective-permute-start(bf16[1,272,128]{2,1,0:T(8,128)(2,1)S(1)} %bitcast.23), channel_id=1, source_target_pairs={{0,3},{1,2},{2,1},{3,0},{4,7},{5,6},{6,5},{7,4},{8,11},{9,10},{10,... | collective-permute-start | bytes 208904 | tf_op jit(solution)/shard_map/ppermute | solution.py:258
  12.4 14.4 %collective-permute-start.4 = (bf16[512,128]{1,0:T(8,128)(2,1)S(1)}, bf16[512,128]{1,0:T(8,128)(2,1)S(1)}, u32[]{:S(2)}, u32[]{:S(2)}) collective-permute-start(bf16[512,128]{1,0:T(8,128)(2,1)S(1)} %collective-permute-done.2.first), channel_id=1, source_target_pairs={{0,2},{1,3},{2,0},{3,1},{4,6},{5,7},{6,4},{7,5},{8,10},{9,11},{10,... | collective-permute-start | bytes 393224 | tf_op jit(solution)/shard_map/ppermute | solution.py:258
  14.4 10.0 %collective-permute-start.3 = (bf16[1,272,128]{2,1,0:T(8,128)(2,1)S(1)}, bf16[1,272,128]{2,1,0:T(8,128)(2,1)S(1)}, u32[]{:S(2)}, u32[]{:S(2)}) collective-permute-start(bf16[1,272,128]{2,1,0:T(8,128)(2,1)S(1)} %bitcast.22), channel_id=1, source_target_pairs={{0,4},{1,5},{2,6},{3,7},{4,0},{5,1},{6,2},{7,3},{8,12},{9,13},{10,... | collective-permute-start | bytes 208904 | tf_op jit(solution)/shard_map/ppermute | solution.py:258
  14.4 12.4 %collective-permute-start.5 = (bf16[1,272,128]{2,1,0:T(8,128)(2,1)S(1)}, bf16[1,272,128]{2,1,0:T(8,128)(2,1)S(1)}, u32[]{:S(2)}, u32[]{:S(2)}) collective-permute-start(bf16[1,272,128]{2,1,0:T(8,128)(2,1)S(1)} %bitcast.21), channel_id=1, source_target_pairs={{0,5},{1,4},{2,7},{3,6},{4,1},{5,0},{6,3},{7,2},{8,13},{9,12},{10,... | collective-permute-start | bytes 208904 | tf_op jit(solution)/shard_map/ppermute | solution.py:258
  17.3 9.5 %collective-permute-start.6 = (bf16[1,272,128]{2,1,0:T(8,128)(2,1)S(1)}, bf16[1,272,128]{2,1,0:T(8,128)(2,1)S(1)}, u32[]{:S(2)}, u32[]{:S(2)}) collective-permute-start(bf16[1,272,128]{2,1,0:T(8,128)(2,1)S(1)} %bitcast.20), channel_id=1, source_target_pairs={{0,6},{1,7},{2,4},{3,5},{4,2},{5,3},{6,0},{7,1},{8,14},{9,15},{10,... | collective-permute-start | bytes 208904 | tf_op jit(solution)/shard_map/ppermute | solution.py:258
  18.5 8.3 %collective-permute-start.7 = (bf16[1,272,128]{2,1,0:T(8,128)(2,1)S(1)}, bf16[1,272,128]{2,1,0:T(8,128)(2,1)S(1)}, u32[]{:S(2)}, u32[]{:S(2)}) collective-permute-start(bf16[1,272,128]{2,1,0:T(8,128)(2,1)S(1)} %bitcast.19), channel_id=1, source_target_pairs={{0,7},{1,6},{2,5},{3,4},{4,3},{5,2},{6,1},{7,0},{8,15},{9,14},{10,... | collective-permute-start | bytes 208904 | tf_op jit(solution)/shard_map/ppermute | solution.py:258
  24.4 8.7 %collective-permute-start.14 = (bf16[4,272,128]{2,1,0:T(8,128)(2,1)S(1)}, bf16[4,272,128]{2,1,0:T(8,128)(2,1)S(1)}, u32[]{:S(2)}, u32[]{:S(2)}) collective-permute-start(bf16[4,272,128]{2,1,0:T(8,128)(2,1)S(1)} %join.3.refs_4_), channel_id=1, source_target_pairs={{0,16},{8,24},{16,0},{24,8},{1,17},{9,25},{17,1},{25,9},{2,18},{10... | collective-permute-start | bytes 835592 | tf_op jit(solution)/shard_map/ppermute | solution.py:258
  25.9 0.9 %copy-start = (bf16[512,128]{1,0:T(8,128)(2,1)S(1)}, bf16[512,128]{1,0:T(8,128)(2,1)}, u32[]{:S(2)}) copy-start(bf16[512,128]{1,0:T(8,128)(2,1)} %refs_11_.1) | copy-start | bytes 393220
  26.9 10.4 %collective-permute-start.8 = (bf16[4,272,128]{2,1,0:T(8,128)(2,1)S(1)}, bf16[4,272,128]{2,1,0:T(8,128)(2,1)S(1)}, u32[]{:S(2)}, u32[]{:S(2)}) collective-permute-start(bf16[4,272,128]{2,1,0:T(8,128)(2,1)S(1)} %join.2.refs_0_), channel_id=1, source_target_pairs={{0,16},{8,24},{16,0},{24,8},{1,17},{9,25},{17,1},{25,9},{2,18},{10... | collective-permute-start | bytes 835592 | tf_op jit(solution)/shard_map/ppermute | solution.py:258
  28.0 7.8 %collective-permute-start.15 = (bf16[512,128]{1,0:T(8,128)(2,1)S(1)}, bf16[512,128]{1,0:T(8,128)(2,1)S(1)}, u32[]{:S(2)}, u32[]{:S(2)}) collective-permute-start(bf16[512,128]{1,0:T(8,128)(2,1)S(1)} %choose.2), channel_id=1, source_target_pairs={{0,4},{1,5},{2,6},{3,7},{4,0},{5,1},{6,2},{7,3},{8,12},{9,13},{10,... | collective-permute-start | bytes 393224 | tf_op jit(solution)/shard_map/ppermute | solution.py:258
  30.9 5.3 %collective-permute-start.9 = (bf16[512,128]{1,0:T(8,128)(2,1)S(1)}, bf16[512,128]{1,0:T(8,128)(2,1)S(1)}, u32[]{:S(2)}, u32[]{:S(2)}) collective-permute-start(bf16[512,128]{1,0:T(8,128)(2,1)S(1)} %collective-permute-done.1.first.refs_9_), channel_id=1, source_target_pairs={{0,1},{1,0},{2,3},{3,2},{4,5},{5,4},{6,7},{7,6},{8,9},{9,8},{10,11... | collective-permute-start | bytes 393224 | tf_op jit(solution)/shard_map/ppermute | solution.py:258
  31.7 5.6 %collective-permute-start.10 = (bf16[512,128]{1,0:T(8,128)(2,1)S(1)}, bf16[512,128]{1,0:T(8,128)(2,1)S(1)}, u32[]{:S(2)}, u32[]{:S(2)}) collective-permute-start(bf16[512,128]{1,0:T(8,128)(2,1)S(1)} %choose.3.refs_0_), channel_id=1, source_target_pairs={{0,1},{1,0},{2,3},{3,2},{4,5},{5,4},{6,7},{7,6},{8,9},{9,8},{10,11... | collective-permute-start | bytes 393224 | tf_op jit(solution)/shard_map/ppermute | solution.py:258
  35.7 3.1 %collective-permute-start.19 = (bf16[4,272,128]{2,1,0:T(8,128)(2,1)S(1)}, bf16[4,272,128]{2,1,0:T(8,128)(2,1)S(1)}, u32[]{:S(2)}, u32[]{:S(2)}) collective-permute-start(bf16[4,272,128]{2,1,0:T(8,128)(2,1)S(1)} %join.3.refs_4_), channel_id=1, source_target_pairs={{0,8},{8,0},{16,24},{24,16},{1,9},{9,1},{17,25},{25,17},{2,10},{10... | collective-permute-start | bytes 835592 | tf_op jit(solution)/shard_map/ppermute | solution.py:258
  35.7 3.1 %collective-permute-start.20 = (bf16[4,272,128]{2,1,0:T(8,128)(2,1)S(1)}, bf16[4,272,128]{2,1,0:T(8,128)(2,1)S(1)}, u32[]{:S(2)}, u32[]{:S(2)}) collective-permute-start(bf16[4,272,128]{2,1,0:T(8,128)(2,1)S(1)} %collective-permute-done.14.refs_6_), channel_id=1, source_target_pairs={{0,8},{8,0},{16,24},{24,16},{1,9},{9,1},{17,25},{25,17},{2,10},{10... | collective-permute-start | bytes 835592 | tf_op jit(solution)/shard_map/ppermute | solution.py:258
  37.3 1.6 %collective-permute-start.17 = (bf16[4,272,128]{2,1,0:T(8,128)(2,1)S(1)}, bf16[4,272,128]{2,1,0:T(8,128)(2,1)S(1)}, u32[]{:S(2)}, u32[]{:S(2)}) collective-permute-start(bf16[4,272,128]{2,1,0:T(8,128)(2,1)S(1)} %join.2.refs_0_), channel_id=1, source_target_pairs={{0,8},{8,0},{16,24},{24,16},{1,9},{9,1},{17,25},{25,17},{2,10},{10... | collective-permute-start | bytes 835592 | tf_op jit(solution)/shard_map/ppermute | solution.py:258
  37.3 2.0 %collective-permute-start.18 = (bf16[4,272,128]{2,1,0:T(8,128)(2,1)S(1)}, bf16[4,272,128]{2,1,0:T(8,128)(2,1)S(1)}, u32[]{:S(2)}, u32[]{:S(2)}) collective-permute-start(bf16[4,272,128]{2,1,0:T(8,128)(2,1)S(1)} %collective-permute-done.8.refs_2_), channel_id=1, source_target_pairs={{0,8},{8,0},{16,24},{24,16},{1,9},{9,1},{17,25},{25,17},{2,10},{10... | collective-permute-start | bytes 835592 | tf_op jit(solution)/shard_map/ppermute | solution.py:258
  37.9 5.5 %collective-permute-start.16 = (bf16[512,128]{1,0:T(8,128)(2,1)S(1)}, bf16[512,128]{1,0:T(8,128)(2,1)S(1)}, u32[]{:S(2)}, u32[]{:S(2)}) collective-permute-start(bf16[512,128]{1,0:T(8,128)(2,1)S(1)} %collective-permute-done.15.refs_2_), channel_id=1, source_target_pairs={{0,1},{1,0},{2,3},{3,2},{4,5},{5,4},{6,7},{7,6},{8,9},{9,8},{10,11... | collective-permute-start | bytes 393224 | tf_op jit(solution)/shard_map/ppermute | solution.py:258

commit v6 on v5

--- a/solution.py
+++ b/solution.py
@@ -121,7 +121,20 @@
         copy.wait()
 
 
-def near_kernel(n_pieces, n_amps, capacity, where_ref, *refs):
+def put_in_order(flag, amps, offsets, first, amp):
+    width = amps[0].shape[2]
+    for kind in (0, 1):
+
+        @pl.when(flag == kind)
+        def _(kind=kind):
+            for source, slots in zip(amps, offsets):
+                for i, slot in enumerate(slots[kind]):
+                    at = (slot - first) * width
+                    amp[:, at : at + width] = source[i]
+
+
+def near_kernel(n_pieces, offsets, capacity, where_ref, *refs):
+    n_amps = len(offsets)
     pieces = refs[:n_pieces]
     amps = refs[n_pieces : n_pieces + n_amps]
     own, residual, total, far = refs[n_pieces + n_amps : n_pieces + n_amps + 4]
@@ -141,9 +154,7 @@
         ).astype(jnp.int32)
     table_copy = pltpu.make_async_copy(places, table, table_sem)
     table_copy.start()
-    for i, source in enumerate(amps):
-        at = pl.multiple_of(where_ref[n_pieces + 1 + i] * width, width)
-        amp[:, pl.ds(at, width)] = source[...]
+    put_in_order(where_ref[n_pieces + 1], amps, offsets, 0, amp)
     table_copy.wait()
     col = where_ref[n_pieces]
     for p, piece in enumerate(pieces):
@@ -174,17 +185,17 @@
     multiply(amp, near, res, total, None, 2 * width)
 
 
-def near_half(where, pieces, amps, own, residual, capacity):
+def near_half(where, pieces, amps, offsets, own, residual, capacity):
     columns, _, width = pieces[0].shape
     n_pieces, n_amps = len(pieces), len(amps)
     rows, n_cols = residual.shape
-    depth = (1 + n_amps) * width
+    depth = (1 + sum(len(s[0]) for s in offsets)) * width
     hbm = pl.BlockSpec(memory_space=pltpu.HBM)
     vmem = pl.BlockSpec(memory_space=pltpu.VMEM)
     held = 2 * rows * depth + 4 * depth * n_cols + 8 * rows * n_cols
     held += sum(x.size * x.dtype.itemsize for x in pieces) // 2
     return pl.pallas_call(
-        functools.partial(near_kernel, n_pieces, n_amps, capacity),
+        functools.partial(near_kernel, n_pieces, offsets, capacity),
         out_shape=[
             jax.ShapeDtypeStruct(residual.shape, residual.dtype),
             jax.ShapeDtypeStruct((depth, n_cols), pieces[0].dtype),
@@ -219,22 +230,20 @@
     )
 
 
-def far_kernel(half, slots_ref, *refs):
+def far_kernel(offsets, half, flag_ref, *refs):
     amps, (start, far, out, amp, total, sems) = refs[:-6], refs[-6:]
-    width = amps[0].shape[1]
-    for i, source in enumerate(amps):
-        at = pl.multiple_of((slots_ref[i] - half) * width, width)
-        amp[:, pl.ds(at, width)] = source[...]
+    width = amps[0].shape[2]
+    put_in_order(flag_ref[0], amps, offsets, half, amp)
     multiply(amp, far, start, (total, out), sems, 2 * width)
 
 
-def far_half(slots, amps, total, far):
+def far_half(flag, amps, offsets, total, far):
     rows, n_cols = total.shape
-    depth, width = far.shape[0], amps[0].shape[1]
+    depth, width = far.shape[0], amps[0].shape[2]
     vmem = pl.BlockSpec(memory_space=pltpu.VMEM)
     held = 4 * rows * depth + 2 * depth * n_cols + 8 * rows * n_cols
     return pl.pallas_call(
-        functools.partial(far_kernel, depth // width),
+        functools.partial(far_kernel, offsets, depth // width),
         out_shape=jax.ShapeDtypeStruct(total.shape, total.dtype),
         in_specs=[pl.BlockSpec(memory_space=pltpu.SMEM)] + [vmem] * (len(amps) + 2),
         out_specs=pl.BlockSpec(memory_space=pltpu.HBM),
@@ -250,7 +259,7 @@
             transcendentals=0,
         ),
         name="far_half",
-    )(slots, *amps, total, far)
+    )(flag[None], *amps, total, far)
 
 
 def exchange(x, axis, flip):
@@ -258,26 +267,53 @@
     return lax.ppermute(x, axis, [(i, i ^ flip) for i in range(size)])
 
 
-def choose_kernel(flag_ref, first, second, out):
-    @pl.when(flag_ref[0] == 1)
-    def _():
-        out[...] = first[...]
-
-    @pl.when(flag_ref[0] == 0)
-    def _():
-        out[...] = second[...]
-
-
-def choose(flag, first, second):
+def choose_kernel(flag_ref, pair, out):
+    out[0] = pair[flag_ref[0]]
+
+
+def choose(flag, pair):
     vmem = pl.BlockSpec(memory_space=pltpu.VMEM)
     return pl.pallas_call(
         choose_kernel,
-        out_shape=jax.ShapeDtypeStruct(first.shape, first.dtype),
-        in_specs=[pl.BlockSpec(memory_space=pltpu.SMEM), vmem, vmem],
+        out_shape=jax.ShapeDtypeStruct((1, *pair.shape[1:]), pair.dtype),
+        in_specs=[pl.BlockSpec(memory_space=pltpu.SMEM), vmem],
         out_specs=vmem,
         compiler_params=pltpu.CompilerParams(vmem_limit_bytes=4 * MIB),
         name="choose",
-    )(flag[None], first, second)
+    )(flag[None], pair)
+
+
+def leave_kernel(flag_ref, beside, own, out, sem):
+    @pl.when(flag_ref[0] == 1)
+    def _():
+        out[...] = beside[...]
+
+    @pl.when(flag_ref[0] == 0)
+    def _():
+        copy = pltpu.make_async_copy(own, out, sem)
+        copy.start()
+        copy.wait()
+
+
+def leave(flag, beside, own):
+    vmem = pl.BlockSpec(memory_space=pltpu.VMEM)
+    return pl.pallas_call(
+        leave_kernel,
+        out_shape=jax.ShapeDtypeStruct(beside.shape, beside.dtype),
+        in_specs=[
+            pl.BlockSpec(memory_space=pltpu.SMEM),
+            vmem,
+            pl.BlockSpec(memory_space=pltpu.HBM),
+        ],
+        out_specs=vmem,
+        scratch_shapes=[pltpu.SemaphoreType.DMA],
+        compiler_params=pltpu.CompilerParams(vmem_limit_bytes=4 * MIB),
+        name="leave",
+    )(flag[None], beside, pltpu.with_memory_space_constraint(own, pltpu.HBM))
+
+
+def pick(flag, first, second):
+    return choose(1 - flag, join([first, second]))
 
 
 def tie(late, *early):
@@ -293,62 +329,64 @@
     lanes = range(1, inner)
     outgoing = list(pack(col, packed_tiles, tile_ids, n_col, capacity))
 
-    amps = {0: amplitudes}
-    for s in [*lanes, inner]:
-        amps[s] = exchange(amplitudes, "col", s)
     mids = [(i // inner) % 4 in (1, 2) for i in range(n_col)]
-    swap = [(i, i ^ (3 * inner) if m else i) for i, m in enumerate(mids)]
-    across = lax.ppermute(amplitudes, "col", swap)
-    outgoing[half:], amps, across = tie(outgoing[half:], amps, across)
+    swap = [(i, i ^ (3 * inner) if m else i ^ 1) for i, m in enumerate(mids)]
+    own = amplitudes[None]
+    across = lax.ppermute(own, "col", swap)
+    beside = exchange(own, "col", inner)
+    outgoing[half:], across, beside = tie(outgoing[half:], across, beside)
 
     chunks = [outgoing[0][None]]
     chunks += [exchange(outgoing[s][None], "col", s) for s in range(1, n_col)]
     outer = col // inner % 4
     is_mid = ((outer == 1) | (outer == 2)).astype(jnp.int32)
     onward = exchange(across, "col", inner)
-    leaving = choose(is_mid, amps[inner], amplitudes)
+    leaving = leave(is_mid, beside, own)
     chunks[half], onward, leaving = tie(chunks[half], onward, leaving)
-    passed_on = choose(is_mid, across, onward)
+    own_over = [exchange(own, "col", lane) for lane in lanes]
+    chunks[half + 1], own_over = tie(chunks[half + 1], own_over)
+    beside_over = [exchange(beside, "col", lane) for lane in lanes]
+    passed_on = pick(is_mid, across, onward)
     straight = exchange(leaving, "col", 2 * inner)
-    for lane in lanes:
-        amps[inner ^ lane] = exchange(amps[inner], "col", lane)
     passed_over = [exchange(passed_on, "col", lane) for lane in lanes]
 
-    early = [inner ^ lane for lane in lanes]
     pieces, rows = [], []
     for group in (join(chunks[half:]), join(chunks[:half])):
         passed = [exchange(group, "row", flip) for flip in range(CORES, n_row, CORES)]
         if pieces:
             passed, straight = tie(passed, straight)
         else:
-            passed, got, passed_over = tie(passed, [amps[s] for s in early], passed_over)
-            amps.update(zip(early, got))
-        own, passed = tie(group, passed)
-        for flip, mine in zip(range(0, n_row, CORES), [own, *passed]):
+            passed, beside_over, passed_over = tie(passed, beside_over, passed_over)
+        mine, passed = tie(group, passed)
+        for flip, mine in zip(range(0, n_row, CORES), [mine, *passed]):
             pieces += [mine, exchange(mine, "row", 1)]
             rows += [row ^ flip, row ^ flip ^ 1]
     straight_over = [exchange(straight, "col", lane) for lane in lanes]
 
-    here, there = (2 + is_mid) * inner, (3 - is_mid) * inner
-    far = [(here, passed_on), *zip([here ^ x for x in lanes], passed_over)]
-    far += [(there, straight), *zip([there ^ x for x in lanes], straight_over)]
-    near = [(s, amps[s]) for s in sorted(amps) if s]
+    def over(shards, ends, middles):
+        return [
+            (x, [[s ^ lane for s in kind] for kind in (ends, middles)])
+            for lane, x in enumerate(shards)
+            if x is not None
+        ]
+
+    near = over([None, *own_over], [0], [0]) + over([beside, *beside_over], [inner], [inner])
+    far = over([passed_on, *passed_over], [2 * inner], [3 * inner])
+    far += over([straight, *straight_over], [3 * inner], [2 * inner])
     flip = 4 * inner
     while flip < n_col:
-        near, far = near + far, [
-            (s ^ flip, exchange(x, "col", flip)) for s, x in [(0, amplitudes), *near, *far]
+        held = [(own, [[0], [0]]), *near, *far]
+        near = near + far
+        far = [
+            (exchange(x, "col", flip), [[s ^ flip for s in kind] for kind in slots])
+            for x, slots in held
         ]
         flip *= 2
-    where = jnp.stack(rows + [col]).astype(jnp.int32)
-    near_slots, near_amps = zip(*near)
-    far_slots, far_amps = zip(*far)
-    near_slots = jnp.stack([jnp.asarray(s, jnp.int32) for s in near_slots])
-    far_slots = jnp.stack([jnp.asarray(s, jnp.int32) for s in far_slots])
-    where = jnp.concatenate([where, near_slots])
+    where = jnp.stack([*rows, col, is_mid]).astype(jnp.int32)
     total, far_block = near_half(
-        where, pieces, near_amps, amplitudes, residual_in, capacity
+        where, pieces, *zip(*near), amplitudes, residual_in, capacity
     )
-    return far_half(far_slots, far_amps, total, far_block)
+    return far_half(is_mid, *zip(*far), total, far_block)
 
 
 def solution(mesh):

time: 46 us -> 45.8 us (level)
  waiting for transfers between devices: 6.93 us -> 10.4 us
  starting transfers between devices: 30.3 us -> 27.2 us
  local copies, waits for them, and re-layouts: 0.99 us -> 0.08 us
    ppermute x20, starting transfers between devices: 28.7 us -> 24.3 us  [exchange(): return lax.ppermute(x, axis, [(i, i ^ flip) for i in range(size)])]
    ppermute x20, waiting for transfers between devices: 6.93 us -> 10.4 us  [exchange(): return lax.ppermute(x, axis, [(i, i ^ flip) for i in range(size)])]
    ppermute x1, starting transfers between devices: 1.55 us -> 2.94 us  [body(): across = lax.ppermute(own, 'col', swap)]
    unnamed x2 -> x0, local copies, waits for them, and re-layouts: 0.9 us -> none
  transfers between devices with their start and end apart: 21 -> 21, of which waited for: 5 -> 6; matrix products, arithmetic and copies ran while one was open for 0% -> 0% of each run, Pallas kernels for 11% -> 13%
where the time goes in v6:
time: 45.8 us; the launch traced here: 45.6 us
  starting transfers between devices  27.2 us (59%)
  waiting for transfers between devices  10.4 us (23%)
  Pallas kernels  7.83 us (17%)
    ppermute x20, starting transfers between devices, exchange(): return lax.ppermute(x, axis, [(i, i ^ flip) for i in range(size)])  24.3 us
    ppermute x20, waiting for transfers between devices, exchange(): return lax.ppermute(x, axis, [(i, i ^ flip) for i in range(size)])  10.4 us
    pallas_call x1, Pallas kernels, near_half(): pl.pallas_call(functools.partial(near_kernel, n_pieces, offsets, capacity...  3.66 us
    ppermute x1, starting transfers between devices, body(): across = lax.ppermute(own, 'col', swap)  2.94 us
    pallas_call x1, Pallas kernels, far_half(): pl.pallas_call(functools.partial(far_kernel, offsets, depth // width), ou...  1.93 us
    pallas_call x1, Pallas kernels, pack(): pl.pallas_call(functools.partial(pack_kernel, columns, capacity), out_sha...  1.25 us
  transfers between devices with their start and end apart: 21, of which 6 were waited for; matrix products, arithmetic and copies ran while one was open for 0% of the time, Pallas kernels for 13%

profile of v6, /device:TPU:0, one launch (start us, length us, event | category | flops | bytes accessed | tf_op | source)
XLA Modules:
  0.0 45.6 jit_solution(1041543921406351696)
XLA Ops:
  0.0 2.9 %collective-permute-start = (bf16[1,512,128]{2,1,0:T(8,128)(2,1)}, bf16[1,512,128]{2,1,0:T(8,128)(2,1)S(1)}, u32[]{:S(2)}, u32[]{:S(2)}) collective-permute-start(bf16[1,512,128]{2,1,0:T(8,128)(2,1)} %bitcast.24), channel_id=1, source_target_pairs={{0,1},{1,0},{2,4},{3,5},{4,2},{5,3},{6,7},{7,6},{8,9},{9,8},{10,12... | collective-permute-start | bytes 393224 | tf_op jit(solution)/shard_map/ppermute | solution.py:335
  2.9 1.7 %collective-permute-start.1 = (bf16[1,512,128]{2,1,0:T(8,128)(2,1)}, bf16[1,512,128]{2,1,0:T(8,128)(2,1)S(1)}, u32[]{:S(2)}, u32[]{:S(2)}) collective-permute-start(bf16[1,512,128]{2,1,0:T(8,128)(2,1)} %bitcast.25), channel_id=1, source_target_pairs={{0,2},{1,3},{2,0},{3,1},{4,6},{5,7},{6,4},{7,5},{8,10},{9,11},{10,... | collective-permute-start | bytes 393224 | tf_op jit(solution)/shard_map/ppermute | solution.py:267
  4.6 1.5 %collective-permute-start.5 = (bf16[1,512,128]{2,1,0:T(8,128)(2,1)}, bf16[1,512,128]{2,1,0:T(8,128)(2,1)S(1)}, u32[]{:S(2)}, u32[]{:S(2)}) collective-permute-start(bf16[1,512,128]{2,1,0:T(8,128)(2,1)} %bitcast.26), channel_id=1, source_target_pairs={{0,1},{1,0},{2,3},{3,2},{4,5},{5,4},{6,7},{7,6},{8,9},{9,8},{10,11... | collective-permute-start | bytes 393224 | tf_op jit(solution)/shard_map/ppermute | solution.py:267
  6.1 1.3 %pack.1 = (bf16[272,128]{1,0:T(8,128)(2,1)S(1)}, bf16[272,128]{1,0:T(8,128)(2,1)S(1)}, bf16[272,128]{1,0:T(8,128)(2,1)S(1)}, bf16[272,128]{1,0:T(8,128)(2,1)S(1)...) custom-call(s32[1]{0:T(128)} %bitcast.2.me_ref, ...), custom_call_target="tpu_custom_call" | custom-call | tf_op jit(solution)/shard_map/pack/pallas_call | solution.py:63
  7.4 0.6 %collective-permute-start.11 = (bf16[1,272,128]{2,1,0:T(8,128)(2,1)S(1)}, bf16[1,272,128]{2,1,0:T(8,128)(2,1)S(1)}, u32[]{:S(2)}, u32[]{:S(2)}) collective-permute-start(bf16[1,272,128]{2,1,0:T(8,128)(2,1)S(1)} %bitcast.23), channel_id=1, source_target_pairs={{0,1},{1,0},{2,3},{3,2},{4,5},{5,4},{6,7},{7,6},{8,9},{9,8},{10,11... | collective-permute-start | bytes 208904 | tf_op jit(solution)/shard_map/ppermute | solution.py:267
  8.3 2.6 %collective-permute-start.13 = (bf16[1,272,128]{2,1,0:T(8,128)(2,1)S(1)}, bf16[1,272,128]{2,1,0:T(8,128)(2,1)S(1)}, u32[]{:S(2)}, u32[]{:S(2)}) collective-permute-start(bf16[1,272,128]{2,1,0:T(8,128)(2,1)S(1)} %bitcast.21), channel_id=1, source_target_pairs={{0,3},{1,2},{2,1},{3,0},{4,7},{5,6},{6,5},{7,4},{8,11},{9,10},{10,... | collective-permute-start | bytes 208904 | tf_op jit(solution)/shard_map/ppermute | solution.py:267
  10.9 1.5 %collective-permute-done.11.refs_1_ = bf16[1,272,128]{2,1,0:T(8,128)(2,1)S(1)} collective-permute-done((bf16[1,272,128]{2,1,0:T(8,128)(2,1)S(1)}, bf16[1,272,128]{2,1,0:T(8,128)(2,1)S(1)}, u32[]{:S(2)}, u32[]{:S(2)}) %collective-permute-start.11) | collective-permute-done | bytes 69664 | tf_op jit(solution)/shard_map/ppermute | solution.py:267
  12.4 2.5 %collective-permute-start.4 = (bf16[1,272,128]{2,1,0:T(8,128)(2,1)S(1)}, bf16[1,272,128]{2,1,0:T(8,128)(2,1)S(1)}, u32[]{:S(2)}, u32[]{:S(2)}) collective-permute-start(bf16[1,272,128]{2,1,0:T(8,128)(2,1)S(1)} %bitcast.20), channel_id=1, source_target_pairs={{0,5},{1,4},{2,7},{3,6},{4,1},{5,0},{6,3},{7,2},{8,13},{9,12},{10,... | collective-permute-start | bytes 208904 | tf_op jit(solution)/shard_map/ppermute | solution.py:267
  14.9 0.9 %collective-permute-start.2 = (bf16[1,272,128]{2,1,0:T(8,128)(2,1)S(1)}, bf16[1,272,128]{2,1,0:T(8,128)(2,1)S(1)}, u32[]{:S(2)}, u32[]{:S(2)}) collective-permute-start(bf16[1,272,128]{2,1,0:T(8,128)(2,1)S(1)} %bitcast.19), channel_id=1, source_target_pairs={{0,4},{1,5},{2,6},{3,7},{4,0},{5,1},{6,2},{7,3},{8,12},{9,13},{10,... | collective-permute-start | bytes 208904 | tf_op jit(solution)/shard_map/ppermute | solution.py:267
  15.8 3.6 %collective-permute-start.6 = (bf16[1,272,128]{2,1,0:T(8,128)(2,1)S(1)}, bf16[1,272,128]{2,1,0:T(8,128)(2,1)S(1)}, u32[]{:S(2)}, u32[]{:S(2)}) collective-permute-start(bf16[1,272,128]{2,1,0:T(8,128)(2,1)S(1)} %bitcast.18), channel_id=1, source_target_pairs={{0,6},{1,7},{2,4},{3,5},{4,2},{5,3},{6,0},{7,1},{8,14},{9,15},{10,... | collective-permute-start | bytes 208904 | tf_op jit(solution)/shard_map/ppermute | solution.py:267
  19.4 0.7 %collective-permute-start.7 = (bf16[1,272,128]{2,1,0:T(8,128)(2,1)S(1)}, bf16[1,272,128]{2,1,0:T(8,128)(2,1)S(1)}, u32[]{:S(2)}, u32[]{:S(2)}) collective-permute-start(bf16[1,272,128]{2,1,0:T(8,128)(2,1)S(1)} %bitcast.17), channel_id=1, source_target_pairs={{0,7},{1,6},{2,5},{3,4},{4,3},{5,2},{6,1},{7,0},{8,15},{9,14},{10,... | collective-permute-start | bytes 208904 | tf_op jit(solution)/shard_map/ppermute | solution.py:267
  20.1 3.6 %collective-permute-done.4.refs_1_ = bf16[1,272,128]{2,1,0:T(8,128)(2,1)S(1)} collective-permute-done((bf16[1,272,128]{2,1,0:T(8,128)(2,1)S(1)}, bf16[1,272,128]{2,1,0:T(8,128)(2,1)S(1)}, u32[]{:S(2)}, u32[]{:S(2)}) %collective-permute-start.4) | collective-permute-done | bytes 69664 | tf_op jit(solution)/shard_map/ppermute | solution.py:267
  23.8 1.5 %collective-permute-start.14 = (bf16[4,272,128]{2,1,0:T(8,128)(2,1)S(1)}, bf16[4,272,128]{2,1,0:T(8,128)(2,1)S(1)}, u32[]{:S(2)}, u32[]{:S(2)}) collective-permute-start(bf16[4,272,128]{2,1,0:T(8,128)(2,1)S(1)} %join.5.refs_4_), channel_id=1, source_target_pairs={{0,16},{8,24},{16,0},{24,8},{1,17},{9,25},{17,1},{25,9},{2,18},{10... | collective-permute-start | bytes 835592 | tf_op jit(solution)/shard_map/ppermute | solution.py:267
  25.3 0.9 %leave.1 = bf16[1,512,128]{2,1,0:T(8,128)(2,1)S(1)} custom-call(s32[1]{0:T(128)} %bitcast.flag_ref, bf16[1,512,128]{2,1,0:T(8,128)(2,1)S(1)} %collective-permute-done.1.beside.refs_9_, bf16[1,512,128]{2,1,0:T(8,128)(2,1)} %bitcast.27), custom_call_target="tpu_custom_call" | custom-call | tf_op jit(solution)/shard_map/leave/pallas_call | solution.py:300
  26.5 1.6 %collective-permute-start.8 = (bf16[4,272,128]{2,1,0:T(8,128)(2,1)S(1)}, bf16[4,272,128]{2,1,0:T(8,128)(2,1)S(1)}, u32[]{:S(2)}, u32[]{:S(2)}) collective-permute-start(bf16[4,272,128]{2,1,0:T(8,128)(2,1)S(1)} %join.4.refs_0_), channel_id=1, source_target_pairs={{0,16},{8,24},{16,0},{24,8},{1,17},{9,25},{17,1},{25,9},{2,18},{10... | collective-permute-start | bytes 835592 | tf_op jit(solution)/shard_map/ppermute | solution.py:267
  28.1 2.1 %collective-permute-start.15 = (bf16[1,512,128]{2,1,0:T(8,128)(2,1)S(1)}, bf16[1,512,128]{2,1,0:T(8,128)(2,1)S(1)}, u32[]{:S(2)}, u32[]{:S(2)}) collective-permute-start(bf16[1,512,128]{2,1,0:T(8,128)(2,1)S(1)} %leave.1), channel_id=1, source_target_pairs={{0,4},{1,5},{2,6},{3,7},{4,0},{5,1},{6,2},{7,3},{8,12},{9,13},{10,... | collective-permute-start | bytes 393224 | tf_op jit(solution)/shard_map/ppermute | solution.py:267
  30.3 2.0 %collective-permute-start.9 = (bf16[1,512,128]{2,1,0:T(8,128)(2,1)S(1)}, bf16[1,512,128]{2,1,0:T(8,128)(2,1)S(1)}, u32[]{:S(2)}, u32[]{:S(2)}) collective-permute-start(bf16[1,512,128]{2,1,0:T(8,128)(2,1)S(1)} %collective-permute-done.1.beside.refs_9_), channel_id=1, source_target_pairs={{0,1},{1,0},{2,3},{3,2},{4,5},{5,4},{6,7},{7,6},{8,9},{9,8},{10,11... | collective-permute-start | bytes 393224 | tf_op jit(solution)/shard_map/ppermute | solution.py:267
  32.4 3.0 %collective-permute-done.15.refs_2_ = bf16[1,512,128]{2,1,0:T(8,128)(2,1)S(1)} collective-permute-done((bf16[1,512,128]{2,1,0:T(8,128)(2,1)S(1)}, bf16[1,512,128]{2,1,0:T(8,128)(2,1)S(1)}, u32[]{:S(2)}, u32[]{:S(2)}) %collective-permute-start.15) | collective-permute-done | bytes 131104 | tf_op jit(solution)/shard_map/ppermute | solution.py:267
  35.4 0.5 %collective-permute-start.20 = (bf16[4,272,128]{2,1,0:T(8,128)(2,1)S(1)}, bf16[4,272,128]{2,1,0:T(8,128)(2,1)S(1)}, u32[]{:S(2)}, u32[]{:S(2)}) collective-permute-start(bf16[4,272,128]{2,1,0:T(8,128)(2,1)S(1)} %collective-permute-done.14.refs_6_), channel_id=1, source_target_pairs={{0,8},{8,0},{16,24},{24,16},{1,9},{9,1},{17,25},{25,17},{2,10},{10... | collective-permute-start | bytes 835592 | tf_op jit(solution)/shard_map/ppermute | solution.py:267
  36.4 1.4 %collective-permute-done.10.refs_1_ = bf16[1,512,128]{2,1,0:T(8,128)(2,1)S(1)} collective-permute-done((bf16[1,512,128]{2,1,0:T(8,128)(2,1)S(1)}, bf16[1,512,128]{2,1,0:T(8,128)(2,1)S(1)}, u32[]{:S(2)}, u32[]{:S(2)}) %collective-permute-start.10) | collective-permute-done | bytes 131104 | tf_op jit(solution)/shard_map/ppermute | solution.py:267
  37.8 0.5 %collective-permute-start.18 = (bf16[4,272,128]{2,1,0:T(8,128)(2,1)S(1)}, bf16[4,272,128]{2,1,0:T(8,128)(2,1)S(1)}, u32[]{:S(2)}, u32[]{:S(2)}) collective-permute-start(bf16[4,272,128]{2,1,0:T(8,128)(2,1)S(1)} %collective-permute-done.8.refs_2_), channel_id=1, source_target_pairs={{0,8},{8,0},{16,24},{24,16},{1,9},{9,1},{17,25},{25,17},{2,10},{10... | collective-permute-start | bytes 835592 | tf_op jit(solution)/shard_map/ppermute | solution.py:267
  38.3 1.6 %collective-permute-start.16 = (bf16[1,512,128]{2,1,0:T(8,128)(2,1)S(1)}, bf16[1,512,128]{2,1,0:T(8,128)(2,1)S(1)}, u32[]{:S(2)}, u32[]{:S(2)}) collective-permute-start(bf16[1,512,128]{2,1,0:T(8,128)(2,1)S(1)} %collective-permute-done.15.refs_2_), channel_id=1, source_target_pairs={{0,1},{1,0},{2,3},{3,2},{4,5},{5,4},{6,7},{7,6},{8,9},{9,8},{10,11... | collective-permute-start | bytes 393224 | tf_op jit(solution)/shard_map/ppermute | solution.py:267
  40.0 3.7 %near_half.1 = (f32[512,1024]{1,0:T(8,128)S(1)}, bf16[512,1024]{1,0:T(8,128)(2,1)S(1)}) custom-call(s32[10]{0:T(128)S(1)} %stack.25.where_ref, bf16[4,272,128]{2,1,0:T(8,128)(2,1)S(1)} %join.4.refs_0_, bf16[4,272,128]{2,1,0:T(8,128)(2,1)S(1)} %collective-permute-done.17.refs_1_, bf16[4,272,128]{2,1,0:T(8,128)(2,1)S(1)} %collective-permute-done.8.refs_2_, ...), custom_call_target="tpu_custom_call" | custom-call | flops 536870912 | bytes 8388608 | tf_op jit(solution)/shard_map/near_half/pallas_call | solution.py:197
  43.7 1.9 %far_half.1 = f32[512,1024]{1,0:T(8,128)} custom-call(s32[1]{0:T(128)} %bitcast.flag_ref, bf16[1,512,128]{2,1,0:T(8,128)(2,1)S(1)} %choose.1.refs_0_, bf16[1,512,128]{2,1,0:T(8,128)(2,1)S(1)} %collective-permute-done.10.refs_1_, bf16[1,512,128]{2,1,0:T(8,128)(2,1)S(1)} %collective-permute-done.15.refs_2_, ...), custom_call_target="tpu_custom_call" | custom-call | flops 536870912 | bytes 8388608 | tf_op jit(solution)/shard_map/far_half/pallas_call | solution.py:245
  (27 shorter events, 1.4 us)
Async XLA Ops:
  0.0 8.3 %collective-permute-start = (bf16[1,512,128]{2,1,0:T(8,128)(2,1)}, bf16[1,512,128]{2,1,0:T(8,128)(2,1)S(1)}, u32[]{:S(2)}, u32[]{:S(2)}) collective-permute-start(bf16[1,512,128]{2,1,0:T(8,128)(2,1)} %bitcast.24), channel_id=1, source_target_pairs={{0,1},{1,0},{2,4},{3,5},{4,2},{5,3},{6,7},{7,6},{8,9},{9,8},{10,12... | collective-permute-start | bytes 393224 | tf_op jit(solution)/shard_map/ppermute | solution.py:335
  2.9 8.0 %collective-permute-start.1 = (bf16[1,512,128]{2,1,0:T(8,128)(2,1)}, bf16[1,512,128]{2,1,0:T(8,128)(2,1)S(1)}, u32[]{:S(2)}, u32[]{:S(2)}) collective-permute-start(bf16[1,512,128]{2,1,0:T(8,128)(2,1)} %bitcast.25), channel_id=1, source_target_pairs={{0,2},{1,3},{2,0},{3,1},{4,6},{5,7},{6,4},{7,5},{8,10},{9,11},{10,... | collective-permute-start | bytes 393224 | tf_op jit(solution)/shard_map/ppermute | solution.py:267
  4.6 14.8 %collective-permute-start.5 = (bf16[1,512,128]{2,1,0:T(8,128)(2,1)}, bf16[1,512,128]{2,1,0:T(8,128)(2,1)S(1)}, u32[]{:S(2)}, u32[]{:S(2)}) collective-permute-start(bf16[1,512,128]{2,1,0:T(8,128)(2,1)} %bitcast.26), channel_id=1, source_target_pairs={{0,1},{1,0},{2,3},{3,2},{4,5},{5,4},{6,7},{7,6},{8,9},{9,8},{10,11... | collective-permute-start | bytes 393224 | tf_op jit(solution)/shard_map/ppermute | solution.py:267
  7.4 5.1 %collective-permute-start.11 = (bf16[1,272,128]{2,1,0:T(8,128)(2,1)S(1)}, bf16[1,272,128]{2,1,0:T(8,128)(2,1)S(1)}, u32[]{:S(2)}, u32[]{:S(2)}) collective-permute-start(bf16[1,272,128]{2,1,0:T(8,128)(2,1)S(1)} %bitcast.23), channel_id=1, source_target_pairs={{0,1},{1,0},{2,3},{3,2},{4,5},{5,4},{6,7},{7,6},{8,9},{9,8},{10,11... | collective-permute-start | bytes 208904 | tf_op jit(solution)/shard_map/ppermute | solution.py:267
  8.0 7.0 %collective-permute-start.12 = (bf16[1,272,128]{2,1,0:T(8,128)(2,1)S(1)}, bf16[1,272,128]{2,1,0:T(8,128)(2,1)S(1)}, u32[]{:S(2)}, u32[]{:S(2)}) collective-permute-start(bf16[1,272,128]{2,1,0:T(8,128)(2,1)S(1)} %bitcast.22), channel_id=1, source_target_pairs={{0,2},{1,3},{2,0},{3,1},{4,6},{5,7},{6,4},{7,5},{8,10},{9,11},{10,... | collective-permute-start | bytes 208904 | tf_op jit(solution)/shard_map/ppermute | solution.py:267
  8.3 7.5 %collective-permute-start.13 = (bf16[1,272,128]{2,1,0:T(8,128)(2,1)S(1)}, bf16[1,272,128]{2,1,0:T(8,128)(2,1)S(1)}, u32[]{:S(2)}, u32[]{:S(2)}) collective-permute-start(bf16[1,272,128]{2,1,0:T(8,128)(2,1)S(1)} %bitcast.21), channel_id=1, source_target_pairs={{0,3},{1,2},{2,1},{3,0},{4,7},{5,6},{6,5},{7,4},{8,11},{9,10},{10,... | collective-permute-start | bytes 208904 | tf_op jit(solution)/shard_map/ppermute | solution.py:267
  10.9 15.3 %collective-permute-start.3 = (bf16[1,512,128]{2,1,0:T(8,128)(2,1)S(1)}, bf16[1,512,128]{2,1,0:T(8,128)(2,1)S(1)}, u32[]{:S(2)}, u32[]{:S(2)}) collective-permute-start(bf16[1,512,128]{2,1,0:T(8,128)(2,1)S(1)} %collective-permute-done.refs_0_), channel_id=1, source_target_pairs={{0,2},{1,3},{2,0},{3,1},{4,6},{5,7},{6,4},{7,5},{8,10},{9,11},{10,... | collective-permute-start | bytes 393224 | tf_op jit(solution)/shard_map/ppermute | solution.py:267
  12.4 11.3 %collective-permute-start.4 = (bf16[1,272,128]{2,1,0:T(8,128)(2,1)S(1)}, bf16[1,272,128]{2,1,0:T(8,128)(2,1)S(1)}, u32[]{:S(2)}, u32[]{:S(2)}) collective-permute-start(bf16[1,272,128]{2,1,0:T(8,128)(2,1)S(1)} %bitcast.20), channel_id=1, source_target_pairs={{0,5},{1,4},{2,7},{3,6},{4,1},{5,0},{6,3},{7,2},{8,13},{9,12},{10,... | collective-permute-start | bytes 208904 | tf_op jit(solution)/shard_map/ppermute | solution.py:267
  14.9 11.3 %collective-permute-start.2 = (bf16[1,272,128]{2,1,0:T(8,128)(2,1)S(1)}, bf16[1,272,128]{2,1,0:T(8,128)(2,1)S(1)}, u32[]{:S(2)}, u32[]{:S(2)}) collective-permute-start(bf16[1,272,128]{2,1,0:T(8,128)(2,1)S(1)} %bitcast.19), channel_id=1, source_target_pairs={{0,4},{1,5},{2,6},{3,7},{4,0},{5,1},{6,2},{7,3},{8,12},{9,13},{10,... | collective-permute-start | bytes 208904 | tf_op jit(solution)/shard_map/ppermute | solution.py:267
  15.8 10.4 %collective-permute-start.6 = (bf16[1,272,128]{2,1,0:T(8,128)(2,1)S(1)}, bf16[1,272,128]{2,1,0:T(8,128)(2,1)S(1)}, u32[]{:S(2)}, u32[]{:S(2)}) collective-permute-start(bf16[1,272,128]{2,1,0:T(8,128)(2,1)S(1)} %bitcast.18), channel_id=1, source_target_pairs={{0,6},{1,7},{2,4},{3,5},{4,2},{5,3},{6,0},{7,1},{8,14},{9,15},{10,... | collective-permute-start | bytes 208904 | tf_op jit(solution)/shard_map/ppermute | solution.py:267
  19.4 7.1 %collective-permute-start.7 = (bf16[1,272,128]{2,1,0:T(8,128)(2,1)S(1)}, bf16[1,272,128]{2,1,0:T(8,128)(2,1)S(1)}, u32[]{:S(2)}, u32[]{:S(2)}) collective-permute-start(bf16[1,272,128]{2,1,0:T(8,128)(2,1)S(1)} %bitcast.17), channel_id=1, source_target_pairs={{0,7},{1,6},{2,5},{3,4},{4,3},{5,2},{6,1},{7,0},{8,15},{9,14},{10,... | collective-permute-start | bytes 208904 | tf_op jit(solution)/shard_map/ppermute | solution.py:267
  23.8 8.7 %collective-permute-start.14 = (bf16[4,272,128]{2,1,0:T(8,128)(2,1)S(1)}, bf16[4,272,128]{2,1,0:T(8,128)(2,1)S(1)}, u32[]{:S(2)}, u32[]{:S(2)}) collective-permute-start(bf16[4,272,128]{2,1,0:T(8,128)(2,1)S(1)} %join.5.refs_4_), channel_id=1, source_target_pairs={{0,16},{8,24},{16,0},{24,8},{1,17},{9,25},{17,1},{25,9},{2,18},{10... | collective-permute-start | bytes 835592 | tf_op jit(solution)/shard_map/ppermute | solution.py:267
  26.5 11.2 %collective-permute-start.8 = (bf16[4,272,128]{2,1,0:T(8,128)(2,1)S(1)}, bf16[4,272,128]{2,1,0:T(8,128)(2,1)S(1)}, u32[]{:S(2)}, u32[]{:S(2)}) collective-permute-start(bf16[4,272,128]{2,1,0:T(8,128)(2,1)S(1)} %join.4.refs_0_), channel_id=1, source_target_pairs={{0,16},{8,24},{16,0},{24,8},{1,17},{9,25},{17,1},{25,9},{2,18},{10... | collective-permute-start | bytes 835592 | tf_op jit(solution)/shard_map/ppermute | solution.py:267
  28.1 7.3 %collective-permute-start.15 = (bf16[1,512,128]{2,1,0:T(8,128)(2,1)S(1)}, bf16[1,512,128]{2,1,0:T(8,128)(2,1)S(1)}, u32[]{:S(2)}, u32[]{:S(2)}) collective-permute-start(bf16[1,512,128]{2,1,0:T(8,128)(2,1)S(1)} %leave.1), channel_id=1, source_target_pairs={{0,4},{1,5},{2,6},{3,7},{4,0},{5,1},{6,2},{7,3},{8,12},{9,13},{10,... | collective-permute-start | bytes 393224 | tf_op jit(solution)/shard_map/ppermute | solution.py:267
  30.3 6.1 %collective-permute-start.9 = (bf16[1,512,128]{2,1,0:T(8,128)(2,1)S(1)}, bf16[1,512,128]{2,1,0:T(8,128)(2,1)S(1)}, u32[]{:S(2)}, u32[]{:S(2)}) collective-permute-start(bf16[1,512,128]{2,1,0:T(8,128)(2,1)S(1)} %collective-permute-done.1.beside.refs_9_), channel_id=1, source_target_pairs={{0,1},{1,0},{2,3},{3,2},{4,5},{5,4},{6,7},{7,6},{8,9},{9,8},{10,11... | collective-permute-start | bytes 393224 | tf_op jit(solution)/shard_map/ppermute | solution.py:267
  32.3 5.4 %collective-permute-start.10 = (bf16[1,512,128]{2,1,0:T(8,128)(2,1)S(1)}, bf16[1,512,128]{2,1,0:T(8,128)(2,1)S(1)}, u32[]{:S(2)}, u32[]{:S(2)}) collective-permute-start(bf16[1,512,128]{2,1,0:T(8,128)(2,1)S(1)} %choose.1.refs_0_), channel_id=1, source_target_pairs={{0,1},{1,0},{2,3},{3,2},{4,5},{5,4},{6,7},{7,6},{8,9},{9,8},{10,11... | collective-permute-start | bytes 393224 | tf_op jit(solution)/shard_map/ppermute | solution.py:267
  35.4 4.6 %collective-permute-start.19 = (bf16[4,272,128]{2,1,0:T(8,128)(2,1)S(1)}, bf16[4,272,128]{2,1,0:T(8,128)(2,1)S(1)}, u32[]{:S(2)}, u32[]{:S(2)}) collective-permute-start(bf16[4,272,128]{2,1,0:T(8,128)(2,1)S(1)} %join.5.refs_4_), channel_id=1, source_target_pairs={{0,8},{8,0},{16,24},{24,16},{1,9},{9,1},{17,25},{25,17},{2,10},{10... | collective-permute-start | bytes 835592 | tf_op jit(solution)/shard_map/ppermute | solution.py:267
  35.4 4.6 %collective-permute-start.20 = (bf16[4,272,128]{2,1,0:T(8,128)(2,1)S(1)}, bf16[4,272,128]{2,1,0:T(8,128)(2,1)S(1)}, u32[]{:S(2)}, u32[]{:S(2)}) collective-permute-start(bf16[4,272,128]{2,1,0:T(8,128)(2,1)S(1)} %collective-permute-done.14.refs_6_), channel_id=1, source_target_pairs={{0,8},{8,0},{16,24},{24,16},{1,9},{9,1},{17,25},{25,17},{2,10},{10... | collective-permute-start | bytes 835592 | tf_op jit(solution)/shard_map/ppermute | solution.py:267
  37.8 2.2 %collective-permute-start.17 = (bf16[4,272,128]{2,1,0:T(8,128)(2,1)S(1)}, bf16[4,272,128]{2,1,0:T(8,128)(2,1)S(1)}, u32[]{:S(2)}, u32[]{:S(2)}) collective-permute-start(bf16[4,272,128]{2,1,0:T(8,128)(2,1)S(1)} %join.4.refs_0_), channel_id=1, source_target_pairs={{0,8},{8,0},{16,24},{24,16},{1,9},{9,1},{17,25},{25,17},{2,10},{10... | collective-permute-start | bytes 835592 | tf_op jit(solution)/shard_map/ppermute | solution.py:267
  37.8 2.2 %collective-permute-start.18 = (bf16[4,272,128]{2,1,0:T(8,128)(2,1)S(1)}, bf16[4,272,128]{2,1,0:T(8,128)(2,1)S(1)}, u32[]{:S(2)}, u32[]{:S(2)}) collective-permute-start(bf16[4,272,128]{2,1,0:T(8,128)(2,1)S(1)} %collective-permute-done.8.refs_2_), channel_id=1, source_target_pairs={{0,8},{8,0},{16,24},{24,16},{1,9},{9,1},{17,25},{25,17},{2,10},{10... | collective-permute-start | bytes 835592 | tf_op jit(solution)/shard_map/ppermute | solution.py:267
  38.3 5.4 %collective-permute-start.16 = (bf16[1,512,128]{2,1,0:T(8,128)(2,1)S(1)}, bf16[1,512,128]{2,1,0:T(8,128)(2,1)S(1)}, u32[]{:S(2)}, u32[]{:S(2)}) collective-permute-start(bf16[1,512,128]{2,1,0:T(8,128)(2,1)S(1)} %collective-permute-done.15.refs_2_), channel_id=1, source_target_pairs={{0,1},{1,0},{2,3},{3,2},{4,5},{5,4},{6,7},{7,6},{8,9},{9,8},{10,11... | collective-permute-start | bytes 393224 | tf_op jit(solution)/shard_map/ppermute | solution.py:267

commit v7 on v6

--- a/solution.py
+++ b/solution.py
@@ -334,7 +334,6 @@
     own = amplitudes[None]
     across = lax.ppermute(own, "col", swap)
     beside = exchange(own, "col", inner)
-    outgoing[half:], across, beside = tie(outgoing[half:], across, beside)
 
     chunks = [outgoing[0][None]]
     chunks += [exchange(outgoing[s][None], "col", s) for s in range(1, n_col)]
@@ -342,21 +341,20 @@
     is_mid = ((outer == 1) | (outer == 2)).astype(jnp.int32)
     onward = exchange(across, "col", inner)
     leaving = leave(is_mid, beside, own)
-    chunks[half], onward, leaving = tie(chunks[half], onward, leaving)
     own_over = [exchange(own, "col", lane) for lane in lanes]
-    chunks[half + 1], own_over = tie(chunks[half + 1], own_over)
+    chunks[half + 1], own_over, leaving = tie(chunks[half + 1], own_over, leaving)
+    straight = exchange(leaving, "col", 2 * inner)
     beside_over = [exchange(beside, "col", lane) for lane in lanes]
     passed_on = pick(is_mid, across, onward)
-    straight = exchange(leaving, "col", 2 * inner)
     passed_over = [exchange(passed_on, "col", lane) for lane in lanes]
 
     pieces, rows = [], []
     for group in (join(chunks[half:]), join(chunks[:half])):
         passed = [exchange(group, "row", flip) for flip in range(CORES, n_row, CORES)]
         if pieces:
-            passed, straight = tie(passed, straight)
+            passed, straight, passed_over = tie(passed, straight, passed_over)
         else:
-            passed, beside_over, passed_over = tie(passed, beside_over, passed_over)
+            passed, beside_over = tie(passed, beside_over)
         mine, passed = tie(group, passed)
         for flip, mine in zip(range(0, n_row, CORES), [mine, *passed]):
             pieces += [mine, exchange(mine, "row", 1)]

time: 45.8 us -> 47.2 us (1.031)
  waiting for transfers between devices: 10.4 us -> 12.5 us
  starting transfers between devices: 27.2 us -> 26.6 us
    ppermute x20, waiting for transfers between devices: 10.4 us -> 12.5 us  [exchange(): return lax.ppermute(x, axis, [(i, i ^ flip) for i in range(size)])]
    ppermute x1, starting transfers between devices: 2.94 us -> 1.21 us  [body(): across = lax.ppermute(own, 'col', swap)]
    ppermute x20, starting transfers between devices: 24.3 us -> 25.4 us  [exchange(): return lax.ppermute(x, axis, [(i, i ^ flip) for i in range(size)])]
  transfers between devices with their start and end apart: 21 -> 21, of which waited for: 6 -> 11; matrix products, arithmetic and copies ran while one was open for 0% -> 0% of each run, Pallas kernels for 13% -> 10%
where the time goes in v7:
time: 47.2 us; the launch traced here: 47.1 us
  starting transfers between devices  26.6 us (56%)
  waiting for transfers between devices  12.5 us (26%)
  Pallas kernels  7.82 us (17%)
    ppermute x20, starting transfers between devices, exchange(): return lax.ppermute(x, axis, [(i, i ^ flip) for i in range(size)])  25.4 us
    ppermute x20, waiting for transfers between devices, exchange(): return lax.ppermute(x, axis, [(i, i ^ flip) for i in range(size)])  12.5 us
    pallas_call x1, Pallas kernels, near_half(): pl.pallas_call(functools.partial(near_kernel, n_pieces, offsets, capacity...  3.66 us
    pallas_call x1, Pallas kernels, far_half(): pl.pallas_call(functools.partial(far_kernel, offsets, depth // width), ou...  1.93 us
    pallas_call x1, Pallas kernels, pack(): pl.pallas_call(functools.partial(pack_kernel, columns, capacity), out_sha...  1.25 us
    ppermute x1, starting transfers between devices, body(): across = lax.ppermute(own, 'col', swap)  1.21 us
  transfers between devices with their start and end apart: 21, of which 11 were waited for; matrix products, arithmetic and copies ran while one was open for 0% of the time, Pallas kernels for 10%

profile of v7, /device:TPU:0, one launch (start us, length us, event | category | flops | bytes accessed | tf_op | source)
XLA Modules:
  0.0 47.1 jit_solution(11303964045037279255)
XLA Ops:
  0.0 1.3 %pack.1 = (bf16[272,128]{1,0:T(8,128)(2,1)S(1)}, bf16[272,128]{1,0:T(8,128)(2,1)S(1)}, bf16[272,128]{1,0:T(8,128)(2,1)S(1)}, bf16[272,128]{1,0:T(8,128)(2,1)S(1)...) custom-call(s32[1]{0:T(128)} %bitcast.3.me_ref, ...), custom_call_target="tpu_custom_call" | custom-call | tf_op jit(solution)/shard_map/pack/pallas_call | solution.py:63
  1.3 5.0 %collective-permute-start.6 = (bf16[1,272,128]{2,1,0:T(8,128)(2,1)S(1)}, bf16[1,272,128]{2,1,0:T(8,128)(2,1)S(1)}, u32[]{:S(2)}, u32[]{:S(2)}) collective-permute-start(bf16[1,272,128]{2,1,0:T(8,128)(2,1)S(1)} %bitcast.23), channel_id=1, source_target_pairs={{0,5},{1,4},{2,7},{3,6},{4,1},{5,0},{6,3},{7,2},{8,13},{9,12},{10,... | collective-permute-start | bytes 208904 | tf_op jit(solution)/shard_map/ppermute | solution.py:267
  6.3 1.6 %collective-permute-start.8 = (bf16[1,512,128]{2,1,0:T(8,128)(2,1)}, bf16[1,512,128]{2,1,0:T(8,128)(2,1)S(1)}, u32[]{:S(2)}, u32[]{:S(2)}) collective-permute-start(bf16[1,512,128]{2,1,0:T(8,128)(2,1)} %bitcast.24), channel_id=1, source_target_pairs={{0,2},{1,3},{2,0},{3,1},{4,6},{5,7},{6,4},{7,5},{8,10},{9,11},{10,... | collective-permute-start | bytes 393224 | tf_op jit(solution)/shard_map/ppermute | solution.py:267
  8.9 2.5 %collective-permute-start.4 = (bf16[1,272,128]{2,1,0:T(8,128)(2,1)S(1)}, bf16[1,272,128]{2,1,0:T(8,128)(2,1)S(1)}, u32[]{:S(2)}, u32[]{:S(2)}) collective-permute-start(bf16[1,272,128]{2,1,0:T(8,128)(2,1)S(1)} %bitcast.20), channel_id=1, source_target_pairs={{0,3},{1,2},{2,1},{3,0},{4,7},{5,6},{6,5},{7,4},{8,11},{9,10},{10,... | collective-permute-start | bytes 208904 | tf_op jit(solution)/shard_map/ppermute | solution.py:267
  12.2 1.2 %collective-permute-start = (bf16[1,512,128]{2,1,0:T(8,128)(2,1)}, bf16[1,512,128]{2,1,0:T(8,128)(2,1)S(1)}, u32[]{:S(2)}, u32[]{:S(2)}) collective-permute-start(bf16[1,512,128]{2,1,0:T(8,128)(2,1)} %bitcast.26), channel_id=1, source_target_pairs={{0,1},{1,0},{2,4},{3,5},{4,2},{5,3},{6,7},{7,6},{8,9},{9,8},{10,12... | collective-permute-start | bytes 393224 | tf_op jit(solution)/shard_map/ppermute | solution.py:335
  13.4 1.0 %collective-permute-done.3.refs_2_ = bf16[1,272,128]{2,1,0:T(8,128)(2,1)S(1)} collective-permute-done((bf16[1,272,128]{2,1,0:T(8,128)(2,1)S(1)}, bf16[1,272,128]{2,1,0:T(8,128)(2,1)S(1)}, u32[]{:S(2)}, u32[]{:S(2)}) %collective-permute-start.3) | collective-permute-done | bytes 69664 | tf_op jit(solution)/shard_map/ppermute | solution.py:267
  14.4 0.7 %collective-permute-start.12 = (bf16[1,272,128]{2,1,0:T(8,128)(2,1)S(1)}, bf16[1,272,128]{2,1,0:T(8,128)(2,1)S(1)}, u32[]{:S(2)}, u32[]{:S(2)}) collective-permute-start(bf16[1,272,128]{2,1,0:T(8,128)(2,1)S(1)} %bitcast.19), channel_id=1, source_target_pairs={{0,4},{1,5},{2,6},{3,7},{4,0},{5,1},{6,2},{7,3},{8,12},{9,13},{10,... | collective-permute-start | bytes 208904 | tf_op jit(solution)/shard_map/ppermute | solution.py:267
  15.1 2.9 %collective-permute-start.13 = (bf16[1,272,128]{2,1,0:T(8,128)(2,1)S(1)}, bf16[1,272,128]{2,1,0:T(8,128)(2,1)S(1)}, u32[]{:S(2)}, u32[]{:S(2)}) collective-permute-start(bf16[1,272,128]{2,1,0:T(8,128)(2,1)S(1)} %bitcast.18), channel_id=1, source_target_pairs={{0,6},{1,7},{2,4},{3,5},{4,2},{5,3},{6,0},{7,1},{8,14},{9,15},{10,... | collective-permute-start | bytes 208904 | tf_op jit(solution)/shard_map/ppermute | solution.py:267
  18.0 2.0 %collective-permute-start.14 = (bf16[1,272,128]{2,1,0:T(8,128)(2,1)S(1)}, bf16[1,272,128]{2,1,0:T(8,128)(2,1)S(1)}, u32[]{:S(2)}, u32[]{:S(2)}) collective-permute-start(bf16[1,272,128]{2,1,0:T(8,128)(2,1)S(1)} %bitcast.17), channel_id=1, source_target_pairs={{0,7},{1,6},{2,5},{3,4},{4,3},{5,2},{6,1},{7,0},{8,15},{9,14},{10,... | collective-permute-start | bytes 208904 | tf_op jit(solution)/shard_map/ppermute | solution.py:267
  20.0 1.6 %collective-permute-start.5 = (bf16[4,272,128]{2,1,0:T(8,128)(2,1)S(1)}, bf16[4,272,128]{2,1,0:T(8,128)(2,1)S(1)}, u32[]{:S(2)}, u32[]{:S(2)}) collective-permute-start(bf16[4,272,128]{2,1,0:T(8,128)(2,1)S(1)} %join.4.refs_4_), channel_id=1, source_target_pairs={{0,16},{8,24},{16,0},{24,8},{1,17},{9,25},{17,1},{25,9},{2,18},{10... | collective-permute-start | bytes 835592 | tf_op jit(solution)/shard_map/ppermute | solution.py:267
  21.6 0.9 %leave.1 = bf16[1,512,128]{2,1,0:T(8,128)(2,1)S(1)} custom-call(s32[1]{0:T(128)} %bitcast.flag_ref, bf16[1,512,128]{2,1,0:T(8,128)(2,1)S(1)} %collective-permute-done.8.beside.refs_9_, bf16[1,512,128]{2,1,0:T(8,128)(2,1)} %bitcast.27), custom_call_target="tpu_custom_call" | custom-call | tf_op jit(solution)/shard_map/leave/pallas_call | solution.py:300
  22.5 0.9 %collective-permute-done.12.refs_0_ = bf16[1,272,128]{2,1,0:T(8,128)(2,1)S(1)} collective-permute-done((bf16[1,272,128]{2,1,0:T(8,128)(2,1)S(1)}, bf16[1,272,128]{2,1,0:T(8,128)(2,1)S(1)}, u32[]{:S(2)}, u32[]{:S(2)}) %collective-permute-start.12) | collective-permute-done | bytes 69664 | tf_op jit(solution)/shard_map/ppermute | solution.py:267
  23.4 1.7 %collective-permute-done.14.refs_3_ = bf16[1,272,128]{2,1,0:T(8,128)(2,1)S(1)} collective-permute-done((bf16[1,272,128]{2,1,0:T(8,128)(2,1)S(1)}, bf16[1,272,128]{2,1,0:T(8,128)(2,1)S(1)}, u32[]{:S(2)}, u32[]{:S(2)}) %collective-permute-start.14) | collective-permute-done | bytes 69664 | tf_op jit(solution)/shard_map/ppermute | solution.py:267
  25.2 1.6 %collective-permute-start.15 = (bf16[4,272,128]{2,1,0:T(8,128)(2,1)S(1)}, bf16[4,272,128]{2,1,0:T(8,128)(2,1)S(1)}, u32[]{:S(2)}, u32[]{:S(2)}) collective-permute-start(bf16[4,272,128]{2,1,0:T(8,128)(2,1)S(1)} %join.5.refs_0_), channel_id=1, source_target_pairs={{0,16},{8,24},{16,0},{24,8},{1,17},{9,25},{17,1},{25,9},{2,18},{10... | collective-permute-start | bytes 835592 | tf_op jit(solution)/shard_map/ppermute | solution.py:267
  26.7 2.3 %collective-permute-start.1 = (bf16[1,512,128]{2,1,0:T(8,128)(2,1)S(1)}, bf16[1,512,128]{2,1,0:T(8,128)(2,1)S(1)}, u32[]{:S(2)}, u32[]{:S(2)}) collective-permute-start(bf16[1,512,128]{2,1,0:T(8,128)(2,1)S(1)} %collective-permute-done.refs_0_), channel_id=1, source_target_pairs={{0,2},{1,3},{2,0},{3,1},{4,6},{5,7},{6,4},{7,5},{8,10},{9,11},{10,... | collective-permute-start | bytes 393224 | tf_op jit(solution)/shard_map/ppermute | solution.py:267
  29.0 3.8 %collective-permute-done.1.refs_1_ = bf16[1,512,128]{2,1,0:T(8,128)(2,1)S(1)} collective-permute-done((bf16[1,512,128]{2,1,0:T(8,128)(2,1)S(1)}, bf16[1,512,128]{2,1,0:T(8,128)(2,1)S(1)}, u32[]{:S(2)}, u32[]{:S(2)}) %collective-permute-start.1) | collective-permute-done | bytes 131104 | tf_op jit(solution)/shard_map/ppermute | solution.py:267
  32.8 0.6 %collective-permute-start.10 = (bf16[1,512,128]{2,1,0:T(8,128)(2,1)S(1)}, bf16[1,512,128]{2,1,0:T(8,128)(2,1)S(1)}, u32[]{:S(2)}, u32[]{:S(2)}) collective-permute-start(bf16[1,512,128]{2,1,0:T(8,128)(2,1)S(1)} %choose.1.refs_0_), channel_id=1, source_target_pairs={{0,1},{1,0},{2,3},{3,2},{4,5},{5,4},{6,7},{7,6},{8,9},{9,8},{10,11... | collective-permute-start | bytes 393224 | tf_op jit(solution)/shard_map/ppermute | solution.py:267
  33.4 1.5 %collective-permute-start.16 = (bf16[1,512,128]{2,1,0:T(8,128)(2,1)S(1)}, bf16[1,512,128]{2,1,0:T(8,128)(2,1)S(1)}, u32[]{:S(2)}, u32[]{:S(2)}) collective-permute-start(bf16[1,512,128]{2,1,0:T(8,128)(2,1)S(1)} %collective-permute-done.8.beside.refs_9_), channel_id=1, source_target_pairs={{0,1},{1,0},{2,3},{3,2},{4,5},{5,4},{6,7},{7,6},{8,9},{9,8},{10,11... | collective-permute-start | bytes 393224 | tf_op jit(solution)/shard_map/ppermute | solution.py:267
  34.9 1.4 %collective-permute-done.9.refs_2_ = bf16[1,512,128]{2,1,0:T(8,128)(2,1)S(1)} collective-permute-done((bf16[1,512,128]{2,1,0:T(8,128)(2,1)S(1)}, bf16[1,512,128]{2,1,0:T(8,128)(2,1)S(1)}, u32[]{:S(2)}, u32[]{:S(2)}) %collective-permute-start.9) | collective-permute-done | bytes 131104 | tf_op jit(solution)/shard_map/ppermute | solution.py:267
  36.3 1.6 %collective-permute-done.10.refs_1_ = bf16[1,512,128]{2,1,0:T(8,128)(2,1)S(1)} collective-permute-done((bf16[1,512,128]{2,1,0:T(8,128)(2,1)S(1)}, bf16[1,512,128]{2,1,0:T(8,128)(2,1)S(1)}, u32[]{:S(2)}, u32[]{:S(2)}) %collective-permute-start.10) | collective-permute-done | bytes 131104 | tf_op jit(solution)/shard_map/ppermute | solution.py:267
  38.4 0.9 %collective-permute-done.16.refs_10_ = bf16[1,512,128]{2,1,0:T(8,128)(2,1)S(1)} collective-permute-done((bf16[1,512,128]{2,1,0:T(8,128)(2,1)S(1)}, bf16[1,512,128]{2,1,0:T(8,128)(2,1)S(1)}, u32[]{:S(2)}, u32[]{:S(2)}) %collective-permute-start.16) | collective-permute-done | bytes 131104 | tf_op jit(solution)/shard_map/ppermute | solution.py:267
  39.8 0.6 %collective-permute-start.11 = (bf16[1,512,128]{2,1,0:T(8,128)(2,1)S(1)}, bf16[1,512,128]{2,1,0:T(8,128)(2,1)S(1)}, u32[]{:S(2)}, u32[]{:S(2)}) collective-permute-start(bf16[1,512,128]{2,1,0:T(8,128)(2,1)S(1)} %collective-permute-done.9.refs_2_), channel_id=1, source_target_pairs={{0,1},{1,0},{2,3},{3,2},{4,5},{5,4},{6,7},{7,6},{8,9},{9,8},{10,11... | collective-permute-start | bytes 393224 | tf_op jit(solution)/shard_map/ppermute | solution.py:267
  41.2 3.7 %near_half.1 = (f32[512,1024]{1,0:T(8,128)S(1)}, bf16[512,1024]{1,0:T(8,128)(2,1)S(1)}) custom-call(s32[10]{0:T(128)S(1)} %stack.25.where_ref, bf16[4,272,128]{2,1,0:T(8,128)(2,1)S(1)} %join.5.refs_0_, bf16[4,272,128]{2,1,0:T(8,128)(2,1)S(1)} %collective-permute-done.17.refs_1_, bf16[4,272,128]{2,1,0:T(8,128)(2,1)S(1)} %collective-permute-done.15.refs_2_, ...), custom_call_target="tpu_custom_call" | custom-call | flops 536870912 | bytes 8388608 | tf_op jit(solution)/shard_map/near_half/pallas_call | solution.py:197
  45.2 1.9 %far_half.1 = f32[512,1024]{1,0:T(8,128)} custom-call(s32[1]{0:T(128)} %bitcast.flag_ref, bf16[1,512,128]{2,1,0:T(8,128)(2,1)S(1)} %choose.1.refs_0_, bf16[1,512,128]{2,1,0:T(8,128)(2,1)S(1)} %collective-permute-done.10.refs_1_, bf16[1,512,128]{2,1,0:T(8,128)(2,1)S(1)} %collective-permute-done.9.refs_2_, ...), custom_call_target="tpu_custom_call" | custom-call | flops 536870912 | bytes 8388608 | tf_op jit(solution)/shard_map/far_half/pallas_call | solution.py:245
  (27 shorter events, 4.0 us)
Async XLA Ops:
  1.3 10.1 %collective-permute-start.6 = (bf16[1,272,128]{2,1,0:T(8,128)(2,1)S(1)}, bf16[1,272,128]{2,1,0:T(8,128)(2,1)S(1)}, u32[]{:S(2)}, u32[]{:S(2)}) collective-permute-start(bf16[1,272,128]{2,1,0:T(8,128)(2,1)S(1)} %bitcast.23), channel_id=1, source_target_pairs={{0,5},{1,4},{2,7},{3,6},{4,1},{5,0},{6,3},{7,2},{8,13},{9,12},{10,... | collective-permute-start | bytes 208904 | tf_op jit(solution)/shard_map/ppermute | solution.py:267
  6.3 11.7 %collective-permute-start.8 = (bf16[1,512,128]{2,1,0:T(8,128)(2,1)}, bf16[1,512,128]{2,1,0:T(8,128)(2,1)S(1)}, u32[]{:S(2)}, u32[]{:S(2)}) collective-permute-start(bf16[1,512,128]{2,1,0:T(8,128)(2,1)} %bitcast.24), channel_id=1, source_target_pairs={{0,2},{1,3},{2,0},{3,1},{4,6},{5,7},{6,4},{7,5},{8,10},{9,11},{10,... | collective-permute-start | bytes 393224 | tf_op jit(solution)/shard_map/ppermute | solution.py:267
  7.9 4.3 %collective-permute-start.2 = (bf16[1,272,128]{2,1,0:T(8,128)(2,1)S(1)}, bf16[1,272,128]{2,1,0:T(8,128)(2,1)S(1)}, u32[]{:S(2)}, u32[]{:S(2)}) collective-permute-start(bf16[1,272,128]{2,1,0:T(8,128)(2,1)S(1)} %bitcast.22), channel_id=1, source_target_pairs={{0,1},{1,0},{2,3},{3,2},{4,5},{5,4},{6,7},{7,6},{8,9},{9,8},{10,11... | collective-permute-start | bytes 208904 | tf_op jit(solution)/shard_map/ppermute | solution.py:267
  8.4 6.0 %collective-permute-start.3 = (bf16[1,272,128]{2,1,0:T(8,128)(2,1)S(1)}, bf16[1,272,128]{2,1,0:T(8,128)(2,1)S(1)}, u32[]{:S(2)}, u32[]{:S(2)}) collective-permute-start(bf16[1,272,128]{2,1,0:T(8,128)(2,1)S(1)} %bitcast.21), channel_id=1, source_target_pairs={{0,2},{1,3},{2,0},{3,1},{4,6},{5,7},{6,4},{7,5},{8,10},{9,11},{10,... | collective-permute-start | bytes 208904 | tf_op jit(solution)/shard_map/ppermute | solution.py:267
  8.9 6.3 %collective-permute-start.4 = (bf16[1,272,128]{2,1,0:T(8,128)(2,1)S(1)}, bf16[1,272,128]{2,1,0:T(8,128)(2,1)S(1)}, u32[]{:S(2)}, u32[]{:S(2)}) collective-permute-start(bf16[1,272,128]{2,1,0:T(8,128)(2,1)S(1)} %bitcast.20), channel_id=1, source_target_pairs={{0,3},{1,2},{2,1},{3,0},{4,7},{5,6},{6,5},{7,4},{8,11},{9,10},{10,... | collective-permute-start | bytes 208904 | tf_op jit(solution)/shard_map/ppermute | solution.py:267
  11.4 8.6 %collective-permute-start.7 = (bf16[1,512,128]{2,1,0:T(8,128)(2,1)}, bf16[1,512,128]{2,1,0:T(8,128)(2,1)S(1)}, u32[]{:S(2)}, u32[]{:S(2)}) collective-permute-start(bf16[1,512,128]{2,1,0:T(8,128)(2,1)} %bitcast.25), channel_id=1, source_target_pairs={{0,1},{1,0},{2,3},{3,2},{4,5},{5,4},{6,7},{7,6},{8,9},{9,8},{10,11... | collective-permute-start | bytes 393224 | tf_op jit(solution)/shard_map/ppermute | solution.py:267
  12.2 14.6 %collective-permute-start = (bf16[1,512,128]{2,1,0:T(8,128)(2,1)}, bf16[1,512,128]{2,1,0:T(8,128)(2,1)S(1)}, u32[]{:S(2)}, u32[]{:S(2)}) collective-permute-start(bf16[1,512,128]{2,1,0:T(8,128)(2,1)} %bitcast.26), channel_id=1, source_target_pairs={{0,1},{1,0},{2,4},{3,5},{4,2},{5,3},{6,7},{7,6},{8,9},{9,8},{10,12... | collective-permute-start | bytes 393224 | tf_op jit(solution)/shard_map/ppermute | solution.py:335
  14.4 9.0 %collective-permute-start.12 = (bf16[1,272,128]{2,1,0:T(8,128)(2,1)S(1)}, bf16[1,272,128]{2,1,0:T(8,128)(2,1)S(1)}, u32[]{:S(2)}, u32[]{:S(2)}) collective-permute-start(bf16[1,272,128]{2,1,0:T(8,128)(2,1)S(1)} %bitcast.19), channel_id=1, source_target_pairs={{0,4},{1,5},{2,6},{3,7},{4,0},{5,1},{6,2},{7,3},{8,12},{9,13},{10,... | collective-permute-start | bytes 208904 | tf_op jit(solution)/shard_map/ppermute | solution.py:267
  15.1 8.3 %collective-permute-start.13 = (bf16[1,272,128]{2,1,0:T(8,128)(2,1)S(1)}, bf16[1,272,128]{2,1,0:T(8,128)(2,1)S(1)}, u32[]{:S(2)}, u32[]{:S(2)}) collective-permute-start(bf16[1,272,128]{2,1,0:T(8,128)(2,1)S(1)} %bitcast.18), channel_id=1, source_target_pairs={{0,6},{1,7},{2,4},{3,5},{4,2},{5,3},{6,0},{7,1},{8,14},{9,15},{10,... | collective-permute-start | bytes 208904 | tf_op jit(solution)/shard_map/ppermute | solution.py:267
  18.0 7.1 %collective-permute-start.14 = (bf16[1,272,128]{2,1,0:T(8,128)(2,1)S(1)}, bf16[1,272,128]{2,1,0:T(8,128)(2,1)S(1)}, u32[]{:S(2)}, u32[]{:S(2)}) collective-permute-start(bf16[1,272,128]{2,1,0:T(8,128)(2,1)S(1)} %bitcast.17), channel_id=1, source_target_pairs={{0,7},{1,6},{2,5},{3,4},{4,3},{5,2},{6,1},{7,0},{8,15},{9,14},{10,... | collective-permute-start | bytes 208904 | tf_op jit(solution)/shard_map/ppermute | solution.py:267
  20.0 16.3 %collective-permute-start.5 = (bf16[4,272,128]{2,1,0:T(8,128)(2,1)S(1)}, bf16[4,272,128]{2,1,0:T(8,128)(2,1)S(1)}, u32[]{:S(2)}, u32[]{:S(2)}) collective-permute-start(bf16[4,272,128]{2,1,0:T(8,128)(2,1)S(1)} %join.4.refs_4_), channel_id=1, source_target_pairs={{0,16},{8,24},{16,0},{24,8},{1,17},{9,25},{17,1},{25,9},{2,18},{10... | collective-permute-start | bytes 835592 | tf_op jit(solution)/shard_map/ppermute | solution.py:267
  25.2 14.1 %collective-permute-start.15 = (bf16[4,272,128]{2,1,0:T(8,128)(2,1)S(1)}, bf16[4,272,128]{2,1,0:T(8,128)(2,1)S(1)}, u32[]{:S(2)}, u32[]{:S(2)}) collective-permute-start(bf16[4,272,128]{2,1,0:T(8,128)(2,1)S(1)} %join.5.refs_0_), channel_id=1, source_target_pairs={{0,16},{8,24},{16,0},{24,8},{1,17},{9,25},{17,1},{25,9},{2,18},{10... | collective-permute-start | bytes 835592 | tf_op jit(solution)/shard_map/ppermute | solution.py:267
  26.7 6.0 %collective-permute-start.1 = (bf16[1,512,128]{2,1,0:T(8,128)(2,1)S(1)}, bf16[1,512,128]{2,1,0:T(8,128)(2,1)S(1)}, u32[]{:S(2)}, u32[]{:S(2)}) collective-permute-start(bf16[1,512,128]{2,1,0:T(8,128)(2,1)S(1)} %collective-permute-done.refs_0_), channel_id=1, source_target_pairs={{0,2},{1,3},{2,0},{3,1},{4,6},{5,7},{6,4},{7,5},{8,10},{9,11},{10,... | collective-permute-start | bytes 393224 | tf_op jit(solution)/shard_map/ppermute | solution.py:267
  29.0 7.3 %collective-permute-start.9 = (bf16[1,512,128]{2,1,0:T(8,128)(2,1)S(1)}, bf16[1,512,128]{2,1,0:T(8,128)(2,1)S(1)}, u32[]{:S(2)}, u32[]{:S(2)}) collective-permute-start(bf16[1,512,128]{2,1,0:T(8,128)(2,1)S(1)} %leave.1), channel_id=1, source_target_pairs={{0,4},{1,5},{2,6},{3,7},{4,0},{5,1},{6,2},{7,3},{8,12},{9,13},{10,... | collective-permute-start | bytes 393224 | tf_op jit(solution)/shard_map/ppermute | solution.py:267
  32.8 5.0 %collective-permute-start.10 = (bf16[1,512,128]{2,1,0:T(8,128)(2,1)S(1)}, bf16[1,512,128]{2,1,0:T(8,128)(2,1)S(1)}, u32[]{:S(2)}, u32[]{:S(2)}) collective-permute-start(bf16[1,512,128]{2,1,0:T(8,128)(2,1)S(1)} %choose.1.refs_0_), channel_id=1, source_target_pairs={{0,1},{1,0},{2,3},{3,2},{4,5},{5,4},{6,7},{7,6},{8,9},{9,8},{10,11... | collective-permute-start | bytes 393224 | tf_op jit(solution)/shard_map/ppermute | solution.py:267
  33.4 5.9 %collective-permute-start.16 = (bf16[1,512,128]{2,1,0:T(8,128)(2,1)S(1)}, bf16[1,512,128]{2,1,0:T(8,128)(2,1)S(1)}, u32[]{:S(2)}, u32[]{:S(2)}) collective-permute-start(bf16[1,512,128]{2,1,0:T(8,128)(2,1)S(1)} %collective-permute-done.8.beside.refs_9_), channel_id=1, source_target_pairs={{0,1},{1,0},{2,3},{3,2},{4,5},{5,4},{6,7},{7,6},{8,9},{9,8},{10,11... | collective-permute-start | bytes 393224 | tf_op jit(solution)/shard_map/ppermute | solution.py:267
  37.8 2.6 %collective-permute-start.19 = (bf16[4,272,128]{2,1,0:T(8,128)(2,1)S(1)}, bf16[4,272,128]{2,1,0:T(8,128)(2,1)S(1)}, u32[]{:S(2)}, u32[]{:S(2)}) collective-permute-start(bf16[4,272,128]{2,1,0:T(8,128)(2,1)S(1)} %join.4.refs_4_), channel_id=1, source_target_pairs={{0,8},{8,0},{16,24},{24,16},{1,9},{9,1},{17,25},{25,17},{2,10},{10... | collective-permute-start | bytes 835592 | tf_op jit(solution)/shard_map/ppermute | solution.py:267
  37.8 2.6 %collective-permute-start.20 = (bf16[4,272,128]{2,1,0:T(8,128)(2,1)S(1)}, bf16[4,272,128]{2,1,0:T(8,128)(2,1)S(1)}, u32[]{:S(2)}, u32[]{:S(2)}) collective-permute-start(bf16[4,272,128]{2,1,0:T(8,128)(2,1)S(1)} %collective-permute-done.5.refs_6_), channel_id=1, source_target_pairs={{0,8},{8,0},{16,24},{24,16},{1,9},{9,1},{17,25},{25,17},{2,10},{10... | collective-permute-start | bytes 835592 | tf_op jit(solution)/shard_map/ppermute | solution.py:267
  39.3 1.6 %collective-permute-start.17 = (bf16[4,272,128]{2,1,0:T(8,128)(2,1)S(1)}, bf16[4,272,128]{2,1,0:T(8,128)(2,1)S(1)}, u32[]{:S(2)}, u32[]{:S(2)}) collective-permute-start(bf16[4,272,128]{2,1,0:T(8,128)(2,1)S(1)} %join.5.refs_0_), channel_id=1, source_target_pairs={{0,8},{8,0},{16,24},{24,16},{1,9},{9,1},{17,25},{25,17},{2,10},{10... | collective-permute-start | bytes 835592 | tf_op jit(solution)/shard_map/ppermute | solution.py:267
  39.3 2.0 %collective-permute-start.18 = (bf16[4,272,128]{2,1,0:T(8,128)(2,1)S(1)}, bf16[4,272,128]{2,1,0:T(8,128)(2,1)S(1)}, u32[]{:S(2)}, u32[]{:S(2)}) collective-permute-start(bf16[4,272,128]{2,1,0:T(8,128)(2,1)S(1)} %collective-permute-done.15.refs_2_), channel_id=1, source_target_pairs={{0,8},{8,0},{16,24},{24,16},{1,9},{9,1},{17,25},{25,17},{2,10},{10... | collective-permute-start | bytes 835592 | tf_op jit(solution)/shard_map/ppermute | solution.py:267
  39.8 5.4 %collective-permute-start.11 = (bf16[1,512,128]{2,1,0:T(8,128)(2,1)S(1)}, bf16[1,512,128]{2,1,0:T(8,128)(2,1)S(1)}, u32[]{:S(2)}, u32[]{:S(2)}) collective-permute-start(bf16[1,512,128]{2,1,0:T(8,128)(2,1)S(1)} %collective-permute-done.9.refs_2_), channel_id=1, source_target_pairs={{0,1},{1,0},{2,3},{3,2},{4,5},{5,4},{6,7},{7,6},{8,9},{9,8},{10,11... | collective-permute-start | bytes 393224 | tf_op jit(solution)/shard_map/ppermute | solution.py:267

commit v8 on v4

--- a/solution.py
+++ b/solution.py
@@ -103,13 +103,15 @@
     )(*chunks)
 
 
-def multiply(amp, block, start, out, sems, step):
+def multiply(amp, block, first, start, out, sems, step):
     copies = []
     for n in range(block.shape[1] // step):
         cols = slice(n * step, (n + 1) * step)
         held = out[0] if sems is not None else out
         held[:, cols] = start[:, cols] + jnp.dot(
-            amp[...], block[:, cols], preferred_element_type=jnp.float32
+            amp[...],
+            block[first : first + amp.shape[1], cols],
+            preferred_element_type=jnp.float32,
         )
         if sems is not None:
             part = pl.ds(n * step, step)
@@ -121,62 +123,63 @@
         copy.wait()
 
 
-def near_kernel(n_pieces, offsets, capacity, where_ref, *refs):
+def near_kernel(n_pieces, offsets, capacity, n_columns, where_ref, *refs):
     n_amps = len(offsets)
     pieces = refs[:n_pieces]
     amps = refs[n_pieces : n_pieces + n_amps]
-    own, residual, total, far = refs[n_pieces + n_amps : n_pieces + n_amps + 4]
-    places, table, amp, near, res, table_sem, own_sem, res_sem = refs[n_pieces + n_amps + 4 :]
-    columns = pieces[0].shape[0]
+    own, residual, total, block = refs[n_pieces + n_amps : n_pieces + n_amps + 4]
+    places, table, amp, res, table_sem, own_sem, res_sem = refs[n_pieces + n_amps + 4 :]
     width = pieces[0].shape[2]
     per_device = KT_DEV * QT_DEV
-    half = amp.shape[1] // width
     own_copy = pltpu.make_async_copy(own, amp.at[:, pl.ds(0, width)], own_sem)
     own_copy.start()
     res_copy = pltpu.make_async_copy(residual, res, res_sem)
     res_copy.start()
-    for p, piece in enumerate(pieces):
+    at = 0
+    for piece in pieces:
         rows = piece[:, capacity * width :, :]
-        places[p * columns : (p + 1) * columns] = jnp.max(
-            rows.astype(jnp.float32), axis=1
-        ).astype(jnp.int32)
+        places[at : at + piece.shape[0]] = jnp.max(rows.astype(jnp.float32), axis=1).astype(
+            jnp.int32
+        )
+        at += piece.shape[0]
     table_copy = pltpu.make_async_copy(places, table, table_sem)
     table_copy.start()
     for source, slot in zip(amps, offsets):
         amp[:, slot * width : (slot + 1) * width] = source[...]
     table_copy.wait()
     col = where_ref[n_pieces]
+    full = capacity * n_columns == per_device
+    at = 0
     for p, piece in enumerate(pieces):
         row = where_ref[p]
-
-        def place(c, _, p=p, piece=piece, row=row):
+        for c in range(piece.shape[0]):
             for s in range(capacity):
-                position = table[p * columns + c, s]
-                k = row * KT_DEV + lax.shift_right_logical(position, QT_DEV.bit_length() - 1)
-                slot = k ^ col
-                q = pl.multiple_of((position & (QT_DEV - 1)) * width, width)
-                at = pl.multiple_of((slot & (half - 1)) * width, width)
-                tile = piece.at[c, pl.ds(s * width, width), :]
-
-                @pl.when((position < per_device) & (slot < half))
-                def _():
-                    near[pl.ds(at, width), pl.ds(q, width)] = tile[...]
-
-                @pl.when((position < per_device) & (slot >= half))
-                def _():
-                    far[pl.ds(at, width), pl.ds(q, width)] = tile[...]
-
-            return 0
-
-        lax.fori_loop(0, columns, place, 0)
+                position = table[at, s]
+
+                def put(position=position, piece=piece, c=c, s=s, row=row):
+                    k = row * KT_DEV + lax.shift_right_logical(
+                        position, QT_DEV.bit_length() - 1
+                    )
+                    q = position & (QT_DEV - 1)
+                    block[
+                        pl.ds(pl.multiple_of((k ^ col) * width, width), width),
+                        pl.ds(pl.multiple_of(q * width, width), width),
+                    ] = piece[c, s * width : (s + 1) * width, :]
+
+                if full:
+                    put()
+                else:
+                    pl.when(position < per_device)(put)
+            at += 1
     own_copy.wait()
     res_copy.wait()
-    multiply(amp, near, res, total, None, 2 * width)
+    multiply(amp, block, 0, res, total, None, 2 * width)
 
 
 def near_half(where, pieces, amps, offsets, own, residual, capacity):
-    columns, _, width = pieces[0].shape
+    width = pieces[0].shape[2]
     n_pieces, n_amps = len(pieces), len(amps)
+    chunks = sum(p.shape[0] for p in pieces)
     rows, n_cols = residual.shape
     depth = (1 + n_amps) * width
     hbm = pl.BlockSpec(memory_space=pltpu.HBM)
@@ -184,20 +187,19 @@
     held = 2 * rows * depth + 4 * depth * n_cols + 8 * rows * n_cols
     held += sum(x.size * x.dtype.itemsize for x in pieces) // 2
     return pl.pallas_call(
-        functools.partial(near_kernel, n_pieces, offsets, capacity),
+        functools.partial(near_kernel, n_pieces, offsets, capacity, 1 + 2 * n_amps + 1),
         out_shape=[
             jax.ShapeDtypeStruct(residual.shape, residual.dtype),
-            jax.ShapeDtypeStruct((depth, n_cols), pieces[0].dtype),
+            jax.ShapeDtypeStruct((2 * depth, n_cols), pieces[0].dtype),
         ],
         in_specs=[pl.BlockSpec(memory_space=pltpu.SMEM)]
         + [vmem] * (n_pieces + n_amps)
         + [hbm, hbm],
         out_specs=[vmem, vmem],
         scratch_shapes=[
-            pltpu.VMEM((n_pieces * columns, width), jnp.int32),
-            pltpu.SMEM((n_pieces * columns, width), jnp.int32),
+            pltpu.VMEM((chunks, width), jnp.int32),
+            pltpu.SMEM((chunks, width), jnp.int32),
             pltpu.VMEM((rows, depth), pieces[0].dtype),
-            pltpu.VMEM((depth, n_cols), pieces[0].dtype),
             pltpu.VMEM((rows, n_cols), residual.dtype),
             pltpu.SemaphoreType.DMA,
             pltpu.SemaphoreType.DMA,
@@ -221,26 +223,26 @@
 
 def far_kernel(offsets, half, *refs):
     amps = refs[: len(offsets)]
-    start, far, out, amp, total, sems = refs[len(offsets) :]
+    start, block, out, amp, total, sems = refs[len(offsets) :]
     width = amps[0].shape[1]
     for source, slot in zip(amps, offsets):
         at = (slot - half) * width
         amp[:, at : at + width] = source[...]
-    multiply(amp, far, start, (total, out), sems, 2 * width)
-
-
-def far_half(amps, offsets, total, far):
+    multiply(amp, block, block.shape[0] - amp.shape[1], start, (total, out), sems, 2 * width)
+
+
+def far_half(amps, offsets, total, block):
     rows, n_cols = total.shape
-    depth, width = far.shape[0], amps[0].shape[1]
+    depth, width = block.shape[0] // 2, amps[0].shape[1]
     vmem = pl.BlockSpec(memory_space=pltpu.VMEM)
-    held = 4 * rows * depth + 2 * depth * n_cols + 8 * rows * n_cols
+    held = 4 * rows * depth + 4 * depth * n_cols + 8 * rows * n_cols
     return pl.pallas_call(
         functools.partial(far_kernel, offsets, depth // width),
         out_shape=jax.ShapeDtypeStruct(total.shape, total.dtype),
         in_specs=[vmem] * (len(amps) + 2),
         out_specs=pl.BlockSpec(memory_space=pltpu.HBM),
         scratch_shapes=[
-            pltpu.VMEM((rows, depth), far.dtype),
+            pltpu.VMEM((rows, depth), block.dtype),
             pltpu.VMEM((rows, n_cols), total.dtype),
             pltpu.SemaphoreType.DMA((n_cols // (2 * width),)),
         ],
@@ -251,7 +253,7 @@
             transcendentals=0,
         ),
         name="far_half",
-    )(*amps, total, far)
+    )(*amps, total, block)
 
 
 def exchange(x, axis, flip):
@@ -272,7 +274,7 @@
     outgoing = list(pack(col, packed_tiles, tile_ids, n_col, capacity))
 
     amps = {0: amplitudes}
-    for s in [*range(1, inner), *range(inner, half, inner), half]:
+    for s in [half, *range(inner, half, inner), *range(1, inner)]:
         amps[s] = exchange(amplitudes, "col", s)
     outgoing[half:], amps = tie(outgoing[half:], amps)
 
@@ -287,13 +289,21 @@
 
     early = [s for s in amps if s and (s < half or half < s < half + inner)]
     late = [flip ^ half for flip in range(inner, half, inner)]
+    flips = range(CORES, n_row, CORES)
+    far_groups = [join(chunks[half:])]
+    near_group = join(chunks[:half])
+    far_passed = [[exchange(g, "row", flip) for flip in flips] for g in far_groups]
+    near_passed = [exchange(near_group, "row", flip) for flip in flips]
+    near_passed, got = tie(near_passed, [amps[s] for s in late])
+    amps.update(zip(late, got))
+    far_passed, got = tie(far_passed, [amps[s] for s in early])
+    amps.update(zip(early, got))
     pieces, rows = [], []
-    for group in (join(chunks[half:]), join(chunks[:half])):
-        passed = [exchange(group, "row", flip) for flip in range(CORES, n_row, CORES)]
-        due = late if pieces else early
-        passed, got = tie(passed, [amps[s] for s in due])
-        amps.update(zip(due, got))
-        own, passed = tie(group, passed)
+    for held, passed in (
+        (far_groups[0], far_passed[0]),
+        (near_group, near_passed),
+    ):
+        own, passed = tie(held, passed)
         for flip, mine in zip(range(0, n_row, CORES), [own, *passed]):
             pieces += [mine, exchange(mine, "row", 1)]
             rows += [row ^ flip, row ^ flip ^ 1]

time: 44 us -> 44 us (level)
  Pallas kernels: 6.84 us -> 6.09 us
  waiting for transfers between devices: 9.71 us -> 10.4 us
    ppermute x20, waiting for transfers between devices: 9.71 us -> 10.4 us  [exchange(): return lax.ppermute(x, axis, [(i, i ^ flip) for i in range(size)])]
    pallas_call x1, Pallas kernels: 3.69 us -> 2.95 us  [near_half(): pl.pallas_call(functools.partial(near_kernel, n_pieces, offsets, capacity...]
  transfers between devices with their start and end apart: 20 -> 20, of which waited for: 7 -> 7; matrix products, arithmetic and copies ran while one was open for 0% -> 0% of each run, Pallas kernels for 11% -> 10%
where the time goes in v8:
time: 44 us; the launch traced here: 43.8 us
  starting transfers between devices  27.1 us (62%)
  waiting for transfers between devices  10.4 us (24%)
  Pallas kernels  6.09 us (14%)
    ppermute x20, starting transfers between devices, exchange(): return lax.ppermute(x, axis, [(i, i ^ flip) for i in range(size)])  27.1 us
    ppermute x20, waiting for transfers between devices, exchange(): return lax.ppermute(x, axis, [(i, i ^ flip) for i in range(size)])  10.4 us
    pallas_call x1, Pallas kernels, near_half(): pl.pallas_call(functools.partial(near_kernel, n_pieces, offsets, capacity...  2.95 us
    pallas_call x1, Pallas kernels, far_half(): pl.pallas_call(functools.partial(far_kernel, offsets, depth // width), ou...  1.85 us
    pallas_call x1, Pallas kernels, pack(): pl.pallas_call(functools.partial(pack_kernel, columns, capacity), out_sha...  1.25 us
  transfers between devices with their start and end apart: 20, of which 7 were waited for; matrix products, arithmetic and copies ran while one was open for 0% of the time, Pallas kernels for 10%

profile of v8, /device:TPU:0, one launch (start us, length us, event | category | flops | bytes accessed | tf_op | source)
XLA Modules:
  0.0 43.8 jit_solution(8821597820528729183)
XLA Ops:
  0.0 2.9 %collective-permute-start = (bf16[512,128]{1,0:T(8,128)(2,1)}, bf16[512,128]{1,0:T(8,128)(2,1)S(1)}, u32[]{:S(2)}, u32[]{:S(2)}) collective-permute-start(bf16[512,128]{1,0:T(8,128)(2,1)} %refs_11_.1), channel_id=1, source_target_pairs={{0,1},{1,0},{2,3},{3,2},{4,5},{5,4},{6,7},{7,6},{8,9},{9,8},{10,11... | collective-permute-start | bytes 393224 | tf_op jit(solution)/shard_map/ppermute | solution.py:261
  2.9 1.6 %collective-permute-start.1 = (bf16[512,128]{1,0:T(8,128)(2,1)}, bf16[512,128]{1,0:T(8,128)(2,1)S(1)}, u32[]{:S(2)}, u32[]{:S(2)}) collective-permute-start(bf16[512,128]{1,0:T(8,128)(2,1)} %refs_11_.1), channel_id=1, source_target_pairs={{0,2},{1,3},{2,0},{3,1},{4,6},{5,7},{6,4},{7,5},{8,10},{9,11},{10,... | collective-permute-start | bytes 393224 | tf_op jit(solution)/shard_map/ppermute | solution.py:261
  4.5 2.6 %collective-permute-start.2 = (bf16[512,128]{1,0:T(8,128)(2,1)}, bf16[512,128]{1,0:T(8,128)(2,1)S(1)}, u32[]{:S(2)}, u32[]{:S(2)}) collective-permute-start(bf16[512,128]{1,0:T(8,128)(2,1)} %refs_11_.1), channel_id=1, source_target_pairs={{0,4},{1,5},{2,6},{3,7},{4,0},{5,1},{6,2},{7,3},{8,12},{9,13},{10,... | collective-permute-start | bytes 393224 | tf_op jit(solution)/shard_map/ppermute | solution.py:261
  7.1 1.3 %pack.1 = (bf16[272,128]{1,0:T(8,128)(2,1)S(1)}, bf16[272,128]{1,0:T(8,128)(2,1)S(1)}, bf16[272,128]{1,0:T(8,128)(2,1)S(1)}, bf16[272,128]{1,0:T(8,128)(2,1)S(1)...) custom-call(s32[1]{0:T(128)} %bitcast.me_ref, ...), custom_call_target="tpu_custom_call" | custom-call | tf_op jit(solution)/shard_map/pack/pallas_call | solution.py:63
  8.4 0.6 %collective-permute-start.10 = (bf16[1,272,128]{2,1,0:T(8,128)(2,1)S(1)}, bf16[1,272,128]{2,1,0:T(8,128)(2,1)S(1)}, u32[]{:S(2)}, u32[]{:S(2)}) collective-permute-start(bf16[1,272,128]{2,1,0:T(8,128)(2,1)S(1)} %bitcast.20), channel_id=1, source_target_pairs={{0,1},{1,0},{2,3},{3,2},{4,5},{5,4},{6,7},{7,6},{8,9},{9,8},{10,11... | collective-permute-start | bytes 208904 | tf_op jit(solution)/shard_map/ppermute | solution.py:261
  9.4 2.5 %collective-permute-start.12 = (bf16[1,272,128]{2,1,0:T(8,128)(2,1)S(1)}, bf16[1,272,128]{2,1,0:T(8,128)(2,1)S(1)}, u32[]{:S(2)}, u32[]{:S(2)}) collective-permute-start(bf16[1,272,128]{2,1,0:T(8,128)(2,1)S(1)} %bitcast.18), channel_id=1, source_target_pairs={{0,3},{1,2},{2,1},{3,0},{4,7},{5,6},{6,5},{7,4},{8,11},{9,10},{10,... | collective-permute-start | bytes 208904 | tf_op jit(solution)/shard_map/ppermute | solution.py:261
  11.9 2.4 %collective-permute-start.3 = (bf16[1,272,128]{2,1,0:T(8,128)(2,1)S(1)}, bf16[1,272,128]{2,1,0:T(8,128)(2,1)S(1)}, u32[]{:S(2)}, u32[]{:S(2)}) collective-permute-start(bf16[1,272,128]{2,1,0:T(8,128)(2,1)S(1)} %bitcast.17), channel_id=1, source_target_pairs={{0,4},{1,5},{2,6},{3,7},{4,0},{5,1},{6,2},{7,3},{8,12},{9,13},{10,... | collective-permute-start | bytes 208904 | tf_op jit(solution)/shard_map/ppermute | solution.py:261
  14.4 0.5 %collective-permute-start.4 = (bf16[1,272,128]{2,1,0:T(8,128)(2,1)S(1)}, bf16[1,272,128]{2,1,0:T(8,128)(2,1)S(1)}, u32[]{:S(2)}, u32[]{:S(2)}) collective-permute-start(bf16[1,272,128]{2,1,0:T(8,128)(2,1)S(1)} %bitcast.16), channel_id=1, source_target_pairs={{0,5},{1,4},{2,7},{3,6},{4,1},{5,0},{6,3},{7,2},{8,13},{9,12},{10,... | collective-permute-start | bytes 208904 | tf_op jit(solution)/shard_map/ppermute | solution.py:261
  14.8 4.6 %collective-permute-start.5 = (bf16[1,272,128]{2,1,0:T(8,128)(2,1)S(1)}, bf16[1,272,128]{2,1,0:T(8,128)(2,1)S(1)}, u32[]{:S(2)}, u32[]{:S(2)}) collective-permute-start(bf16[1,272,128]{2,1,0:T(8,128)(2,1)S(1)} %bitcast.15), channel_id=1, source_target_pairs={{0,6},{1,7},{2,4},{3,5},{4,2},{5,3},{6,0},{7,1},{8,14},{9,15},{10,... | collective-permute-start | bytes 208904 | tf_op jit(solution)/shard_map/ppermute | solution.py:261
  19.4 1.0 %collective-permute-start.6 = (bf16[1,272,128]{2,1,0:T(8,128)(2,1)S(1)}, bf16[1,272,128]{2,1,0:T(8,128)(2,1)S(1)}, u32[]{:S(2)}, u32[]{:S(2)}) collective-permute-start(bf16[1,272,128]{2,1,0:T(8,128)(2,1)S(1)} %bitcast.14), channel_id=1, source_target_pairs={{0,7},{1,6},{2,5},{3,4},{4,3},{5,2},{6,1},{7,0},{8,15},{9,14},{10,... | collective-permute-start | bytes 208904 | tf_op jit(solution)/shard_map/ppermute | solution.py:261
  20.4 1.6 %collective-permute-start.13 = (bf16[4,272,128]{2,1,0:T(8,128)(2,1)S(1)}, bf16[4,272,128]{2,1,0:T(8,128)(2,1)S(1)}, u32[]{:S(2)}, u32[]{:S(2)}) collective-permute-start(bf16[4,272,128]{2,1,0:T(8,128)(2,1)S(1)} %join.3.refs_4_), channel_id=1, source_target_pairs={{0,16},{8,24},{16,0},{24,8},{1,17},{9,25},{17,1},{25,9},{2,18},{10... | collective-permute-start | bytes 835592 | tf_op jit(solution)/shard_map/ppermute | solution.py:261
  22.0 1.8 %collective-permute-done.4.refs_1_ = bf16[1,272,128]{2,1,0:T(8,128)(2,1)S(1)} collective-permute-done((bf16[1,272,128]{2,1,0:T(8,128)(2,1)S(1)}, bf16[1,272,128]{2,1,0:T(8,128)(2,1)S(1)}, u32[]{:S(2)}, u32[]{:S(2)}) %collective-permute-start.4) | collective-permute-done | bytes 69664 | tf_op jit(solution)/shard_map/ppermute | solution.py:261
  23.8 2.7 %collective-permute-done.6.refs_3_ = bf16[1,272,128]{2,1,0:T(8,128)(2,1)S(1)} collective-permute-done((bf16[1,272,128]{2,1,0:T(8,128)(2,1)S(1)}, bf16[1,272,128]{2,1,0:T(8,128)(2,1)S(1)}, u32[]{:S(2)}, u32[]{:S(2)}) %collective-permute-start.6) | collective-permute-done | bytes 69664 | tf_op jit(solution)/shard_map/ppermute | solution.py:261
  26.5 1.6 %collective-permute-start.7 = (bf16[4,272,128]{2,1,0:T(8,128)(2,1)S(1)}, bf16[4,272,128]{2,1,0:T(8,128)(2,1)S(1)}, u32[]{:S(2)}, u32[]{:S(2)}) collective-permute-start(bf16[4,272,128]{2,1,0:T(8,128)(2,1)S(1)} %join.2.refs_0_), channel_id=1, source_target_pairs={{0,16},{8,24},{16,0},{24,8},{1,17},{9,25},{17,1},{25,9},{2,18},{10... | collective-permute-start | bytes 835592 | tf_op jit(solution)/shard_map/ppermute | solution.py:261
  28.1 1.2 %collective-permute-start.14 = (bf16[512,128]{1,0:T(8,128)(2,1)S(1)}, bf16[512,128]{1,0:T(8,128)(2,1)S(1)}, u32[]{:S(2)}, u32[]{:S(2)}) collective-permute-start(bf16[512,128]{1,0:T(8,128)(2,1)S(1)} %collective-permute-done.1.refs_9_), channel_id=1, source_target_pairs={{0,4},{1,5},{2,6},{3,7},{4,0},{5,1},{6,2},{7,3},{8,12},{9,13},{10,... | collective-permute-start | bytes 393224 | tf_op jit(solution)/shard_map/ppermute | solution.py:261
  29.3 0.8 %collective-permute-start.8 = (bf16[512,128]{1,0:T(8,128)(2,1)S(1)}, bf16[512,128]{1,0:T(8,128)(2,1)S(1)}, u32[]{:S(2)}, u32[]{:S(2)}) collective-permute-start(bf16[512,128]{1,0:T(8,128)(2,1)S(1)} %collective-permute-done.1.refs_9_), channel_id=1, source_target_pairs={{0,1},{1,0},{2,3},{3,2},{4,5},{5,4},{6,7},{7,6},{8,9},{9,8},{10,11... | collective-permute-start | bytes 393224 | tf_op jit(solution)/shard_map/ppermute | solution.py:261
  30.1 1.2 %collective-permute-start.9 = (bf16[512,128]{1,0:T(8,128)(2,1)S(1)}, bf16[512,128]{1,0:T(8,128)(2,1)S(1)}, u32[]{:S(2)}, u32[]{:S(2)}) collective-permute-start(bf16[512,128]{1,0:T(8,128)(2,1)S(1)} %collective-permute-done.2.refs_0_), channel_id=1, source_target_pairs={{0,1},{1,0},{2,3},{3,2},{4,5},{5,4},{6,7},{7,6},{8,9},{9,8},{10,11... | collective-permute-start | bytes 393224 | tf_op jit(solution)/shard_map/ppermute | solution.py:261
  31.3 4.0 %collective-permute-done.14.refs_2_ = bf16[512,128]{1,0:T(8,128)(2,1)S(1)} collective-permute-done((bf16[512,128]{1,0:T(8,128)(2,1)S(1)}, bf16[512,128]{1,0:T(8,128)(2,1)S(1)}, u32[]{:S(2)}, u32[]{:S(2)}) %collective-permute-start.14) | collective-permute-done | bytes 131104 | tf_op jit(solution)/shard_map/ppermute | solution.py:261
  35.4 0.5 %collective-permute-start.19 = (bf16[4,272,128]{2,1,0:T(8,128)(2,1)S(1)}, bf16[4,272,128]{2,1,0:T(8,128)(2,1)S(1)}, u32[]{:S(2)}, u32[]{:S(2)}) collective-permute-start(bf16[4,272,128]{2,1,0:T(8,128)(2,1)S(1)} %collective-permute-done.13.refs_6_), channel_id=1, source_target_pairs={{0,8},{8,0},{16,24},{24,16},{1,9},{9,1},{17,25},{25,17},{2,10},{10... | collective-permute-start | bytes 835592 | tf_op jit(solution)/shard_map/ppermute | solution.py:261
  36.0 0.5 %collective-permute-start.17 = (bf16[4,272,128]{2,1,0:T(8,128)(2,1)S(1)}, bf16[4,272,128]{2,1,0:T(8,128)(2,1)S(1)}, u32[]{:S(2)}, u32[]{:S(2)}) collective-permute-start(bf16[4,272,128]{2,1,0:T(8,128)(2,1)S(1)} %collective-permute-done.7.refs_2_), channel_id=1, source_target_pairs={{0,8},{8,0},{16,24},{24,16},{1,9},{9,1},{17,25},{25,17},{2,10},{10... | collective-permute-start | bytes 835592 | tf_op jit(solution)/shard_map/ppermute | solution.py:261
  36.5 0.6 %collective-permute-start.15 = (bf16[512,128]{1,0:T(8,128)(2,1)S(1)}, bf16[512,128]{1,0:T(8,128)(2,1)S(1)}, u32[]{:S(2)}, u32[]{:S(2)}) collective-permute-start(bf16[512,128]{1,0:T(8,128)(2,1)S(1)} %collective-permute-done.14.refs_2_), channel_id=1, source_target_pairs={{0,1},{1,0},{2,3},{3,2},{4,5},{5,4},{6,7},{7,6},{8,9},{9,8},{10,11... | collective-permute-start | bytes 393224 | tf_op jit(solution)/shard_map/ppermute | solution.py:261
  38.1 3.0 %near_half.1 = (f32[512,1024]{1,0:T(8,128)S(1)}, bf16[1024,1024]{1,0:T(8,128)(2,1)S(1)}) custom-call(s32[9]{0:T(128)S(1)} %stack.24.where_ref, bf16[4,272,128]{2,1,0:T(8,128)(2,1)S(1)} %join.2.refs_0_, bf16[4,272,128]{2,1,0:T(8,128)(2,1)S(1)} %collective-permute-done.16.refs_1_, bf16[4,272,128]{2,1,0:T(8,128)(2,1)S(1)} %collective-permute-done.7.refs_2_, ...), custom_call_target="tpu_custom_call" | custom-call | flops 536870912 | bytes 8388608 | tf_op jit(solution)/shard_map/near_half/pallas_call | solution.py:189
  41.1 0.9 %collective-permute-done.15.refs_3_ = bf16[512,128]{1,0:T(8,128)(2,1)S(1)} collective-permute-done((bf16[512,128]{1,0:T(8,128)(2,1)S(1)}, bf16[512,128]{1,0:T(8,128)(2,1)S(1)}, u32[]{:S(2)}, u32[]{:S(2)}) %collective-permute-start.15) | collective-permute-done | bytes 131104 | tf_op jit(solution)/shard_map/ppermute | solution.py:261
  42.0 1.8 %far_half.1 = f32[512,1024]{1,0:T(8,128)} custom-call(bf16[512,128]{1,0:T(8,128)(2,1)S(1)} %collective-permute-done.2.refs_0_, bf16[512,128]{1,0:T(8,128)(2,1)S(1)} %collective-permute-done.9.refs_1_, bf16[512,128]{1,0:T(8,128)(2,1)S(1)} %collective-permute-done.14.refs_2_, bf16[512,128]{1,0:T(8,128)(2,1)S(1)} %collective-permute-done.15.refs_3_, ...), custom_call_target="tpu_custom_call" | custom-call | flops 536870912 | bytes 8388608 | tf_op jit(solution)/shard_map/far_half/pallas_call | solution.py:239
  (22 shorter events, 1.7 us)
Async XLA Ops:
  0.0 9.4 %collective-permute-start = (bf16[512,128]{1,0:T(8,128)(2,1)}, bf16[512,128]{1,0:T(8,128)(2,1)S(1)}, u32[]{:S(2)}, u32[]{:S(2)}) collective-permute-start(bf16[512,128]{1,0:T(8,128)(2,1)} %refs_11_.1), channel_id=1, source_target_pairs={{0,1},{1,0},{2,3},{3,2},{4,5},{5,4},{6,7},{7,6},{8,9},{9,8},{10,11... | collective-permute-start | bytes 393224 | tf_op jit(solution)/shard_map/ppermute | solution.py:261
  2.9 9.0 %collective-permute-start.1 = (bf16[512,128]{1,0:T(8,128)(2,1)}, bf16[512,128]{1,0:T(8,128)(2,1)S(1)}, u32[]{:S(2)}, u32[]{:S(2)}) collective-permute-start(bf16[512,128]{1,0:T(8,128)(2,1)} %refs_11_.1), channel_id=1, source_target_pairs={{0,2},{1,3},{2,0},{3,1},{4,6},{5,7},{6,4},{7,5},{8,10},{9,11},{10,... | collective-permute-start | bytes 393224 | tf_op jit(solution)/shard_map/ppermute | solution.py:261
  4.5 7.4 %collective-permute-start.2 = (bf16[512,128]{1,0:T(8,128)(2,1)}, bf16[512,128]{1,0:T(8,128)(2,1)S(1)}, u32[]{:S(2)}, u32[]{:S(2)}) collective-permute-start(bf16[512,128]{1,0:T(8,128)(2,1)} %refs_11_.1), channel_id=1, source_target_pairs={{0,4},{1,5},{2,6},{3,7},{4,0},{5,1},{6,2},{7,3},{8,12},{9,13},{10,... | collective-permute-start | bytes 393224 | tf_op jit(solution)/shard_map/ppermute | solution.py:261
  8.4 6.5 %collective-permute-start.10 = (bf16[1,272,128]{2,1,0:T(8,128)(2,1)S(1)}, bf16[1,272,128]{2,1,0:T(8,128)(2,1)S(1)}, u32[]{:S(2)}, u32[]{:S(2)}) collective-permute-start(bf16[1,272,128]{2,1,0:T(8,128)(2,1)S(1)} %bitcast.20), channel_id=1, source_target_pairs={{0,1},{1,0},{2,3},{3,2},{4,5},{5,4},{6,7},{7,6},{8,9},{9,8},{10,11... | collective-permute-start | bytes 208904 | tf_op jit(solution)/shard_map/ppermute | solution.py:261
  9.0 10.4 %collective-permute-start.11 = (bf16[1,272,128]{2,1,0:T(8,128)(2,1)S(1)}, bf16[1,272,128]{2,1,0:T(8,128)(2,1)S(1)}, u32[]{:S(2)}, u32[]{:S(2)}) collective-permute-start(bf16[1,272,128]{2,1,0:T(8,128)(2,1)S(1)} %bitcast.19), channel_id=1, source_target_pairs={{0,2},{1,3},{2,0},{3,1},{4,6},{5,7},{6,4},{7,5},{8,10},{9,11},{10,... | collective-permute-start | bytes 208904 | tf_op jit(solution)/shard_map/ppermute | solution.py:261
  9.4 11.0 %collective-permute-start.12 = (bf16[1,272,128]{2,1,0:T(8,128)(2,1)S(1)}, bf16[1,272,128]{2,1,0:T(8,128)(2,1)S(1)}, u32[]{:S(2)}, u32[]{:S(2)}) collective-permute-start(bf16[1,272,128]{2,1,0:T(8,128)(2,1)S(1)} %bitcast.18), channel_id=1, source_target_pairs={{0,3},{1,2},{2,1},{3,0},{4,7},{5,6},{6,5},{7,4},{8,11},{9,10},{10,... | collective-permute-start | bytes 208904 | tf_op jit(solution)/shard_map/ppermute | solution.py:261
  11.9 10.1 %collective-permute-start.3 = (bf16[1,272,128]{2,1,0:T(8,128)(2,1)S(1)}, bf16[1,272,128]{2,1,0:T(8,128)(2,1)S(1)}, u32[]{:S(2)}, u32[]{:S(2)}) collective-permute-start(bf16[1,272,128]{2,1,0:T(8,128)(2,1)S(1)} %bitcast.17), channel_id=1, source_target_pairs={{0,4},{1,5},{2,6},{3,7},{4,0},{5,1},{6,2},{7,3},{8,12},{9,13},{10,... | collective-permute-start | bytes 208904 | tf_op jit(solution)/shard_map/ppermute | solution.py:261
  14.4 9.4 %collective-permute-start.4 = (bf16[1,272,128]{2,1,0:T(8,128)(2,1)S(1)}, bf16[1,272,128]{2,1,0:T(8,128)(2,1)S(1)}, u32[]{:S(2)}, u32[]{:S(2)}) collective-permute-start(bf16[1,272,128]{2,1,0:T(8,128)(2,1)S(1)} %bitcast.16), channel_id=1, source_target_pairs={{0,5},{1,4},{2,7},{3,6},{4,1},{5,0},{6,3},{7,2},{8,13},{9,12},{10,... | collective-permute-start | bytes 208904 | tf_op jit(solution)/shard_map/ppermute | solution.py:261
  14.8 9.0 %collective-permute-start.5 = (bf16[1,272,128]{2,1,0:T(8,128)(2,1)S(1)}, bf16[1,272,128]{2,1,0:T(8,128)(2,1)S(1)}, u32[]{:S(2)}, u32[]{:S(2)}) collective-permute-start(bf16[1,272,128]{2,1,0:T(8,128)(2,1)S(1)} %bitcast.15), channel_id=1, source_target_pairs={{0,6},{1,7},{2,4},{3,5},{4,2},{5,3},{6,0},{7,1},{8,14},{9,15},{10,... | collective-permute-start | bytes 208904 | tf_op jit(solution)/shard_map/ppermute | solution.py:261
  19.4 7.1 %collective-permute-start.6 = (bf16[1,272,128]{2,1,0:T(8,128)(2,1)S(1)}, bf16[1,272,128]{2,1,0:T(8,128)(2,1)S(1)}, u32[]{:S(2)}, u32[]{:S(2)}) collective-permute-start(bf16[1,272,128]{2,1,0:T(8,128)(2,1)S(1)} %bitcast.14), channel_id=1, source_target_pairs={{0,7},{1,6},{2,5},{3,4},{4,3},{5,2},{6,1},{7,0},{8,15},{9,14},{10,... | collective-permute-start | bytes 208904 | tf_op jit(solution)/shard_map/ppermute | solution.py:261
  20.4 15.0 %collective-permute-start.13 = (bf16[4,272,128]{2,1,0:T(8,128)(2,1)S(1)}, bf16[4,272,128]{2,1,0:T(8,128)(2,1)S(1)}, u32[]{:S(2)}, u32[]{:S(2)}) collective-permute-start(bf16[4,272,128]{2,1,0:T(8,128)(2,1)S(1)} %join.3.refs_4_), channel_id=1, source_target_pairs={{0,16},{8,24},{16,0},{24,8},{1,17},{9,25},{17,1},{25,9},{2,18},{10... | collective-permute-start | bytes 835592 | tf_op jit(solution)/shard_map/ppermute | solution.py:261
  26.5 9.4 %collective-permute-start.7 = (bf16[4,272,128]{2,1,0:T(8,128)(2,1)S(1)}, bf16[4,272,128]{2,1,0:T(8,128)(2,1)S(1)}, u32[]{:S(2)}, u32[]{:S(2)}) collective-permute-start(bf16[4,272,128]{2,1,0:T(8,128)(2,1)S(1)} %join.2.refs_0_), channel_id=1, source_target_pairs={{0,16},{8,24},{16,0},{24,8},{1,17},{9,25},{17,1},{25,9},{2,18},{10... | collective-permute-start | bytes 835592 | tf_op jit(solution)/shard_map/ppermute | solution.py:261
  28.1 7.3 %collective-permute-start.14 = (bf16[512,128]{1,0:T(8,128)(2,1)S(1)}, bf16[512,128]{1,0:T(8,128)(2,1)S(1)}, u32[]{:S(2)}, u32[]{:S(2)}) collective-permute-start(bf16[512,128]{1,0:T(8,128)(2,1)S(1)} %collective-permute-done.1.refs_9_), channel_id=1, source_target_pairs={{0,4},{1,5},{2,6},{3,7},{4,0},{5,1},{6,2},{7,3},{8,12},{9,13},{10,... | collective-permute-start | bytes 393224 | tf_op jit(solution)/shard_map/ppermute | solution.py:261
  29.3 6.6 %collective-permute-start.8 = (bf16[512,128]{1,0:T(8,128)(2,1)S(1)}, bf16[512,128]{1,0:T(8,128)(2,1)S(1)}, u32[]{:S(2)}, u32[]{:S(2)}) collective-permute-start(bf16[512,128]{1,0:T(8,128)(2,1)S(1)} %collective-permute-done.1.refs_9_), channel_id=1, source_target_pairs={{0,1},{1,0},{2,3},{3,2},{4,5},{5,4},{6,7},{7,6},{8,9},{9,8},{10,11... | collective-permute-start | bytes 393224 | tf_op jit(solution)/shard_map/ppermute | solution.py:261
  30.1 5.8 %collective-permute-start.9 = (bf16[512,128]{1,0:T(8,128)(2,1)S(1)}, bf16[512,128]{1,0:T(8,128)(2,1)S(1)}, u32[]{:S(2)}, u32[]{:S(2)}) collective-permute-start(bf16[512,128]{1,0:T(8,128)(2,1)S(1)} %collective-permute-done.2.refs_0_), channel_id=1, source_target_pairs={{0,1},{1,0},{2,3},{3,2},{4,5},{5,4},{6,7},{7,6},{8,9},{9,8},{10,11... | collective-permute-start | bytes 393224 | tf_op jit(solution)/shard_map/ppermute | solution.py:261
  35.4 1.8 %collective-permute-start.18 = (bf16[4,272,128]{2,1,0:T(8,128)(2,1)S(1)}, bf16[4,272,128]{2,1,0:T(8,128)(2,1)S(1)}, u32[]{:S(2)}, u32[]{:S(2)}) collective-permute-start(bf16[4,272,128]{2,1,0:T(8,128)(2,1)S(1)} %join.3.refs_4_), channel_id=1, source_target_pairs={{0,8},{8,0},{16,24},{24,16},{1,9},{9,1},{17,25},{25,17},{2,10},{10... | collective-permute-start | bytes 835592 | tf_op jit(solution)/shard_map/ppermute | solution.py:261
  35.4 2.0 %collective-permute-start.19 = (bf16[4,272,128]{2,1,0:T(8,128)(2,1)S(1)}, bf16[4,272,128]{2,1,0:T(8,128)(2,1)S(1)}, u32[]{:S(2)}, u32[]{:S(2)}) collective-permute-start(bf16[4,272,128]{2,1,0:T(8,128)(2,1)S(1)} %collective-permute-done.13.refs_6_), channel_id=1, source_target_pairs={{0,8},{8,0},{16,24},{24,16},{1,9},{9,1},{17,25},{25,17},{2,10},{10... | collective-permute-start | bytes 835592 | tf_op jit(solution)/shard_map/ppermute | solution.py:261
  35.9 1.8 %collective-permute-start.16 = (bf16[4,272,128]{2,1,0:T(8,128)(2,1)S(1)}, bf16[4,272,128]{2,1,0:T(8,128)(2,1)S(1)}, u32[]{:S(2)}, u32[]{:S(2)}) collective-permute-start(bf16[4,272,128]{2,1,0:T(8,128)(2,1)S(1)} %join.2.refs_0_), channel_id=1, source_target_pairs={{0,8},{8,0},{16,24},{24,16},{1,9},{9,1},{17,25},{25,17},{2,10},{10... | collective-permute-start | bytes 835592 | tf_op jit(solution)/shard_map/ppermute | solution.py:261
  36.0 2.2 %collective-permute-start.17 = (bf16[4,272,128]{2,1,0:T(8,128)(2,1)S(1)}, bf16[4,272,128]{2,1,0:T(8,128)(2,1)S(1)}, u32[]{:S(2)}, u32[]{:S(2)}) collective-permute-start(bf16[4,272,128]{2,1,0:T(8,128)(2,1)S(1)} %collective-permute-done.7.refs_2_), channel_id=1, source_target_pairs={{0,8},{8,0},{16,24},{24,16},{1,9},{9,1},{17,25},{25,17},{2,10},{10... | collective-permute-start | bytes 835592 | tf_op jit(solution)/shard_map/ppermute | solution.py:261
  36.5 5.5 %collective-permute-start.15 = (bf16[512,128]{1,0:T(8,128)(2,1)S(1)}, bf16[512,128]{1,0:T(8,128)(2,1)S(1)}, u32[]{:S(2)}, u32[]{:S(2)}) collective-permute-start(bf16[512,128]{1,0:T(8,128)(2,1)S(1)} %collective-permute-done.14.refs_2_), channel_id=1, source_target_pairs={{0,1},{1,0},{2,3},{3,2},{4,5},{5,4},{6,7},{7,6},{8,9},{9,8},{10,11... | collective-permute-start | bytes 393224 | tf_op jit(solution)/shard_map/ppermute | solution.py:261

commit v9 on v8

--- a/solution.py
+++ b/solution.py
@@ -13,6 +13,8 @@
 CORES = 2
 META = 16
 MIB = 1024 * 1024
+WEIGHT = 10**9
+WEIGHT_FAR = 4 * 10**9
 
 
 def pack_kernel(columns, capacity, me_ref, ids_hbm, tiles_hbm, *refs):
@@ -90,7 +92,7 @@
         at += part.shape[0]
 
 
-def join(chunks):
+def join(chunks, flops=0):
     vmem = pl.BlockSpec(memory_space=pltpu.VMEM)
     total = sum(c.shape[0] for c in chunks)
     return pl.pallas_call(
@@ -99,6 +101,7 @@
         in_specs=[vmem] * len(chunks),
         out_specs=vmem,
         compiler_params=pltpu.CompilerParams(vmem_limit_bytes=8 * MIB),
+        cost_estimate=pl.CostEstimate(flops=flops, bytes_accessed=0, transcendentals=0),
         name="join",
     )(*chunks)
 
@@ -274,7 +277,7 @@
     outgoing = list(pack(col, packed_tiles, tile_ids, n_col, capacity))
 
     amps = {0: amplitudes}
-    for s in [half, *range(inner, half, inner), *range(1, inner)]:
+    for s in [*range(1, inner), *range(inner, half, inner), half]:
         amps[s] = exchange(amplitudes, "col", s)
     outgoing[half:], amps = tie(outgoing[half:], amps)
 
@@ -288,19 +291,17 @@
         amps[half ^ lane] = exchange(amps[half], "col", lane)
 
     early = [s for s in amps if s and (s < half or half < s < half + inner)]
-    late = [flip ^ half for flip in range(inner, half, inner)]
     flips = range(CORES, n_row, CORES)
-    far_groups = [join(chunks[half:])]
+    cut = half + half // 2
+    far_groups = [join(chunks[half:cut], WEIGHT), join(chunks[cut:], WEIGHT)]
     near_group = join(chunks[:half])
     far_passed = [[exchange(g, "row", flip) for flip in flips] for g in far_groups]
     near_passed = [exchange(near_group, "row", flip) for flip in flips]
-    near_passed, got = tie(near_passed, [amps[s] for s in late])
-    amps.update(zip(late, got))
     far_passed, got = tie(far_passed, [amps[s] for s in early])
     amps.update(zip(early, got))
     pieces, rows = [], []
     for held, passed in (
-        (far_groups[0], far_passed[0]),
+        (join(far_groups), [join(x) for x in zip(*far_passed)]),
         (near_group, near_passed),
     ):
         own, passed = tie(held, passed)
@@ -308,8 +309,9 @@
             pieces += [mine, exchange(mine, "row", 1)]
             rows += [row ^ flip, row ^ flip ^ 1]
     for flip in range(half + inner, n_col, inner):
+        there = join([amps[flip]], WEIGHT_FAR)
         for lane in range(1, inner):
-            amps[flip ^ lane] = exchange(amps[flip], "col", lane)
+            amps[flip ^ lane] = exchange(there, "col", lane)
 
     where = jnp.stack(rows + [col]).astype(jnp.int32)
     near = [s for s in sorted(amps) if 0 < s < half]

time: 44 us -> 43 us (0.977)
  waiting for transfers between devices: 10.4 us -> 9.73 us
    ppermute x20 -> x21, waiting for transfers between devices: 10.4 us -> 9.73 us  [exchange(): return lax.ppermute(x, axis, [(i, i ^ flip) for i in range(size)])]
    ppermute x20 -> x21, starting transfers between devices: 27.1 us -> 26.8 us  [exchange(): return lax.ppermute(x, axis, [(i, i ^ flip) for i in range(size)])]
  transfers between devices with their start and end apart: 20 -> 21, of which waited for: 7 -> 6; matrix products, arithmetic and copies ran while one was open for 0% -> 0% of each run, Pallas kernels for 10% -> 10%
where the time goes in v9:
time: 43 us; the launch traced here: 42.9 us
  starting transfers between devices  26.8 us (62%)
  waiting for transfers between devices  9.73 us (23%)
  Pallas kernels  6.15 us (14%)
    ppermute x21, starting transfers between devices, exchange(): return lax.ppermute(x, axis, [(i, i ^ flip) for i in range(size)])  26.8 us
    ppermute x21, waiting for transfers between devices, exchange(): return lax.ppermute(x, axis, [(i, i ^ flip) for i in range(size)])  9.73 us
    pallas_call x1, Pallas kernels, near_half(): pl.pallas_call(functools.partial(near_kernel, n_pieces, offsets, capacity...  2.96 us
    pallas_call x1, Pallas kernels, far_half(): pl.pallas_call(functools.partial(far_kernel, offsets, depth // width), ou...  1.85 us
    pallas_call x1, Pallas kernels, pack(): pl.pallas_call(functools.partial(pack_kernel, columns, capacity), out_sha...  1.25 us
  transfers between devices with their start and end apart: 21, of which 6 were waited for; matrix products, arithmetic and copies ran while one was open for 0% of the time, Pallas kernels for 10%

profile of v9, /device:TPU:0, one launch (start us, length us, event | category | flops | bytes accessed | tf_op | source)
XLA Modules:
  0.0 42.9 jit_solution(5768908797290238997)
XLA Ops:
  0.0 2.9 %collective-permute-start = (bf16[512,128]{1,0:T(8,128)(2,1)}, bf16[512,128]{1,0:T(8,128)(2,1)S(1)}, u32[]{:S(2)}, u32[]{:S(2)}) collective-permute-start(bf16[512,128]{1,0:T(8,128)(2,1)} %refs_11_.1), channel_id=1, source_target_pairs={{0,1},{1,0},{2,3},{3,2},{4,5},{5,4},{6,7},{7,6},{8,9},{9,8},{10,11... | collective-permute-start | bytes 393224 | tf_op jit(solution)/shard_map/ppermute | solution.py:264
  2.9 1.6 %collective-permute-start.1 = (bf16[512,128]{1,0:T(8,128)(2,1)}, bf16[512,128]{1,0:T(8,128)(2,1)S(1)}, u32[]{:S(2)}, u32[]{:S(2)}) collective-permute-start(bf16[512,128]{1,0:T(8,128)(2,1)} %refs_11_.1), channel_id=1, source_target_pairs={{0,2},{1,3},{2,0},{3,1},{4,6},{5,7},{6,4},{7,5},{8,10},{9,11},{10,... | collective-permute-start | bytes 393224 | tf_op jit(solution)/shard_map/ppermute | solution.py:264
  4.5 2.6 %collective-permute-start.2 = (bf16[512,128]{1,0:T(8,128)(2,1)}, bf16[512,128]{1,0:T(8,128)(2,1)S(1)}, u32[]{:S(2)}, u32[]{:S(2)}) collective-permute-start(bf16[512,128]{1,0:T(8,128)(2,1)} %refs_11_.1), channel_id=1, source_target_pairs={{0,4},{1,5},{2,6},{3,7},{4,0},{5,1},{6,2},{7,3},{8,12},{9,13},{10,... | collective-permute-start | bytes 393224 | tf_op jit(solution)/shard_map/ppermute | solution.py:264
  7.1 1.3 %pack.1 = (bf16[272,128]{1,0:T(8,128)(2,1)S(1)}, bf16[272,128]{1,0:T(8,128)(2,1)S(1)}, bf16[272,128]{1,0:T(8,128)(2,1)S(1)}, bf16[272,128]{1,0:T(8,128)(2,1)S(1)...) custom-call(s32[1]{0:T(128)} %bitcast.me_ref, ...), custom_call_target="tpu_custom_call" | custom-call | tf_op jit(solution)/shard_map/pack/pallas_call | solution.py:65
  8.4 0.6 %collective-permute-start.15 = (bf16[1,272,128]{2,1,0:T(8,128)(2,1)S(1)}, bf16[1,272,128]{2,1,0:T(8,128)(2,1)S(1)}, u32[]{:S(2)}, u32[]{:S(2)}) collective-permute-start(bf16[1,272,128]{2,1,0:T(8,128)(2,1)S(1)} %bitcast.20), channel_id=1, source_target_pairs={{0,1},{1,0},{2,3},{3,2},{4,5},{5,4},{6,7},{7,6},{8,9},{9,8},{10,11... | collective-permute-start | bytes 208904 | tf_op jit(solution)/shard_map/ppermute | solution.py:264
  9.0 0.4 %collective-permute-start.16 = (bf16[1,272,128]{2,1,0:T(8,128)(2,1)S(1)}, bf16[1,272,128]{2,1,0:T(8,128)(2,1)S(1)}, u32[]{:S(2)}, u32[]{:S(2)}) collective-permute-start(bf16[1,272,128]{2,1,0:T(8,128)(2,1)S(1)} %bitcast.19), channel_id=1, source_target_pairs={{0,2},{1,3},{2,0},{3,1},{4,6},{5,7},{6,4},{7,5},{8,10},{9,11},{10,... | collective-permute-start | bytes 208904 | tf_op jit(solution)/shard_map/ppermute | solution.py:264
  9.4 2.5 %collective-permute-start.17 = (bf16[1,272,128]{2,1,0:T(8,128)(2,1)S(1)}, bf16[1,272,128]{2,1,0:T(8,128)(2,1)S(1)}, u32[]{:S(2)}, u32[]{:S(2)}) collective-permute-start(bf16[1,272,128]{2,1,0:T(8,128)(2,1)S(1)} %bitcast.18), channel_id=1, source_target_pairs={{0,3},{1,2},{2,1},{3,0},{4,7},{5,6},{6,5},{7,4},{8,11},{9,10},{10,... | collective-permute-start | bytes 208904 | tf_op jit(solution)/shard_map/ppermute | solution.py:264
  11.9 3.8 %collective-permute-start.6 = (bf16[1,272,128]{2,1,0:T(8,128)(2,1)S(1)}, bf16[1,272,128]{2,1,0:T(8,128)(2,1)S(1)}, u32[]{:S(2)}, u32[]{:S(2)}) collective-permute-start(bf16[1,272,128]{2,1,0:T(8,128)(2,1)S(1)} %bitcast.17), channel_id=1, source_target_pairs={{0,6},{1,7},{2,4},{3,5},{4,2},{5,3},{6,0},{7,1},{8,14},{9,15},{10,... | collective-permute-start | bytes 208904 | tf_op jit(solution)/shard_map/ppermute | solution.py:264
  15.8 1.6 %collective-permute-start.18 = (bf16[4,272,128]{2,1,0:T(8,128)(2,1)S(1)}, bf16[4,272,128]{2,1,0:T(8,128)(2,1)S(1)}, u32[]{:S(2)}, u32[]{:S(2)}) collective-permute-start(bf16[4,272,128]{2,1,0:T(8,128)(2,1)S(1)} %join.11.refs_4_), channel_id=1, source_target_pairs={{0,16},{8,24},{16,0},{24,8},{1,17},{9,25},{17,1},{25,9},{2,18},{10... | collective-permute-start | bytes 835592 | tf_op jit(solution)/shard_map/ppermute | solution.py:264
  17.4 2.1 %collective-permute-start.3 = (bf16[1,272,128]{2,1,0:T(8,128)(2,1)S(1)}, bf16[1,272,128]{2,1,0:T(8,128)(2,1)S(1)}, u32[]{:S(2)}, u32[]{:S(2)}) collective-permute-start(bf16[1,272,128]{2,1,0:T(8,128)(2,1)S(1)} %bitcast.15), channel_id=1, source_target_pairs={{0,4},{1,5},{2,6},{3,7},{4,0},{5,1},{6,2},{7,3},{8,12},{9,13},{10,... | collective-permute-start | bytes 208904 | tf_op jit(solution)/shard_map/ppermute | solution.py:264
  19.5 1.7 %collective-permute-start.4 = (bf16[1,272,128]{2,1,0:T(8,128)(2,1)S(1)}, bf16[1,272,128]{2,1,0:T(8,128)(2,1)S(1)}, u32[]{:S(2)}, u32[]{:S(2)}) collective-permute-start(bf16[1,272,128]{2,1,0:T(8,128)(2,1)S(1)} %bitcast.14), channel_id=1, source_target_pairs={{0,5},{1,4},{2,7},{3,6},{4,1},{5,0},{6,3},{7,2},{8,13},{9,12},{10,... | collective-permute-start | bytes 208904 | tf_op jit(solution)/shard_map/ppermute | solution.py:264
  21.2 0.6 %collective-permute-start.9 = (bf16[512,128]{1,0:T(8,128)(2,1)S(1)}, bf16[512,128]{1,0:T(8,128)(2,1)S(1)}, u32[]{:S(2)}, u32[]{:S(2)}) collective-permute-start(bf16[512,128]{1,0:T(8,128)(2,1)S(1)} %collective-permute-done.1.refs_9_), channel_id=1, source_target_pairs={{0,1},{1,0},{2,3},{3,2},{4,5},{5,4},{6,7},{7,6},{8,9},{9,8},{10,11... | collective-permute-start | bytes 393224 | tf_op jit(solution)/shard_map/ppermute | solution.py:264
  21.8 1.3 %collective-permute-done.7.refs_1_ = bf16[1,272,128]{2,1,0:T(8,128)(2,1)S(1)} collective-permute-done((bf16[1,272,128]{2,1,0:T(8,128)(2,1)S(1)}, bf16[1,272,128]{2,1,0:T(8,128)(2,1)S(1)}, u32[]{:S(2)}, u32[]{:S(2)}) %collective-permute-start.7) | collective-permute-done | bytes 69664 | tf_op jit(solution)/shard_map/ppermute | solution.py:264
  23.1 1.3 %collective-permute-start.8 = (bf16[2,272,128]{2,1,0:T(8,128)(2,1)S(1)}, bf16[2,272,128]{2,1,0:T(8,128)(2,1)S(1)}, u32[]{:S(2)}, u32[]{:S(2)}) collective-permute-start(bf16[2,272,128]{2,1,0:T(8,128)(2,1)S(1)} %join.7.refs_1_), channel_id=1, source_target_pairs={{0,16},{8,24},{16,0},{24,8},{1,17},{9,25},{17,1},{25,9},{2,18},{10... | collective-permute-start | bytes 417800 | tf_op jit(solution)/shard_map/ppermute | solution.py:264
  24.4 0.4 %collective-permute-done.3.refs_0_ = bf16[1,272,128]{2,1,0:T(8,128)(2,1)S(1)} collective-permute-done((bf16[1,272,128]{2,1,0:T(8,128)(2,1)S(1)}, bf16[1,272,128]{2,1,0:T(8,128)(2,1)S(1)}, u32[]{:S(2)}, u32[]{:S(2)}) %collective-permute-start.3) | collective-permute-done | bytes 69664 | tf_op jit(solution)/shard_map/ppermute | solution.py:264
  24.9 1.2 %collective-permute-done.4.refs_1_ = bf16[1,272,128]{2,1,0:T(8,128)(2,1)S(1)} collective-permute-done((bf16[1,272,128]{2,1,0:T(8,128)(2,1)S(1)}, bf16[1,272,128]{2,1,0:T(8,128)(2,1)S(1)}, u32[]{:S(2)}, u32[]{:S(2)}) %collective-permute-start.4) | collective-permute-done | bytes 69664 | tf_op jit(solution)/shard_map/ppermute | solution.py:264
  26.1 2.2 %collective-permute-start.5 = (bf16[2,272,128]{2,1,0:T(8,128)(2,1)S(1)}, bf16[2,272,128]{2,1,0:T(8,128)(2,1)S(1)}, u32[]{:S(2)}, u32[]{:S(2)}) collective-permute-start(bf16[2,272,128]{2,1,0:T(8,128)(2,1)S(1)} %join.6.refs_0_), channel_id=1, source_target_pairs={{0,16},{8,24},{16,0},{24,8},{1,17},{9,25},{17,1},{25,9},{2,18},{10... | collective-permute-start | bytes 417800 | tf_op jit(solution)/shard_map/ppermute | solution.py:264
  28.7 4.6 %collective-permute-done.10.refs_1_ = bf16[512,128]{1,0:T(8,128)(2,1)S(1)} collective-permute-done((bf16[512,128]{1,0:T(8,128)(2,1)S(1)}, bf16[512,128]{1,0:T(8,128)(2,1)S(1)}, u32[]{:S(2)}, u32[]{:S(2)}) %collective-permute-start.10) | collective-permute-done | bytes 131104 | tf_op jit(solution)/shard_map/ppermute | solution.py:264
  33.4 0.5 %collective-permute-start.14 = (bf16[4,272,128]{2,1,0:T(8,128)(2,1)S(1)}, bf16[4,272,128]{2,1,0:T(8,128)(2,1)S(1)}, u32[]{:S(2)}, u32[]{:S(2)}) collective-permute-start(bf16[4,272,128]{2,1,0:T(8,128)(2,1)S(1)} %join.10.refs_2_), channel_id=1, source_target_pairs={{0,8},{8,0},{16,24},{24,16},{1,9},{9,1},{17,25},{25,17},{2,10},{10... | collective-permute-start | bytes 835592 | tf_op jit(solution)/shard_map/ppermute | solution.py:264
  34.4 1.5 %collective-permute-done.11.refs_0_.refs_2_ = bf16[512,128]{1,0:T(8,128)(2,1)S(1)} collective-permute-done((bf16[512,128]{1,0:T(8,128)(2,1)S(1)}, bf16[512,128]{1,0:T(8,128)(2,1)S(1)}, u32[]{:S(2)}, u32[]{:S(2)}) %collective-permute-start.11) | collective-permute-done | bytes 131104 | tf_op jit(solution)/shard_map/ppermute | solution.py:264
  36.0 1.4 %collective-permute-start.12 = (bf16[512,128]{1,0:T(8,128)(2,1)S(1)}, bf16[512,128]{1,0:T(8,128)(2,1)S(1)}, u32[]{:S(2)}, u32[]{:S(2)}) collective-permute-start(bf16[512,128]{1,0:T(8,128)(2,1)S(1)} %join.8), channel_id=1, source_target_pairs={{0,1},{1,0},{2,3},{3,2},{4,5},{5,4},{6,7},{7,6},{8,9},{9,8},{10,11... | collective-permute-start | bytes 393224 | tf_op jit(solution)/shard_map/ppermute | solution.py:264
  37.5 3.0 %near_half.1 = (f32[512,1024]{1,0:T(8,128)S(1)}, bf16[1024,1024]{1,0:T(8,128)(2,1)S(1)}) custom-call(s32[9]{0:T(128)S(1)} %stack.24.where_ref, bf16[4,272,128]{2,1,0:T(8,128)(2,1)S(1)} %join.9.refs_0_, bf16[4,272,128]{2,1,0:T(8,128)(2,1)S(1)} %collective-permute-done.13.refs_1_, bf16[4,272,128]{2,1,0:T(8,128)(2,1)S(1)} %join.10.refs_2_, ...), custom_call_target="tpu_custom_call" | custom-call | flops 536870912 | bytes 8388608 | tf_op jit(solution)/shard_map/near_half/pallas_call | solution.py:192
  40.5 0.5 %collective-permute-done.12.refs_3_ = bf16[512,128]{1,0:T(8,128)(2,1)S(1)} collective-permute-done((bf16[512,128]{1,0:T(8,128)(2,1)S(1)}, bf16[512,128]{1,0:T(8,128)(2,1)S(1)}, u32[]{:S(2)}, u32[]{:S(2)}) %collective-permute-start.12) | collective-permute-done | bytes 131104 | tf_op jit(solution)/shard_map/ppermute | solution.py:264
  41.0 1.8 %far_half.1 = f32[512,1024]{1,0:T(8,128)} custom-call(bf16[512,128]{1,0:T(8,128)(2,1)S(1)} %collective-permute-done.2.refs_0_, bf16[512,128]{1,0:T(8,128)(2,1)S(1)} %collective-permute-done.10.refs_1_, bf16[512,128]{1,0:T(8,128)(2,1)S(1)} %collective-permute-done.11.refs_0_.refs_2_, bf16[512,128]{1,0:T(8,128)(2,1)S(1)} %collective-permute-done.12.refs_3_, ...), custom_call_target="tpu_custom_call" | custom-call | flops 536870912 | bytes 8388608 | tf_op jit(solution)/shard_map/far_half/pallas_call | solution.py:242
  (28 shorter events, 1.2 us)
Async XLA Ops:
  0.0 9.4 %collective-permute-start = (bf16[512,128]{1,0:T(8,128)(2,1)}, bf16[512,128]{1,0:T(8,128)(2,1)S(1)}, u32[]{:S(2)}, u32[]{:S(2)}) collective-permute-start(bf16[512,128]{1,0:T(8,128)(2,1)} %refs_11_.1), channel_id=1, source_target_pairs={{0,1},{1,0},{2,3},{3,2},{4,5},{5,4},{6,7},{7,6},{8,9},{9,8},{10,11... | collective-permute-start | bytes 393224 | tf_op jit(solution)/shard_map/ppermute | solution.py:264
  2.9 9.0 %collective-permute-start.1 = (bf16[512,128]{1,0:T(8,128)(2,1)}, bf16[512,128]{1,0:T(8,128)(2,1)S(1)}, u32[]{:S(2)}, u32[]{:S(2)}) collective-permute-start(bf16[512,128]{1,0:T(8,128)(2,1)} %refs_11_.1), channel_id=1, source_target_pairs={{0,2},{1,3},{2,0},{3,1},{4,6},{5,7},{6,4},{7,5},{8,10},{9,11},{10,... | collective-permute-start | bytes 393224 | tf_op jit(solution)/shard_map/ppermute | solution.py:264
  4.5 7.4 %collective-permute-start.2 = (bf16[512,128]{1,0:T(8,128)(2,1)}, bf16[512,128]{1,0:T(8,128)(2,1)S(1)}, u32[]{:S(2)}, u32[]{:S(2)}) collective-permute-start(bf16[512,128]{1,0:T(8,128)(2,1)} %refs_11_.1), channel_id=1, source_target_pairs={{0,4},{1,5},{2,6},{3,7},{4,0},{5,1},{6,2},{7,3},{8,12},{9,13},{10,... | collective-permute-start | bytes 393224 | tf_op jit(solution)/shard_map/ppermute | solution.py:264
  8.4 7.4 %collective-permute-start.15 = (bf16[1,272,128]{2,1,0:T(8,128)(2,1)S(1)}, bf16[1,272,128]{2,1,0:T(8,128)(2,1)S(1)}, u32[]{:S(2)}, u32[]{:S(2)}) collective-permute-start(bf16[1,272,128]{2,1,0:T(8,128)(2,1)S(1)} %bitcast.20), channel_id=1, source_target_pairs={{0,1},{1,0},{2,3},{3,2},{4,5},{5,4},{6,7},{7,6},{8,9},{9,8},{10,11... | collective-permute-start | bytes 208904 | tf_op jit(solution)/shard_map/ppermute | solution.py:264
  9.0 6.8 %collective-permute-start.16 = (bf16[1,272,128]{2,1,0:T(8,128)(2,1)S(1)}, bf16[1,272,128]{2,1,0:T(8,128)(2,1)S(1)}, u32[]{:S(2)}, u32[]{:S(2)}) collective-permute-start(bf16[1,272,128]{2,1,0:T(8,128)(2,1)S(1)} %bitcast.19), channel_id=1, source_target_pairs={{0,2},{1,3},{2,0},{3,1},{4,6},{5,7},{6,4},{7,5},{8,10},{9,11},{10,... | collective-permute-start | bytes 208904 | tf_op jit(solution)/shard_map/ppermute | solution.py:264
  9.4 6.3 %collective-permute-start.17 = (bf16[1,272,128]{2,1,0:T(8,128)(2,1)S(1)}, bf16[1,272,128]{2,1,0:T(8,128)(2,1)S(1)}, u32[]{:S(2)}, u32[]{:S(2)}) collective-permute-start(bf16[1,272,128]{2,1,0:T(8,128)(2,1)S(1)} %bitcast.18), channel_id=1, source_target_pairs={{0,3},{1,2},{2,1},{3,0},{4,7},{5,6},{6,5},{7,4},{8,11},{9,10},{10,... | collective-permute-start | bytes 208904 | tf_op jit(solution)/shard_map/ppermute | solution.py:264
  11.9 9.3 %collective-permute-start.6 = (bf16[1,272,128]{2,1,0:T(8,128)(2,1)S(1)}, bf16[1,272,128]{2,1,0:T(8,128)(2,1)S(1)}, u32[]{:S(2)}, u32[]{:S(2)}) collective-permute-start(bf16[1,272,128]{2,1,0:T(8,128)(2,1)S(1)} %bitcast.17), channel_id=1, source_target_pairs={{0,6},{1,7},{2,4},{3,5},{4,2},{5,3},{6,0},{7,1},{8,14},{9,15},{10,... | collective-permute-start | bytes 208904 | tf_op jit(solution)/shard_map/ppermute | solution.py:264
  15.7 7.4 %collective-permute-start.7 = (bf16[1,272,128]{2,1,0:T(8,128)(2,1)S(1)}, bf16[1,272,128]{2,1,0:T(8,128)(2,1)S(1)}, u32[]{:S(2)}, u32[]{:S(2)}) collective-permute-start(bf16[1,272,128]{2,1,0:T(8,128)(2,1)S(1)} %bitcast.16), channel_id=1, source_target_pairs={{0,7},{1,6},{2,5},{3,4},{4,3},{5,2},{6,1},{7,0},{8,15},{9,14},{10,... | collective-permute-start | bytes 208904 | tf_op jit(solution)/shard_map/ppermute | solution.py:264
  15.8 18.1 %collective-permute-start.18 = (bf16[4,272,128]{2,1,0:T(8,128)(2,1)S(1)}, bf16[4,272,128]{2,1,0:T(8,128)(2,1)S(1)}, u32[]{:S(2)}, u32[]{:S(2)}) collective-permute-start(bf16[4,272,128]{2,1,0:T(8,128)(2,1)S(1)} %join.11.refs_4_), channel_id=1, source_target_pairs={{0,16},{8,24},{16,0},{24,8},{1,17},{9,25},{17,1},{25,9},{2,18},{10... | collective-permute-start | bytes 835592 | tf_op jit(solution)/shard_map/ppermute | solution.py:264
  17.4 7.5 %collective-permute-start.3 = (bf16[1,272,128]{2,1,0:T(8,128)(2,1)S(1)}, bf16[1,272,128]{2,1,0:T(8,128)(2,1)S(1)}, u32[]{:S(2)}, u32[]{:S(2)}) collective-permute-start(bf16[1,272,128]{2,1,0:T(8,128)(2,1)S(1)} %bitcast.15), channel_id=1, source_target_pairs={{0,4},{1,5},{2,6},{3,7},{4,0},{5,1},{6,2},{7,3},{8,12},{9,13},{10,... | collective-permute-start | bytes 208904 | tf_op jit(solution)/shard_map/ppermute | solution.py:264
  19.5 6.7 %collective-permute-start.4 = (bf16[1,272,128]{2,1,0:T(8,128)(2,1)S(1)}, bf16[1,272,128]{2,1,0:T(8,128)(2,1)S(1)}, u32[]{:S(2)}, u32[]{:S(2)}) collective-permute-start(bf16[1,272,128]{2,1,0:T(8,128)(2,1)S(1)} %bitcast.14), channel_id=1, source_target_pairs={{0,5},{1,4},{2,7},{3,6},{4,1},{5,0},{6,3},{7,2},{8,13},{9,12},{10,... | collective-permute-start | bytes 208904 | tf_op jit(solution)/shard_map/ppermute | solution.py:264
  21.2 7.5 %collective-permute-start.9 = (bf16[512,128]{1,0:T(8,128)(2,1)S(1)}, bf16[512,128]{1,0:T(8,128)(2,1)S(1)}, u32[]{:S(2)}, u32[]{:S(2)}) collective-permute-start(bf16[512,128]{1,0:T(8,128)(2,1)S(1)} %collective-permute-done.1.refs_9_), channel_id=1, source_target_pairs={{0,1},{1,0},{2,3},{3,2},{4,5},{5,4},{6,7},{7,6},{8,9},{9,8},{10,11... | collective-permute-start | bytes 393224 | tf_op jit(solution)/shard_map/ppermute | solution.py:264
  23.1 10.2 %collective-permute-start.8 = (bf16[2,272,128]{2,1,0:T(8,128)(2,1)S(1)}, bf16[2,272,128]{2,1,0:T(8,128)(2,1)S(1)}, u32[]{:S(2)}, u32[]{:S(2)}) collective-permute-start(bf16[2,272,128]{2,1,0:T(8,128)(2,1)S(1)} %join.7.refs_1_), channel_id=1, source_target_pairs={{0,16},{8,24},{16,0},{24,8},{1,17},{9,25},{17,1},{25,9},{2,18},{10... | collective-permute-start | bytes 417800 | tf_op jit(solution)/shard_map/ppermute | solution.py:264
  26.1 7.2 %collective-permute-start.5 = (bf16[2,272,128]{2,1,0:T(8,128)(2,1)S(1)}, bf16[2,272,128]{2,1,0:T(8,128)(2,1)S(1)}, u32[]{:S(2)}, u32[]{:S(2)}) collective-permute-start(bf16[2,272,128]{2,1,0:T(8,128)(2,1)S(1)} %join.6.refs_0_), channel_id=1, source_target_pairs={{0,16},{8,24},{16,0},{24,8},{1,17},{9,25},{17,1},{25,9},{2,18},{10... | collective-permute-start | bytes 417800 | tf_op jit(solution)/shard_map/ppermute | solution.py:264
  28.4 5.0 %collective-permute-start.10 = (bf16[512,128]{1,0:T(8,128)(2,1)S(1)}, bf16[512,128]{1,0:T(8,128)(2,1)S(1)}, u32[]{:S(2)}, u32[]{:S(2)}) collective-permute-start(bf16[512,128]{1,0:T(8,128)(2,1)S(1)} %collective-permute-done.2.refs_0_), channel_id=1, source_target_pairs={{0,1},{1,0},{2,3},{3,2},{4,5},{5,4},{6,7},{7,6},{8,9},{9,8},{10,11... | collective-permute-start | bytes 393224 | tf_op jit(solution)/shard_map/ppermute | solution.py:264
  28.7 7.3 %collective-permute-start.11 = (bf16[512,128]{1,0:T(8,128)(2,1)S(1)}, bf16[512,128]{1,0:T(8,128)(2,1)S(1)}, u32[]{:S(2)}, u32[]{:S(2)}) collective-permute-start(bf16[512,128]{1,0:T(8,128)(2,1)S(1)} %collective-permute-done.1.refs_9_), channel_id=1, source_target_pairs={{0,4},{1,5},{2,6},{3,7},{4,0},{5,1},{6,2},{7,3},{8,12},{9,13},{10,... | collective-permute-start | bytes 393224 | tf_op jit(solution)/shard_map/ppermute | solution.py:264
  33.4 4.1 %collective-permute-start.13 = (bf16[4,272,128]{2,1,0:T(8,128)(2,1)S(1)}, bf16[4,272,128]{2,1,0:T(8,128)(2,1)S(1)}, u32[]{:S(2)}, u32[]{:S(2)}) collective-permute-start(bf16[4,272,128]{2,1,0:T(8,128)(2,1)S(1)} %join.9.refs_0_), channel_id=1, source_target_pairs={{0,8},{8,0},{16,24},{24,16},{1,9},{9,1},{17,25},{25,17},{2,10},{10... | collective-permute-start | bytes 835592 | tf_op jit(solution)/shard_map/ppermute | solution.py:264
  33.4 4.0 %collective-permute-start.14 = (bf16[4,272,128]{2,1,0:T(8,128)(2,1)S(1)}, bf16[4,272,128]{2,1,0:T(8,128)(2,1)S(1)}, u32[]{:S(2)}, u32[]{:S(2)}) collective-permute-start(bf16[4,272,128]{2,1,0:T(8,128)(2,1)S(1)} %join.10.refs_2_), channel_id=1, source_target_pairs={{0,8},{8,0},{16,24},{24,16},{1,9},{9,1},{17,25},{25,17},{2,10},{10... | collective-permute-start | bytes 835592 | tf_op jit(solution)/shard_map/ppermute | solution.py:264
  33.9 3.6 %collective-permute-start.19 = (bf16[4,272,128]{2,1,0:T(8,128)(2,1)S(1)}, bf16[4,272,128]{2,1,0:T(8,128)(2,1)S(1)}, u32[]{:S(2)}, u32[]{:S(2)}) collective-permute-start(bf16[4,272,128]{2,1,0:T(8,128)(2,1)S(1)} %join.11.refs_4_), channel_id=1, source_target_pairs={{0,8},{8,0},{16,24},{24,16},{1,9},{9,1},{17,25},{25,17},{2,10},{10... | collective-permute-start | bytes 835592 | tf_op jit(solution)/shard_map/ppermute | solution.py:264
  34.0 3.5 %collective-permute-start.20 = (bf16[4,272,128]{2,1,0:T(8,128)(2,1)S(1)}, bf16[4,272,128]{2,1,0:T(8,128)(2,1)S(1)}, u32[]{:S(2)}, u32[]{:S(2)}) collective-permute-start(bf16[4,272,128]{2,1,0:T(8,128)(2,1)S(1)} %collective-permute-done.18.refs_6_), channel_id=1, source_target_pairs={{0,8},{8,0},{16,24},{24,16},{1,9},{9,1},{17,25},{25,17},{2,10},{10... | collective-permute-start | bytes 835592 | tf_op jit(solution)/shard_map/ppermute | solution.py:264
  36.0 5.0 %collective-permute-start.12 = (bf16[512,128]{1,0:T(8,128)(2,1)S(1)}, bf16[512,128]{1,0:T(8,128)(2,1)S(1)}, u32[]{:S(2)}, u32[]{:S(2)}) collective-permute-start(bf16[512,128]{1,0:T(8,128)(2,1)S(1)} %join.8), channel_id=1, source_target_pairs={{0,1},{1,0},{2,3},{3,2},{4,5},{5,4},{6,7},{7,6},{8,9},{9,8},{10,11... | collective-permute-start | bytes 393224 | tf_op jit(solution)/shard_map/ppermute | solution.py:264

commit v10 on v9

--- a/solution.py
+++ b/solution.py
@@ -15,6 +15,7 @@
 MIB = 1024 * 1024
 WEIGHT = 10**9
 WEIGHT_FAR = 4 * 10**9
+WEIGHT_LATE = 10**9
 
 
 def pack_kernel(columns, capacity, me_ref, ids_hbm, tiles_hbm, *refs):
@@ -279,7 +280,9 @@
     amps = {0: amplitudes}
     for s in [*range(1, inner), *range(inner, half, inner), half]:
         amps[s] = exchange(amplitudes, "col", s)
-    outgoing[half:], amps = tie(outgoing[half:], amps)
+    order = sorted(amps, reverse=True)[:-1]
+    outgoing[half:], got = tie(outgoing[half:], [amps[s] for s in order])
+    amps.update(zip(order, got))
 
     chunks = [outgoing[0][None]]
     chunks += [exchange(outgoing[s][None], "col", s) for s in range(1, n_col)]
@@ -290,13 +293,16 @@
     for lane in range(1, inner):
         amps[half ^ lane] = exchange(amps[half], "col", lane)
 
-    early = [s for s in amps if s and (s < half or half < s < half + inner)]
+    early = [s for s in amps if 0 < s < half]
+    late = [s for s in amps if half < s < half + inner]
     flips = range(CORES, n_row, CORES)
     cut = half + half // 2
     far_groups = [join(chunks[half:cut], WEIGHT), join(chunks[cut:], WEIGHT)]
     near_group = join(chunks[:half])
     far_passed = [[exchange(g, "row", flip) for flip in flips] for g in far_groups]
     near_passed = [exchange(near_group, "row", flip) for flip in flips]
+    for s in late:
+        amps[s] = join([amps[s]], WEIGHT_LATE)
     far_passed, got = tie(far_passed, [amps[s] for s in early])
     amps.update(zip(early, got))
     pieces, rows = [], []

time: 43 us -> 47.2 us (1.098); the launches traced: 42.9 us -> 46.6 us
  waiting for transfers between devices: 9.73 us -> 15.1 us
  starting transfers between devices: 26.8 us -> 25.1 us
    ppermute x21, waiting for transfers between devices: 9.73 us -> 15.1 us  [exchange(): return lax.ppermute(x, axis, [(i, i ^ flip) for i in range(size)])]
    ppermute x21, starting transfers between devices: 26.8 us -> 25.1 us  [exchange(): return lax.ppermute(x, axis, [(i, i ^ flip) for i in range(size)])]
  transfers between devices with their start and end apart: 21 -> 21, of which waited for: 6 -> 7; matrix products, arithmetic and copies ran while one was open for 0% -> 0% of each run, Pallas kernels for 10% -> 9%
where the time goes in v10:
time: 47.2 us; the launch traced here: 46.6 us
  starting transfers between devices  25.1 us (53%)
  waiting for transfers between devices  15.1 us (32%)
  Pallas kernels  6.16 us (13%)
    ppermute x21, starting transfers between devices, exchange(): return lax.ppermute(x, axis, [(i, i ^ flip) for i in range(size)])  25.1 us
    ppermute x21, waiting for transfers between devices, exchange(): return lax.ppermute(x, axis, [(i, i ^ flip) for i in range(size)])  15.1 us
    pallas_call x1, Pallas kernels, near_half(): pl.pallas_call(functools.partial(near_kernel, n_pieces, offsets, capacity...  2.96 us
    pallas_call x1, Pallas kernels, far_half(): pl.pallas_call(functools.partial(far_kernel, offsets, depth // width), ou...  1.85 us
    pallas_call x1, Pallas kernels, pack(): pl.pallas_call(functools.partial(pack_kernel, columns, capacity), out_sha...  1.25 us
  transfers between devices with their start and end apart: 21, of which 7 were waited for; matrix products, arithmetic and copies ran while one was open for 0% of the time, Pallas kernels for 9%

profile of v10, /device:TPU:0, one launch (start us, length us, event | category | flops | bytes accessed | tf_op | source)
XLA Modules:
  0.0 46.6 jit_solution(6489461727712258817)
XLA Ops:
  0.0 4.0 %collective-permute-start = (bf16[512,128]{1,0:T(8,128)(2,1)}, bf16[512,128]{1,0:T(8,128)(2,1)S(1)}, u32[]{:S(2)}, u32[]{:S(2)}) collective-permute-start(bf16[512,128]{1,0:T(8,128)(2,1)} %refs_11_.1), channel_id=1, source_target_pairs={{0,4},{1,5},{2,6},{3,7},{4,0},{5,1},{6,2},{7,3},{8,12},{9,13},{10,... | collective-permute-start | bytes 393224 | tf_op jit(solution)/shard_map/ppermute | solution.py:265
  4.0 1.6 %collective-permute-start.1 = (bf16[512,128]{1,0:T(8,128)(2,1)}, bf16[512,128]{1,0:T(8,128)(2,1)S(1)}, u32[]{:S(2)}, u32[]{:S(2)}) collective-permute-start(bf16[512,128]{1,0:T(8,128)(2,1)} %refs_11_.1), channel_id=1, source_target_pairs={{0,2},{1,3},{2,0},{3,1},{4,6},{5,7},{6,4},{7,5},{8,10},{9,11},{10,... | collective-permute-start | bytes 393224 | tf_op jit(solution)/shard_map/ppermute | solution.py:265
  5.6 1.5 %collective-permute-start.2 = (bf16[512,128]{1,0:T(8,128)(2,1)}, bf16[512,128]{1,0:T(8,128)(2,1)S(1)}, u32[]{:S(2)}, u32[]{:S(2)}) collective-permute-start(bf16[512,128]{1,0:T(8,128)(2,1)} %refs_11_.1), channel_id=1, source_target_pairs={{0,1},{1,0},{2,3},{3,2},{4,5},{5,4},{6,7},{7,6},{8,9},{9,8},{10,11... | collective-permute-start | bytes 393224 | tf_op jit(solution)/shard_map/ppermute | solution.py:265
  7.1 1.3 %pack.1 = (bf16[272,128]{1,0:T(8,128)(2,1)S(1)}, bf16[272,128]{1,0:T(8,128)(2,1)S(1)}, bf16[272,128]{1,0:T(8,128)(2,1)S(1)}, bf16[272,128]{1,0:T(8,128)(2,1)S(1)...) custom-call(s32[1]{0:T(128)} %bitcast.me_ref, ...), custom_call_target="tpu_custom_call" | custom-call | tf_op jit(solution)/shard_map/pack/pallas_call | solution.py:66
  8.4 0.6 %collective-permute-start.15 = (bf16[1,272,128]{2,1,0:T(8,128)(2,1)S(1)}, bf16[1,272,128]{2,1,0:T(8,128)(2,1)S(1)}, u32[]{:S(2)}, u32[]{:S(2)}) collective-permute-start(bf16[1,272,128]{2,1,0:T(8,128)(2,1)S(1)} %bitcast.20), channel_id=1, source_target_pairs={{0,1},{1,0},{2,3},{3,2},{4,5},{5,4},{6,7},{7,6},{8,9},{9,8},{10,11... | collective-permute-start | bytes 208904 | tf_op jit(solution)/shard_map/ppermute | solution.py:265
  9.4 1.2 %collective-permute-done.refs_0_ = bf16[512,128]{1,0:T(8,128)(2,1)S(1)} collective-permute-done((bf16[512,128]{1,0:T(8,128)(2,1)}, bf16[512,128]{1,0:T(8,128)(2,1)S(1)}, u32[]{:S(2)}, u32[]{:S(2)}) %collective-permute-start) | collective-permute-done | bytes 131104 | tf_op jit(solution)/shard_map/ppermute | solution.py:265
  10.7 1.7 %collective-permute-start.17 = (bf16[1,272,128]{2,1,0:T(8,128)(2,1)S(1)}, bf16[1,272,128]{2,1,0:T(8,128)(2,1)S(1)}, u32[]{:S(2)}, u32[]{:S(2)}) collective-permute-start(bf16[1,272,128]{2,1,0:T(8,128)(2,1)S(1)} %bitcast.18), channel_id=1, source_target_pairs={{0,3},{1,2},{2,1},{3,0},{4,7},{5,6},{6,5},{7,4},{8,11},{9,10},{10,... | collective-permute-start | bytes 208904 | tf_op jit(solution)/shard_map/ppermute | solution.py:265
  12.3 2.0 %collective-permute-start.8 = (bf16[1,272,128]{2,1,0:T(8,128)(2,1)S(1)}, bf16[1,272,128]{2,1,0:T(8,128)(2,1)S(1)}, u32[]{:S(2)}, u32[]{:S(2)}) collective-permute-start(bf16[1,272,128]{2,1,0:T(8,128)(2,1)S(1)} %bitcast.17), channel_id=1, source_target_pairs={{0,6},{1,7},{2,4},{3,5},{4,2},{5,3},{6,0},{7,1},{8,14},{9,15},{10,... | collective-permute-start | bytes 208904 | tf_op jit(solution)/shard_map/ppermute | solution.py:265
  14.3 1.9 %collective-permute-start.9 = (bf16[1,272,128]{2,1,0:T(8,128)(2,1)S(1)}, bf16[1,272,128]{2,1,0:T(8,128)(2,1)S(1)}, u32[]{:S(2)}, u32[]{:S(2)}) collective-permute-start(bf16[1,272,128]{2,1,0:T(8,128)(2,1)S(1)} %bitcast.16), channel_id=1, source_target_pairs={{0,7},{1,6},{2,5},{3,4},{4,3},{5,2},{6,1},{7,0},{8,15},{9,14},{10,... | collective-permute-start | bytes 208904 | tf_op jit(solution)/shard_map/ppermute | solution.py:265
  16.2 1.6 %collective-permute-start.18 = (bf16[4,272,128]{2,1,0:T(8,128)(2,1)S(1)}, bf16[4,272,128]{2,1,0:T(8,128)(2,1)S(1)}, u32[]{:S(2)}, u32[]{:S(2)}) collective-permute-start(bf16[4,272,128]{2,1,0:T(8,128)(2,1)S(1)} %join.13.refs_4_), channel_id=1, source_target_pairs={{0,16},{8,24},{16,0},{24,8},{1,17},{9,25},{17,1},{25,9},{2,18},{10... | collective-permute-start | bytes 835592 | tf_op jit(solution)/shard_map/ppermute | solution.py:265
  17.7 3.5 %collective-permute-start.6 = (bf16[1,272,128]{2,1,0:T(8,128)(2,1)S(1)}, bf16[1,272,128]{2,1,0:T(8,128)(2,1)S(1)}, u32[]{:S(2)}, u32[]{:S(2)}) collective-permute-start(bf16[1,272,128]{2,1,0:T(8,128)(2,1)S(1)} %bitcast.15), channel_id=1, source_target_pairs={{0,4},{1,5},{2,6},{3,7},{4,0},{5,1},{6,2},{7,3},{8,12},{9,13},{10,... | collective-permute-start | bytes 208904 | tf_op jit(solution)/shard_map/ppermute | solution.py:265
  21.6 1.7 %collective-permute-start.11 = (bf16[2,272,128]{2,1,0:T(8,128)(2,1)S(1)}, bf16[2,272,128]{2,1,0:T(8,128)(2,1)S(1)}, u32[]{:S(2)}, u32[]{:S(2)}) collective-permute-start(bf16[2,272,128]{2,1,0:T(8,128)(2,1)S(1)} %join.10.refs_1_), channel_id=1, source_target_pairs={{0,16},{8,24},{16,0},{24,8},{1,17},{9,25},{17,1},{25,9},{2,18},{10... | collective-permute-start | bytes 417800 | tf_op jit(solution)/shard_map/ppermute | solution.py:265
  23.4 2.9 %collective-permute-done.6.refs_0_ = bf16[1,272,128]{2,1,0:T(8,128)(2,1)S(1)} collective-permute-done((bf16[1,272,128]{2,1,0:T(8,128)(2,1)S(1)}, bf16[1,272,128]{2,1,0:T(8,128)(2,1)S(1)}, u32[]{:S(2)}, u32[]{:S(2)}) %collective-permute-start.6) | collective-permute-done | bytes 69664 | tf_op jit(solution)/shard_map/ppermute | solution.py:265
  26.3 1.9 %collective-permute-done.7.refs_1_ = bf16[1,272,128]{2,1,0:T(8,128)(2,1)S(1)} collective-permute-done((bf16[1,272,128]{2,1,0:T(8,128)(2,1)S(1)}, bf16[1,272,128]{2,1,0:T(8,128)(2,1)S(1)}, u32[]{:S(2)}, u32[]{:S(2)}) %collective-permute-start.7) | collective-permute-done | bytes 69664 | tf_op jit(solution)/shard_map/ppermute | solution.py:265
  28.2 1.6 %collective-permute-start.10 = (bf16[2,272,128]{2,1,0:T(8,128)(2,1)S(1)}, bf16[2,272,128]{2,1,0:T(8,128)(2,1)S(1)}, u32[]{:S(2)}, u32[]{:S(2)}) collective-permute-start(bf16[2,272,128]{2,1,0:T(8,128)(2,1)S(1)} %join.9.refs_0_), channel_id=1, source_target_pairs={{0,16},{8,24},{16,0},{24,8},{1,17},{9,25},{17,1},{25,9},{2,18},{10... | collective-permute-start | bytes 417800 | tf_op jit(solution)/shard_map/ppermute | solution.py:265
  29.7 0.7 %collective-permute-start.12 = (bf16[512,128]{1,0:T(8,128)(2,1)S(1)}, bf16[512,128]{1,0:T(8,128)(2,1)S(1)}, u32[]{:S(2)}, u32[]{:S(2)}) collective-permute-start(bf16[512,128]{1,0:T(8,128)(2,1)S(1)} %collective-permute-done.1.refs_9_), channel_id=1, source_target_pairs={{0,1},{1,0},{2,3},{3,2},{4,5},{5,4},{6,7},{7,6},{8,9},{9,8},{10,11... | collective-permute-start | bytes 393224 | tf_op jit(solution)/shard_map/ppermute | solution.py:265
  30.5 4.1 %collective-permute-done.12.refs_10_ = bf16[512,128]{1,0:T(8,128)(2,1)S(1)} collective-permute-done((bf16[512,128]{1,0:T(8,128)(2,1)S(1)}, bf16[512,128]{1,0:T(8,128)(2,1)S(1)}, u32[]{:S(2)}, u32[]{:S(2)}) %collective-permute-start.12) | collective-permute-done | bytes 131104 | tf_op jit(solution)/shard_map/ppermute | solution.py:265
  34.7 0.7 %collective-permute-start.3 = (bf16[512,128]{1,0:T(8,128)(2,1)S(1)}, bf16[512,128]{1,0:T(8,128)(2,1)S(1)}, u32[]{:S(2)}, u32[]{:S(2)}) collective-permute-start(bf16[512,128]{1,0:T(8,128)(2,1)S(1)} %collective-permute-done.refs_0_), channel_id=1, source_target_pairs={{0,1},{1,0},{2,3},{3,2},{4,5},{5,4},{6,7},{7,6},{8,9},{9,8},{10,11... | collective-permute-start | bytes 393224 | tf_op jit(solution)/shard_map/ppermute | solution.py:265
  36.1 2.6 %collective-permute-done.4.refs_0_.refs_2_ = bf16[512,128]{1,0:T(8,128)(2,1)S(1)} collective-permute-done((bf16[512,128]{1,0:T(8,128)(2,1)S(1)}, bf16[512,128]{1,0:T(8,128)(2,1)S(1)}, u32[]{:S(2)}, u32[]{:S(2)}) %collective-permute-start.4) | collective-permute-done | bytes 131104 | tf_op jit(solution)/shard_map/ppermute | solution.py:265
  38.7 0.9 %collective-permute-done.3.refs_0_ = bf16[512,128]{1,0:T(8,128)(2,1)S(1)} collective-permute-done((bf16[512,128]{1,0:T(8,128)(2,1)S(1)}, bf16[512,128]{1,0:T(8,128)(2,1)S(1)}, u32[]{:S(2)}, u32[]{:S(2)}) %collective-permute-start.3) | collective-permute-done | bytes 131104 | tf_op jit(solution)/shard_map/ppermute | solution.py:265
  39.7 0.7 %collective-permute-start.5 = (bf16[512,128]{1,0:T(8,128)(2,1)S(1)}, bf16[512,128]{1,0:T(8,128)(2,1)S(1)}, u32[]{:S(2)}, u32[]{:S(2)}) collective-permute-start(bf16[512,128]{1,0:T(8,128)(2,1)S(1)} %join.8), channel_id=1, source_target_pairs={{0,1},{1,0},{2,3},{3,2},{4,5},{5,4},{6,7},{7,6},{8,9},{9,8},{10,11... | collective-permute-start | bytes 393224 | tf_op jit(solution)/shard_map/ppermute | solution.py:265
  40.4 3.0 %near_half.1 = (f32[512,1024]{1,0:T(8,128)S(1)}, bf16[1024,1024]{1,0:T(8,128)(2,1)S(1)}) custom-call(s32[9]{0:T(128)S(1)} %stack.24.where_ref, bf16[4,272,128]{2,1,0:T(8,128)(2,1)S(1)} %join.11.refs_0_, bf16[4,272,128]{2,1,0:T(8,128)(2,1)S(1)} %collective-permute-done.13.refs_1_, bf16[4,272,128]{2,1,0:T(8,128)(2,1)S(1)} %join.12.refs_2_, ...), custom_call_target="tpu_custom_call" | custom-call | flops 536870912 | bytes 8388608 | tf_op jit(solution)/shard_map/near_half/pallas_call | solution.py:193
  43.4 1.3 %collective-permute-done.5.refs_3_ = bf16[512,128]{1,0:T(8,128)(2,1)S(1)} collective-permute-done((bf16[512,128]{1,0:T(8,128)(2,1)S(1)}, bf16[512,128]{1,0:T(8,128)(2,1)S(1)}, u32[]{:S(2)}, u32[]{:S(2)}) %collective-permute-start.5) | collective-permute-done | bytes 131104 | tf_op jit(solution)/shard_map/ppermute | solution.py:265
  44.7 1.8 %far_half.1 = f32[512,1024]{1,0:T(8,128)} custom-call(bf16[512,128]{1,0:T(8,128)(2,1)S(1)} %collective-permute-done.refs_0_, bf16[512,128]{1,0:T(8,128)(2,1)S(1)} %join.7.refs_1_, bf16[512,128]{1,0:T(8,128)(2,1)S(1)} %collective-permute-done.4.refs_0_.refs_2_, bf16[512,128]{1,0:T(8,128)(2,1)S(1)} %collective-permute-done.5.refs_3_, ...), custom_call_target="tpu_custom_call" | custom-call | flops 536870912 | bytes 8388608 | tf_op jit(solution)/shard_map/far_half/pallas_call | solution.py:243
  (29 shorter events, 1.6 us)
Async XLA Ops:
  0.0 10.7 %collective-permute-start = (bf16[512,128]{1,0:T(8,128)(2,1)}, bf16[512,128]{1,0:T(8,128)(2,1)S(1)}, u32[]{:S(2)}, u32[]{:S(2)}) collective-permute-start(bf16[512,128]{1,0:T(8,128)(2,1)} %refs_11_.1), channel_id=1, source_target_pairs={{0,4},{1,5},{2,6},{3,7},{4,0},{5,1},{6,2},{7,3},{8,12},{9,13},{10,... | collective-permute-start | bytes 393224 | tf_op jit(solution)/shard_map/ppermute | solution.py:265
  4.0 8.3 %collective-permute-start.1 = (bf16[512,128]{1,0:T(8,128)(2,1)}, bf16[512,128]{1,0:T(8,128)(2,1)S(1)}, u32[]{:S(2)}, u32[]{:S(2)}) collective-permute-start(bf16[512,128]{1,0:T(8,128)(2,1)} %refs_11_.1), channel_id=1, source_target_pairs={{0,2},{1,3},{2,0},{3,1},{4,6},{5,7},{6,4},{7,5},{8,10},{9,11},{10,... | collective-permute-start | bytes 393224 | tf_op jit(solution)/shard_map/ppermute | solution.py:265
  5.6 6.7 %collective-permute-start.2 = (bf16[512,128]{1,0:T(8,128)(2,1)}, bf16[512,128]{1,0:T(8,128)(2,1)S(1)}, u32[]{:S(2)}, u32[]{:S(2)}) collective-permute-start(bf16[512,128]{1,0:T(8,128)(2,1)} %refs_11_.1), channel_id=1, source_target_pairs={{0,1},{1,0},{2,3},{3,2},{4,5},{5,4},{6,7},{7,6},{8,9},{9,8},{10,11... | collective-permute-start | bytes 393224 | tf_op jit(solution)/shard_map/ppermute | solution.py:265
  8.4 7.8 %collective-permute-start.15 = (bf16[1,272,128]{2,1,0:T(8,128)(2,1)S(1)}, bf16[1,272,128]{2,1,0:T(8,128)(2,1)S(1)}, u32[]{:S(2)}, u32[]{:S(2)}) collective-permute-start(bf16[1,272,128]{2,1,0:T(8,128)(2,1)S(1)} %bitcast.20), channel_id=1, source_target_pairs={{0,1},{1,0},{2,3},{3,2},{4,5},{5,4},{6,7},{7,6},{8,9},{9,8},{10,11... | collective-permute-start | bytes 208904 | tf_op jit(solution)/shard_map/ppermute | solution.py:265
  9.0 7.2 %collective-permute-start.16 = (bf16[1,272,128]{2,1,0:T(8,128)(2,1)S(1)}, bf16[1,272,128]{2,1,0:T(8,128)(2,1)S(1)}, u32[]{:S(2)}, u32[]{:S(2)}) collective-permute-start(bf16[1,272,128]{2,1,0:T(8,128)(2,1)S(1)} %bitcast.19), channel_id=1, source_target_pairs={{0,2},{1,3},{2,0},{3,1},{4,6},{5,7},{6,4},{7,5},{8,10},{9,11},{10,... | collective-permute-start | bytes 208904 | tf_op jit(solution)/shard_map/ppermute | solution.py:265
  10.7 5.5 %collective-permute-start.17 = (bf16[1,272,128]{2,1,0:T(8,128)(2,1)S(1)}, bf16[1,272,128]{2,1,0:T(8,128)(2,1)S(1)}, u32[]{:S(2)}, u32[]{:S(2)}) collective-permute-start(bf16[1,272,128]{2,1,0:T(8,128)(2,1)S(1)} %bitcast.18), channel_id=1, source_target_pairs={{0,3},{1,2},{2,1},{3,0},{4,7},{5,6},{6,5},{7,4},{8,11},{9,10},{10,... | collective-permute-start | bytes 208904 | tf_op jit(solution)/shard_map/ppermute | solution.py:265
  12.3 9.3 %collective-permute-start.8 = (bf16[1,272,128]{2,1,0:T(8,128)(2,1)S(1)}, bf16[1,272,128]{2,1,0:T(8,128)(2,1)S(1)}, u32[]{:S(2)}, u32[]{:S(2)}) collective-permute-start(bf16[1,272,128]{2,1,0:T(8,128)(2,1)S(1)} %bitcast.17), channel_id=1, source_target_pairs={{0,6},{1,7},{2,4},{3,5},{4,2},{5,3},{6,0},{7,1},{8,14},{9,15},{10,... | collective-permute-start | bytes 208904 | tf_op jit(solution)/shard_map/ppermute | solution.py:265
  14.3 7.3 %collective-permute-start.9 = (bf16[1,272,128]{2,1,0:T(8,128)(2,1)S(1)}, bf16[1,272,128]{2,1,0:T(8,128)(2,1)S(1)}, u32[]{:S(2)}, u32[]{:S(2)}) collective-permute-start(bf16[1,272,128]{2,1,0:T(8,128)(2,1)S(1)} %bitcast.16), channel_id=1, source_target_pairs={{0,7},{1,6},{2,5},{3,4},{4,3},{5,2},{6,1},{7,0},{8,15},{9,14},{10,... | collective-permute-start | bytes 208904 | tf_op jit(solution)/shard_map/ppermute | solution.py:265
  16.2 19.8 %collective-permute-start.18 = (bf16[4,272,128]{2,1,0:T(8,128)(2,1)S(1)}, bf16[4,272,128]{2,1,0:T(8,128)(2,1)S(1)}, u32[]{:S(2)}, u32[]{:S(2)}) collective-permute-start(bf16[4,272,128]{2,1,0:T(8,128)(2,1)S(1)} %join.13.refs_4_), channel_id=1, source_target_pairs={{0,16},{8,24},{16,0},{24,8},{1,17},{9,25},{17,1},{25,9},{2,18},{10... | collective-permute-start | bytes 835592 | tf_op jit(solution)/shard_map/ppermute | solution.py:265
  17.7 8.5 %collective-permute-start.6 = (bf16[1,272,128]{2,1,0:T(8,128)(2,1)S(1)}, bf16[1,272,128]{2,1,0:T(8,128)(2,1)S(1)}, u32[]{:S(2)}, u32[]{:S(2)}) collective-permute-start(bf16[1,272,128]{2,1,0:T(8,128)(2,1)S(1)} %bitcast.15), channel_id=1, source_target_pairs={{0,4},{1,5},{2,6},{3,7},{4,0},{5,1},{6,2},{7,3},{8,12},{9,13},{10,... | collective-permute-start | bytes 208904 | tf_op jit(solution)/shard_map/ppermute | solution.py:265
  21.3 6.9 %collective-permute-start.7 = (bf16[1,272,128]{2,1,0:T(8,128)(2,1)S(1)}, bf16[1,272,128]{2,1,0:T(8,128)(2,1)S(1)}, u32[]{:S(2)}, u32[]{:S(2)}) collective-permute-start(bf16[1,272,128]{2,1,0:T(8,128)(2,1)S(1)} %bitcast.14), channel_id=1, source_target_pairs={{0,5},{1,4},{2,7},{3,6},{4,1},{5,0},{6,3},{7,2},{8,13},{9,12},{10,... | collective-permute-start | bytes 208904 | tf_op jit(solution)/shard_map/ppermute | solution.py:265
  21.6 13.8 %collective-permute-start.11 = (bf16[2,272,128]{2,1,0:T(8,128)(2,1)S(1)}, bf16[2,272,128]{2,1,0:T(8,128)(2,1)S(1)}, u32[]{:S(2)}, u32[]{:S(2)}) collective-permute-start(bf16[2,272,128]{2,1,0:T(8,128)(2,1)S(1)} %join.10.refs_1_), channel_id=1, source_target_pairs={{0,16},{8,24},{16,0},{24,8},{1,17},{9,25},{17,1},{25,9},{2,18},{10... | collective-permute-start | bytes 417800 | tf_op jit(solution)/shard_map/ppermute | solution.py:265
  28.2 7.3 %collective-permute-start.10 = (bf16[2,272,128]{2,1,0:T(8,128)(2,1)S(1)}, bf16[2,272,128]{2,1,0:T(8,128)(2,1)S(1)}, u32[]{:S(2)}, u32[]{:S(2)}) collective-permute-start(bf16[2,272,128]{2,1,0:T(8,128)(2,1)S(1)} %join.9.refs_0_), channel_id=1, source_target_pairs={{0,16},{8,24},{16,0},{24,8},{1,17},{9,25},{17,1},{25,9},{2,18},{10... | collective-permute-start | bytes 417800 | tf_op jit(solution)/shard_map/ppermute | solution.py:265
  29.7 5.0 %collective-permute-start.12 = (bf16[512,128]{1,0:T(8,128)(2,1)S(1)}, bf16[512,128]{1,0:T(8,128)(2,1)S(1)}, u32[]{:S(2)}, u32[]{:S(2)}) collective-permute-start(bf16[512,128]{1,0:T(8,128)(2,1)S(1)} %collective-permute-done.1.refs_9_), channel_id=1, source_target_pairs={{0,1},{1,0},{2,3},{3,2},{4,5},{5,4},{6,7},{7,6},{8,9},{9,8},{10,11... | collective-permute-start | bytes 393224 | tf_op jit(solution)/shard_map/ppermute | solution.py:265
  30.4 8.3 %collective-permute-start.4 = (bf16[512,128]{1,0:T(8,128)(2,1)S(1)}, bf16[512,128]{1,0:T(8,128)(2,1)S(1)}, u32[]{:S(2)}, u32[]{:S(2)}) collective-permute-start(bf16[512,128]{1,0:T(8,128)(2,1)S(1)} %collective-permute-done.1.refs_9_), channel_id=1, source_target_pairs={{0,4},{1,5},{2,6},{3,7},{4,0},{5,1},{6,2},{7,3},{8,12},{9,13},{10,... | collective-permute-start | bytes 393224 | tf_op jit(solution)/shard_map/ppermute | solution.py:265
  34.7 5.0 %collective-permute-start.3 = (bf16[512,128]{1,0:T(8,128)(2,1)S(1)}, bf16[512,128]{1,0:T(8,128)(2,1)S(1)}, u32[]{:S(2)}, u32[]{:S(2)}) collective-permute-start(bf16[512,128]{1,0:T(8,128)(2,1)S(1)} %collective-permute-done.refs_0_), channel_id=1, source_target_pairs={{0,1},{1,0},{2,3},{3,2},{4,5},{5,4},{6,7},{7,6},{8,9},{9,8},{10,11... | collective-permute-start | bytes 393224 | tf_op jit(solution)/shard_map/ppermute | solution.py:265
  35.4 5.0 %collective-permute-start.13 = (bf16[4,272,128]{2,1,0:T(8,128)(2,1)S(1)}, bf16[4,272,128]{2,1,0:T(8,128)(2,1)S(1)}, u32[]{:S(2)}, u32[]{:S(2)}) collective-permute-start(bf16[4,272,128]{2,1,0:T(8,128)(2,1)S(1)} %join.11.refs_0_), channel_id=1, source_target_pairs={{0,8},{8,0},{16,24},{24,16},{1,9},{9,1},{17,25},{25,17},{2,10},{10... | collective-permute-start | bytes 835592 | tf_op jit(solution)/shard_map/ppermute | solution.py:265
  35.5 4.9 %collective-permute-start.14 = (bf16[4,272,128]{2,1,0:T(8,128)(2,1)S(1)}, bf16[4,272,128]{2,1,0:T(8,128)(2,1)S(1)}, u32[]{:S(2)}, u32[]{:S(2)}) collective-permute-start(bf16[4,272,128]{2,1,0:T(8,128)(2,1)S(1)} %join.12.refs_2_), channel_id=1, source_target_pairs={{0,8},{8,0},{16,24},{24,16},{1,9},{9,1},{17,25},{25,17},{2,10},{10... | collective-permute-start | bytes 835592 | tf_op jit(solution)/shard_map/ppermute | solution.py:265
  36.0 4.4 %collective-permute-start.19 = (bf16[4,272,128]{2,1,0:T(8,128)(2,1)S(1)}, bf16[4,272,128]{2,1,0:T(8,128)(2,1)S(1)}, u32[]{:S(2)}, u32[]{:S(2)}) collective-permute-start(bf16[4,272,128]{2,1,0:T(8,128)(2,1)S(1)} %join.13.refs_4_), channel_id=1, source_target_pairs={{0,8},{8,0},{16,24},{24,16},{1,9},{9,1},{17,25},{25,17},{2,10},{10... | collective-permute-start | bytes 835592 | tf_op jit(solution)/shard_map/ppermute | solution.py:265
  38.7 1.7 %collective-permute-start.20 = (bf16[4,272,128]{2,1,0:T(8,128)(2,1)S(1)}, bf16[4,272,128]{2,1,0:T(8,128)(2,1)S(1)}, u32[]{:S(2)}, u32[]{:S(2)}) collective-permute-start(bf16[4,272,128]{2,1,0:T(8,128)(2,1)S(1)} %collective-permute-done.18.refs_6_), channel_id=1, source_target_pairs={{0,8},{8,0},{16,24},{24,16},{1,9},{9,1},{17,25},{25,17},{2,10},{10... | collective-permute-start | bytes 835592 | tf_op jit(solution)/shard_map/ppermute | solution.py:265
  39.7 5.1 %collective-permute-start.5 = (bf16[512,128]{1,0:T(8,128)(2,1)S(1)}, bf16[512,128]{1,0:T(8,128)(2,1)S(1)}, u32[]{:S(2)}, u32[]{:S(2)}) collective-permute-start(bf16[512,128]{1,0:T(8,128)(2,1)S(1)} %join.8), channel_id=1, source_target_pairs={{0,1},{1,0},{2,3},{3,2},{4,5},{5,4},{6,7},{7,6},{8,9},{9,8},{10,11... | collective-permute-start | bytes 393224 | tf_op jit(solution)/shard_map/ppermute | solution.py:265

commit v11 on v10

--- a/solution.py
+++ b/solution.py
@@ -15,7 +15,6 @@
 MIB = 1024 * 1024
 WEIGHT = 10**9
 WEIGHT_FAR = 4 * 10**9
-WEIGHT_LATE = 10**9
 
 
 def pack_kernel(columns, capacity, me_ref, ids_hbm, tiles_hbm, *refs):
@@ -280,7 +279,7 @@
     amps = {0: amplitudes}
     for s in [*range(1, inner), *range(inner, half, inner), half]:
         amps[s] = exchange(amplitudes, "col", s)
-    order = sorted(amps, reverse=True)[:-1]
+    order = sorted(amps)[1:]
     outgoing[half:], got = tie(outgoing[half:], [amps[s] for s in order])
     amps.update(zip(order, got))
 
@@ -301,8 +300,8 @@
     near_group = join(chunks[:half])
     far_passed = [[exchange(g, "row", flip) for flip in flips] for g in far_groups]
     near_passed = [exchange(near_group, "row", flip) for flip in flips]
-    for s in late:
-        amps[s] = join([amps[s]], WEIGHT_LATE)
+    near_passed, got = tie(near_passed, [amps[s] for s in late])
+    amps.update(zip(late, got))
     far_passed, got = tie(far_passed, [amps[s] for s in early])
     amps.update(zip(early, got))
     pieces, rows = [], []

time: 47.2 us -> 43.1 us (0.913)
  waiting for transfers between devices: 15.1 us -> 8.93 us
  starting transfers between devices: 25.1 us -> 27.7 us
    ppermute x21, waiting for transfers between devices: 15.1 us -> 8.93 us  [exchange(): return lax.ppermute(x, axis, [(i, i ^ flip) for i in range(size)])]
    ppermute x21, starting transfers between devices: 25.1 us -> 27.7 us  [exchange(): return lax.ppermute(x, axis, [(i, i ^ flip) for i in range(size)])]
  transfers between devices with their start and end apart: 21 -> 21, of which waited for: 7 -> 6; matrix products, arithmetic and copies ran while one was open for 0% -> 0% of each run, Pallas kernels for 9% -> 10%
where the time goes in v11:
time: 43.1 us; the launch traced here: 42.9 us
  starting transfers between devices  27.7 us (64%)
  waiting for transfers between devices  8.93 us (21%)
  Pallas kernels  6.14 us (14%)
    ppermute x21, starting transfers between devices, exchange(): return lax.ppermute(x, axis, [(i, i ^ flip) for i in range(size)])  27.7 us
    ppermute x21, waiting for transfers between devices, exchange(): return lax.ppermute(x, axis, [(i, i ^ flip) for i in range(size)])  8.93 us
    pallas_call x1, Pallas kernels, near_half(): pl.pallas_call(functools.partial(near_kernel, n_pieces, offsets, capacity...  2.96 us
    pallas_call x1, Pallas kernels, far_half(): pl.pallas_call(functools.partial(far_kernel, offsets, depth // width), ou...  1.85 us
    pallas_call x1, Pallas kernels, pack(): pl.pallas_call(functools.partial(pack_kernel, columns, capacity), out_sha...  1.25 us
  transfers between devices with their start and end apart: 21, of which 6 were waited for; matrix products, arithmetic and copies ran while one was open for 0% of the time, Pallas kernels for 10%

profile of v11, /device:TPU:0, one launch (start us, length us, event | category | flops | bytes accessed | tf_op | source)
XLA Modules:
  0.0 42.9 jit_solution(666637307291793037)
XLA Ops:
  0.0 2.9 %collective-permute-start = (bf16[512,128]{1,0:T(8,128)(2,1)}, bf16[512,128]{1,0:T(8,128)(2,1)S(1)}, u32[]{:S(2)}, u32[]{:S(2)}) collective-permute-start(bf16[512,128]{1,0:T(8,128)(2,1)} %refs_11_.1), channel_id=1, source_target_pairs={{0,1},{1,0},{2,3},{3,2},{4,5},{5,4},{6,7},{7,6},{8,9},{9,8},{10,11... | collective-permute-start | bytes 393224 | tf_op jit(solution)/shard_map/ppermute | solution.py:264
  2.9 1.6 %collective-permute-start.1 = (bf16[512,128]{1,0:T(8,128)(2,1)}, bf16[512,128]{1,0:T(8,128)(2,1)S(1)}, u32[]{:S(2)}, u32[]{:S(2)}) collective-permute-start(bf16[512,128]{1,0:T(8,128)(2,1)} %refs_11_.1), channel_id=1, source_target_pairs={{0,2},{1,3},{2,0},{3,1},{4,6},{5,7},{6,4},{7,5},{8,10},{9,11},{10,... | collective-permute-start | bytes 393224 | tf_op jit(solution)/shard_map/ppermute | solution.py:264
  4.5 2.6 %collective-permute-start.2 = (bf16[512,128]{1,0:T(8,128)(2,1)}, bf16[512,128]{1,0:T(8,128)(2,1)S(1)}, u32[]{:S(2)}, u32[]{:S(2)}) collective-permute-start(bf16[512,128]{1,0:T(8,128)(2,1)} %refs_11_.1), channel_id=1, source_target_pairs={{0,4},{1,5},{2,6},{3,7},{4,0},{5,1},{6,2},{7,3},{8,12},{9,13},{10,... | collective-permute-start | bytes 393224 | tf_op jit(solution)/shard_map/ppermute | solution.py:264
  7.1 1.3 %pack.1 = (bf16[272,128]{1,0:T(8,128)(2,1)S(1)}, bf16[272,128]{1,0:T(8,128)(2,1)S(1)}, bf16[272,128]{1,0:T(8,128)(2,1)S(1)}, bf16[272,128]{1,0:T(8,128)(2,1)S(1)...) custom-call(s32[1]{0:T(128)} %bitcast.me_ref, ...), custom_call_target="tpu_custom_call" | custom-call | tf_op jit(solution)/shard_map/pack/pallas_call | solution.py:65
  8.4 0.6 %collective-permute-start.3 = (bf16[1,272,128]{2,1,0:T(8,128)(2,1)S(1)}, bf16[1,272,128]{2,1,0:T(8,128)(2,1)S(1)}, u32[]{:S(2)}, u32[]{:S(2)}) collective-permute-start(bf16[1,272,128]{2,1,0:T(8,128)(2,1)S(1)} %bitcast.20), channel_id=1, source_target_pairs={{0,1},{1,0},{2,3},{3,2},{4,5},{5,4},{6,7},{7,6},{8,9},{9,8},{10,11... | collective-permute-start | bytes 208904 | tf_op jit(solution)/shard_map/ppermute | solution.py:264
  9.4 2.5 %collective-permute-start.5 = (bf16[1,272,128]{2,1,0:T(8,128)(2,1)S(1)}, bf16[1,272,128]{2,1,0:T(8,128)(2,1)S(1)}, u32[]{:S(2)}, u32[]{:S(2)}) collective-permute-start(bf16[1,272,128]{2,1,0:T(8,128)(2,1)S(1)} %bitcast.18), channel_id=1, source_target_pairs={{0,3},{1,2},{2,1},{3,0},{4,7},{5,6},{6,5},{7,4},{8,11},{9,10},{10,... | collective-permute-start | bytes 208904 | tf_op jit(solution)/shard_map/ppermute | solution.py:264
  11.9 2.4 %collective-permute-start.10 = (bf16[1,272,128]{2,1,0:T(8,128)(2,1)S(1)}, bf16[1,272,128]{2,1,0:T(8,128)(2,1)S(1)}, u32[]{:S(2)}, u32[]{:S(2)}) collective-permute-start(bf16[1,272,128]{2,1,0:T(8,128)(2,1)S(1)} %bitcast.17), channel_id=1, source_target_pairs={{0,4},{1,5},{2,6},{3,7},{4,0},{5,1},{6,2},{7,3},{8,12},{9,13},{10,... | collective-permute-start | bytes 208904 | tf_op jit(solution)/shard_map/ppermute | solution.py:264
  14.4 0.5 %collective-permute-start.11 = (bf16[1,272,128]{2,1,0:T(8,128)(2,1)S(1)}, bf16[1,272,128]{2,1,0:T(8,128)(2,1)S(1)}, u32[]{:S(2)}, u32[]{:S(2)}) collective-permute-start(bf16[1,272,128]{2,1,0:T(8,128)(2,1)S(1)} %bitcast.16), channel_id=1, source_target_pairs={{0,5},{1,4},{2,7},{3,6},{4,1},{5,0},{6,3},{7,2},{8,13},{9,12},{10,... | collective-permute-start | bytes 208904 | tf_op jit(solution)/shard_map/ppermute | solution.py:264
  14.8 0.9 %collective-permute-done.5.refs_3_ = bf16[1,272,128]{2,1,0:T(8,128)(2,1)S(1)} collective-permute-done((bf16[1,272,128]{2,1,0:T(8,128)(2,1)S(1)}, bf16[1,272,128]{2,1,0:T(8,128)(2,1)S(1)}, u32[]{:S(2)}, u32[]{:S(2)}) %collective-permute-start.5) | collective-permute-done | bytes 69664 | tf_op jit(solution)/shard_map/ppermute | solution.py:264
  15.7 1.6 %collective-permute-start.6 = (bf16[4,272,128]{2,1,0:T(8,128)(2,1)S(1)}, bf16[4,272,128]{2,1,0:T(8,128)(2,1)S(1)}, u32[]{:S(2)}, u32[]{:S(2)}) collective-permute-start(bf16[4,272,128]{2,1,0:T(8,128)(2,1)S(1)} %join.6.refs_4_), channel_id=1, source_target_pairs={{0,16},{8,24},{16,0},{24,8},{1,17},{9,25},{17,1},{25,9},{2,18},{10... | collective-permute-start | bytes 835592 | tf_op jit(solution)/shard_map/ppermute | solution.py:264
  17.3 3.7 %collective-permute-start.12 = (bf16[1,272,128]{2,1,0:T(8,128)(2,1)S(1)}, bf16[1,272,128]{2,1,0:T(8,128)(2,1)S(1)}, u32[]{:S(2)}, u32[]{:S(2)}) collective-permute-start(bf16[1,272,128]{2,1,0:T(8,128)(2,1)S(1)} %bitcast.15), channel_id=1, source_target_pairs={{0,6},{1,7},{2,4},{3,5},{4,2},{5,3},{6,0},{7,1},{8,14},{9,15},{10,... | collective-permute-start | bytes 208904 | tf_op jit(solution)/shard_map/ppermute | solution.py:264
  21.0 0.9 %collective-permute-start.13 = (bf16[1,272,128]{2,1,0:T(8,128)(2,1)S(1)}, bf16[1,272,128]{2,1,0:T(8,128)(2,1)S(1)}, u32[]{:S(2)}, u32[]{:S(2)}) collective-permute-start(bf16[1,272,128]{2,1,0:T(8,128)(2,1)S(1)} %bitcast.14), channel_id=1, source_target_pairs={{0,7},{1,6},{2,5},{3,4},{4,3},{5,2},{6,1},{7,0},{8,15},{9,14},{10,... | collective-permute-start | bytes 208904 | tf_op jit(solution)/shard_map/ppermute | solution.py:264
  21.9 0.7 %collective-permute-start.16 = (bf16[512,128]{1,0:T(8,128)(2,1)S(1)}, bf16[512,128]{1,0:T(8,128)(2,1)S(1)}, u32[]{:S(2)}, u32[]{:S(2)}) collective-permute-start(bf16[512,128]{1,0:T(8,128)(2,1)S(1)} %collective-permute-done.1.refs_9_), channel_id=1, source_target_pairs={{0,1},{1,0},{2,3},{3,2},{4,5},{5,4},{6,7},{7,6},{8,9},{9,8},{10,11... | collective-permute-start | bytes 393224 | tf_op jit(solution)/shard_map/ppermute | solution.py:264
  22.8 3.1 %collective-permute-start.14 = (bf16[2,272,128]{2,1,0:T(8,128)(2,1)S(1)}, bf16[2,272,128]{2,1,0:T(8,128)(2,1)S(1)}, u32[]{:S(2)}, u32[]{:S(2)}) collective-permute-start(bf16[2,272,128]{2,1,0:T(8,128)(2,1)S(1)} %join.8.refs_0_), channel_id=1, source_target_pairs={{0,16},{8,24},{16,0},{24,8},{1,17},{9,25},{17,1},{25,9},{2,18},{10... | collective-permute-start | bytes 417800 | tf_op jit(solution)/shard_map/ppermute | solution.py:264
  25.8 2.2 %collective-permute-done.13.refs_1_ = bf16[1,272,128]{2,1,0:T(8,128)(2,1)S(1)} collective-permute-done((bf16[1,272,128]{2,1,0:T(8,128)(2,1)S(1)}, bf16[1,272,128]{2,1,0:T(8,128)(2,1)S(1)}, u32[]{:S(2)}, u32[]{:S(2)}) %collective-permute-start.13) | collective-permute-done | bytes 69664 | tf_op jit(solution)/shard_map/ppermute | solution.py:264
  28.1 0.5 %collective-permute-start.15 = (bf16[2,272,128]{2,1,0:T(8,128)(2,1)S(1)}, bf16[2,272,128]{2,1,0:T(8,128)(2,1)S(1)}, u32[]{:S(2)}, u32[]{:S(2)}) collective-permute-start(bf16[2,272,128]{2,1,0:T(8,128)(2,1)S(1)} %join.9.refs_1_), channel_id=1, source_target_pairs={{0,16},{8,24},{16,0},{24,8},{1,17},{9,25},{17,1},{25,9},{2,18},{10... | collective-permute-start | bytes 417800 | tf_op jit(solution)/shard_map/ppermute | solution.py:264
  28.6 1.5 %collective-permute-start.7 = (bf16[512,128]{1,0:T(8,128)(2,1)S(1)}, bf16[512,128]{1,0:T(8,128)(2,1)S(1)}, u32[]{:S(2)}, u32[]{:S(2)}) collective-permute-start(bf16[512,128]{1,0:T(8,128)(2,1)S(1)} %collective-permute-done.2.refs_0_), channel_id=1, source_target_pairs={{0,1},{1,0},{2,3},{3,2},{4,5},{5,4},{6,7},{7,6},{8,9},{9,8},{10,11... | collective-permute-start | bytes 393224 | tf_op jit(solution)/shard_map/ppermute | solution.py:264
  30.1 3.1 %collective-permute-done.15.refs_1_ = bf16[2,272,128]{2,1,0:T(8,128)(2,1)S(1)} collective-permute-done((bf16[2,272,128]{2,1,0:T(8,128)(2,1)S(1)}, bf16[2,272,128]{2,1,0:T(8,128)(2,1)S(1)}, u32[]{:S(2)}, u32[]{:S(2)}) %collective-permute-start.15) | collective-permute-done | bytes 139296 | tf_op jit(solution)/shard_map/ppermute | solution.py:264
  33.3 0.5 %collective-permute-start.18 = (bf16[4,272,128]{2,1,0:T(8,128)(2,1)S(1)}, bf16[4,272,128]{2,1,0:T(8,128)(2,1)S(1)}, u32[]{:S(2)}, u32[]{:S(2)}) collective-permute-start(bf16[4,272,128]{2,1,0:T(8,128)(2,1)S(1)} %join.11.refs_2_), channel_id=1, source_target_pairs={{0,8},{8,0},{16,24},{24,16},{1,9},{9,1},{17,25},{25,17},{2,10},{10... | collective-permute-start | bytes 835592 | tf_op jit(solution)/shard_map/ppermute | solution.py:264
  34.3 1.7 %collective-permute-done.8.refs_0_.refs_2_ = bf16[512,128]{1,0:T(8,128)(2,1)S(1)} collective-permute-done((bf16[512,128]{1,0:T(8,128)(2,1)S(1)}, bf16[512,128]{1,0:T(8,128)(2,1)S(1)}, u32[]{:S(2)}, u32[]{:S(2)}) %collective-permute-start.8) | collective-permute-done | bytes 131104 | tf_op jit(solution)/shard_map/ppermute | solution.py:264
  36.0 1.1 %collective-permute-start.9 = (bf16[512,128]{1,0:T(8,128)(2,1)S(1)}, bf16[512,128]{1,0:T(8,128)(2,1)S(1)}, u32[]{:S(2)}, u32[]{:S(2)}) collective-permute-start(bf16[512,128]{1,0:T(8,128)(2,1)S(1)} %join.7), channel_id=1, source_target_pairs={{0,1},{1,0},{2,3},{3,2},{4,5},{5,4},{6,7},{7,6},{8,9},{9,8},{10,11... | collective-permute-start | bytes 393224 | tf_op jit(solution)/shard_map/ppermute | solution.py:264
  37.2 3.0 %near_half.1 = (f32[512,1024]{1,0:T(8,128)S(1)}, bf16[1024,1024]{1,0:T(8,128)(2,1)S(1)}) custom-call(s32[9]{0:T(128)S(1)} %stack.24.where_ref, bf16[4,272,128]{2,1,0:T(8,128)(2,1)S(1)} %join.10.refs_0_, bf16[4,272,128]{2,1,0:T(8,128)(2,1)S(1)} %collective-permute-done.17.refs_1_, bf16[4,272,128]{2,1,0:T(8,128)(2,1)S(1)} %join.11.refs_2_, ...), custom_call_target="tpu_custom_call" | custom-call | flops 536870912 | bytes 8388608 | tf_op jit(solution)/shard_map/near_half/pallas_call | solution.py:192
  40.2 0.9 %collective-permute-done.9.refs_3_ = bf16[512,128]{1,0:T(8,128)(2,1)S(1)} collective-permute-done((bf16[512,128]{1,0:T(8,128)(2,1)S(1)}, bf16[512,128]{1,0:T(8,128)(2,1)S(1)}, u32[]{:S(2)}, u32[]{:S(2)}) %collective-permute-start.9) | collective-permute-done | bytes 131104 | tf_op jit(solution)/shard_map/ppermute | solution.py:264
  41.1 1.8 %far_half.1 = f32[512,1024]{1,0:T(8,128)} custom-call(bf16[512,128]{1,0:T(8,128)(2,1)S(1)} %collective-permute-done.2.refs_0_, bf16[512,128]{1,0:T(8,128)(2,1)S(1)} %collective-permute-done.7.refs_1_, bf16[512,128]{1,0:T(8,128)(2,1)S(1)} %collective-permute-done.8.refs_0_.refs_2_, bf16[512,128]{1,0:T(8,128)(2,1)S(1)} %collective-permute-done.9.refs_3_, ...), custom_call_target="tpu_custom_call" | custom-call | flops 536870912 | bytes 8388608 | tf_op jit(solution)/shard_map/far_half/pallas_call | solution.py:242
  (28 shorter events, 1.4 us)
Async XLA Ops:
  0.0 9.4 %collective-permute-start = (bf16[512,128]{1,0:T(8,128)(2,1)}, bf16[512,128]{1,0:T(8,128)(2,1)S(1)}, u32[]{:S(2)}, u32[]{:S(2)}) collective-permute-start(bf16[512,128]{1,0:T(8,128)(2,1)} %refs_11_.1), channel_id=1, source_target_pairs={{0,1},{1,0},{2,3},{3,2},{4,5},{5,4},{6,7},{7,6},{8,9},{9,8},{10,11... | collective-permute-start | bytes 393224 | tf_op jit(solution)/shard_map/ppermute | solution.py:264
  2.9 9.0 %collective-permute-start.1 = (bf16[512,128]{1,0:T(8,128)(2,1)}, bf16[512,128]{1,0:T(8,128)(2,1)S(1)}, u32[]{:S(2)}, u32[]{:S(2)}) collective-permute-start(bf16[512,128]{1,0:T(8,128)(2,1)} %refs_11_.1), channel_id=1, source_target_pairs={{0,2},{1,3},{2,0},{3,1},{4,6},{5,7},{6,4},{7,5},{8,10},{9,11},{10,... | collective-permute-start | bytes 393224 | tf_op jit(solution)/shard_map/ppermute | solution.py:264
  4.5 7.4 %collective-permute-start.2 = (bf16[512,128]{1,0:T(8,128)(2,1)}, bf16[512,128]{1,0:T(8,128)(2,1)S(1)}, u32[]{:S(2)}, u32[]{:S(2)}) collective-permute-start(bf16[512,128]{1,0:T(8,128)(2,1)} %refs_11_.1), channel_id=1, source_target_pairs={{0,4},{1,5},{2,6},{3,7},{4,0},{5,1},{6,2},{7,3},{8,12},{9,13},{10,... | collective-permute-start | bytes 393224 | tf_op jit(solution)/shard_map/ppermute | solution.py:264
  8.4 6.5 %collective-permute-start.3 = (bf16[1,272,128]{2,1,0:T(8,128)(2,1)S(1)}, bf16[1,272,128]{2,1,0:T(8,128)(2,1)S(1)}, u32[]{:S(2)}, u32[]{:S(2)}) collective-permute-start(bf16[1,272,128]{2,1,0:T(8,128)(2,1)S(1)} %bitcast.20), channel_id=1, source_target_pairs={{0,1},{1,0},{2,3},{3,2},{4,5},{5,4},{6,7},{7,6},{8,9},{9,8},{10,11... | collective-permute-start | bytes 208904 | tf_op jit(solution)/shard_map/ppermute | solution.py:264
  9.0 5.9 %collective-permute-start.4 = (bf16[1,272,128]{2,1,0:T(8,128)(2,1)S(1)}, bf16[1,272,128]{2,1,0:T(8,128)(2,1)S(1)}, u32[]{:S(2)}, u32[]{:S(2)}) collective-permute-start(bf16[1,272,128]{2,1,0:T(8,128)(2,1)S(1)} %bitcast.19), channel_id=1, source_target_pairs={{0,2},{1,3},{2,0},{3,1},{4,6},{5,7},{6,4},{7,5},{8,10},{9,11},{10,... | collective-permute-start | bytes 208904 | tf_op jit(solution)/shard_map/ppermute | solution.py:264
  9.4 6.3 %collective-permute-start.5 = (bf16[1,272,128]{2,1,0:T(8,128)(2,1)S(1)}, bf16[1,272,128]{2,1,0:T(8,128)(2,1)S(1)}, u32[]{:S(2)}, u32[]{:S(2)}) collective-permute-start(bf16[1,272,128]{2,1,0:T(8,128)(2,1)S(1)} %bitcast.18), channel_id=1, source_target_pairs={{0,3},{1,2},{2,1},{3,0},{4,7},{5,6},{6,5},{7,4},{8,11},{9,10},{10,... | collective-permute-start | bytes 208904 | tf_op jit(solution)/shard_map/ppermute | solution.py:264
  11.9 10.0 %collective-permute-start.10 = (bf16[1,272,128]{2,1,0:T(8,128)(2,1)S(1)}, bf16[1,272,128]{2,1,0:T(8,128)(2,1)S(1)}, u32[]{:S(2)}, u32[]{:S(2)}) collective-permute-start(bf16[1,272,128]{2,1,0:T(8,128)(2,1)S(1)} %bitcast.17), channel_id=1, source_target_pairs={{0,4},{1,5},{2,6},{3,7},{4,0},{5,1},{6,2},{7,3},{8,12},{9,13},{10,... | collective-permute-start | bytes 208904 | tf_op jit(solution)/shard_map/ppermute | solution.py:264
  14.4 8.4 %collective-permute-start.11 = (bf16[1,272,128]{2,1,0:T(8,128)(2,1)S(1)}, bf16[1,272,128]{2,1,0:T(8,128)(2,1)S(1)}, u32[]{:S(2)}, u32[]{:S(2)}) collective-permute-start(bf16[1,272,128]{2,1,0:T(8,128)(2,1)S(1)} %bitcast.16), channel_id=1, source_target_pairs={{0,5},{1,4},{2,7},{3,6},{4,1},{5,0},{6,3},{7,2},{8,13},{9,12},{10,... | collective-permute-start | bytes 208904 | tf_op jit(solution)/shard_map/ppermute | solution.py:264
  15.7 18.1 %collective-permute-start.6 = (bf16[4,272,128]{2,1,0:T(8,128)(2,1)S(1)}, bf16[4,272,128]{2,1,0:T(8,128)(2,1)S(1)}, u32[]{:S(2)}, u32[]{:S(2)}) collective-permute-start(bf16[4,272,128]{2,1,0:T(8,128)(2,1)S(1)} %join.6.refs_4_), channel_id=1, source_target_pairs={{0,16},{8,24},{16,0},{24,8},{1,17},{9,25},{17,1},{25,9},{2,18},{10... | collective-permute-start | bytes 835592 | tf_op jit(solution)/shard_map/ppermute | solution.py:264
  17.3 8.5 %collective-permute-start.12 = (bf16[1,272,128]{2,1,0:T(8,128)(2,1)S(1)}, bf16[1,272,128]{2,1,0:T(8,128)(2,1)S(1)}, u32[]{:S(2)}, u32[]{:S(2)}) collective-permute-start(bf16[1,272,128]{2,1,0:T(8,128)(2,1)S(1)} %bitcast.15), channel_id=1, source_target_pairs={{0,6},{1,7},{2,4},{3,5},{4,2},{5,3},{6,0},{7,1},{8,14},{9,15},{10,... | collective-permute-start | bytes 208904 | tf_op jit(solution)/shard_map/ppermute | solution.py:264
  21.0 7.1 %collective-permute-start.13 = (bf16[1,272,128]{2,1,0:T(8,128)(2,1)S(1)}, bf16[1,272,128]{2,1,0:T(8,128)(2,1)S(1)}, u32[]{:S(2)}, u32[]{:S(2)}) collective-permute-start(bf16[1,272,128]{2,1,0:T(8,128)(2,1)S(1)} %bitcast.14), channel_id=1, source_target_pairs={{0,7},{1,6},{2,5},{3,4},{4,3},{5,2},{6,1},{7,0},{8,15},{9,14},{10,... | collective-permute-start | bytes 208904 | tf_op jit(solution)/shard_map/ppermute | solution.py:264
  21.9 8.2 %collective-permute-start.16 = (bf16[512,128]{1,0:T(8,128)(2,1)S(1)}, bf16[512,128]{1,0:T(8,128)(2,1)S(1)}, u32[]{:S(2)}, u32[]{:S(2)}) collective-permute-start(bf16[512,128]{1,0:T(8,128)(2,1)S(1)} %collective-permute-done.1.refs_9_), channel_id=1, source_target_pairs={{0,1},{1,0},{2,3},{3,2},{4,5},{5,4},{6,7},{7,6},{8,9},{9,8},{10,11... | collective-permute-start | bytes 393224 | tf_op jit(solution)/shard_map/ppermute | solution.py:264
  22.8 7.4 %collective-permute-start.14 = (bf16[2,272,128]{2,1,0:T(8,128)(2,1)S(1)}, bf16[2,272,128]{2,1,0:T(8,128)(2,1)S(1)}, u32[]{:S(2)}, u32[]{:S(2)}) collective-permute-start(bf16[2,272,128]{2,1,0:T(8,128)(2,1)S(1)} %join.8.refs_0_), channel_id=1, source_target_pairs={{0,16},{8,24},{16,0},{24,8},{1,17},{9,25},{17,1},{25,9},{2,18},{10... | collective-permute-start | bytes 417800 | tf_op jit(solution)/shard_map/ppermute | solution.py:264
  28.1 5.1 %collective-permute-start.15 = (bf16[2,272,128]{2,1,0:T(8,128)(2,1)S(1)}, bf16[2,272,128]{2,1,0:T(8,128)(2,1)S(1)}, u32[]{:S(2)}, u32[]{:S(2)}) collective-permute-start(bf16[2,272,128]{2,1,0:T(8,128)(2,1)S(1)} %join.9.refs_1_), channel_id=1, source_target_pairs={{0,16},{8,24},{16,0},{24,8},{1,17},{9,25},{17,1},{25,9},{2,18},{10... | collective-permute-start | bytes 417800 | tf_op jit(solution)/shard_map/ppermute | solution.py:264
  28.6 5.2 %collective-permute-start.7 = (bf16[512,128]{1,0:T(8,128)(2,1)S(1)}, bf16[512,128]{1,0:T(8,128)(2,1)S(1)}, u32[]{:S(2)}, u32[]{:S(2)}) collective-permute-start(bf16[512,128]{1,0:T(8,128)(2,1)S(1)} %collective-permute-done.2.refs_0_), channel_id=1, source_target_pairs={{0,1},{1,0},{2,3},{3,2},{4,5},{5,4},{6,7},{7,6},{8,9},{9,8},{10,11... | collective-permute-start | bytes 393224 | tf_op jit(solution)/shard_map/ppermute | solution.py:264
  30.1 5.9 %collective-permute-start.8 = (bf16[512,128]{1,0:T(8,128)(2,1)S(1)}, bf16[512,128]{1,0:T(8,128)(2,1)S(1)}, u32[]{:S(2)}, u32[]{:S(2)}) collective-permute-start(bf16[512,128]{1,0:T(8,128)(2,1)S(1)} %collective-permute-done.1.refs_9_), channel_id=1, source_target_pairs={{0,4},{1,5},{2,6},{3,7},{4,0},{5,1},{6,2},{7,3},{8,12},{9,13},{10,... | collective-permute-start | bytes 393224 | tf_op jit(solution)/shard_map/ppermute | solution.py:264
  33.2 4.0 %collective-permute-start.17 = (bf16[4,272,128]{2,1,0:T(8,128)(2,1)S(1)}, bf16[4,272,128]{2,1,0:T(8,128)(2,1)S(1)}, u32[]{:S(2)}, u32[]{:S(2)}) collective-permute-start(bf16[4,272,128]{2,1,0:T(8,128)(2,1)S(1)} %join.10.refs_0_), channel_id=1, source_target_pairs={{0,8},{8,0},{16,24},{24,16},{1,9},{9,1},{17,25},{25,17},{2,10},{10... | collective-permute-start | bytes 835592 | tf_op jit(solution)/shard_map/ppermute | solution.py:264
  33.3 3.9 %collective-permute-start.18 = (bf16[4,272,128]{2,1,0:T(8,128)(2,1)S(1)}, bf16[4,272,128]{2,1,0:T(8,128)(2,1)S(1)}, u32[]{:S(2)}, u32[]{:S(2)}) collective-permute-start(bf16[4,272,128]{2,1,0:T(8,128)(2,1)S(1)} %join.11.refs_2_), channel_id=1, source_target_pairs={{0,8},{8,0},{16,24},{24,16},{1,9},{9,1},{17,25},{25,17},{2,10},{10... | collective-permute-start | bytes 835592 | tf_op jit(solution)/shard_map/ppermute | solution.py:264
  33.8 3.4 %collective-permute-start.19 = (bf16[4,272,128]{2,1,0:T(8,128)(2,1)S(1)}, bf16[4,272,128]{2,1,0:T(8,128)(2,1)S(1)}, u32[]{:S(2)}, u32[]{:S(2)}) collective-permute-start(bf16[4,272,128]{2,1,0:T(8,128)(2,1)S(1)} %join.6.refs_4_), channel_id=1, source_target_pairs={{0,8},{8,0},{16,24},{24,16},{1,9},{9,1},{17,25},{25,17},{2,10},{10... | collective-permute-start | bytes 835592 | tf_op jit(solution)/shard_map/ppermute | solution.py:264
  33.9 3.3 %collective-permute-start.20 = (bf16[4,272,128]{2,1,0:T(8,128)(2,1)S(1)}, bf16[4,272,128]{2,1,0:T(8,128)(2,1)S(1)}, u32[]{:S(2)}, u32[]{:S(2)}) collective-permute-start(bf16[4,272,128]{2,1,0:T(8,128)(2,1)S(1)} %collective-permute-done.6.refs_6_), channel_id=1, source_target_pairs={{0,8},{8,0},{16,24},{24,16},{1,9},{9,1},{17,25},{25,17},{2,10},{10... | collective-permute-start | bytes 835592 | tf_op jit(solution)/shard_map/ppermute | solution.py:264
  36.0 5.0 %collective-permute-start.9 = (bf16[512,128]{1,0:T(8,128)(2,1)S(1)}, bf16[512,128]{1,0:T(8,128)(2,1)S(1)}, u32[]{:S(2)}, u32[]{:S(2)}) collective-permute-start(bf16[512,128]{1,0:T(8,128)(2,1)S(1)} %join.7), channel_id=1, source_target_pairs={{0,1},{1,0},{2,3},{3,2},{4,5},{5,4},{6,7},{7,6},{8,9},{9,8},{10,11... | collective-permute-start | bytes 393224 | tf_op jit(solution)/shard_map/ppermute | solution.py:264

commit v12 on v9

--- a/solution.py
+++ b/solution.py
@@ -23,7 +23,8 @@
     ids_copy = pltpu.make_async_copy(ids_hbm, ids_ref, ids_sem)
     tiles_copy = pltpu.make_async_copy(tiles_hbm, tiles_ref, tiles_sem)
     ids_copy.start()
-    tiles_copy.start()
+    for t in range(tiles_ref.shape[1]):
+        pltpu.make_async_copy(tiles_hbm.at[0, t], tiles_ref.at[0, t], tiles_sem).start()
     per_device, width = tiles_ref.shape[1], tiles_ref.shape[2]
     shift = per_device.bit_length() - 1
     for d in range(columns):
@@ -137,7 +138,10 @@
     own_copy = pltpu.make_async_copy(own, amp.at[:, pl.ds(0, width)], own_sem)
     own_copy.start()
     res_copy = pltpu.make_async_copy(residual, res, res_sem)
-    res_copy.start()
+    share = residual.shape[0] // 8
+    for i in range(8):
+        part = pl.ds(i * share, share)
+        pltpu.make_async_copy(residual.at[part, :], res.at[part, :], res_sem).start()
     at = 0
     for piece in pieces:
         rows = piece[:, capacity * width :, :]

time: 43 us -> 43.1 us (level)
  transfers between devices with their start and end apart: 21 -> 21, of which waited for: 6 -> 7; matrix products, arithmetic and copies ran while one was open for 0% -> 0% of each run, Pallas kernels for 10% -> 10%
where the time goes in v12:
time: 43.1 us; the launch traced here: 42.9 us
  starting transfers between devices  27 us (63%)
  waiting for transfers between devices  9.73 us (23%)
  Pallas kernels  5.97 us (14%)
    ppermute x21, starting transfers between devices, exchange(): return lax.ppermute(x, axis, [(i, i ^ flip) for i in range(size)])  27 us
    ppermute x21, waiting for transfers between devices, exchange(): return lax.ppermute(x, axis, [(i, i ^ flip) for i in range(size)])  9.73 us
    pallas_call x1, Pallas kernels, near_half(): pl.pallas_call(functools.partial(near_kernel, n_pieces, offsets, capacity...  2.83 us
    pallas_call x1, Pallas kernels, far_half(): pl.pallas_call(functools.partial(far_kernel, offsets, depth // width), ou...  1.85 us
    pallas_call x1, Pallas kernels, pack(): pl.pallas_call(functools.partial(pack_kernel, columns, capacity), out_sha...  1.2 us
  transfers between devices with their start and end apart: 21, of which 7 were waited for; matrix products, arithmetic and copies ran while one was open for 0% of the time, Pallas kernels for 10%

profile of v12, /device:TPU:0, one launch (start us, length us, event | category | flops | bytes accessed | tf_op | source)
XLA Modules:
  0.0 42.9 jit_solution(2994561002892004534)
XLA Ops:
  0.0 2.9 %collective-permute-start = (bf16[512,128]{1,0:T(8,128)(2,1)}, bf16[512,128]{1,0:T(8,128)(2,1)S(1)}, u32[]{:S(2)}, u32[]{:S(2)}) collective-permute-start(bf16[512,128]{1,0:T(8,128)(2,1)} %refs_11_.1), channel_id=1, source_target_pairs={{0,1},{1,0},{2,3},{3,2},{4,5},{5,4},{6,7},{7,6},{8,9},{9,8},{10,11... | collective-permute-start | bytes 393224 | tf_op jit(solution)/shard_map/ppermute | solution.py:268
  2.9 1.6 %collective-permute-start.1 = (bf16[512,128]{1,0:T(8,128)(2,1)}, bf16[512,128]{1,0:T(8,128)(2,1)S(1)}, u32[]{:S(2)}, u32[]{:S(2)}) collective-permute-start(bf16[512,128]{1,0:T(8,128)(2,1)} %refs_11_.1), channel_id=1, source_target_pairs={{0,2},{1,3},{2,0},{3,1},{4,6},{5,7},{6,4},{7,5},{8,10},{9,11},{10,... | collective-permute-start | bytes 393224 | tf_op jit(solution)/shard_map/ppermute | solution.py:268
  4.5 2.6 %collective-permute-start.2 = (bf16[512,128]{1,0:T(8,128)(2,1)}, bf16[512,128]{1,0:T(8,128)(2,1)S(1)}, u32[]{:S(2)}, u32[]{:S(2)}) collective-permute-start(bf16[512,128]{1,0:T(8,128)(2,1)} %refs_11_.1), channel_id=1, source_target_pairs={{0,4},{1,5},{2,6},{3,7},{4,0},{5,1},{6,2},{7,3},{8,12},{9,13},{10,... | collective-permute-start | bytes 393224 | tf_op jit(solution)/shard_map/ppermute | solution.py:268
  7.1 1.2 %pack.1 = (bf16[272,128]{1,0:T(8,128)(2,1)S(1)}, bf16[272,128]{1,0:T(8,128)(2,1)S(1)}, bf16[272,128]{1,0:T(8,128)(2,1)S(1)}, bf16[272,128]{1,0:T(8,128)(2,1)S(1)...) custom-call(s32[1]{0:T(128)} %bitcast.me_ref, ...), custom_call_target="tpu_custom_call" | custom-call | tf_op jit(solution)/shard_map/pack/pallas_call | solution.py:66
  8.3 0.6 %collective-permute-start.15 = (bf16[1,272,128]{2,1,0:T(8,128)(2,1)S(1)}, bf16[1,272,128]{2,1,0:T(8,128)(2,1)S(1)}, u32[]{:S(2)}, u32[]{:S(2)}) collective-permute-start(bf16[1,272,128]{2,1,0:T(8,128)(2,1)S(1)} %bitcast.20), channel_id=1, source_target_pairs={{0,1},{1,0},{2,3},{3,2},{4,5},{5,4},{6,7},{7,6},{8,9},{9,8},{10,11... | collective-permute-start | bytes 208904 | tf_op jit(solution)/shard_map/ppermute | solution.py:268
  8.9 0.4 %collective-permute-start.16 = (bf16[1,272,128]{2,1,0:T(8,128)(2,1)S(1)}, bf16[1,272,128]{2,1,0:T(8,128)(2,1)S(1)}, u32[]{:S(2)}, u32[]{:S(2)}) collective-permute-start(bf16[1,272,128]{2,1,0:T(8,128)(2,1)S(1)} %bitcast.19), channel_id=1, source_target_pairs={{0,2},{1,3},{2,0},{3,1},{4,6},{5,7},{6,4},{7,5},{8,10},{9,11},{10,... | collective-permute-start | bytes 208904 | tf_op jit(solution)/shard_map/ppermute | solution.py:268
  9.4 2.5 %collective-permute-start.17 = (bf16[1,272,128]{2,1,0:T(8,128)(2,1)S(1)}, bf16[1,272,128]{2,1,0:T(8,128)(2,1)S(1)}, u32[]{:S(2)}, u32[]{:S(2)}) collective-permute-start(bf16[1,272,128]{2,1,0:T(8,128)(2,1)S(1)} %bitcast.18), channel_id=1, source_target_pairs={{0,3},{1,2},{2,1},{3,0},{4,7},{5,6},{6,5},{7,4},{8,11},{9,10},{10,... | collective-permute-start | bytes 208904 | tf_op jit(solution)/shard_map/ppermute | solution.py:268
  11.9 3.8 %collective-permute-start.6 = (bf16[1,272,128]{2,1,0:T(8,128)(2,1)S(1)}, bf16[1,272,128]{2,1,0:T(8,128)(2,1)S(1)}, u32[]{:S(2)}, u32[]{:S(2)}) collective-permute-start(bf16[1,272,128]{2,1,0:T(8,128)(2,1)S(1)} %bitcast.17), channel_id=1, source_target_pairs={{0,6},{1,7},{2,4},{3,5},{4,2},{5,3},{6,0},{7,1},{8,14},{9,15},{10,... | collective-permute-start | bytes 208904 | tf_op jit(solution)/shard_map/ppermute | solution.py:268
  15.8 1.6 %collective-permute-start.18 = (bf16[4,272,128]{2,1,0:T(8,128)(2,1)S(1)}, bf16[4,272,128]{2,1,0:T(8,128)(2,1)S(1)}, u32[]{:S(2)}, u32[]{:S(2)}) collective-permute-start(bf16[4,272,128]{2,1,0:T(8,128)(2,1)S(1)} %join.11.refs_4_), channel_id=1, source_target_pairs={{0,16},{8,24},{16,0},{24,8},{1,17},{9,25},{17,1},{25,9},{2,18},{10... | collective-permute-start | bytes 835592 | tf_op jit(solution)/shard_map/ppermute | solution.py:268
  17.4 2.1 %collective-permute-start.3 = (bf16[1,272,128]{2,1,0:T(8,128)(2,1)S(1)}, bf16[1,272,128]{2,1,0:T(8,128)(2,1)S(1)}, u32[]{:S(2)}, u32[]{:S(2)}) collective-permute-start(bf16[1,272,128]{2,1,0:T(8,128)(2,1)S(1)} %bitcast.15), channel_id=1, source_target_pairs={{0,4},{1,5},{2,6},{3,7},{4,0},{5,1},{6,2},{7,3},{8,12},{9,13},{10,... | collective-permute-start | bytes 208904 | tf_op jit(solution)/shard_map/ppermute | solution.py:268
  19.5 1.7 %collective-permute-start.4 = (bf16[1,272,128]{2,1,0:T(8,128)(2,1)S(1)}, bf16[1,272,128]{2,1,0:T(8,128)(2,1)S(1)}, u32[]{:S(2)}, u32[]{:S(2)}) collective-permute-start(bf16[1,272,128]{2,1,0:T(8,128)(2,1)S(1)} %bitcast.14), channel_id=1, source_target_pairs={{0,5},{1,4},{2,7},{3,6},{4,1},{5,0},{6,3},{7,2},{8,13},{9,12},{10,... | collective-permute-start | bytes 208904 | tf_op jit(solution)/shard_map/ppermute | solution.py:268
  21.2 0.6 %collective-permute-start.9 = (bf16[512,128]{1,0:T(8,128)(2,1)S(1)}, bf16[512,128]{1,0:T(8,128)(2,1)S(1)}, u32[]{:S(2)}, u32[]{:S(2)}) collective-permute-start(bf16[512,128]{1,0:T(8,128)(2,1)S(1)} %collective-permute-done.1.refs_9_), channel_id=1, source_target_pairs={{0,1},{1,0},{2,3},{3,2},{4,5},{5,4},{6,7},{7,6},{8,9},{9,8},{10,11... | collective-permute-start | bytes 393224 | tf_op jit(solution)/shard_map/ppermute | solution.py:268
  21.8 1.3 %collective-permute-done.7.refs_1_ = bf16[1,272,128]{2,1,0:T(8,128)(2,1)S(1)} collective-permute-done((bf16[1,272,128]{2,1,0:T(8,128)(2,1)S(1)}, bf16[1,272,128]{2,1,0:T(8,128)(2,1)S(1)}, u32[]{:S(2)}, u32[]{:S(2)}) %collective-permute-start.7) | collective-permute-done | bytes 69664 | tf_op jit(solution)/shard_map/ppermute | solution.py:268
  23.1 1.3 %collective-permute-start.8 = (bf16[2,272,128]{2,1,0:T(8,128)(2,1)S(1)}, bf16[2,272,128]{2,1,0:T(8,128)(2,1)S(1)}, u32[]{:S(2)}, u32[]{:S(2)}) collective-permute-start(bf16[2,272,128]{2,1,0:T(8,128)(2,1)S(1)} %join.7.refs_1_), channel_id=1, source_target_pairs={{0,16},{8,24},{16,0},{24,8},{1,17},{9,25},{17,1},{25,9},{2,18},{10... | collective-permute-start | bytes 417800 | tf_op jit(solution)/shard_map/ppermute | solution.py:268
  24.4 0.4 %collective-permute-done.3.refs_0_ = bf16[1,272,128]{2,1,0:T(8,128)(2,1)S(1)} collective-permute-done((bf16[1,272,128]{2,1,0:T(8,128)(2,1)S(1)}, bf16[1,272,128]{2,1,0:T(8,128)(2,1)S(1)}, u32[]{:S(2)}, u32[]{:S(2)}) %collective-permute-start.3) | collective-permute-done | bytes 69664 | tf_op jit(solution)/shard_map/ppermute | solution.py:268
  24.9 1.2 %collective-permute-done.4.refs_1_ = bf16[1,272,128]{2,1,0:T(8,128)(2,1)S(1)} collective-permute-done((bf16[1,272,128]{2,1,0:T(8,128)(2,1)S(1)}, bf16[1,272,128]{2,1,0:T(8,128)(2,1)S(1)}, u32[]{:S(2)}, u32[]{:S(2)}) %collective-permute-start.4) | collective-permute-done | bytes 69664 | tf_op jit(solution)/shard_map/ppermute | solution.py:268
  26.1 2.2 %collective-permute-start.5 = (bf16[2,272,128]{2,1,0:T(8,128)(2,1)S(1)}, bf16[2,272,128]{2,1,0:T(8,128)(2,1)S(1)}, u32[]{:S(2)}, u32[]{:S(2)}) collective-permute-start(bf16[2,272,128]{2,1,0:T(8,128)(2,1)S(1)} %join.6.refs_0_), channel_id=1, source_target_pairs={{0,16},{8,24},{16,0},{24,8},{1,17},{9,25},{17,1},{25,9},{2,18},{10... | collective-permute-start | bytes 417800 | tf_op jit(solution)/shard_map/ppermute | solution.py:268
  28.9 4.5 %collective-permute-done.10.refs_1_ = bf16[512,128]{1,0:T(8,128)(2,1)S(1)} collective-permute-done((bf16[512,128]{1,0:T(8,128)(2,1)S(1)}, bf16[512,128]{1,0:T(8,128)(2,1)S(1)}, u32[]{:S(2)}, u32[]{:S(2)}) %collective-permute-start.10) | collective-permute-done | bytes 131104 | tf_op jit(solution)/shard_map/ppermute | solution.py:268
  33.4 0.5 %collective-permute-start.14 = (bf16[4,272,128]{2,1,0:T(8,128)(2,1)S(1)}, bf16[4,272,128]{2,1,0:T(8,128)(2,1)S(1)}, u32[]{:S(2)}, u32[]{:S(2)}) collective-permute-start(bf16[4,272,128]{2,1,0:T(8,128)(2,1)S(1)} %join.10.refs_2_), channel_id=1, source_target_pairs={{0,8},{8,0},{16,24},{24,16},{1,9},{9,1},{17,25},{25,17},{2,10},{10... | collective-permute-start | bytes 835592 | tf_op jit(solution)/shard_map/ppermute | solution.py:268
  34.4 1.5 %collective-permute-done.11.refs_0_.refs_2_ = bf16[512,128]{1,0:T(8,128)(2,1)S(1)} collective-permute-done((bf16[512,128]{1,0:T(8,128)(2,1)S(1)}, bf16[512,128]{1,0:T(8,128)(2,1)S(1)}, u32[]{:S(2)}, u32[]{:S(2)}) %collective-permute-start.11) | collective-permute-done | bytes 131104 | tf_op jit(solution)/shard_map/ppermute | solution.py:268
  36.0 1.4 %collective-permute-start.12 = (bf16[512,128]{1,0:T(8,128)(2,1)S(1)}, bf16[512,128]{1,0:T(8,128)(2,1)S(1)}, u32[]{:S(2)}, u32[]{:S(2)}) collective-permute-start(bf16[512,128]{1,0:T(8,128)(2,1)S(1)} %join.8), channel_id=1, source_target_pairs={{0,1},{1,0},{2,3},{3,2},{4,5},{5,4},{6,7},{7,6},{8,9},{9,8},{10,11... | collective-permute-start | bytes 393224 | tf_op jit(solution)/shard_map/ppermute | solution.py:268
  37.5 2.8 %near_half.1 = (f32[512,1024]{1,0:T(8,128)S(1)}, bf16[1024,1024]{1,0:T(8,128)(2,1)S(1)}) custom-call(s32[9]{0:T(128)S(1)} %stack.24.where_ref, bf16[4,272,128]{2,1,0:T(8,128)(2,1)S(1)} %join.9.refs_0_, bf16[4,272,128]{2,1,0:T(8,128)(2,1)S(1)} %collective-permute-done.13.refs_1_, bf16[4,272,128]{2,1,0:T(8,128)(2,1)S(1)} %join.10.refs_2_, ...), custom_call_target="tpu_custom_call" | custom-call | flops 536870912 | bytes 8388608 | tf_op jit(solution)/shard_map/near_half/pallas_call | solution.py:196
  40.4 0.7 %collective-permute-done.12.refs_3_ = bf16[512,128]{1,0:T(8,128)(2,1)S(1)} collective-permute-done((bf16[512,128]{1,0:T(8,128)(2,1)S(1)}, bf16[512,128]{1,0:T(8,128)(2,1)S(1)}, u32[]{:S(2)}, u32[]{:S(2)}) %collective-permute-start.12) | collective-permute-done | bytes 131104 | tf_op jit(solution)/shard_map/ppermute | solution.py:268
  41.0 1.8 %far_half.1 = f32[512,1024]{1,0:T(8,128)} custom-call(bf16[512,128]{1,0:T(8,128)(2,1)S(1)} %collective-permute-done.2.refs_0_, bf16[512,128]{1,0:T(8,128)(2,1)S(1)} %collective-permute-done.10.refs_1_, bf16[512,128]{1,0:T(8,128)(2,1)S(1)} %collective-permute-done.11.refs_0_.refs_2_, bf16[512,128]{1,0:T(8,128)(2,1)S(1)} %collective-permute-done.12.refs_3_, ...), custom_call_target="tpu_custom_call" | custom-call | flops 536870912 | bytes 8388608 | tf_op jit(solution)/shard_map/far_half/pallas_call | solution.py:246
  (28 shorter events, 1.3 us)
Async XLA Ops:
  0.0 9.4 %collective-permute-start = (bf16[512,128]{1,0:T(8,128)(2,1)}, bf16[512,128]{1,0:T(8,128)(2,1)S(1)}, u32[]{:S(2)}, u32[]{:S(2)}) collective-permute-start(bf16[512,128]{1,0:T(8,128)(2,1)} %refs_11_.1), channel_id=1, source_target_pairs={{0,1},{1,0},{2,3},{3,2},{4,5},{5,4},{6,7},{7,6},{8,9},{9,8},{10,11... | collective-permute-start | bytes 393224 | tf_op jit(solution)/shard_map/ppermute | solution.py:268
  2.9 8.9 %collective-permute-start.1 = (bf16[512,128]{1,0:T(8,128)(2,1)}, bf16[512,128]{1,0:T(8,128)(2,1)S(1)}, u32[]{:S(2)}, u32[]{:S(2)}) collective-permute-start(bf16[512,128]{1,0:T(8,128)(2,1)} %refs_11_.1), channel_id=1, source_target_pairs={{0,2},{1,3},{2,0},{3,1},{4,6},{5,7},{6,4},{7,5},{8,10},{9,11},{10,... | collective-permute-start | bytes 393224 | tf_op jit(solution)/shard_map/ppermute | solution.py:268
  4.5 7.4 %collective-permute-start.2 = (bf16[512,128]{1,0:T(8,128)(2,1)}, bf16[512,128]{1,0:T(8,128)(2,1)S(1)}, u32[]{:S(2)}, u32[]{:S(2)}) collective-permute-start(bf16[512,128]{1,0:T(8,128)(2,1)} %refs_11_.1), channel_id=1, source_target_pairs={{0,4},{1,5},{2,6},{3,7},{4,0},{5,1},{6,2},{7,3},{8,12},{9,13},{10,... | collective-permute-start | bytes 393224 | tf_op jit(solution)/shard_map/ppermute | solution.py:268
  8.3 7.4 %collective-permute-start.15 = (bf16[1,272,128]{2,1,0:T(8,128)(2,1)S(1)}, bf16[1,272,128]{2,1,0:T(8,128)(2,1)S(1)}, u32[]{:S(2)}, u32[]{:S(2)}) collective-permute-start(bf16[1,272,128]{2,1,0:T(8,128)(2,1)S(1)} %bitcast.20), channel_id=1, source_target_pairs={{0,1},{1,0},{2,3},{3,2},{4,5},{5,4},{6,7},{7,6},{8,9},{9,8},{10,11... | collective-permute-start | bytes 208904 | tf_op jit(solution)/shard_map/ppermute | solution.py:268
  8.9 6.8 %collective-permute-start.16 = (bf16[1,272,128]{2,1,0:T(8,128)(2,1)S(1)}, bf16[1,272,128]{2,1,0:T(8,128)(2,1)S(1)}, u32[]{:S(2)}, u32[]{:S(2)}) collective-permute-start(bf16[1,272,128]{2,1,0:T(8,128)(2,1)S(1)} %bitcast.19), channel_id=1, source_target_pairs={{0,2},{1,3},{2,0},{3,1},{4,6},{5,7},{6,4},{7,5},{8,10},{9,11},{10,... | collective-permute-start | bytes 208904 | tf_op jit(solution)/shard_map/ppermute | solution.py:268
  9.4 6.4 %collective-permute-start.17 = (bf16[1,272,128]{2,1,0:T(8,128)(2,1)S(1)}, bf16[1,272,128]{2,1,0:T(8,128)(2,1)S(1)}, u32[]{:S(2)}, u32[]{:S(2)}) collective-permute-start(bf16[1,272,128]{2,1,0:T(8,128)(2,1)S(1)} %bitcast.18), channel_id=1, source_target_pairs={{0,3},{1,2},{2,1},{3,0},{4,7},{5,6},{6,5},{7,4},{8,11},{9,10},{10,... | collective-permute-start | bytes 208904 | tf_op jit(solution)/shard_map/ppermute | solution.py:268
  11.9 9.3 %collective-permute-start.6 = (bf16[1,272,128]{2,1,0:T(8,128)(2,1)S(1)}, bf16[1,272,128]{2,1,0:T(8,128)(2,1)S(1)}, u32[]{:S(2)}, u32[]{:S(2)}) collective-permute-start(bf16[1,272,128]{2,1,0:T(8,128)(2,1)S(1)} %bitcast.17), channel_id=1, source_target_pairs={{0,6},{1,7},{2,4},{3,5},{4,2},{5,3},{6,0},{7,1},{8,14},{9,15},{10,... | collective-permute-start | bytes 208904 | tf_op jit(solution)/shard_map/ppermute | solution.py:268
  15.7 7.4 %collective-permute-start.7 = (bf16[1,272,128]{2,1,0:T(8,128)(2,1)S(1)}, bf16[1,272,128]{2,1,0:T(8,128)(2,1)S(1)}, u32[]{:S(2)}, u32[]{:S(2)}) collective-permute-start(bf16[1,272,128]{2,1,0:T(8,128)(2,1)S(1)} %bitcast.16), channel_id=1, source_target_pairs={{0,7},{1,6},{2,5},{3,4},{4,3},{5,2},{6,1},{7,0},{8,15},{9,14},{10,... | collective-permute-start | bytes 208904 | tf_op jit(solution)/shard_map/ppermute | solution.py:268
  15.8 18.1 %collective-permute-start.18 = (bf16[4,272,128]{2,1,0:T(8,128)(2,1)S(1)}, bf16[4,272,128]{2,1,0:T(8,128)(2,1)S(1)}, u32[]{:S(2)}, u32[]{:S(2)}) collective-permute-start(bf16[4,272,128]{2,1,0:T(8,128)(2,1)S(1)} %join.11.refs_4_), channel_id=1, source_target_pairs={{0,16},{8,24},{16,0},{24,8},{1,17},{9,25},{17,1},{25,9},{2,18},{10... | collective-permute-start | bytes 835592 | tf_op jit(solution)/shard_map/ppermute | solution.py:268
  17.4 7.5 %collective-permute-start.3 = (bf16[1,272,128]{2,1,0:T(8,128)(2,1)S(1)}, bf16[1,272,128]{2,1,0:T(8,128)(2,1)S(1)}, u32[]{:S(2)}, u32[]{:S(2)}) collective-permute-start(bf16[1,272,128]{2,1,0:T(8,128)(2,1)S(1)} %bitcast.15), channel_id=1, source_target_pairs={{0,4},{1,5},{2,6},{3,7},{4,0},{5,1},{6,2},{7,3},{8,12},{9,13},{10,... | collective-permute-start | bytes 208904 | tf_op jit(solution)/shard_map/ppermute | solution.py:268
  19.5 6.6 %collective-permute-start.4 = (bf16[1,272,128]{2,1,0:T(8,128)(2,1)S(1)}, bf16[1,272,128]{2,1,0:T(8,128)(2,1)S(1)}, u32[]{:S(2)}, u32[]{:S(2)}) collective-permute-start(bf16[1,272,128]{2,1,0:T(8,128)(2,1)S(1)} %bitcast.14), channel_id=1, source_target_pairs={{0,5},{1,4},{2,7},{3,6},{4,1},{5,0},{6,3},{7,2},{8,13},{9,12},{10,... | collective-permute-start | bytes 208904 | tf_op jit(solution)/shard_map/ppermute | solution.py:268
  21.2 7.5 %collective-permute-start.9 = (bf16[512,128]{1,0:T(8,128)(2,1)S(1)}, bf16[512,128]{1,0:T(8,128)(2,1)S(1)}, u32[]{:S(2)}, u32[]{:S(2)}) collective-permute-start(bf16[512,128]{1,0:T(8,128)(2,1)S(1)} %collective-permute-done.1.refs_9_), channel_id=1, source_target_pairs={{0,1},{1,0},{2,3},{3,2},{4,5},{5,4},{6,7},{7,6},{8,9},{9,8},{10,11... | collective-permute-start | bytes 393224 | tf_op jit(solution)/shard_map/ppermute | solution.py:268
  23.1 10.2 %collective-permute-start.8 = (bf16[2,272,128]{2,1,0:T(8,128)(2,1)S(1)}, bf16[2,272,128]{2,1,0:T(8,128)(2,1)S(1)}, u32[]{:S(2)}, u32[]{:S(2)}) collective-permute-start(bf16[2,272,128]{2,1,0:T(8,128)(2,1)S(1)} %join.7.refs_1_), channel_id=1, source_target_pairs={{0,16},{8,24},{16,0},{24,8},{1,17},{9,25},{17,1},{25,9},{2,18},{10... | collective-permute-start | bytes 417800 | tf_op jit(solution)/shard_map/ppermute | solution.py:268
  26.1 7.2 %collective-permute-start.5 = (bf16[2,272,128]{2,1,0:T(8,128)(2,1)S(1)}, bf16[2,272,128]{2,1,0:T(8,128)(2,1)S(1)}, u32[]{:S(2)}, u32[]{:S(2)}) collective-permute-start(bf16[2,272,128]{2,1,0:T(8,128)(2,1)S(1)} %join.6.refs_0_), channel_id=1, source_target_pairs={{0,16},{8,24},{16,0},{24,8},{1,17},{9,25},{17,1},{25,9},{2,18},{10... | collective-permute-start | bytes 417800 | tf_op jit(solution)/shard_map/ppermute | solution.py:268
  28.4 5.0 %collective-permute-start.10 = (bf16[512,128]{1,0:T(8,128)(2,1)S(1)}, bf16[512,128]{1,0:T(8,128)(2,1)S(1)}, u32[]{:S(2)}, u32[]{:S(2)}) collective-permute-start(bf16[512,128]{1,0:T(8,128)(2,1)S(1)} %collective-permute-done.2.refs_0_), channel_id=1, source_target_pairs={{0,1},{1,0},{2,3},{3,2},{4,5},{5,4},{6,7},{7,6},{8,9},{9,8},{10,11... | collective-permute-start | bytes 393224 | tf_op jit(solution)/shard_map/ppermute | solution.py:268
  28.7 7.3 %collective-permute-start.11 = (bf16[512,128]{1,0:T(8,128)(2,1)S(1)}, bf16[512,128]{1,0:T(8,128)(2,1)S(1)}, u32[]{:S(2)}, u32[]{:S(2)}) collective-permute-start(bf16[512,128]{1,0:T(8,128)(2,1)S(1)} %collective-permute-done.1.refs_9_), channel_id=1, source_target_pairs={{0,4},{1,5},{2,6},{3,7},{4,0},{5,1},{6,2},{7,3},{8,12},{9,13},{10,... | collective-permute-start | bytes 393224 | tf_op jit(solution)/shard_map/ppermute | solution.py:268
  33.4 4.1 %collective-permute-start.13 = (bf16[4,272,128]{2,1,0:T(8,128)(2,1)S(1)}, bf16[4,272,128]{2,1,0:T(8,128)(2,1)S(1)}, u32[]{:S(2)}, u32[]{:S(2)}) collective-permute-start(bf16[4,272,128]{2,1,0:T(8,128)(2,1)S(1)} %join.9.refs_0_), channel_id=1, source_target_pairs={{0,8},{8,0},{16,24},{24,16},{1,9},{9,1},{17,25},{25,17},{2,10},{10... | collective-permute-start | bytes 835592 | tf_op jit(solution)/shard_map/ppermute | solution.py:268
  33.4 4.0 %collective-permute-start.14 = (bf16[4,272,128]{2,1,0:T(8,128)(2,1)S(1)}, bf16[4,272,128]{2,1,0:T(8,128)(2,1)S(1)}, u32[]{:S(2)}, u32[]{:S(2)}) collective-permute-start(bf16[4,272,128]{2,1,0:T(8,128)(2,1)S(1)} %join.10.refs_2_), channel_id=1, source_target_pairs={{0,8},{8,0},{16,24},{24,16},{1,9},{9,1},{17,25},{25,17},{2,10},{10... | collective-permute-start | bytes 835592 | tf_op jit(solution)/shard_map/ppermute | solution.py:268
  33.9 3.6 %collective-permute-start.19 = (bf16[4,272,128]{2,1,0:T(8,128)(2,1)S(1)}, bf16[4,272,128]{2,1,0:T(8,128)(2,1)S(1)}, u32[]{:S(2)}, u32[]{:S(2)}) collective-permute-start(bf16[4,272,128]{2,1,0:T(8,128)(2,1)S(1)} %join.11.refs_4_), channel_id=1, source_target_pairs={{0,8},{8,0},{16,24},{24,16},{1,9},{9,1},{17,25},{25,17},{2,10},{10... | collective-permute-start | bytes 835592 | tf_op jit(solution)/shard_map/ppermute | solution.py:268
  34.0 3.5 %collective-permute-start.20 = (bf16[4,272,128]{2,1,0:T(8,128)(2,1)S(1)}, bf16[4,272,128]{2,1,0:T(8,128)(2,1)S(1)}, u32[]{:S(2)}, u32[]{:S(2)}) collective-permute-start(bf16[4,272,128]{2,1,0:T(8,128)(2,1)S(1)} %collective-permute-done.18.refs_6_), channel_id=1, source_target_pairs={{0,8},{8,0},{16,24},{24,16},{1,9},{9,1},{17,25},{25,17},{2,10},{10... | collective-permute-start | bytes 835592 | tf_op jit(solution)/shard_map/ppermute | solution.py:268
  36.0 5.0 %collective-permute-start.12 = (bf16[512,128]{1,0:T(8,128)(2,1)S(1)}, bf16[512,128]{1,0:T(8,128)(2,1)S(1)}, u32[]{:S(2)}, u32[]{:S(2)}) collective-permute-start(bf16[512,128]{1,0:T(8,128)(2,1)S(1)} %join.8), channel_id=1, source_target_pairs={{0,1},{1,0},{2,3},{3,2},{4,5},{5,4},{6,7},{7,6},{8,9},{9,8},{10,11... | collective-permute-start | bytes 393224 | tf_op jit(solution)/shard_map/ppermute | solution.py:268

commit v13 on v12

--- a/solution.py
+++ b/solution.py
@@ -283,7 +283,9 @@
     amps = {0: amplitudes}
     for s in [*range(1, inner), *range(inner, half, inner), half]:
         amps[s] = exchange(amplitudes, "col", s)
-    outgoing[half:], amps = tie(outgoing[half:], amps)
+    first = [*range(inner, half, inner), half]
+    outgoing[half:], got = tie(outgoing[half:], [amps[s] for s in first])
+    amps.update(zip(first, got))
 
     chunks = [outgoing[0][None]]
     chunks += [exchange(outgoing[s][None], "col", s) for s in range(1, n_col)]

time: 43.1 us -> 43.2 us (level)
  starting transfers between devices: 27 us -> 30.6 us
  waiting for transfers between devices: 9.73 us -> 6.22 us
    ppermute x21, starting transfers between devices: 27 us -> 30.6 us  [exchange(): return lax.ppermute(x, axis, [(i, i ^ flip) for i in range(size)])]
    ppermute x21, waiting for transfers between devices: 9.73 us -> 6.22 us  [exchange(): return lax.ppermute(x, axis, [(i, i ^ flip) for i in range(size)])]
  transfers between devices with their start and end apart: 21 -> 21, of which waited for: 7 -> 4; matrix products, arithmetic and copies ran while one was open for 0% -> 0% of each run, Pallas kernels for 10% -> 10%
where the time goes in v13:
time: 43.2 us; the launch traced here: 42.9 us
  starting transfers between devices  30.6 us (71%)
  waiting for transfers between devices  6.22 us (14%)
  Pallas kernels  5.97 us (14%)
    ppermute x21, starting transfers between devices, exchange(): return lax.ppermute(x, axis, [(i, i ^ flip) for i in range(size)])  30.6 us
    ppermute x21, waiting for transfers between devices, exchange(): return lax.ppermute(x, axis, [(i, i ^ flip) for i in range(size)])  6.22 us
    pallas_call x1, Pallas kernels, near_half(): pl.pallas_call(functools.partial(near_kernel, n_pieces, offsets, capacity...  2.83 us
    pallas_call x1, Pallas kernels, far_half(): pl.pallas_call(functools.partial(far_kernel, offsets, depth // width), ou...  1.85 us
    pallas_call x1, Pallas kernels, pack(): pl.pallas_call(functools.partial(pack_kernel, columns, capacity), out_sha...  1.2 us
  transfers between devices with their start and end apart: 21, of which 4 were waited for; matrix products, arithmetic and copies ran while one was open for 0% of the time, Pallas kernels for 10%

profile of v13, /device:TPU:0, one launch (start us, length us, event | category | flops | bytes accessed | tf_op | source)
XLA Modules:
  0.0 42.9 jit_solution(17453924777638002954)
XLA Ops:
  0.0 3.0 %collective-permute-start = (bf16[512,128]{1,0:T(8,128)(2,1)}, bf16[512,128]{1,0:T(8,128)(2,1)S(1)}, u32[]{:S(2)}, u32[]{:S(2)}) collective-permute-start(bf16[512,128]{1,0:T(8,128)(2,1)} %refs_11_.1), channel_id=1, source_target_pairs={{0,2},{1,3},{2,0},{3,1},{4,6},{5,7},{6,4},{7,5},{8,10},{9,11},{10,... | collective-permute-start | bytes 393224 | tf_op jit(solution)/shard_map/ppermute | solution.py:268
  3.0 2.6 %collective-permute-start.1 = (bf16[512,128]{1,0:T(8,128)(2,1)}, bf16[512,128]{1,0:T(8,128)(2,1)S(1)}, u32[]{:S(2)}, u32[]{:S(2)}) collective-permute-start(bf16[512,128]{1,0:T(8,128)(2,1)} %refs_11_.1), channel_id=1, source_target_pairs={{0,4},{1,5},{2,6},{3,7},{4,0},{5,1},{6,2},{7,3},{8,12},{9,13},{10,... | collective-permute-start | bytes 393224 | tf_op jit(solution)/shard_map/ppermute | solution.py:268
  5.6 1.2 %pack.1 = (bf16[272,128]{1,0:T(8,128)(2,1)S(1)}, bf16[272,128]{1,0:T(8,128)(2,1)S(1)}, bf16[272,128]{1,0:T(8,128)(2,1)S(1)}, bf16[272,128]{1,0:T(8,128)(2,1)S(1)...) custom-call(s32[1]{0:T(128)} %bitcast.me_ref, ...), custom_call_target="tpu_custom_call" | custom-call | tf_op jit(solution)/shard_map/pack/pallas_call | solution.py:66
  6.8 1.6 %collective-permute-start.15 = (bf16[1,272,128]{2,1,0:T(8,128)(2,1)S(1)}, bf16[1,272,128]{2,1,0:T(8,128)(2,1)S(1)}, u32[]{:S(2)}, u32[]{:S(2)}) collective-permute-start(bf16[1,272,128]{2,1,0:T(8,128)(2,1)S(1)} %bitcast.20), channel_id=1, source_target_pairs={{0,1},{1,0},{2,3},{3,2},{4,5},{5,4},{6,7},{7,6},{8,9},{9,8},{10,11... | collective-permute-start | bytes 208904 | tf_op jit(solution)/shard_map/ppermute | solution.py:268
  8.4 0.4 %collective-permute-start.16 = (bf16[1,272,128]{2,1,0:T(8,128)(2,1)S(1)}, bf16[1,272,128]{2,1,0:T(8,128)(2,1)S(1)}, u32[]{:S(2)}, u32[]{:S(2)}) collective-permute-start(bf16[1,272,128]{2,1,0:T(8,128)(2,1)S(1)} %bitcast.19), channel_id=1, source_target_pairs={{0,2},{1,3},{2,0},{3,1},{4,6},{5,7},{6,4},{7,5},{8,10},{9,11},{10,... | collective-permute-start | bytes 208904 | tf_op jit(solution)/shard_map/ppermute | solution.py:268
  8.8 1.5 %collective-permute-start.17 = (bf16[1,272,128]{2,1,0:T(8,128)(2,1)S(1)}, bf16[1,272,128]{2,1,0:T(8,128)(2,1)S(1)}, u32[]{:S(2)}, u32[]{:S(2)}) collective-permute-start(bf16[1,272,128]{2,1,0:T(8,128)(2,1)S(1)} %bitcast.18), channel_id=1, source_target_pairs={{0,3},{1,2},{2,1},{3,0},{4,7},{5,6},{6,5},{7,4},{8,11},{9,10},{10,... | collective-permute-start | bytes 208904 | tf_op jit(solution)/shard_map/ppermute | solution.py:268
  10.4 0.7 %collective-permute-done.1.refs_0_ = bf16[512,128]{1,0:T(8,128)(2,1)S(1)} collective-permute-done((bf16[512,128]{1,0:T(8,128)(2,1)}, bf16[512,128]{1,0:T(8,128)(2,1)S(1)}, u32[]{:S(2)}, u32[]{:S(2)}) %collective-permute-start.1) | collective-permute-done | bytes 131104 | tf_op jit(solution)/shard_map/ppermute | solution.py:268
  11.0 3.5 %collective-permute-start.5 = (bf16[1,272,128]{2,1,0:T(8,128)(2,1)S(1)}, bf16[1,272,128]{2,1,0:T(8,128)(2,1)S(1)}, u32[]{:S(2)}, u32[]{:S(2)}) collective-permute-start(bf16[1,272,128]{2,1,0:T(8,128)(2,1)S(1)} %bitcast.17), channel_id=1, source_target_pairs={{0,6},{1,7},{2,4},{3,5},{4,2},{5,3},{6,0},{7,1},{8,14},{9,15},{10,... | collective-permute-start | bytes 208904 | tf_op jit(solution)/shard_map/ppermute | solution.py:268
  14.5 1.3 %collective-permute-start.6 = (bf16[1,272,128]{2,1,0:T(8,128)(2,1)S(1)}, bf16[1,272,128]{2,1,0:T(8,128)(2,1)S(1)}, u32[]{:S(2)}, u32[]{:S(2)}) collective-permute-start(bf16[1,272,128]{2,1,0:T(8,128)(2,1)S(1)} %bitcast.16), channel_id=1, source_target_pairs={{0,7},{1,6},{2,5},{3,4},{4,3},{5,2},{6,1},{7,0},{8,15},{9,14},{10,... | collective-permute-start | bytes 208904 | tf_op jit(solution)/shard_map/ppermute | solution.py:268
  15.8 0.5 %collective-permute-start.8 = (bf16[512,128]{1,0:T(8,128)(2,1)}, bf16[512,128]{1,0:T(8,128)(2,1)S(1)}, u32[]{:S(2)}, u32[]{:S(2)}) collective-permute-start(bf16[512,128]{1,0:T(8,128)(2,1)} %refs_11_.1), channel_id=1, source_target_pairs={{0,1},{1,0},{2,3},{3,2},{4,5},{5,4},{6,7},{7,6},{8,9},{9,8},{10,11... | collective-permute-start | bytes 393224 | tf_op jit(solution)/shard_map/ppermute | solution.py:268
  16.4 1.6 %collective-permute-start.18 = (bf16[4,272,128]{2,1,0:T(8,128)(2,1)S(1)}, bf16[4,272,128]{2,1,0:T(8,128)(2,1)S(1)}, u32[]{:S(2)}, u32[]{:S(2)}) collective-permute-start(bf16[4,272,128]{2,1,0:T(8,128)(2,1)S(1)} %join.11.refs_4_), channel_id=1, source_target_pairs={{0,16},{8,24},{16,0},{24,8},{1,17},{9,25},{17,1},{25,9},{2,18},{10... | collective-permute-start | bytes 835592 | tf_op jit(solution)/shard_map/ppermute | solution.py:268
  17.9 1.1 %collective-permute-start.2 = (bf16[1,272,128]{2,1,0:T(8,128)(2,1)S(1)}, bf16[1,272,128]{2,1,0:T(8,128)(2,1)S(1)}, u32[]{:S(2)}, u32[]{:S(2)}) collective-permute-start(bf16[1,272,128]{2,1,0:T(8,128)(2,1)S(1)} %bitcast.15), channel_id=1, source_target_pairs={{0,4},{1,5},{2,6},{3,7},{4,0},{5,1},{6,2},{7,3},{8,12},{9,13},{10,... | collective-permute-start | bytes 208904 | tf_op jit(solution)/shard_map/ppermute | solution.py:268
  19.1 2.7 %collective-permute-start.3 = (bf16[1,272,128]{2,1,0:T(8,128)(2,1)S(1)}, bf16[1,272,128]{2,1,0:T(8,128)(2,1)S(1)}, u32[]{:S(2)}, u32[]{:S(2)}) collective-permute-start(bf16[1,272,128]{2,1,0:T(8,128)(2,1)S(1)} %bitcast.14), channel_id=1, source_target_pairs={{0,5},{1,4},{2,7},{3,6},{4,1},{5,0},{6,3},{7,2},{8,13},{9,12},{10,... | collective-permute-start | bytes 208904 | tf_op jit(solution)/shard_map/ppermute | solution.py:268
  21.8 1.4 %collective-permute-start.9 = (bf16[512,128]{1,0:T(8,128)(2,1)S(1)}, bf16[512,128]{1,0:T(8,128)(2,1)S(1)}, u32[]{:S(2)}, u32[]{:S(2)}) collective-permute-start(bf16[512,128]{1,0:T(8,128)(2,1)S(1)} %collective-permute-done.refs_9_), channel_id=1, source_target_pairs={{0,1},{1,0},{2,3},{3,2},{4,5},{5,4},{6,7},{7,6},{8,9},{9,8},{10,11... | collective-permute-start | bytes 393224 | tf_op jit(solution)/shard_map/ppermute | solution.py:268
  23.2 1.4 %collective-permute-done.2.refs_0_ = bf16[1,272,128]{2,1,0:T(8,128)(2,1)S(1)} collective-permute-done((bf16[1,272,128]{2,1,0:T(8,128)(2,1)S(1)}, bf16[1,272,128]{2,1,0:T(8,128)(2,1)S(1)}, u32[]{:S(2)}, u32[]{:S(2)}) %collective-permute-start.2) | collective-permute-done | bytes 69664 | tf_op jit(solution)/shard_map/ppermute | solution.py:268
  24.6 1.5 %collective-permute-start.7 = (bf16[2,272,128]{2,1,0:T(8,128)(2,1)S(1)}, bf16[2,272,128]{2,1,0:T(8,128)(2,1)S(1)}, u32[]{:S(2)}, u32[]{:S(2)}) collective-permute-start(bf16[2,272,128]{2,1,0:T(8,128)(2,1)S(1)} %join.7.refs_1_), channel_id=1, source_target_pairs={{0,16},{8,24},{16,0},{24,8},{1,17},{9,25},{17,1},{25,9},{2,18},{10... | collective-permute-start | bytes 417800 | tf_op jit(solution)/shard_map/ppermute | solution.py:268
  26.4 2.3 %collective-permute-start.4 = (bf16[2,272,128]{2,1,0:T(8,128)(2,1)S(1)}, bf16[2,272,128]{2,1,0:T(8,128)(2,1)S(1)}, u32[]{:S(2)}, u32[]{:S(2)}) collective-permute-start(bf16[2,272,128]{2,1,0:T(8,128)(2,1)S(1)} %join.6.refs_0_), channel_id=1, source_target_pairs={{0,16},{8,24},{16,0},{24,8},{1,17},{9,25},{17,1},{25,9},{2,18},{10... | collective-permute-start | bytes 417800 | tf_op jit(solution)/shard_map/ppermute | solution.py:268
  28.7 1.1 %collective-permute-start.11 = (bf16[512,128]{1,0:T(8,128)(2,1)S(1)}, bf16[512,128]{1,0:T(8,128)(2,1)S(1)}, u32[]{:S(2)}, u32[]{:S(2)}) collective-permute-start(bf16[512,128]{1,0:T(8,128)(2,1)S(1)} %collective-permute-done.refs_9_), channel_id=1, source_target_pairs={{0,4},{1,5},{2,6},{3,7},{4,0},{5,1},{6,2},{7,3},{8,12},{9,13},{10,... | collective-permute-start | bytes 393224 | tf_op jit(solution)/shard_map/ppermute | solution.py:268
  29.9 3.8 %collective-permute-done.10.refs_1_ = bf16[512,128]{1,0:T(8,128)(2,1)S(1)} collective-permute-done((bf16[512,128]{1,0:T(8,128)(2,1)S(1)}, bf16[512,128]{1,0:T(8,128)(2,1)S(1)}, u32[]{:S(2)}, u32[]{:S(2)}) %collective-permute-start.10) | collective-permute-done | bytes 131104 | tf_op jit(solution)/shard_map/ppermute | solution.py:268
  33.8 0.5 %collective-permute-start.14 = (bf16[4,272,128]{2,1,0:T(8,128)(2,1)S(1)}, bf16[4,272,128]{2,1,0:T(8,128)(2,1)S(1)}, u32[]{:S(2)}, u32[]{:S(2)}) collective-permute-start(bf16[4,272,128]{2,1,0:T(8,128)(2,1)S(1)} %join.10.refs_2_), channel_id=1, source_target_pairs={{0,8},{8,0},{16,24},{24,16},{1,9},{9,1},{17,25},{25,17},{2,10},{10... | collective-permute-start | bytes 835592 | tf_op jit(solution)/shard_map/ppermute | solution.py:268
  34.4 0.4 %collective-permute-start.20 = (bf16[4,272,128]{2,1,0:T(8,128)(2,1)S(1)}, bf16[4,272,128]{2,1,0:T(8,128)(2,1)S(1)}, u32[]{:S(2)}, u32[]{:S(2)}) collective-permute-start(bf16[4,272,128]{2,1,0:T(8,128)(2,1)S(1)} %collective-permute-done.18.refs_6_), channel_id=1, source_target_pairs={{0,8},{8,0},{16,24},{24,16},{1,9},{9,1},{17,25},{25,17},{2,10},{10... | collective-permute-start | bytes 835592 | tf_op jit(solution)/shard_map/ppermute | solution.py:268
  34.8 3.3 %collective-permute-start.12 = (bf16[512,128]{1,0:T(8,128)(2,1)S(1)}, bf16[512,128]{1,0:T(8,128)(2,1)S(1)}, u32[]{:S(2)}, u32[]{:S(2)}) collective-permute-start(bf16[512,128]{1,0:T(8,128)(2,1)S(1)} %join.8), channel_id=1, source_target_pairs={{0,1},{1,0},{2,3},{3,2},{4,5},{5,4},{6,7},{7,6},{8,9},{9,8},{10,11... | collective-permute-start | bytes 393224 | tf_op jit(solution)/shard_map/ppermute | solution.py:268
  38.2 2.8 %near_half.1 = (f32[512,1024]{1,0:T(8,128)S(1)}, bf16[1024,1024]{1,0:T(8,128)(2,1)S(1)}) custom-call(s32[9]{0:T(128)S(1)} %stack.24.where_ref, bf16[4,272,128]{2,1,0:T(8,128)(2,1)S(1)} %join.9.refs_0_, bf16[4,272,128]{2,1,0:T(8,128)(2,1)S(1)} %collective-permute-done.13.refs_1_, bf16[4,272,128]{2,1,0:T(8,128)(2,1)S(1)} %join.10.refs_2_, ...), custom_call_target="tpu_custom_call" | custom-call | flops 536870912 | bytes 8388608 | tf_op jit(solution)/shard_map/near_half/pallas_call | solution.py:196
  41.1 1.9 %far_half.1 = f32[512,1024]{1,0:T(8,128)} custom-call(bf16[512,128]{1,0:T(8,128)(2,1)S(1)} %collective-permute-done.1.refs_0_, bf16[512,128]{1,0:T(8,128)(2,1)S(1)} %collective-permute-done.10.refs_1_, bf16[512,128]{1,0:T(8,128)(2,1)S(1)} %collective-permute-done.11.refs_0_.refs_2_, bf16[512,128]{1,0:T(8,128)(2,1)S(1)} %collective-permute-done.12.refs_3_, ...), custom_call_target="tpu_custom_call" | custom-call | flops 536870912 | bytes 8388608 | tf_op jit(solution)/shard_map/far_half/pallas_call | solution.py:246
  (28 shorter events, 0.6 us)
Async XLA Ops:
  0.0 10.4 %collective-permute-start = (bf16[512,128]{1,0:T(8,128)(2,1)}, bf16[512,128]{1,0:T(8,128)(2,1)S(1)}, u32[]{:S(2)}, u32[]{:S(2)}) collective-permute-start(bf16[512,128]{1,0:T(8,128)(2,1)} %refs_11_.1), channel_id=1, source_target_pairs={{0,2},{1,3},{2,0},{3,1},{4,6},{5,7},{6,4},{7,5},{8,10},{9,11},{10,... | collective-permute-start | bytes 393224 | tf_op jit(solution)/shard_map/ppermute | solution.py:268
  3.0 8.0 %collective-permute-start.1 = (bf16[512,128]{1,0:T(8,128)(2,1)}, bf16[512,128]{1,0:T(8,128)(2,1)S(1)}, u32[]{:S(2)}, u32[]{:S(2)}) collective-permute-start(bf16[512,128]{1,0:T(8,128)(2,1)} %refs_11_.1), channel_id=1, source_target_pairs={{0,4},{1,5},{2,6},{3,7},{4,0},{5,1},{6,2},{7,3},{8,12},{9,13},{10,... | collective-permute-start | bytes 393224 | tf_op jit(solution)/shard_map/ppermute | solution.py:268
  6.8 9.0 %collective-permute-start.15 = (bf16[1,272,128]{2,1,0:T(8,128)(2,1)S(1)}, bf16[1,272,128]{2,1,0:T(8,128)(2,1)S(1)}, u32[]{:S(2)}, u32[]{:S(2)}) collective-permute-start(bf16[1,272,128]{2,1,0:T(8,128)(2,1)S(1)} %bitcast.20), channel_id=1, source_target_pairs={{0,1},{1,0},{2,3},{3,2},{4,5},{5,4},{6,7},{7,6},{8,9},{9,8},{10,11... | collective-permute-start | bytes 208904 | tf_op jit(solution)/shard_map/ppermute | solution.py:268
  8.4 8.0 %collective-permute-start.16 = (bf16[1,272,128]{2,1,0:T(8,128)(2,1)S(1)}, bf16[1,272,128]{2,1,0:T(8,128)(2,1)S(1)}, u32[]{:S(2)}, u32[]{:S(2)}) collective-permute-start(bf16[1,272,128]{2,1,0:T(8,128)(2,1)S(1)} %bitcast.19), channel_id=1, source_target_pairs={{0,2},{1,3},{2,0},{3,1},{4,6},{5,7},{6,4},{7,5},{8,10},{9,11},{10,... | collective-permute-start | bytes 208904 | tf_op jit(solution)/shard_map/ppermute | solution.py:268
  8.8 7.5 %collective-permute-start.17 = (bf16[1,272,128]{2,1,0:T(8,128)(2,1)S(1)}, bf16[1,272,128]{2,1,0:T(8,128)(2,1)S(1)}, u32[]{:S(2)}, u32[]{:S(2)}) collective-permute-start(bf16[1,272,128]{2,1,0:T(8,128)(2,1)S(1)} %bitcast.18), channel_id=1, source_target_pairs={{0,3},{1,2},{2,1},{3,0},{4,7},{5,6},{6,5},{7,4},{8,11},{9,10},{10,... | collective-permute-start | bytes 208904 | tf_op jit(solution)/shard_map/ppermute | solution.py:268
  11.0 8.0 %collective-permute-start.5 = (bf16[1,272,128]{2,1,0:T(8,128)(2,1)S(1)}, bf16[1,272,128]{2,1,0:T(8,128)(2,1)S(1)}, u32[]{:S(2)}, u32[]{:S(2)}) collective-permute-start(bf16[1,272,128]{2,1,0:T(8,128)(2,1)S(1)} %bitcast.17), channel_id=1, source_target_pairs={{0,6},{1,7},{2,4},{3,5},{4,2},{5,3},{6,0},{7,1},{8,14},{9,15},{10,... | collective-permute-start | bytes 208904 | tf_op jit(solution)/shard_map/ppermute | solution.py:268
  14.5 7.3 %collective-permute-start.6 = (bf16[1,272,128]{2,1,0:T(8,128)(2,1)S(1)}, bf16[1,272,128]{2,1,0:T(8,128)(2,1)S(1)}, u32[]{:S(2)}, u32[]{:S(2)}) collective-permute-start(bf16[1,272,128]{2,1,0:T(8,128)(2,1)S(1)} %bitcast.16), channel_id=1, source_target_pairs={{0,7},{1,6},{2,5},{3,4},{4,3},{5,2},{6,1},{7,0},{8,15},{9,14},{10,... | collective-permute-start | bytes 208904 | tf_op jit(solution)/shard_map/ppermute | solution.py:268
  15.8 12.9 %collective-permute-start.8 = (bf16[512,128]{1,0:T(8,128)(2,1)}, bf16[512,128]{1,0:T(8,128)(2,1)S(1)}, u32[]{:S(2)}, u32[]{:S(2)}) collective-permute-start(bf16[512,128]{1,0:T(8,128)(2,1)} %refs_11_.1), channel_id=1, source_target_pairs={{0,1},{1,0},{2,3},{3,2},{4,5},{5,4},{6,7},{7,6},{8,9},{9,8},{10,11... | collective-permute-start | bytes 393224 | tf_op jit(solution)/shard_map/ppermute | solution.py:268
  16.4 18.0 %collective-permute-start.18 = (bf16[4,272,128]{2,1,0:T(8,128)(2,1)S(1)}, bf16[4,272,128]{2,1,0:T(8,128)(2,1)S(1)}, u32[]{:S(2)}, u32[]{:S(2)}) collective-permute-start(bf16[4,272,128]{2,1,0:T(8,128)(2,1)S(1)} %join.11.refs_4_), channel_id=1, source_target_pairs={{0,16},{8,24},{16,0},{24,8},{1,17},{9,25},{17,1},{25,9},{2,18},{10... | collective-permute-start | bytes 835592 | tf_op jit(solution)/shard_map/ppermute | solution.py:268
  17.9 6.7 %collective-permute-start.2 = (bf16[1,272,128]{2,1,0:T(8,128)(2,1)S(1)}, bf16[1,272,128]{2,1,0:T(8,128)(2,1)S(1)}, u32[]{:S(2)}, u32[]{:S(2)}) collective-permute-start(bf16[1,272,128]{2,1,0:T(8,128)(2,1)S(1)} %bitcast.15), channel_id=1, source_target_pairs={{0,4},{1,5},{2,6},{3,7},{4,0},{5,1},{6,2},{7,3},{8,12},{9,13},{10,... | collective-permute-start | bytes 208904 | tf_op jit(solution)/shard_map/ppermute | solution.py:268
  19.1 7.3 %collective-permute-start.3 = (bf16[1,272,128]{2,1,0:T(8,128)(2,1)S(1)}, bf16[1,272,128]{2,1,0:T(8,128)(2,1)S(1)}, u32[]{:S(2)}, u32[]{:S(2)}) collective-permute-start(bf16[1,272,128]{2,1,0:T(8,128)(2,1)S(1)} %bitcast.14), channel_id=1, source_target_pairs={{0,5},{1,4},{2,7},{3,6},{4,1},{5,0},{6,3},{7,2},{8,13},{9,12},{10,... | collective-permute-start | bytes 208904 | tf_op jit(solution)/shard_map/ppermute | solution.py:268
  21.8 6.9 %collective-permute-start.9 = (bf16[512,128]{1,0:T(8,128)(2,1)S(1)}, bf16[512,128]{1,0:T(8,128)(2,1)S(1)}, u32[]{:S(2)}, u32[]{:S(2)}) collective-permute-start(bf16[512,128]{1,0:T(8,128)(2,1)S(1)} %collective-permute-done.refs_9_), channel_id=1, source_target_pairs={{0,1},{1,0},{2,3},{3,2},{4,5},{5,4},{6,7},{7,6},{8,9},{9,8},{10,11... | collective-permute-start | bytes 393224 | tf_op jit(solution)/shard_map/ppermute | solution.py:268
  24.6 9.1 %collective-permute-start.7 = (bf16[2,272,128]{2,1,0:T(8,128)(2,1)S(1)}, bf16[2,272,128]{2,1,0:T(8,128)(2,1)S(1)}, u32[]{:S(2)}, u32[]{:S(2)}) collective-permute-start(bf16[2,272,128]{2,1,0:T(8,128)(2,1)S(1)} %join.7.refs_1_), channel_id=1, source_target_pairs={{0,16},{8,24},{16,0},{24,8},{1,17},{9,25},{17,1},{25,9},{2,18},{10... | collective-permute-start | bytes 417800 | tf_op jit(solution)/shard_map/ppermute | solution.py:268
  26.4 7.3 %collective-permute-start.4 = (bf16[2,272,128]{2,1,0:T(8,128)(2,1)S(1)}, bf16[2,272,128]{2,1,0:T(8,128)(2,1)S(1)}, u32[]{:S(2)}, u32[]{:S(2)}) collective-permute-start(bf16[2,272,128]{2,1,0:T(8,128)(2,1)S(1)} %join.6.refs_0_), channel_id=1, source_target_pairs={{0,16},{8,24},{16,0},{24,8},{1,17},{9,25},{17,1},{25,9},{2,18},{10... | collective-permute-start | bytes 417800 | tf_op jit(solution)/shard_map/ppermute | solution.py:268
  28.7 5.0 %collective-permute-start.10 = (bf16[512,128]{1,0:T(8,128)(2,1)S(1)}, bf16[512,128]{1,0:T(8,128)(2,1)S(1)}, u32[]{:S(2)}, u32[]{:S(2)}) collective-permute-start(bf16[512,128]{1,0:T(8,128)(2,1)S(1)} %collective-permute-done.1.refs_0_), channel_id=1, source_target_pairs={{0,1},{1,0},{2,3},{3,2},{4,5},{5,4},{6,7},{7,6},{8,9},{9,8},{10,11... | collective-permute-start | bytes 393224 | tf_op jit(solution)/shard_map/ppermute | solution.py:268
  28.7 6.1 %collective-permute-start.11 = (bf16[512,128]{1,0:T(8,128)(2,1)S(1)}, bf16[512,128]{1,0:T(8,128)(2,1)S(1)}, u32[]{:S(2)}, u32[]{:S(2)}) collective-permute-start(bf16[512,128]{1,0:T(8,128)(2,1)S(1)} %collective-permute-done.refs_9_), channel_id=1, source_target_pairs={{0,4},{1,5},{2,6},{3,7},{4,0},{5,1},{6,2},{7,3},{8,12},{9,13},{10,... | collective-permute-start | bytes 393224 | tf_op jit(solution)/shard_map/ppermute | solution.py:268
  33.7 4.5 %collective-permute-start.13 = (bf16[4,272,128]{2,1,0:T(8,128)(2,1)S(1)}, bf16[4,272,128]{2,1,0:T(8,128)(2,1)S(1)}, u32[]{:S(2)}, u32[]{:S(2)}) collective-permute-start(bf16[4,272,128]{2,1,0:T(8,128)(2,1)S(1)} %join.9.refs_0_), channel_id=1, source_target_pairs={{0,8},{8,0},{16,24},{24,16},{1,9},{9,1},{17,25},{25,17},{2,10},{10... | collective-permute-start | bytes 835592 | tf_op jit(solution)/shard_map/ppermute | solution.py:268
  33.8 4.4 %collective-permute-start.14 = (bf16[4,272,128]{2,1,0:T(8,128)(2,1)S(1)}, bf16[4,272,128]{2,1,0:T(8,128)(2,1)S(1)}, u32[]{:S(2)}, u32[]{:S(2)}) collective-permute-start(bf16[4,272,128]{2,1,0:T(8,128)(2,1)S(1)} %join.10.refs_2_), channel_id=1, source_target_pairs={{0,8},{8,0},{16,24},{24,16},{1,9},{9,1},{17,25},{25,17},{2,10},{10... | collective-permute-start | bytes 835592 | tf_op jit(solution)/shard_map/ppermute | solution.py:268
  34.3 3.9 %collective-permute-start.19 = (bf16[4,272,128]{2,1,0:T(8,128)(2,1)S(1)}, bf16[4,272,128]{2,1,0:T(8,128)(2,1)S(1)}, u32[]{:S(2)}, u32[]{:S(2)}) collective-permute-start(bf16[4,272,128]{2,1,0:T(8,128)(2,1)S(1)} %join.11.refs_4_), channel_id=1, source_target_pairs={{0,8},{8,0},{16,24},{24,16},{1,9},{9,1},{17,25},{25,17},{2,10},{10... | collective-permute-start | bytes 835592 | tf_op jit(solution)/shard_map/ppermute | solution.py:268
  34.4 3.8 %collective-permute-start.20 = (bf16[4,272,128]{2,1,0:T(8,128)(2,1)S(1)}, bf16[4,272,128]{2,1,0:T(8,128)(2,1)S(1)}, u32[]{:S(2)}, u32[]{:S(2)}) collective-permute-start(bf16[4,272,128]{2,1,0:T(8,128)(2,1)S(1)} %collective-permute-done.18.refs_6_), channel_id=1, source_target_pairs={{0,8},{8,0},{16,24},{24,16},{1,9},{9,1},{17,25},{25,17},{2,10},{10... | collective-permute-start | bytes 835592 | tf_op jit(solution)/shard_map/ppermute | solution.py:268
  34.8 6.2 %collective-permute-start.12 = (bf16[512,128]{1,0:T(8,128)(2,1)S(1)}, bf16[512,128]{1,0:T(8,128)(2,1)S(1)}, u32[]{:S(2)}, u32[]{:S(2)}) collective-permute-start(bf16[512,128]{1,0:T(8,128)(2,1)S(1)} %join.8), channel_id=1, source_target_pairs={{0,1},{1,0},{2,3},{3,2},{4,5},{5,4},{6,7},{7,6},{8,9},{9,8},{10,11... | collective-permute-start | bytes 393224 | tf_op jit(solution)/shard_map/ppermute | solution.py:268

commit v14 on v12

--- a/solution.py
+++ b/solution.py
@@ -122,7 +122,12 @@
             copies.append(
                 pltpu.make_async_copy(held.at[:, part], out[1].at[:, part], sems.at[n])
             )
-            copies[-1].start()
+            share = held.shape[0] // 4
+            for i in range(4):
+                rows = pl.ds(i * share, share)
+                pltpu.make_async_copy(
+                    held.at[rows, part], out[1].at[rows, part], sems.at[n]
+                ).start()
     for copy in copies:
         copy.wait()
 

time: 43.1 us -> 43.1 us (level)
  no operation moved by 1% of the time
where the time goes in v14:
time: 43.1 us; the launch traced here: 42.8 us
  starting transfers between devices  27 us (63%)
  waiting for transfers between devices  9.73 us (23%)
  Pallas kernels  5.96 us (14%)
    ppermute x21, starting transfers between devices, exchange(): return lax.ppermute(x, axis, [(i, i ^ flip) for i in range(size)])  27 us
    ppermute x21, waiting for transfers between devices, exchange(): return lax.ppermute(x, axis, [(i, i ^ flip) for i in range(size)])  9.73 us
    pallas_call x1, Pallas kernels, near_half(): pl.pallas_call(functools.partial(near_kernel, n_pieces, offsets, capacity...  2.83 us
    pallas_call x1, Pallas kernels, far_half(): pl.pallas_call(functools.partial(far_kernel, offsets, depth // width), ou...  1.83 us
    pallas_call x1, Pallas kernels, pack(): pl.pallas_call(functools.partial(pack_kernel, columns, capacity), out_sha...  1.2 us
  transfers between devices with their start and end apart: 21, of which 7 were waited for; matrix products, arithmetic and copies ran while one was open for 0% of the time, Pallas kernels for 10%

profile of v14, /device:TPU:0, one launch (start us, length us, event | category | flops | bytes accessed | tf_op | source)
XLA Modules:
  0.0 42.8 jit_solution(12361297020911283348)
XLA Ops:
  0.0 2.9 %collective-permute-start = (bf16[512,128]{1,0:T(8,128)(2,1)}, bf16[512,128]{1,0:T(8,128)(2,1)S(1)}, u32[]{:S(2)}, u32[]{:S(2)}) collective-permute-start(bf16[512,128]{1,0:T(8,128)(2,1)} %refs_11_.1), channel_id=1, source_target_pairs={{0,1},{1,0},{2,3},{3,2},{4,5},{5,4},{6,7},{7,6},{8,9},{9,8},{10,11... | collective-permute-start | bytes 393224 | tf_op jit(solution)/shard_map/ppermute | solution.py:273
  2.9 1.6 %collective-permute-start.1 = (bf16[512,128]{1,0:T(8,128)(2,1)}, bf16[512,128]{1,0:T(8,128)(2,1)S(1)}, u32[]{:S(2)}, u32[]{:S(2)}) collective-permute-start(bf16[512,128]{1,0:T(8,128)(2,1)} %refs_11_.1), channel_id=1, source_target_pairs={{0,2},{1,3},{2,0},{3,1},{4,6},{5,7},{6,4},{7,5},{8,10},{9,11},{10,... | collective-permute-start | bytes 393224 | tf_op jit(solution)/shard_map/ppermute | solution.py:273
  4.5 2.6 %collective-permute-start.2 = (bf16[512,128]{1,0:T(8,128)(2,1)}, bf16[512,128]{1,0:T(8,128)(2,1)S(1)}, u32[]{:S(2)}, u32[]{:S(2)}) collective-permute-start(bf16[512,128]{1,0:T(8,128)(2,1)} %refs_11_.1), channel_id=1, source_target_pairs={{0,4},{1,5},{2,6},{3,7},{4,0},{5,1},{6,2},{7,3},{8,12},{9,13},{10,... | collective-permute-start | bytes 393224 | tf_op jit(solution)/shard_map/ppermute | solution.py:273
  7.1 1.2 %pack.1 = (bf16[272,128]{1,0:T(8,128)(2,1)S(1)}, bf16[272,128]{1,0:T(8,128)(2,1)S(1)}, bf16[272,128]{1,0:T(8,128)(2,1)S(1)}, bf16[272,128]{1,0:T(8,128)(2,1)S(1)...) custom-call(s32[1]{0:T(128)} %bitcast.me_ref, ...), custom_call_target="tpu_custom_call" | custom-call | tf_op jit(solution)/shard_map/pack/pallas_call | solution.py:66
  8.3 0.6 %collective-permute-start.15 = (bf16[1,272,128]{2,1,0:T(8,128)(2,1)S(1)}, bf16[1,272,128]{2,1,0:T(8,128)(2,1)S(1)}, u32[]{:S(2)}, u32[]{:S(2)}) collective-permute-start(bf16[1,272,128]{2,1,0:T(8,128)(2,1)S(1)} %bitcast.20), channel_id=1, source_target_pairs={{0,1},{1,0},{2,3},{3,2},{4,5},{5,4},{6,7},{7,6},{8,9},{9,8},{10,11... | collective-permute-start | bytes 208904 | tf_op jit(solution)/shard_map/ppermute | solution.py:273
  8.9 0.4 %collective-permute-start.16 = (bf16[1,272,128]{2,1,0:T(8,128)(2,1)S(1)}, bf16[1,272,128]{2,1,0:T(8,128)(2,1)S(1)}, u32[]{:S(2)}, u32[]{:S(2)}) collective-permute-start(bf16[1,272,128]{2,1,0:T(8,128)(2,1)S(1)} %bitcast.19), channel_id=1, source_target_pairs={{0,2},{1,3},{2,0},{3,1},{4,6},{5,7},{6,4},{7,5},{8,10},{9,11},{10,... | collective-permute-start | bytes 208904 | tf_op jit(solution)/shard_map/ppermute | solution.py:273
  9.4 2.5 %collective-permute-start.17 = (bf16[1,272,128]{2,1,0:T(8,128)(2,1)S(1)}, bf16[1,272,128]{2,1,0:T(8,128)(2,1)S(1)}, u32[]{:S(2)}, u32[]{:S(2)}) collective-permute-start(bf16[1,272,128]{2,1,0:T(8,128)(2,1)S(1)} %bitcast.18), channel_id=1, source_target_pairs={{0,3},{1,2},{2,1},{3,0},{4,7},{5,6},{6,5},{7,4},{8,11},{9,10},{10,... | collective-permute-start | bytes 208904 | tf_op jit(solution)/shard_map/ppermute | solution.py:273
  11.9 3.8 %collective-permute-start.6 = (bf16[1,272,128]{2,1,0:T(8,128)(2,1)S(1)}, bf16[1,272,128]{2,1,0:T(8,128)(2,1)S(1)}, u32[]{:S(2)}, u32[]{:S(2)}) collective-permute-start(bf16[1,272,128]{2,1,0:T(8,128)(2,1)S(1)} %bitcast.17), channel_id=1, source_target_pairs={{0,6},{1,7},{2,4},{3,5},{4,2},{5,3},{6,0},{7,1},{8,14},{9,15},{10,... | collective-permute-start | bytes 208904 | tf_op jit(solution)/shard_map/ppermute | solution.py:273
  15.8 1.6 %collective-permute-start.18 = (bf16[4,272,128]{2,1,0:T(8,128)(2,1)S(1)}, bf16[4,272,128]{2,1,0:T(8,128)(2,1)S(1)}, u32[]{:S(2)}, u32[]{:S(2)}) collective-permute-start(bf16[4,272,128]{2,1,0:T(8,128)(2,1)S(1)} %join.11.refs_4_), channel_id=1, source_target_pairs={{0,16},{8,24},{16,0},{24,8},{1,17},{9,25},{17,1},{25,9},{2,18},{10... | collective-permute-start | bytes 835592 | tf_op jit(solution)/shard_map/ppermute | solution.py:273
  17.4 2.1 %collective-permute-start.3 = (bf16[1,272,128]{2,1,0:T(8,128)(2,1)S(1)}, bf16[1,272,128]{2,1,0:T(8,128)(2,1)S(1)}, u32[]{:S(2)}, u32[]{:S(2)}) collective-permute-start(bf16[1,272,128]{2,1,0:T(8,128)(2,1)S(1)} %bitcast.15), channel_id=1, source_target_pairs={{0,4},{1,5},{2,6},{3,7},{4,0},{5,1},{6,2},{7,3},{8,12},{9,13},{10,... | collective-permute-start | bytes 208904 | tf_op jit(solution)/shard_map/ppermute | solution.py:273
  19.5 1.7 %collective-permute-start.4 = (bf16[1,272,128]{2,1,0:T(8,128)(2,1)S(1)}, bf16[1,272,128]{2,1,0:T(8,128)(2,1)S(1)}, u32[]{:S(2)}, u32[]{:S(2)}) collective-permute-start(bf16[1,272,128]{2,1,0:T(8,128)(2,1)S(1)} %bitcast.14), channel_id=1, source_target_pairs={{0,5},{1,4},{2,7},{3,6},{4,1},{5,0},{6,3},{7,2},{8,13},{9,12},{10,... | collective-permute-start | bytes 208904 | tf_op jit(solution)/shard_map/ppermute | solution.py:273
  21.2 0.6 %collective-permute-start.9 = (bf16[512,128]{1,0:T(8,128)(2,1)S(1)}, bf16[512,128]{1,0:T(8,128)(2,1)S(1)}, u32[]{:S(2)}, u32[]{:S(2)}) collective-permute-start(bf16[512,128]{1,0:T(8,128)(2,1)S(1)} %collective-permute-done.1.refs_9_), channel_id=1, source_target_pairs={{0,1},{1,0},{2,3},{3,2},{4,5},{5,4},{6,7},{7,6},{8,9},{9,8},{10,11... | collective-permute-start | bytes 393224 | tf_op jit(solution)/shard_map/ppermute | solution.py:273
  21.8 1.3 %collective-permute-done.7.refs_1_ = bf16[1,272,128]{2,1,0:T(8,128)(2,1)S(1)} collective-permute-done((bf16[1,272,128]{2,1,0:T(8,128)(2,1)S(1)}, bf16[1,272,128]{2,1,0:T(8,128)(2,1)S(1)}, u32[]{:S(2)}, u32[]{:S(2)}) %collective-permute-start.7) | collective-permute-done | bytes 69664 | tf_op jit(solution)/shard_map/ppermute | solution.py:273
  23.1 1.3 %collective-permute-start.8 = (bf16[2,272,128]{2,1,0:T(8,128)(2,1)S(1)}, bf16[2,272,128]{2,1,0:T(8,128)(2,1)S(1)}, u32[]{:S(2)}, u32[]{:S(2)}) collective-permute-start(bf16[2,272,128]{2,1,0:T(8,128)(2,1)S(1)} %join.7.refs_1_), channel_id=1, source_target_pairs={{0,16},{8,24},{16,0},{24,8},{1,17},{9,25},{17,1},{25,9},{2,18},{10... | collective-permute-start | bytes 417800 | tf_op jit(solution)/shard_map/ppermute | solution.py:273
  24.4 0.4 %collective-permute-done.3.refs_0_ = bf16[1,272,128]{2,1,0:T(8,128)(2,1)S(1)} collective-permute-done((bf16[1,272,128]{2,1,0:T(8,128)(2,1)S(1)}, bf16[1,272,128]{2,1,0:T(8,128)(2,1)S(1)}, u32[]{:S(2)}, u32[]{:S(2)}) %collective-permute-start.3) | collective-permute-done | bytes 69664 | tf_op jit(solution)/shard_map/ppermute | solution.py:273
  24.9 1.2 %collective-permute-done.4.refs_1_ = bf16[1,272,128]{2,1,0:T(8,128)(2,1)S(1)} collective-permute-done((bf16[1,272,128]{2,1,0:T(8,128)(2,1)S(1)}, bf16[1,272,128]{2,1,0:T(8,128)(2,1)S(1)}, u32[]{:S(2)}, u32[]{:S(2)}) %collective-permute-start.4) | collective-permute-done | bytes 69664 | tf_op jit(solution)/shard_map/ppermute | solution.py:273
  26.1 2.2 %collective-permute-start.5 = (bf16[2,272,128]{2,1,0:T(8,128)(2,1)S(1)}, bf16[2,272,128]{2,1,0:T(8,128)(2,1)S(1)}, u32[]{:S(2)}, u32[]{:S(2)}) collective-permute-start(bf16[2,272,128]{2,1,0:T(8,128)(2,1)S(1)} %join.6.refs_0_), channel_id=1, source_target_pairs={{0,16},{8,24},{16,0},{24,8},{1,17},{9,25},{17,1},{25,9},{2,18},{10... | collective-permute-start | bytes 417800 | tf_op jit(solution)/shard_map/ppermute | solution.py:273
  28.9 4.5 %collective-permute-done.10.refs_1_ = bf16[512,128]{1,0:T(8,128)(2,1)S(1)} collective-permute-done((bf16[512,128]{1,0:T(8,128)(2,1)S(1)}, bf16[512,128]{1,0:T(8,128)(2,1)S(1)}, u32[]{:S(2)}, u32[]{:S(2)}) %collective-permute-start.10) | collective-permute-done | bytes 131104 | tf_op jit(solution)/shard_map/ppermute | solution.py:273
  33.4 0.5 %collective-permute-start.14 = (bf16[4,272,128]{2,1,0:T(8,128)(2,1)S(1)}, bf16[4,272,128]{2,1,0:T(8,128)(2,1)S(1)}, u32[]{:S(2)}, u32[]{:S(2)}) collective-permute-start(bf16[4,272,128]{2,1,0:T(8,128)(2,1)S(1)} %join.10.refs_2_), channel_id=1, source_target_pairs={{0,8},{8,0},{16,24},{24,16},{1,9},{9,1},{17,25},{25,17},{2,10},{10... | collective-permute-start | bytes 835592 | tf_op jit(solution)/shard_map/ppermute | solution.py:273
  34.4 1.5 %collective-permute-done.11.refs_0_.refs_2_ = bf16[512,128]{1,0:T(8,128)(2,1)S(1)} collective-permute-done((bf16[512,128]{1,0:T(8,128)(2,1)S(1)}, bf16[512,128]{1,0:T(8,128)(2,1)S(1)}, u32[]{:S(2)}, u32[]{:S(2)}) %collective-permute-start.11) | collective-permute-done | bytes 131104 | tf_op jit(solution)/shard_map/ppermute | solution.py:273
  36.0 1.4 %collective-permute-start.12 = (bf16[512,128]{1,0:T(8,128)(2,1)S(1)}, bf16[512,128]{1,0:T(8,128)(2,1)S(1)}, u32[]{:S(2)}, u32[]{:S(2)}) collective-permute-start(bf16[512,128]{1,0:T(8,128)(2,1)S(1)} %join.8), channel_id=1, source_target_pairs={{0,1},{1,0},{2,3},{3,2},{4,5},{5,4},{6,7},{7,6},{8,9},{9,8},{10,11... | collective-permute-start | bytes 393224 | tf_op jit(solution)/shard_map/ppermute | solution.py:273
  37.5 2.8 %near_half.1 = (f32[512,1024]{1,0:T(8,128)S(1)}, bf16[1024,1024]{1,0:T(8,128)(2,1)S(1)}) custom-call(s32[9]{0:T(128)S(1)} %stack.24.where_ref, bf16[4,272,128]{2,1,0:T(8,128)(2,1)S(1)} %join.9.refs_0_, bf16[4,272,128]{2,1,0:T(8,128)(2,1)S(1)} %collective-permute-done.13.refs_1_, bf16[4,272,128]{2,1,0:T(8,128)(2,1)S(1)} %join.10.refs_2_, ...), custom_call_target="tpu_custom_call" | custom-call | flops 536870912 | bytes 8388608 | tf_op jit(solution)/shard_map/near_half/pallas_call | solution.py:201
  40.4 0.7 %collective-permute-done.12.refs_3_ = bf16[512,128]{1,0:T(8,128)(2,1)S(1)} collective-permute-done((bf16[512,128]{1,0:T(8,128)(2,1)S(1)}, bf16[512,128]{1,0:T(8,128)(2,1)S(1)}, u32[]{:S(2)}, u32[]{:S(2)}) %collective-permute-start.12) | collective-permute-done | bytes 131104 | tf_op jit(solution)/shard_map/ppermute | solution.py:273
  41.0 1.8 %far_half.1 = f32[512,1024]{1,0:T(8,128)} custom-call(bf16[512,128]{1,0:T(8,128)(2,1)S(1)} %collective-permute-done.2.refs_0_, bf16[512,128]{1,0:T(8,128)(2,1)S(1)} %collective-permute-done.10.refs_1_, bf16[512,128]{1,0:T(8,128)(2,1)S(1)} %collective-permute-done.11.refs_0_.refs_2_, bf16[512,128]{1,0:T(8,128)(2,1)S(1)} %collective-permute-done.12.refs_3_, ...), custom_call_target="tpu_custom_call" | custom-call | flops 536870912 | bytes 8388608 | tf_op jit(solution)/shard_map/far_half/pallas_call | solution.py:251
  (28 shorter events, 1.3 us)
Async XLA Ops:
  0.0 9.4 %collective-permute-start = (bf16[512,128]{1,0:T(8,128)(2,1)}, bf16[512,128]{1,0:T(8,128)(2,1)S(1)}, u32[]{:S(2)}, u32[]{:S(2)}) collective-permute-start(bf16[512,128]{1,0:T(8,128)(2,1)} %refs_11_.1), channel_id=1, source_target_pairs={{0,1},{1,0},{2,3},{3,2},{4,5},{5,4},{6,7},{7,6},{8,9},{9,8},{10,11... | collective-permute-start | bytes 393224 | tf_op jit(solution)/shard_map/ppermute | solution.py:273
  2.9 8.9 %collective-permute-start.1 = (bf16[512,128]{1,0:T(8,128)(2,1)}, bf16[512,128]{1,0:T(8,128)(2,1)S(1)}, u32[]{:S(2)}, u32[]{:S(2)}) collective-permute-start(bf16[512,128]{1,0:T(8,128)(2,1)} %refs_11_.1), channel_id=1, source_target_pairs={{0,2},{1,3},{2,0},{3,1},{4,6},{5,7},{6,4},{7,5},{8,10},{9,11},{10,... | collective-permute-start | bytes 393224 | tf_op jit(solution)/shard_map/ppermute | solution.py:273
  4.5 7.4 %collective-permute-start.2 = (bf16[512,128]{1,0:T(8,128)(2,1)}, bf16[512,128]{1,0:T(8,128)(2,1)S(1)}, u32[]{:S(2)}, u32[]{:S(2)}) collective-permute-start(bf16[512,128]{1,0:T(8,128)(2,1)} %refs_11_.1), channel_id=1, source_target_pairs={{0,4},{1,5},{2,6},{3,7},{4,0},{5,1},{6,2},{7,3},{8,12},{9,13},{10,... | collective-permute-start | bytes 393224 | tf_op jit(solution)/shard_map/ppermute | solution.py:273
  8.3 7.4 %collective-permute-start.15 = (bf16[1,272,128]{2,1,0:T(8,128)(2,1)S(1)}, bf16[1,272,128]{2,1,0:T(8,128)(2,1)S(1)}, u32[]{:S(2)}, u32[]{:S(2)}) collective-permute-start(bf16[1,272,128]{2,1,0:T(8,128)(2,1)S(1)} %bitcast.20), channel_id=1, source_target_pairs={{0,1},{1,0},{2,3},{3,2},{4,5},{5,4},{6,7},{7,6},{8,9},{9,8},{10,11... | collective-permute-start | bytes 208904 | tf_op jit(solution)/shard_map/ppermute | solution.py:273
  8.9 6.8 %collective-permute-start.16 = (bf16[1,272,128]{2,1,0:T(8,128)(2,1)S(1)}, bf16[1,272,128]{2,1,0:T(8,128)(2,1)S(1)}, u32[]{:S(2)}, u32[]{:S(2)}) collective-permute-start(bf16[1,272,128]{2,1,0:T(8,128)(2,1)S(1)} %bitcast.19), channel_id=1, source_target_pairs={{0,2},{1,3},{2,0},{3,1},{4,6},{5,7},{6,4},{7,5},{8,10},{9,11},{10,... | collective-permute-start | bytes 208904 | tf_op jit(solution)/shard_map/ppermute | solution.py:273
  9.4 6.4 %collective-permute-start.17 = (bf16[1,272,128]{2,1,0:T(8,128)(2,1)S(1)}, bf16[1,272,128]{2,1,0:T(8,128)(2,1)S(1)}, u32[]{:S(2)}, u32[]{:S(2)}) collective-permute-start(bf16[1,272,128]{2,1,0:T(8,128)(2,1)S(1)} %bitcast.18), channel_id=1, source_target_pairs={{0,3},{1,2},{2,1},{3,0},{4,7},{5,6},{6,5},{7,4},{8,11},{9,10},{10,... | collective-permute-start | bytes 208904 | tf_op jit(solution)/shard_map/ppermute | solution.py:273
  11.9 9.3 %collective-permute-start.6 = (bf16[1,272,128]{2,1,0:T(8,128)(2,1)S(1)}, bf16[1,272,128]{2,1,0:T(8,128)(2,1)S(1)}, u32[]{:S(2)}, u32[]{:S(2)}) collective-permute-start(bf16[1,272,128]{2,1,0:T(8,128)(2,1)S(1)} %bitcast.17), channel_id=1, source_target_pairs={{0,6},{1,7},{2,4},{3,5},{4,2},{5,3},{6,0},{7,1},{8,14},{9,15},{10,... | collective-permute-start | bytes 208904 | tf_op jit(solution)/shard_map/ppermute | solution.py:273
  15.7 7.4 %collective-permute-start.7 = (bf16[1,272,128]{2,1,0:T(8,128)(2,1)S(1)}, bf16[1,272,128]{2,1,0:T(8,128)(2,1)S(1)}, u32[]{:S(2)}, u32[]{:S(2)}) collective-permute-start(bf16[1,272,128]{2,1,0:T(8,128)(2,1)S(1)} %bitcast.16), channel_id=1, source_target_pairs={{0,7},{1,6},{2,5},{3,4},{4,3},{5,2},{6,1},{7,0},{8,15},{9,14},{10,... | collective-permute-start | bytes 208904 | tf_op jit(solution)/shard_map/ppermute | solution.py:273
  15.8 18.1 %collective-permute-start.18 = (bf16[4,272,128]{2,1,0:T(8,128)(2,1)S(1)}, bf16[4,272,128]{2,1,0:T(8,128)(2,1)S(1)}, u32[]{:S(2)}, u32[]{:S(2)}) collective-permute-start(bf16[4,272,128]{2,1,0:T(8,128)(2,1)S(1)} %join.11.refs_4_), channel_id=1, source_target_pairs={{0,16},{8,24},{16,0},{24,8},{1,17},{9,25},{17,1},{25,9},{2,18},{10... | collective-permute-start | bytes 835592 | tf_op jit(solution)/shard_map/ppermute | solution.py:273
  17.4 7.5 %collective-permute-start.3 = (bf16[1,272,128]{2,1,0:T(8,128)(2,1)S(1)}, bf16[1,272,128]{2,1,0:T(8,128)(2,1)S(1)}, u32[]{:S(2)}, u32[]{:S(2)}) collective-permute-start(bf16[1,272,128]{2,1,0:T(8,128)(2,1)S(1)} %bitcast.15), channel_id=1, source_target_pairs={{0,4},{1,5},{2,6},{3,7},{4,0},{5,1},{6,2},{7,3},{8,12},{9,13},{10,... | collective-permute-start | bytes 208904 | tf_op jit(solution)/shard_map/ppermute | solution.py:273
  19.5 6.6 %collective-permute-start.4 = (bf16[1,272,128]{2,1,0:T(8,128)(2,1)S(1)}, bf16[1,272,128]{2,1,0:T(8,128)(2,1)S(1)}, u32[]{:S(2)}, u32[]{:S(2)}) collective-permute-start(bf16[1,272,128]{2,1,0:T(8,128)(2,1)S(1)} %bitcast.14), channel_id=1, source_target_pairs={{0,5},{1,4},{2,7},{3,6},{4,1},{5,0},{6,3},{7,2},{8,13},{9,12},{10,... | collective-permute-start | bytes 208904 | tf_op jit(solution)/shard_map/ppermute | solution.py:273
  21.2 7.5 %collective-permute-start.9 = (bf16[512,128]{1,0:T(8,128)(2,1)S(1)}, bf16[512,128]{1,0:T(8,128)(2,1)S(1)}, u32[]{:S(2)}, u32[]{:S(2)}) collective-permute-start(bf16[512,128]{1,0:T(8,128)(2,1)S(1)} %collective-permute-done.1.refs_9_), channel_id=1, source_target_pairs={{0,1},{1,0},{2,3},{3,2},{4,5},{5,4},{6,7},{7,6},{8,9},{9,8},{10,11... | collective-permute-start | bytes 393224 | tf_op jit(solution)/shard_map/ppermute | solution.py:273
  23.1 10.2 %collective-permute-start.8 = (bf16[2,272,128]{2,1,0:T(8,128)(2,1)S(1)}, bf16[2,272,128]{2,1,0:T(8,128)(2,1)S(1)}, u32[]{:S(2)}, u32[]{:S(2)}) collective-permute-start(bf16[2,272,128]{2,1,0:T(8,128)(2,1)S(1)} %join.7.refs_1_), channel_id=1, source_target_pairs={{0,16},{8,24},{16,0},{24,8},{1,17},{9,25},{17,1},{25,9},{2,18},{10... | collective-permute-start | bytes 417800 | tf_op jit(solution)/shard_map/ppermute | solution.py:273
  26.1 7.2 %collective-permute-start.5 = (bf16[2,272,128]{2,1,0:T(8,128)(2,1)S(1)}, bf16[2,272,128]{2,1,0:T(8,128)(2,1)S(1)}, u32[]{:S(2)}, u32[]{:S(2)}) collective-permute-start(bf16[2,272,128]{2,1,0:T(8,128)(2,1)S(1)} %join.6.refs_0_), channel_id=1, source_target_pairs={{0,16},{8,24},{16,0},{24,8},{1,17},{9,25},{17,1},{25,9},{2,18},{10... | collective-permute-start | bytes 417800 | tf_op jit(solution)/shard_map/ppermute | solution.py:273
  28.4 5.0 %collective-permute-start.10 = (bf16[512,128]{1,0:T(8,128)(2,1)S(1)}, bf16[512,128]{1,0:T(8,128)(2,1)S(1)}, u32[]{:S(2)}, u32[]{:S(2)}) collective-permute-start(bf16[512,128]{1,0:T(8,128)(2,1)S(1)} %collective-permute-done.2.refs_0_), channel_id=1, source_target_pairs={{0,1},{1,0},{2,3},{3,2},{4,5},{5,4},{6,7},{7,6},{8,9},{9,8},{10,11... | collective-permute-start | bytes 393224 | tf_op jit(solution)/shard_map/ppermute | solution.py:273
  28.7 7.3 %collective-permute-start.11 = (bf16[512,128]{1,0:T(8,128)(2,1)S(1)}, bf16[512,128]{1,0:T(8,128)(2,1)S(1)}, u32[]{:S(2)}, u32[]{:S(2)}) collective-permute-start(bf16[512,128]{1,0:T(8,128)(2,1)S(1)} %collective-permute-done.1.refs_9_), channel_id=1, source_target_pairs={{0,4},{1,5},{2,6},{3,7},{4,0},{5,1},{6,2},{7,3},{8,12},{9,13},{10,... | collective-permute-start | bytes 393224 | tf_op jit(solution)/shard_map/ppermute | solution.py:273
  33.4 4.1 %collective-permute-start.13 = (bf16[4,272,128]{2,1,0:T(8,128)(2,1)S(1)}, bf16[4,272,128]{2,1,0:T(8,128)(2,1)S(1)}, u32[]{:S(2)}, u32[]{:S(2)}) collective-permute-start(bf16[4,272,128]{2,1,0:T(8,128)(2,1)S(1)} %join.9.refs_0_), channel_id=1, source_target_pairs={{0,8},{8,0},{16,24},{24,16},{1,9},{9,1},{17,25},{25,17},{2,10},{10... | collective-permute-start | bytes 835592 | tf_op jit(solution)/shard_map/ppermute | solution.py:273
  33.4 4.0 %collective-permute-start.14 = (bf16[4,272,128]{2,1,0:T(8,128)(2,1)S(1)}, bf16[4,272,128]{2,1,0:T(8,128)(2,1)S(1)}, u32[]{:S(2)}, u32[]{:S(2)}) collective-permute-start(bf16[4,272,128]{2,1,0:T(8,128)(2,1)S(1)} %join.10.refs_2_), channel_id=1, source_target_pairs={{0,8},{8,0},{16,24},{24,16},{1,9},{9,1},{17,25},{25,17},{2,10},{10... | collective-permute-start | bytes 835592 | tf_op jit(solution)/shard_map/ppermute | solution.py:273
  33.9 3.6 %collective-permute-start.19 = (bf16[4,272,128]{2,1,0:T(8,128)(2,1)S(1)}, bf16[4,272,128]{2,1,0:T(8,128)(2,1)S(1)}, u32[]{:S(2)}, u32[]{:S(2)}) collective-permute-start(bf16[4,272,128]{2,1,0:T(8,128)(2,1)S(1)} %join.11.refs_4_), channel_id=1, source_target_pairs={{0,8},{8,0},{16,24},{24,16},{1,9},{9,1},{17,25},{25,17},{2,10},{10... | collective-permute-start | bytes 835592 | tf_op jit(solution)/shard_map/ppermute | solution.py:273
  34.0 3.5 %collective-permute-start.20 = (bf16[4,272,128]{2,1,0:T(8,128)(2,1)S(1)}, bf16[4,272,128]{2,1,0:T(8,128)(2,1)S(1)}, u32[]{:S(2)}, u32[]{:S(2)}) collective-permute-start(bf16[4,272,128]{2,1,0:T(8,128)(2,1)S(1)} %collective-permute-done.18.refs_6_), channel_id=1, source_target_pairs={{0,8},{8,0},{16,24},{24,16},{1,9},{9,1},{17,25},{25,17},{2,10},{10... | collective-permute-start | bytes 835592 | tf_op jit(solution)/shard_map/ppermute | solution.py:273
  36.0 5.0 %collective-permute-start.12 = (bf16[512,128]{1,0:T(8,128)(2,1)S(1)}, bf16[512,128]{1,0:T(8,128)(2,1)S(1)}, u32[]{:S(2)}, u32[]{:S(2)}) collective-permute-start(bf16[512,128]{1,0:T(8,128)(2,1)S(1)} %join.8), channel_id=1, source_target_pairs={{0,1},{1,0},{2,3},{3,2},{4,5},{5,4},{6,7},{7,6},{8,9},{9,8},{10,11... | collective-permute-start | bytes 393224 | tf_op jit(solution)/shard_map/ppermute | solution.py:273

commit v15 on v12

--- a/solution.py
+++ b/solution.py
@@ -180,7 +180,7 @@
             at += 1
     own_copy.wait()
     res_copy.wait()
-    multiply(amp, block, 0, res, total, None, 2 * width)
+    multiply(amp, block, 0, res, total, None, 4 * width)
 
 
 def near_half(where, pieces, amps, offsets, own, residual, capacity):

time: 43.1 us -> 43.1 us (level)
  no operation moved by 1% of the time
where the time goes in v15:
time: 43.1 us; the launch traced here: 42.9 us
  starting transfers between devices  27 us (63%)
  waiting for transfers between devices  9.73 us (23%)
  Pallas kernels  5.97 us (14%)
    ppermute x21, starting transfers between devices, exchange(): return lax.ppermute(x, axis, [(i, i ^ flip) for i in range(size)])  27 us
    ppermute x21, waiting for transfers between devices, exchange(): return lax.ppermute(x, axis, [(i, i ^ flip) for i in range(size)])  9.73 us
    pallas_call x1, Pallas kernels, near_half(): pl.pallas_call(functools.partial(near_kernel, n_pieces, offsets, capacity...  2.83 us
    pallas_call x1, Pallas kernels, far_half(): pl.pallas_call(functools.partial(far_kernel, offsets, depth // width), ou...  1.85 us
    pallas_call x1, Pallas kernels, pack(): pl.pallas_call(functools.partial(pack_kernel, columns, capacity), out_sha...  1.2 us
  transfers between devices with their start and end apart: 21, of which 7 were waited for; matrix products, arithmetic and copies ran while one was open for 0% of the time, Pallas kernels for 10%

profile of v15, /device:TPU:0, one launch (start us, length us, event | category | flops | bytes accessed | tf_op | source)
XLA Modules:
  0.0 42.9 jit_solution(2994561002892004534)
XLA Ops:
  0.0 2.9 %collective-permute-start = (bf16[512,128]{1,0:T(8,128)(2,1)}, bf16[512,128]{1,0:T(8,128)(2,1)S(1)}, u32[]{:S(2)}, u32[]{:S(2)}) collective-permute-start(bf16[512,128]{1,0:T(8,128)(2,1)} %refs_11_.1), channel_id=1, source_target_pairs={{0,1},{1,0},{2,3},{3,2},{4,5},{5,4},{6,7},{7,6},{8,9},{9,8},{10,11... | collective-permute-start | bytes 393224 | tf_op jit(solution)/shard_map/ppermute | solution.py:268
  2.9 1.6 %collective-permute-start.1 = (bf16[512,128]{1,0:T(8,128)(2,1)}, bf16[512,128]{1,0:T(8,128)(2,1)S(1)}, u32[]{:S(2)}, u32[]{:S(2)}) collective-permute-start(bf16[512,128]{1,0:T(8,128)(2,1)} %refs_11_.1), channel_id=1, source_target_pairs={{0,2},{1,3},{2,0},{3,1},{4,6},{5,7},{6,4},{7,5},{8,10},{9,11},{10,... | collective-permute-start | bytes 393224 | tf_op jit(solution)/shard_map/ppermute | solution.py:268
  4.5 2.6 %collective-permute-start.2 = (bf16[512,128]{1,0:T(8,128)(2,1)}, bf16[512,128]{1,0:T(8,128)(2,1)S(1)}, u32[]{:S(2)}, u32[]{:S(2)}) collective-permute-start(bf16[512,128]{1,0:T(8,128)(2,1)} %refs_11_.1), channel_id=1, source_target_pairs={{0,4},{1,5},{2,6},{3,7},{4,0},{5,1},{6,2},{7,3},{8,12},{9,13},{10,... | collective-permute-start | bytes 393224 | tf_op jit(solution)/shard_map/ppermute | solution.py:268
  7.1 1.2 %pack.1 = (bf16[272,128]{1,0:T(8,128)(2,1)S(1)}, bf16[272,128]{1,0:T(8,128)(2,1)S(1)}, bf16[272,128]{1,0:T(8,128)(2,1)S(1)}, bf16[272,128]{1,0:T(8,128)(2,1)S(1)...) custom-call(s32[1]{0:T(128)} %bitcast.me_ref, ...), custom_call_target="tpu_custom_call" | custom-call | tf_op jit(solution)/shard_map/pack/pallas_call | solution.py:66
  8.3 0.6 %collective-permute-start.15 = (bf16[1,272,128]{2,1,0:T(8,128)(2,1)S(1)}, bf16[1,272,128]{2,1,0:T(8,128)(2,1)S(1)}, u32[]{:S(2)}, u32[]{:S(2)}) collective-permute-start(bf16[1,272,128]{2,1,0:T(8,128)(2,1)S(1)} %bitcast.20), channel_id=1, source_target_pairs={{0,1},{1,0},{2,3},{3,2},{4,5},{5,4},{6,7},{7,6},{8,9},{9,8},{10,11... | collective-permute-start | bytes 208904 | tf_op jit(solution)/shard_map/ppermute | solution.py:268
  8.9 0.4 %collective-permute-start.16 = (bf16[1,272,128]{2,1,0:T(8,128)(2,1)S(1)}, bf16[1,272,128]{2,1,0:T(8,128)(2,1)S(1)}, u32[]{:S(2)}, u32[]{:S(2)}) collective-permute-start(bf16[1,272,128]{2,1,0:T(8,128)(2,1)S(1)} %bitcast.19), channel_id=1, source_target_pairs={{0,2},{1,3},{2,0},{3,1},{4,6},{5,7},{6,4},{7,5},{8,10},{9,11},{10,... | collective-permute-start | bytes 208904 | tf_op jit(solution)/shard_map/ppermute | solution.py:268
  9.4 2.5 %collective-permute-start.17 = (bf16[1,272,128]{2,1,0:T(8,128)(2,1)S(1)}, bf16[1,272,128]{2,1,0:T(8,128)(2,1)S(1)}, u32[]{:S(2)}, u32[]{:S(2)}) collective-permute-start(bf16[1,272,128]{2,1,0:T(8,128)(2,1)S(1)} %bitcast.18), channel_id=1, source_target_pairs={{0,3},{1,2},{2,1},{3,0},{4,7},{5,6},{6,5},{7,4},{8,11},{9,10},{10,... | collective-permute-start | bytes 208904 | tf_op jit(solution)/shard_map/ppermute | solution.py:268
  11.9 3.8 %collective-permute-start.6 = (bf16[1,272,128]{2,1,0:T(8,128)(2,1)S(1)}, bf16[1,272,128]{2,1,0:T(8,128)(2,1)S(1)}, u32[]{:S(2)}, u32[]{:S(2)}) collective-permute-start(bf16[1,272,128]{2,1,0:T(8,128)(2,1)S(1)} %bitcast.17), channel_id=1, source_target_pairs={{0,6},{1,7},{2,4},{3,5},{4,2},{5,3},{6,0},{7,1},{8,14},{9,15},{10,... | collective-permute-start | bytes 208904 | tf_op jit(solution)/shard_map/ppermute | solution.py:268
  15.8 1.6 %collective-permute-start.18 = (bf16[4,272,128]{2,1,0:T(8,128)(2,1)S(1)}, bf16[4,272,128]{2,1,0:T(8,128)(2,1)S(1)}, u32[]{:S(2)}, u32[]{:S(2)}) collective-permute-start(bf16[4,272,128]{2,1,0:T(8,128)(2,1)S(1)} %join.11.refs_4_), channel_id=1, source_target_pairs={{0,16},{8,24},{16,0},{24,8},{1,17},{9,25},{17,1},{25,9},{2,18},{10... | collective-permute-start | bytes 835592 | tf_op jit(solution)/shard_map/ppermute | solution.py:268
  17.4 2.1 %collective-permute-start.3 = (bf16[1,272,128]{2,1,0:T(8,128)(2,1)S(1)}, bf16[1,272,128]{2,1,0:T(8,128)(2,1)S(1)}, u32[]{:S(2)}, u32[]{:S(2)}) collective-permute-start(bf16[1,272,128]{2,1,0:T(8,128)(2,1)S(1)} %bitcast.15), channel_id=1, source_target_pairs={{0,4},{1,5},{2,6},{3,7},{4,0},{5,1},{6,2},{7,3},{8,12},{9,13},{10,... | collective-permute-start | bytes 208904 | tf_op jit(solution)/shard_map/ppermute | solution.py:268
  19.5 1.7 %collective-permute-start.4 = (bf16[1,272,128]{2,1,0:T(8,128)(2,1)S(1)}, bf16[1,272,128]{2,1,0:T(8,128)(2,1)S(1)}, u32[]{:S(2)}, u32[]{:S(2)}) collective-permute-start(bf16[1,272,128]{2,1,0:T(8,128)(2,1)S(1)} %bitcast.14), channel_id=1, source_target_pairs={{0,5},{1,4},{2,7},{3,6},{4,1},{5,0},{6,3},{7,2},{8,13},{9,12},{10,... | collective-permute-start | bytes 208904 | tf_op jit(solution)/shard_map/ppermute | solution.py:268
  21.2 0.6 %collective-permute-start.9 = (bf16[512,128]{1,0:T(8,128)(2,1)S(1)}, bf16[512,128]{1,0:T(8,128)(2,1)S(1)}, u32[]{:S(2)}, u32[]{:S(2)}) collective-permute-start(bf16[512,128]{1,0:T(8,128)(2,1)S(1)} %collective-permute-done.1.refs_9_), channel_id=1, source_target_pairs={{0,1},{1,0},{2,3},{3,2},{4,5},{5,4},{6,7},{7,6},{8,9},{9,8},{10,11... | collective-permute-start | bytes 393224 | tf_op jit(solution)/shard_map/ppermute | solution.py:268
  21.8 1.3 %collective-permute-done.7.refs_1_ = bf16[1,272,128]{2,1,0:T(8,128)(2,1)S(1)} collective-permute-done((bf16[1,272,128]{2,1,0:T(8,128)(2,1)S(1)}, bf16[1,272,128]{2,1,0:T(8,128)(2,1)S(1)}, u32[]{:S(2)}, u32[]{:S(2)}) %collective-permute-start.7) | collective-permute-done | bytes 69664 | tf_op jit(solution)/shard_map/ppermute | solution.py:268
  23.1 1.3 %collective-permute-start.8 = (bf16[2,272,128]{2,1,0:T(8,128)(2,1)S(1)}, bf16[2,272,128]{2,1,0:T(8,128)(2,1)S(1)}, u32[]{:S(2)}, u32[]{:S(2)}) collective-permute-start(bf16[2,272,128]{2,1,0:T(8,128)(2,1)S(1)} %join.7.refs_1_), channel_id=1, source_target_pairs={{0,16},{8,24},{16,0},{24,8},{1,17},{9,25},{17,1},{25,9},{2,18},{10... | collective-permute-start | bytes 417800 | tf_op jit(solution)/shard_map/ppermute | solution.py:268
  24.4 0.4 %collective-permute-done.3.refs_0_ = bf16[1,272,128]{2,1,0:T(8,128)(2,1)S(1)} collective-permute-done((bf16[1,272,128]{2,1,0:T(8,128)(2,1)S(1)}, bf16[1,272,128]{2,1,0:T(8,128)(2,1)S(1)}, u32[]{:S(2)}, u32[]{:S(2)}) %collective-permute-start.3) | collective-permute-done | bytes 69664 | tf_op jit(solution)/shard_map/ppermute | solution.py:268
  24.9 1.2 %collective-permute-done.4.refs_1_ = bf16[1,272,128]{2,1,0:T(8,128)(2,1)S(1)} collective-permute-done((bf16[1,272,128]{2,1,0:T(8,128)(2,1)S(1)}, bf16[1,272,128]{2,1,0:T(8,128)(2,1)S(1)}, u32[]{:S(2)}, u32[]{:S(2)}) %collective-permute-start.4) | collective-permute-done | bytes 69664 | tf_op jit(solution)/shard_map/ppermute | solution.py:268
  26.1 2.2 %collective-permute-start.5 = (bf16[2,272,128]{2,1,0:T(8,128)(2,1)S(1)}, bf16[2,272,128]{2,1,0:T(8,128)(2,1)S(1)}, u32[]{:S(2)}, u32[]{:S(2)}) collective-permute-start(bf16[2,272,128]{2,1,0:T(8,128)(2,1)S(1)} %join.6.refs_0_), channel_id=1, source_target_pairs={{0,16},{8,24},{16,0},{24,8},{1,17},{9,25},{17,1},{25,9},{2,18},{10... | collective-permute-start | bytes 417800 | tf_op jit(solution)/shard_map/ppermute | solution.py:268
  28.9 4.5 %collective-permute-done.10.refs_1_ = bf16[512,128]{1,0:T(8,128)(2,1)S(1)} collective-permute-done((bf16[512,128]{1,0:T(8,128)(2,1)S(1)}, bf16[512,128]{1,0:T(8,128)(2,1)S(1)}, u32[]{:S(2)}, u32[]{:S(2)}) %collective-permute-start.10) | collective-permute-done | bytes 131104 | tf_op jit(solution)/shard_map/ppermute | solution.py:268
  33.4 0.5 %collective-permute-start.14 = (bf16[4,272,128]{2,1,0:T(8,128)(2,1)S(1)}, bf16[4,272,128]{2,1,0:T(8,128)(2,1)S(1)}, u32[]{:S(2)}, u32[]{:S(2)}) collective-permute-start(bf16[4,272,128]{2,1,0:T(8,128)(2,1)S(1)} %join.10.refs_2_), channel_id=1, source_target_pairs={{0,8},{8,0},{16,24},{24,16},{1,9},{9,1},{17,25},{25,17},{2,10},{10... | collective-permute-start | bytes 835592 | tf_op jit(solution)/shard_map/ppermute | solution.py:268
  34.4 1.5 %collective-permute-done.11.refs_0_.refs_2_ = bf16[512,128]{1,0:T(8,128)(2,1)S(1)} collective-permute-done((bf16[512,128]{1,0:T(8,128)(2,1)S(1)}, bf16[512,128]{1,0:T(8,128)(2,1)S(1)}, u32[]{:S(2)}, u32[]{:S(2)}) %collective-permute-start.11) | collective-permute-done | bytes 131104 | tf_op jit(solution)/shard_map/ppermute | solution.py:268
  36.0 1.4 %collective-permute-start.12 = (bf16[512,128]{1,0:T(8,128)(2,1)S(1)}, bf16[512,128]{1,0:T(8,128)(2,1)S(1)}, u32[]{:S(2)}, u32[]{:S(2)}) collective-permute-start(bf16[512,128]{1,0:T(8,128)(2,1)S(1)} %join.8), channel_id=1, source_target_pairs={{0,1},{1,0},{2,3},{3,2},{4,5},{5,4},{6,7},{7,6},{8,9},{9,8},{10,11... | collective-permute-start | bytes 393224 | tf_op jit(solution)/shard_map/ppermute | solution.py:268
  37.5 2.8 %near_half.1 = (f32[512,1024]{1,0:T(8,128)S(1)}, bf16[1024,1024]{1,0:T(8,128)(2,1)S(1)}) custom-call(s32[9]{0:T(128)S(1)} %stack.24.where_ref, bf16[4,272,128]{2,1,0:T(8,128)(2,1)S(1)} %join.9.refs_0_, bf16[4,272,128]{2,1,0:T(8,128)(2,1)S(1)} %collective-permute-done.13.refs_1_, bf16[4,272,128]{2,1,0:T(8,128)(2,1)S(1)} %join.10.refs_2_, ...), custom_call_target="tpu_custom_call" | custom-call | flops 536870912 | bytes 8388608 | tf_op jit(solution)/shard_map/near_half/pallas_call | solution.py:196
  40.4 0.7 %collective-permute-done.12.refs_3_ = bf16[512,128]{1,0:T(8,128)(2,1)S(1)} collective-permute-done((bf16[512,128]{1,0:T(8,128)(2,1)S(1)}, bf16[512,128]{1,0:T(8,128)(2,1)S(1)}, u32[]{:S(2)}, u32[]{:S(2)}) %collective-permute-start.12) | collective-permute-done | bytes 131104 | tf_op jit(solution)/shard_map/ppermute | solution.py:268
  41.0 1.8 %far_half.1 = f32[512,1024]{1,0:T(8,128)} custom-call(bf16[512,128]{1,0:T(8,128)(2,1)S(1)} %collective-permute-done.2.refs_0_, bf16[512,128]{1,0:T(8,128)(2,1)S(1)} %collective-permute-done.10.refs_1_, bf16[512,128]{1,0:T(8,128)(2,1)S(1)} %collective-permute-done.11.refs_0_.refs_2_, bf16[512,128]{1,0:T(8,128)(2,1)S(1)} %collective-permute-done.12.refs_3_, ...), custom_call_target="tpu_custom_call" | custom-call | flops 536870912 | bytes 8388608 | tf_op jit(solution)/shard_map/far_half/pallas_call | solution.py:246
  (28 shorter events, 1.3 us)
Async XLA Ops:
  0.0 9.4 %collective-permute-start = (bf16[512,128]{1,0:T(8,128)(2,1)}, bf16[512,128]{1,0:T(8,128)(2,1)S(1)}, u32[]{:S(2)}, u32[]{:S(2)}) collective-permute-start(bf16[512,128]{1,0:T(8,128)(2,1)} %refs_11_.1), channel_id=1, source_target_pairs={{0,1},{1,0},{2,3},{3,2},{4,5},{5,4},{6,7},{7,6},{8,9},{9,8},{10,11... | collective-permute-start | bytes 393224 | tf_op jit(solution)/shard_map/ppermute | solution.py:268
  2.9 8.9 %collective-permute-start.1 = (bf16[512,128]{1,0:T(8,128)(2,1)}, bf16[512,128]{1,0:T(8,128)(2,1)S(1)}, u32[]{:S(2)}, u32[]{:S(2)}) collective-permute-start(bf16[512,128]{1,0:T(8,128)(2,1)} %refs_11_.1), channel_id=1, source_target_pairs={{0,2},{1,3},{2,0},{3,1},{4,6},{5,7},{6,4},{7,5},{8,10},{9,11},{10,... | collective-permute-start | bytes 393224 | tf_op jit(solution)/shard_map/ppermute | solution.py:268
  4.5 7.4 %collective-permute-start.2 = (bf16[512,128]{1,0:T(8,128)(2,1)}, bf16[512,128]{1,0:T(8,128)(2,1)S(1)}, u32[]{:S(2)}, u32[]{:S(2)}) collective-permute-start(bf16[512,128]{1,0:T(8,128)(2,1)} %refs_11_.1), channel_id=1, source_target_pairs={{0,4},{1,5},{2,6},{3,7},{4,0},{5,1},{6,2},{7,3},{8,12},{9,13},{10,... | collective-permute-start | bytes 393224 | tf_op jit(solution)/shard_map/ppermute | solution.py:268
  8.3 7.4 %collective-permute-start.15 = (bf16[1,272,128]{2,1,0:T(8,128)(2,1)S(1)}, bf16[1,272,128]{2,1,0:T(8,128)(2,1)S(1)}, u32[]{:S(2)}, u32[]{:S(2)}) collective-permute-start(bf16[1,272,128]{2,1,0:T(8,128)(2,1)S(1)} %bitcast.20), channel_id=1, source_target_pairs={{0,1},{1,0},{2,3},{3,2},{4,5},{5,4},{6,7},{7,6},{8,9},{9,8},{10,11... | collective-permute-start | bytes 208904 | tf_op jit(solution)/shard_map/ppermute | solution.py:268
  8.9 6.8 %collective-permute-start.16 = (bf16[1,272,128]{2,1,0:T(8,128)(2,1)S(1)}, bf16[1,272,128]{2,1,0:T(8,128)(2,1)S(1)}, u32[]{:S(2)}, u32[]{:S(2)}) collective-permute-start(bf16[1,272,128]{2,1,0:T(8,128)(2,1)S(1)} %bitcast.19), channel_id=1, source_target_pairs={{0,2},{1,3},{2,0},{3,1},{4,6},{5,7},{6,4},{7,5},{8,10},{9,11},{10,... | collective-permute-start | bytes 208904 | tf_op jit(solution)/shard_map/ppermute | solution.py:268
  9.4 6.4 %collective-permute-start.17 = (bf16[1,272,128]{2,1,0:T(8,128)(2,1)S(1)}, bf16[1,272,128]{2,1,0:T(8,128)(2,1)S(1)}, u32[]{:S(2)}, u32[]{:S(2)}) collective-permute-start(bf16[1,272,128]{2,1,0:T(8,128)(2,1)S(1)} %bitcast.18), channel_id=1, source_target_pairs={{0,3},{1,2},{2,1},{3,0},{4,7},{5,6},{6,5},{7,4},{8,11},{9,10},{10,... | collective-permute-start | bytes 208904 | tf_op jit(solution)/shard_map/ppermute | solution.py:268
  11.9 9.3 %collective-permute-start.6 = (bf16[1,272,128]{2,1,0:T(8,128)(2,1)S(1)}, bf16[1,272,128]{2,1,0:T(8,128)(2,1)S(1)}, u32[]{:S(2)}, u32[]{:S(2)}) collective-permute-start(bf16[1,272,128]{2,1,0:T(8,128)(2,1)S(1)} %bitcast.17), channel_id=1, source_target_pairs={{0,6},{1,7},{2,4},{3,5},{4,2},{5,3},{6,0},{7,1},{8,14},{9,15},{10,... | collective-permute-start | bytes 208904 | tf_op jit(solution)/shard_map/ppermute | solution.py:268
  15.7 7.4 %collective-permute-start.7 = (bf16[1,272,128]{2,1,0:T(8,128)(2,1)S(1)}, bf16[1,272,128]{2,1,0:T(8,128)(2,1)S(1)}, u32[]{:S(2)}, u32[]{:S(2)}) collective-permute-start(bf16[1,272,128]{2,1,0:T(8,128)(2,1)S(1)} %bitcast.16), channel_id=1, source_target_pairs={{0,7},{1,6},{2,5},{3,4},{4,3},{5,2},{6,1},{7,0},{8,15},{9,14},{10,... | collective-permute-start | bytes 208904 | tf_op jit(solution)/shard_map/ppermute | solution.py:268
  15.8 18.1 %collective-permute-start.18 = (bf16[4,272,128]{2,1,0:T(8,128)(2,1)S(1)}, bf16[4,272,128]{2,1,0:T(8,128)(2,1)S(1)}, u32[]{:S(2)}, u32[]{:S(2)}) collective-permute-start(bf16[4,272,128]{2,1,0:T(8,128)(2,1)S(1)} %join.11.refs_4_), channel_id=1, source_target_pairs={{0,16},{8,24},{16,0},{24,8},{1,17},{9,25},{17,1},{25,9},{2,18},{10... | collective-permute-start | bytes 835592 | tf_op jit(solution)/shard_map/ppermute | solution.py:268
  17.4 7.5 %collective-permute-start.3 = (bf16[1,272,128]{2,1,0:T(8,128)(2,1)S(1)}, bf16[1,272,128]{2,1,0:T(8,128)(2,1)S(1)}, u32[]{:S(2)}, u32[]{:S(2)}) collective-permute-start(bf16[1,272,128]{2,1,0:T(8,128)(2,1)S(1)} %bitcast.15), channel_id=1, source_target_pairs={{0,4},{1,5},{2,6},{3,7},{4,0},{5,1},{6,2},{7,3},{8,12},{9,13},{10,... | collective-permute-start | bytes 208904 | tf_op jit(solution)/shard_map/ppermute | solution.py:268
  19.5 6.6 %collective-permute-start.4 = (bf16[1,272,128]{2,1,0:T(8,128)(2,1)S(1)}, bf16[1,272,128]{2,1,0:T(8,128)(2,1)S(1)}, u32[]{:S(2)}, u32[]{:S(2)}) collective-permute-start(bf16[1,272,128]{2,1,0:T(8,128)(2,1)S(1)} %bitcast.14), channel_id=1, source_target_pairs={{0,5},{1,4},{2,7},{3,6},{4,1},{5,0},{6,3},{7,2},{8,13},{9,12},{10,... | collective-permute-start | bytes 208904 | tf_op jit(solution)/shard_map/ppermute | solution.py:268
  21.2 7.5 %collective-permute-start.9 = (bf16[512,128]{1,0:T(8,128)(2,1)S(1)}, bf16[512,128]{1,0:T(8,128)(2,1)S(1)}, u32[]{:S(2)}, u32[]{:S(2)}) collective-permute-start(bf16[512,128]{1,0:T(8,128)(2,1)S(1)} %collective-permute-done.1.refs_9_), channel_id=1, source_target_pairs={{0,1},{1,0},{2,3},{3,2},{4,5},{5,4},{6,7},{7,6},{8,9},{9,8},{10,11... | collective-permute-start | bytes 393224 | tf_op jit(solution)/shard_map/ppermute | solution.py:268
  23.1 10.2 %collective-permute-start.8 = (bf16[2,272,128]{2,1,0:T(8,128)(2,1)S(1)}, bf16[2,272,128]{2,1,0:T(8,128)(2,1)S(1)}, u32[]{:S(2)}, u32[]{:S(2)}) collective-permute-start(bf16[2,272,128]{2,1,0:T(8,128)(2,1)S(1)} %join.7.refs_1_), channel_id=1, source_target_pairs={{0,16},{8,24},{16,0},{24,8},{1,17},{9,25},{17,1},{25,9},{2,18},{10... | collective-permute-start | bytes 417800 | tf_op jit(solution)/shard_map/ppermute | solution.py:268
  26.1 7.2 %collective-permute-start.5 = (bf16[2,272,128]{2,1,0:T(8,128)(2,1)S(1)}, bf16[2,272,128]{2,1,0:T(8,128)(2,1)S(1)}, u32[]{:S(2)}, u32[]{:S(2)}) collective-permute-start(bf16[2,272,128]{2,1,0:T(8,128)(2,1)S(1)} %join.6.refs_0_), channel_id=1, source_target_pairs={{0,16},{8,24},{16,0},{24,8},{1,17},{9,25},{17,1},{25,9},{2,18},{10... | collective-permute-start | bytes 417800 | tf_op jit(solution)/shard_map/ppermute | solution.py:268
  28.4 5.0 %collective-permute-start.10 = (bf16[512,128]{1,0:T(8,128)(2,1)S(1)}, bf16[512,128]{1,0:T(8,128)(2,1)S(1)}, u32[]{:S(2)}, u32[]{:S(2)}) collective-permute-start(bf16[512,128]{1,0:T(8,128)(2,1)S(1)} %collective-permute-done.2.refs_0_), channel_id=1, source_target_pairs={{0,1},{1,0},{2,3},{3,2},{4,5},{5,4},{6,7},{7,6},{8,9},{9,8},{10,11... | collective-permute-start | bytes 393224 | tf_op jit(solution)/shard_map/ppermute | solution.py:268
  28.7 7.3 %collective-permute-start.11 = (bf16[512,128]{1,0:T(8,128)(2,1)S(1)}, bf16[512,128]{1,0:T(8,128)(2,1)S(1)}, u32[]{:S(2)}, u32[]{:S(2)}) collective-permute-start(bf16[512,128]{1,0:T(8,128)(2,1)S(1)} %collective-permute-done.1.refs_9_), channel_id=1, source_target_pairs={{0,4},{1,5},{2,6},{3,7},{4,0},{5,1},{6,2},{7,3},{8,12},{9,13},{10,... | collective-permute-start | bytes 393224 | tf_op jit(solution)/shard_map/ppermute | solution.py:268
  33.4 4.1 %collective-permute-start.13 = (bf16[4,272,128]{2,1,0:T(8,128)(2,1)S(1)}, bf16[4,272,128]{2,1,0:T(8,128)(2,1)S(1)}, u32[]{:S(2)}, u32[]{:S(2)}) collective-permute-start(bf16[4,272,128]{2,1,0:T(8,128)(2,1)S(1)} %join.9.refs_0_), channel_id=1, source_target_pairs={{0,8},{8,0},{16,24},{24,16},{1,9},{9,1},{17,25},{25,17},{2,10},{10... | collective-permute-start | bytes 835592 | tf_op jit(solution)/shard_map/ppermute | solution.py:268
  33.4 4.0 %collective-permute-start.14 = (bf16[4,272,128]{2,1,0:T(8,128)(2,1)S(1)}, bf16[4,272,128]{2,1,0:T(8,128)(2,1)S(1)}, u32[]{:S(2)}, u32[]{:S(2)}) collective-permute-start(bf16[4,272,128]{2,1,0:T(8,128)(2,1)S(1)} %join.10.refs_2_), channel_id=1, source_target_pairs={{0,8},{8,0},{16,24},{24,16},{1,9},{9,1},{17,25},{25,17},{2,10},{10... | collective-permute-start | bytes 835592 | tf_op jit(solution)/shard_map/ppermute | solution.py:268
  33.9 3.6 %collective-permute-start.19 = (bf16[4,272,128]{2,1,0:T(8,128)(2,1)S(1)}, bf16[4,272,128]{2,1,0:T(8,128)(2,1)S(1)}, u32[]{:S(2)}, u32[]{:S(2)}) collective-permute-start(bf16[4,272,128]{2,1,0:T(8,128)(2,1)S(1)} %join.11.refs_4_), channel_id=1, source_target_pairs={{0,8},{8,0},{16,24},{24,16},{1,9},{9,1},{17,25},{25,17},{2,10},{10... | collective-permute-start | bytes 835592 | tf_op jit(solution)/shard_map/ppermute | solution.py:268
  34.0 3.5 %collective-permute-start.20 = (bf16[4,272,128]{2,1,0:T(8,128)(2,1)S(1)}, bf16[4,272,128]{2,1,0:T(8,128)(2,1)S(1)}, u32[]{:S(2)}, u32[]{:S(2)}) collective-permute-start(bf16[4,272,128]{2,1,0:T(8,128)(2,1)S(1)} %collective-permute-done.18.refs_6_), channel_id=1, source_target_pairs={{0,8},{8,0},{16,24},{24,16},{1,9},{9,1},{17,25},{25,17},{2,10},{10... | collective-permute-start | bytes 835592 | tf_op jit(solution)/shard_map/ppermute | solution.py:268
  36.0 5.0 %collective-permute-start.12 = (bf16[512,128]{1,0:T(8,128)(2,1)S(1)}, bf16[512,128]{1,0:T(8,128)(2,1)S(1)}, u32[]{:S(2)}, u32[]{:S(2)}) collective-permute-start(bf16[512,128]{1,0:T(8,128)(2,1)S(1)} %join.8), channel_id=1, source_target_pairs={{0,1},{1,0},{2,3},{3,2},{4,5},{5,4},{6,7},{7,6},{8,9},{9,8},{10,11... | collective-permute-start | bytes 393224 | tf_op jit(solution)/shard_map/ppermute | solution.py:268

commit v16 on v15

--- a/solution.py
+++ b/solution.py
@@ -180,7 +180,7 @@
             at += 1
     own_copy.wait()
     res_copy.wait()
-    multiply(amp, block, 0, res, total, None, 4 * width)
+    multiply(amp, block, 0, res, total, None, block.shape[1])
 
 
 def near_half(where, pieces, amps, offsets, own, residual, capacity):

time: 43.1 us -> 43.1 us (level)
  no operation moved by 1% of the time
where the time goes in v16:
time: 43.1 us; the launch traced here: 42.9 us
  starting transfers between devices  27 us (63%)
  waiting for transfers between devices  9.73 us (23%)
  Pallas kernels  5.97 us (14%)
    ppermute x21, starting transfers between devices, exchange(): return lax.ppermute(x, axis, [(i, i ^ flip) for i in range(size)])  27 us
    ppermute x21, waiting for transfers between devices, exchange(): return lax.ppermute(x, axis, [(i, i ^ flip) for i in range(size)])  9.73 us
    pallas_call x1, Pallas kernels, near_half(): pl.pallas_call(functools.partial(near_kernel, n_pieces, offsets, capacity...  2.83 us
    pallas_call x1, Pallas kernels, far_half(): pl.pallas_call(functools.partial(far_kernel, offsets, depth // width), ou...  1.85 us
    pallas_call x1, Pallas kernels, pack(): pl.pallas_call(functools.partial(pack_kernel, columns, capacity), out_sha...  1.2 us
  transfers between devices with their start and end apart: 21, of which 7 were waited for; matrix products, arithmetic and copies ran while one was open for 0% of the time, Pallas kernels for 10%

profile of v16, /device:TPU:0, one launch (start us, length us, event | category | flops | bytes accessed | tf_op | source)
XLA Modules:
  0.0 42.9 jit_solution(15214169188318587833)
XLA Ops:
  0.0 2.9 %collective-permute-start = (bf16[512,128]{1,0:T(8,128)(2,1)}, bf16[512,128]{1,0:T(8,128)(2,1)S(1)}, u32[]{:S(2)}, u32[]{:S(2)}) collective-permute-start(bf16[512,128]{1,0:T(8,128)(2,1)} %refs_11_.1), channel_id=1, source_target_pairs={{0,1},{1,0},{2,3},{3,2},{4,5},{5,4},{6,7},{7,6},{8,9},{9,8},{10,11... | collective-permute-start | bytes 393224 | tf_op jit(solution)/shard_map/ppermute | solution.py:268
  2.9 1.6 %collective-permute-start.1 = (bf16[512,128]{1,0:T(8,128)(2,1)}, bf16[512,128]{1,0:T(8,128)(2,1)S(1)}, u32[]{:S(2)}, u32[]{:S(2)}) collective-permute-start(bf16[512,128]{1,0:T(8,128)(2,1)} %refs_11_.1), channel_id=1, source_target_pairs={{0,2},{1,3},{2,0},{3,1},{4,6},{5,7},{6,4},{7,5},{8,10},{9,11},{10,... | collective-permute-start | bytes 393224 | tf_op jit(solution)/shard_map/ppermute | solution.py:268
  4.5 2.6 %collective-permute-start.2 = (bf16[512,128]{1,0:T(8,128)(2,1)}, bf16[512,128]{1,0:T(8,128)(2,1)S(1)}, u32[]{:S(2)}, u32[]{:S(2)}) collective-permute-start(bf16[512,128]{1,0:T(8,128)(2,1)} %refs_11_.1), channel_id=1, source_target_pairs={{0,4},{1,5},{2,6},{3,7},{4,0},{5,1},{6,2},{7,3},{8,12},{9,13},{10,... | collective-permute-start | bytes 393224 | tf_op jit(solution)/shard_map/ppermute | solution.py:268
  7.1 1.2 %pack.1 = (bf16[272,128]{1,0:T(8,128)(2,1)S(1)}, bf16[272,128]{1,0:T(8,128)(2,1)S(1)}, bf16[272,128]{1,0:T(8,128)(2,1)S(1)}, bf16[272,128]{1,0:T(8,128)(2,1)S(1)...) custom-call(s32[1]{0:T(128)} %bitcast.me_ref, ...), custom_call_target="tpu_custom_call" | custom-call | tf_op jit(solution)/shard_map/pack/pallas_call | solution.py:66
  8.3 0.6 %collective-permute-start.15 = (bf16[1,272,128]{2,1,0:T(8,128)(2,1)S(1)}, bf16[1,272,128]{2,1,0:T(8,128)(2,1)S(1)}, u32[]{:S(2)}, u32[]{:S(2)}) collective-permute-start(bf16[1,272,128]{2,1,0:T(8,128)(2,1)S(1)} %bitcast.20), channel_id=1, source_target_pairs={{0,1},{1,0},{2,3},{3,2},{4,5},{5,4},{6,7},{7,6},{8,9},{9,8},{10,11... | collective-permute-start | bytes 208904 | tf_op jit(solution)/shard_map/ppermute | solution.py:268
  8.9 0.4 %collective-permute-start.16 = (bf16[1,272,128]{2,1,0:T(8,128)(2,1)S(1)}, bf16[1,272,128]{2,1,0:T(8,128)(2,1)S(1)}, u32[]{:S(2)}, u32[]{:S(2)}) collective-permute-start(bf16[1,272,128]{2,1,0:T(8,128)(2,1)S(1)} %bitcast.19), channel_id=1, source_target_pairs={{0,2},{1,3},{2,0},{3,1},{4,6},{5,7},{6,4},{7,5},{8,10},{9,11},{10,... | collective-permute-start | bytes 208904 | tf_op jit(solution)/shard_map/ppermute | solution.py:268
  9.4 2.5 %collective-permute-start.17 = (bf16[1,272,128]{2,1,0:T(8,128)(2,1)S(1)}, bf16[1,272,128]{2,1,0:T(8,128)(2,1)S(1)}, u32[]{:S(2)}, u32[]{:S(2)}) collective-permute-start(bf16[1,272,128]{2,1,0:T(8,128)(2,1)S(1)} %bitcast.18), channel_id=1, source_target_pairs={{0,3},{1,2},{2,1},{3,0},{4,7},{5,6},{6,5},{7,4},{8,11},{9,10},{10,... | collective-permute-start | bytes 208904 | tf_op jit(solution)/shard_map/ppermute | solution.py:268
  11.9 3.8 %collective-permute-start.6 = (bf16[1,272,128]{2,1,0:T(8,128)(2,1)S(1)}, bf16[1,272,128]{2,1,0:T(8,128)(2,1)S(1)}, u32[]{:S(2)}, u32[]{:S(2)}) collective-permute-start(bf16[1,272,128]{2,1,0:T(8,128)(2,1)S(1)} %bitcast.17), channel_id=1, source_target_pairs={{0,6},{1,7},{2,4},{3,5},{4,2},{5,3},{6,0},{7,1},{8,14},{9,15},{10,... | collective-permute-start | bytes 208904 | tf_op jit(solution)/shard_map/ppermute | solution.py:268
  15.8 1.6 %collective-permute-start.18 = (bf16[4,272,128]{2,1,0:T(8,128)(2,1)S(1)}, bf16[4,272,128]{2,1,0:T(8,128)(2,1)S(1)}, u32[]{:S(2)}, u32[]{:S(2)}) collective-permute-start(bf16[4,272,128]{2,1,0:T(8,128)(2,1)S(1)} %join.11.refs_4_), channel_id=1, source_target_pairs={{0,16},{8,24},{16,0},{24,8},{1,17},{9,25},{17,1},{25,9},{2,18},{10... | collective-permute-start | bytes 835592 | tf_op jit(solution)/shard_map/ppermute | solution.py:268
  17.4 2.1 %collective-permute-start.3 = (bf16[1,272,128]{2,1,0:T(8,128)(2,1)S(1)}, bf16[1,272,128]{2,1,0:T(8,128)(2,1)S(1)}, u32[]{:S(2)}, u32[]{:S(2)}) collective-permute-start(bf16[1,272,128]{2,1,0:T(8,128)(2,1)S(1)} %bitcast.15), channel_id=1, source_target_pairs={{0,4},{1,5},{2,6},{3,7},{4,0},{5,1},{6,2},{7,3},{8,12},{9,13},{10,... | collective-permute-start | bytes 208904 | tf_op jit(solution)/shard_map/ppermute | solution.py:268
  19.5 1.7 %collective-permute-start.4 = (bf16[1,272,128]{2,1,0:T(8,128)(2,1)S(1)}, bf16[1,272,128]{2,1,0:T(8,128)(2,1)S(1)}, u32[]{:S(2)}, u32[]{:S(2)}) collective-permute-start(bf16[1,272,128]{2,1,0:T(8,128)(2,1)S(1)} %bitcast.14), channel_id=1, source_target_pairs={{0,5},{1,4},{2,7},{3,6},{4,1},{5,0},{6,3},{7,2},{8,13},{9,12},{10,... | collective-permute-start | bytes 208904 | tf_op jit(solution)/shard_map/ppermute | solution.py:268
  21.2 0.6 %collective-permute-start.9 = (bf16[512,128]{1,0:T(8,128)(2,1)S(1)}, bf16[512,128]{1,0:T(8,128)(2,1)S(1)}, u32[]{:S(2)}, u32[]{:S(2)}) collective-permute-start(bf16[512,128]{1,0:T(8,128)(2,1)S(1)} %collective-permute-done.1.refs_9_), channel_id=1, source_target_pairs={{0,1},{1,0},{2,3},{3,2},{4,5},{5,4},{6,7},{7,6},{8,9},{9,8},{10,11... | collective-permute-start | bytes 393224 | tf_op jit(solution)/shard_map/ppermute | solution.py:268
  21.8 1.3 %collective-permute-done.7.refs_1_ = bf16[1,272,128]{2,1,0:T(8,128)(2,1)S(1)} collective-permute-done((bf16[1,272,128]{2,1,0:T(8,128)(2,1)S(1)}, bf16[1,272,128]{2,1,0:T(8,128)(2,1)S(1)}, u32[]{:S(2)}, u32[]{:S(2)}) %collective-permute-start.7) | collective-permute-done | bytes 69664 | tf_op jit(solution)/shard_map/ppermute | solution.py:268
  23.1 1.3 %collective-permute-start.8 = (bf16[2,272,128]{2,1,0:T(8,128)(2,1)S(1)}, bf16[2,272,128]{2,1,0:T(8,128)(2,1)S(1)}, u32[]{:S(2)}, u32[]{:S(2)}) collective-permute-start(bf16[2,272,128]{2,1,0:T(8,128)(2,1)S(1)} %join.7.refs_1_), channel_id=1, source_target_pairs={{0,16},{8,24},{16,0},{24,8},{1,17},{9,25},{17,1},{25,9},{2,18},{10... | collective-permute-start | bytes 417800 | tf_op jit(solution)/shard_map/ppermute | solution.py:268
  24.4 0.4 %collective-permute-done.3.refs_0_ = bf16[1,272,128]{2,1,0:T(8,128)(2,1)S(1)} collective-permute-done((bf16[1,272,128]{2,1,0:T(8,128)(2,1)S(1)}, bf16[1,272,128]{2,1,0:T(8,128)(2,1)S(1)}, u32[]{:S(2)}, u32[]{:S(2)}) %collective-permute-start.3) | collective-permute-done | bytes 69664 | tf_op jit(solution)/shard_map/ppermute | solution.py:268
  24.9 1.2 %collective-permute-done.4.refs_1_ = bf16[1,272,128]{2,1,0:T(8,128)(2,1)S(1)} collective-permute-done((bf16[1,272,128]{2,1,0:T(8,128)(2,1)S(1)}, bf16[1,272,128]{2,1,0:T(8,128)(2,1)S(1)}, u32[]{:S(2)}, u32[]{:S(2)}) %collective-permute-start.4) | collective-permute-done | bytes 69664 | tf_op jit(solution)/shard_map/ppermute | solution.py:268
  26.1 2.2 %collective-permute-start.5 = (bf16[2,272,128]{2,1,0:T(8,128)(2,1)S(1)}, bf16[2,272,128]{2,1,0:T(8,128)(2,1)S(1)}, u32[]{:S(2)}, u32[]{:S(2)}) collective-permute-start(bf16[2,272,128]{2,1,0:T(8,128)(2,1)S(1)} %join.6.refs_0_), channel_id=1, source_target_pairs={{0,16},{8,24},{16,0},{24,8},{1,17},{9,25},{17,1},{25,9},{2,18},{10... | collective-permute-start | bytes 417800 | tf_op jit(solution)/shard_map/ppermute | solution.py:268
  28.9 4.5 %collective-permute-done.10.refs_1_ = bf16[512,128]{1,0:T(8,128)(2,1)S(1)} collective-permute-done((bf16[512,128]{1,0:T(8,128)(2,1)S(1)}, bf16[512,128]{1,0:T(8,128)(2,1)S(1)}, u32[]{:S(2)}, u32[]{:S(2)}) %collective-permute-start.10) | collective-permute-done | bytes 131104 | tf_op jit(solution)/shard_map/ppermute | solution.py:268
  33.4 0.5 %collective-permute-start.14 = (bf16[4,272,128]{2,1,0:T(8,128)(2,1)S(1)}, bf16[4,272,128]{2,1,0:T(8,128)(2,1)S(1)}, u32[]{:S(2)}, u32[]{:S(2)}) collective-permute-start(bf16[4,272,128]{2,1,0:T(8,128)(2,1)S(1)} %join.10.refs_2_), channel_id=1, source_target_pairs={{0,8},{8,0},{16,24},{24,16},{1,9},{9,1},{17,25},{25,17},{2,10},{10... | collective-permute-start | bytes 835592 | tf_op jit(solution)/shard_map/ppermute | solution.py:268
  34.4 1.5 %collective-permute-done.11.refs_0_.refs_2_ = bf16[512,128]{1,0:T(8,128)(2,1)S(1)} collective-permute-done((bf16[512,128]{1,0:T(8,128)(2,1)S(1)}, bf16[512,128]{1,0:T(8,128)(2,1)S(1)}, u32[]{:S(2)}, u32[]{:S(2)}) %collective-permute-start.11) | collective-permute-done | bytes 131104 | tf_op jit(solution)/shard_map/ppermute | solution.py:268
  36.0 1.4 %collective-permute-start.12 = (bf16[512,128]{1,0:T(8,128)(2,1)S(1)}, bf16[512,128]{1,0:T(8,128)(2,1)S(1)}, u32[]{:S(2)}, u32[]{:S(2)}) collective-permute-start(bf16[512,128]{1,0:T(8,128)(2,1)S(1)} %join.8), channel_id=1, source_target_pairs={{0,1},{1,0},{2,3},{3,2},{4,5},{5,4},{6,7},{7,6},{8,9},{9,8},{10,11... | collective-permute-start | bytes 393224 | tf_op jit(solution)/shard_map/ppermute | solution.py:268
  37.5 2.8 %near_half.1 = (f32[512,1024]{1,0:T(8,128)S(1)}, bf16[1024,1024]{1,0:T(8,128)(2,1)S(1)}) custom-call(s32[9]{0:T(128)S(1)} %stack.24.where_ref, bf16[4,272,128]{2,1,0:T(8,128)(2,1)S(1)} %join.9.refs_0_, bf16[4,272,128]{2,1,0:T(8,128)(2,1)S(1)} %collective-permute-done.13.refs_1_, bf16[4,272,128]{2,1,0:T(8,128)(2,1)S(1)} %join.10.refs_2_, ...), custom_call_target="tpu_custom_call" | custom-call | flops 536870912 | bytes 8388608 | tf_op jit(solution)/shard_map/near_half/pallas_call | solution.py:196
  40.4 0.7 %collective-permute-done.12.refs_3_ = bf16[512,128]{1,0:T(8,128)(2,1)S(1)} collective-permute-done((bf16[512,128]{1,0:T(8,128)(2,1)S(1)}, bf16[512,128]{1,0:T(8,128)(2,1)S(1)}, u32[]{:S(2)}, u32[]{:S(2)}) %collective-permute-start.12) | collective-permute-done | bytes 131104 | tf_op jit(solution)/shard_map/ppermute | solution.py:268
  41.0 1.8 %far_half.1 = f32[512,1024]{1,0:T(8,128)} custom-call(bf16[512,128]{1,0:T(8,128)(2,1)S(1)} %collective-permute-done.2.refs_0_, bf16[512,128]{1,0:T(8,128)(2,1)S(1)} %collective-permute-done.10.refs_1_, bf16[512,128]{1,0:T(8,128)(2,1)S(1)} %collective-permute-done.11.refs_0_.refs_2_, bf16[512,128]{1,0:T(8,128)(2,1)S(1)} %collective-permute-done.12.refs_3_, ...), custom_call_target="tpu_custom_call" | custom-call | flops 536870912 | bytes 8388608 | tf_op jit(solution)/shard_map/far_half/pallas_call | solution.py:246
  (28 shorter events, 1.3 us)
Async XLA Ops:
  0.0 9.4 %collective-permute-start = (bf16[512,128]{1,0:T(8,128)(2,1)}, bf16[512,128]{1,0:T(8,128)(2,1)S(1)}, u32[]{:S(2)}, u32[]{:S(2)}) collective-permute-start(bf16[512,128]{1,0:T(8,128)(2,1)} %refs_11_.1), channel_id=1, source_target_pairs={{0,1},{1,0},{2,3},{3,2},{4,5},{5,4},{6,7},{7,6},{8,9},{9,8},{10,11... | collective-permute-start | bytes 393224 | tf_op jit(solution)/shard_map/ppermute | solution.py:268
  2.9 8.9 %collective-permute-start.1 = (bf16[512,128]{1,0:T(8,128)(2,1)}, bf16[512,128]{1,0:T(8,128)(2,1)S(1)}, u32[]{:S(2)}, u32[]{:S(2)}) collective-permute-start(bf16[512,128]{1,0:T(8,128)(2,1)} %refs_11_.1), channel_id=1, source_target_pairs={{0,2},{1,3},{2,0},{3,1},{4,6},{5,7},{6,4},{7,5},{8,10},{9,11},{10,... | collective-permute-start | bytes 393224 | tf_op jit(solution)/shard_map/ppermute | solution.py:268
  4.5 7.4 %collective-permute-start.2 = (bf16[512,128]{1,0:T(8,128)(2,1)}, bf16[512,128]{1,0:T(8,128)(2,1)S(1)}, u32[]{:S(2)}, u32[]{:S(2)}) collective-permute-start(bf16[512,128]{1,0:T(8,128)(2,1)} %refs_11_.1), channel_id=1, source_target_pairs={{0,4},{1,5},{2,6},{3,7},{4,0},{5,1},{6,2},{7,3},{8,12},{9,13},{10,... | collective-permute-start | bytes 393224 | tf_op jit(solution)/shard_map/ppermute | solution.py:268
  8.3 7.4 %collective-permute-start.15 = (bf16[1,272,128]{2,1,0:T(8,128)(2,1)S(1)}, bf16[1,272,128]{2,1,0:T(8,128)(2,1)S(1)}, u32[]{:S(2)}, u32[]{:S(2)}) collective-permute-start(bf16[1,272,128]{2,1,0:T(8,128)(2,1)S(1)} %bitcast.20), channel_id=1, source_target_pairs={{0,1},{1,0},{2,3},{3,2},{4,5},{5,4},{6,7},{7,6},{8,9},{9,8},{10,11... | collective-permute-start | bytes 208904 | tf_op jit(solution)/shard_map/ppermute | solution.py:268
  8.9 6.8 %collective-permute-start.16 = (bf16[1,272,128]{2,1,0:T(8,128)(2,1)S(1)}, bf16[1,272,128]{2,1,0:T(8,128)(2,1)S(1)}, u32[]{:S(2)}, u32[]{:S(2)}) collective-permute-start(bf16[1,272,128]{2,1,0:T(8,128)(2,1)S(1)} %bitcast.19), channel_id=1, source_target_pairs={{0,2},{1,3},{2,0},{3,1},{4,6},{5,7},{6,4},{7,5},{8,10},{9,11},{10,... | collective-permute-start | bytes 208904 | tf_op jit(solution)/shard_map/ppermute | solution.py:268
  9.4 6.4 %collective-permute-start.17 = (bf16[1,272,128]{2,1,0:T(8,128)(2,1)S(1)}, bf16[1,272,128]{2,1,0:T(8,128)(2,1)S(1)}, u32[]{:S(2)}, u32[]{:S(2)}) collective-permute-start(bf16[1,272,128]{2,1,0:T(8,128)(2,1)S(1)} %bitcast.18), channel_id=1, source_target_pairs={{0,3},{1,2},{2,1},{3,0},{4,7},{5,6},{6,5},{7,4},{8,11},{9,10},{10,... | collective-permute-start | bytes 208904 | tf_op jit(solution)/shard_map/ppermute | solution.py:268
  11.9 9.3 %collective-permute-start.6 = (bf16[1,272,128]{2,1,0:T(8,128)(2,1)S(1)}, bf16[1,272,128]{2,1,0:T(8,128)(2,1)S(1)}, u32[]{:S(2)}, u32[]{:S(2)}) collective-permute-start(bf16[1,272,128]{2,1,0:T(8,128)(2,1)S(1)} %bitcast.17), channel_id=1, source_target_pairs={{0,6},{1,7},{2,4},{3,5},{4,2},{5,3},{6,0},{7,1},{8,14},{9,15},{10,... | collective-permute-start | bytes 208904 | tf_op jit(solution)/shard_map/ppermute | solution.py:268
  15.7 7.4 %collective-permute-start.7 = (bf16[1,272,128]{2,1,0:T(8,128)(2,1)S(1)}, bf16[1,272,128]{2,1,0:T(8,128)(2,1)S(1)}, u32[]{:S(2)}, u32[]{:S(2)}) collective-permute-start(bf16[1,272,128]{2,1,0:T(8,128)(2,1)S(1)} %bitcast.16), channel_id=1, source_target_pairs={{0,7},{1,6},{2,5},{3,4},{4,3},{5,2},{6,1},{7,0},{8,15},{9,14},{10,... | collective-permute-start | bytes 208904 | tf_op jit(solution)/shard_map/ppermute | solution.py:268
  15.8 18.1 %collective-permute-start.18 = (bf16[4,272,128]{2,1,0:T(8,128)(2,1)S(1)}, bf16[4,272,128]{2,1,0:T(8,128)(2,1)S(1)}, u32[]{:S(2)}, u32[]{:S(2)}) collective-permute-start(bf16[4,272,128]{2,1,0:T(8,128)(2,1)S(1)} %join.11.refs_4_), channel_id=1, source_target_pairs={{0,16},{8,24},{16,0},{24,8},{1,17},{9,25},{17,1},{25,9},{2,18},{10... | collective-permute-start | bytes 835592 | tf_op jit(solution)/shard_map/ppermute | solution.py:268
  17.4 7.5 %collective-permute-start.3 = (bf16[1,272,128]{2,1,0:T(8,128)(2,1)S(1)}, bf16[1,272,128]{2,1,0:T(8,128)(2,1)S(1)}, u32[]{:S(2)}, u32[]{:S(2)}) collective-permute-start(bf16[1,272,128]{2,1,0:T(8,128)(2,1)S(1)} %bitcast.15), channel_id=1, source_target_pairs={{0,4},{1,5},{2,6},{3,7},{4,0},{5,1},{6,2},{7,3},{8,12},{9,13},{10,... | collective-permute-start | bytes 208904 | tf_op jit(solution)/shard_map/ppermute | solution.py:268
  19.5 6.6 %collective-permute-start.4 = (bf16[1,272,128]{2,1,0:T(8,128)(2,1)S(1)}, bf16[1,272,128]{2,1,0:T(8,128)(2,1)S(1)}, u32[]{:S(2)}, u32[]{:S(2)}) collective-permute-start(bf16[1,272,128]{2,1,0:T(8,128)(2,1)S(1)} %bitcast.14), channel_id=1, source_target_pairs={{0,5},{1,4},{2,7},{3,6},{4,1},{5,0},{6,3},{7,2},{8,13},{9,12},{10,... | collective-permute-start | bytes 208904 | tf_op jit(solution)/shard_map/ppermute | solution.py:268
  21.2 7.5 %collective-permute-start.9 = (bf16[512,128]{1,0:T(8,128)(2,1)S(1)}, bf16[512,128]{1,0:T(8,128)(2,1)S(1)}, u32[]{:S(2)}, u32[]{:S(2)}) collective-permute-start(bf16[512,128]{1,0:T(8,128)(2,1)S(1)} %collective-permute-done.1.refs_9_), channel_id=1, source_target_pairs={{0,1},{1,0},{2,3},{3,2},{4,5},{5,4},{6,7},{7,6},{8,9},{9,8},{10,11... | collective-permute-start | bytes 393224 | tf_op jit(solution)/shard_map/ppermute | solution.py:268
  23.1 10.2 %collective-permute-start.8 = (bf16[2,272,128]{2,1,0:T(8,128)(2,1)S(1)}, bf16[2,272,128]{2,1,0:T(8,128)(2,1)S(1)}, u32[]{:S(2)}, u32[]{:S(2)}) collective-permute-start(bf16[2,272,128]{2,1,0:T(8,128)(2,1)S(1)} %join.7.refs_1_), channel_id=1, source_target_pairs={{0,16},{8,24},{16,0},{24,8},{1,17},{9,25},{17,1},{25,9},{2,18},{10... | collective-permute-start | bytes 417800 | tf_op jit(solution)/shard_map/ppermute | solution.py:268
  26.1 7.2 %collective-permute-start.5 = (bf16[2,272,128]{2,1,0:T(8,128)(2,1)S(1)}, bf16[2,272,128]{2,1,0:T(8,128)(2,1)S(1)}, u32[]{:S(2)}, u32[]{:S(2)}) collective-permute-start(bf16[2,272,128]{2,1,0:T(8,128)(2,1)S(1)} %join.6.refs_0_), channel_id=1, source_target_pairs={{0,16},{8,24},{16,0},{24,8},{1,17},{9,25},{17,1},{25,9},{2,18},{10... | collective-permute-start | bytes 417800 | tf_op jit(solution)/shard_map/ppermute | solution.py:268
  28.4 5.0 %collective-permute-start.10 = (bf16[512,128]{1,0:T(8,128)(2,1)S(1)}, bf16[512,128]{1,0:T(8,128)(2,1)S(1)}, u32[]{:S(2)}, u32[]{:S(2)}) collective-permute-start(bf16[512,128]{1,0:T(8,128)(2,1)S(1)} %collective-permute-done.2.refs_0_), channel_id=1, source_target_pairs={{0,1},{1,0},{2,3},{3,2},{4,5},{5,4},{6,7},{7,6},{8,9},{9,8},{10,11... | collective-permute-start | bytes 393224 | tf_op jit(solution)/shard_map/ppermute | solution.py:268
  28.7 7.3 %collective-permute-start.11 = (bf16[512,128]{1,0:T(8,128)(2,1)S(1)}, bf16[512,128]{1,0:T(8,128)(2,1)S(1)}, u32[]{:S(2)}, u32[]{:S(2)}) collective-permute-start(bf16[512,128]{1,0:T(8,128)(2,1)S(1)} %collective-permute-done.1.refs_9_), channel_id=1, source_target_pairs={{0,4},{1,5},{2,6},{3,7},{4,0},{5,1},{6,2},{7,3},{8,12},{9,13},{10,... | collective-permute-start | bytes 393224 | tf_op jit(solution)/shard_map/ppermute | solution.py:268
  33.4 4.1 %collective-permute-start.13 = (bf16[4,272,128]{2,1,0:T(8,128)(2,1)S(1)}, bf16[4,272,128]{2,1,0:T(8,128)(2,1)S(1)}, u32[]{:S(2)}, u32[]{:S(2)}) collective-permute-start(bf16[4,272,128]{2,1,0:T(8,128)(2,1)S(1)} %join.9.refs_0_), channel_id=1, source_target_pairs={{0,8},{8,0},{16,24},{24,16},{1,9},{9,1},{17,25},{25,17},{2,10},{10... | collective-permute-start | bytes 835592 | tf_op jit(solution)/shard_map/ppermute | solution.py:268
  33.4 4.0 %collective-permute-start.14 = (bf16[4,272,128]{2,1,0:T(8,128)(2,1)S(1)}, bf16[4,272,128]{2,1,0:T(8,128)(2,1)S(1)}, u32[]{:S(2)}, u32[]{:S(2)}) collective-permute-start(bf16[4,272,128]{2,1,0:T(8,128)(2,1)S(1)} %join.10.refs_2_), channel_id=1, source_target_pairs={{0,8},{8,0},{16,24},{24,16},{1,9},{9,1},{17,25},{25,17},{2,10},{10... | collective-permute-start | bytes 835592 | tf_op jit(solution)/shard_map/ppermute | solution.py:268
  33.9 3.6 %collective-permute-start.19 = (bf16[4,272,128]{2,1,0:T(8,128)(2,1)S(1)}, bf16[4,272,128]{2,1,0:T(8,128)(2,1)S(1)}, u32[]{:S(2)}, u32[]{:S(2)}) collective-permute-start(bf16[4,272,128]{2,1,0:T(8,128)(2,1)S(1)} %join.11.refs_4_), channel_id=1, source_target_pairs={{0,8},{8,0},{16,24},{24,16},{1,9},{9,1},{17,25},{25,17},{2,10},{10... | collective-permute-start | bytes 835592 | tf_op jit(solution)/shard_map/ppermute | solution.py:268
  34.0 3.5 %collective-permute-start.20 = (bf16[4,272,128]{2,1,0:T(8,128)(2,1)S(1)}, bf16[4,272,128]{2,1,0:T(8,128)(2,1)S(1)}, u32[]{:S(2)}, u32[]{:S(2)}) collective-permute-start(bf16[4,272,128]{2,1,0:T(8,128)(2,1)S(1)} %collective-permute-done.18.refs_6_), channel_id=1, source_target_pairs={{0,8},{8,0},{16,24},{24,16},{1,9},{9,1},{17,25},{25,17},{2,10},{10... | collective-permute-start | bytes 835592 | tf_op jit(solution)/shard_map/ppermute | solution.py:268
  36.0 5.0 %collective-permute-start.12 = (bf16[512,128]{1,0:T(8,128)(2,1)S(1)}, bf16[512,128]{1,0:T(8,128)(2,1)S(1)}, u32[]{:S(2)}, u32[]{:S(2)}) collective-permute-start(bf16[512,128]{1,0:T(8,128)(2,1)S(1)} %join.8), channel_id=1, source_target_pairs={{0,1},{1,0},{2,3},{3,2},{4,5},{5,4},{6,7},{7,6},{8,9},{9,8},{10,11... | collective-permute-start | bytes 393224 | tf_op jit(solution)/shard_map/ppermute | solution.py:268
